TPU v7x, 128 devices: a whole 4x4x4 slice. The times are simulated.
128 devices in a mesh: expert: 16 (over z, y), tensor: 8 (over x, core).
Axes of the slice: x: 4, y: 4, z: 4, core: 2. Of those that a mesh axis runs over, the one named last changes fastest.
Arguments:
- conv_input: bfloat16 [1024, 8192], P('expert', 'tensor'), may hold values from -6 to 6
- gate_input: bfloat16 [1024, 8192], P('expert', 'tensor'), may hold values from -6 to 6
- conv_cache: bfloat16 [320, 3, 8192], P('expert', None, 'tensor'), may hold values from -6 to 6
- state_cache: float32 [320, 16, 8192], P('expert', None, 'tensor'), may hold values from -6 to 6
- span_lengths: int32 [16, 4], P('expert'), may hold values from 1 to 28, 48 in all within a row
- span_resumes: int32 [16, 4], P('expert'), may hold values from 0 to 1
- slot_index: int32 [16, 20], P('expert'), may hold values from 0 to 19, each once within a row
- conv_weight: float32 [4, 8192], P(None, 'tensor'), may hold values from -3 to 3
- conv_bias: float32 [8192], P('tensor'), may hold values from -3 to 3
- rank_weight: bfloat16 [8192, 512], P('tensor'), may hold values from -0.0625 to 0.0625
- state_weight: bfloat16 [8192, 32], P('tensor'), may hold values from -0.0625 to 0.0625
- step_gain: float32 [512], replicated, may hold values from 0.1 to 1.9
- step_weight: bfloat16 [512, 8192], P(None, 'tensor'), may hold values from -0.25 to 0.25
- step_bias: float32 [8192], P('tensor'), may hold values from -6.9 to -2.3
- decay_log: float32 [16, 8192], P(None, 'tensor'), may hold values from 0 to 2.77
- skip_gain: float32 [8192], P('tensor'), may hold values from 0.5 to 1.5
- out_weight: bfloat16 [8192, 4096], P('tensor'), may hold values from -0.09375 to 0.09375
- residual: bfloat16 [1024, 4096], P('expert', 'tensor'), may hold values from -8 to 8
- moe_gain: float32 [4096], P('tensor'), may hold values from 0.1 to 1.9
- router_weight: bfloat16 [4096, 4], P('tensor'), may hold values from -0.09375 to 0.09375
- chosen_experts: int32 [1024, 2], P('expert'), may hold values from 0 to 3, all different within a row; in each aligned block of 64 rows (0 to 63, 64 to 127, ...) at most 48 rows name the same one
- gate_weight: bfloat16 [16, 4096, 3072], P('expert', None, 'tensor'), may hold values from -0.09375 to 0.09375
- up_weight: bfloat16 [16, 4096, 3072], P('expert', None, 'tensor'), may hold values from -0.09375 to 0.09375
- down_weight: bfloat16 [16, 3072, 4096], P('expert', 'tensor'), may hold values from -0.078125 to 0.078125
Outputs:
- mixed: bfloat16 [1024, 4096], P('expert', 'tensor')
- new_state_cache: float32 [320, 16, 8192], P('expert', None, 'tensor')
- new_conv_cache: bfloat16 [320, 3, 8192], P('expert', None, 'tensor')
Inputs may be any that keep to these rules, and one draw needn't show every extreme that they name: `chosen_experts`: the rows of one row group name each expert at most 48 times; some expert is named exactly 48 times by some group; every expert is named somewhere. `span_lengths`: a group's 4 lengths sum to 48. `slot_index`: each group's row is an ordering of its 20 cache rows.
All inputs are finite; a program needn't handle non-finite values.
Results may differ from a plain program's by a relative error of at most 0.012.
Values may be sent and summed in bfloat16 or wider, within the bound.
No kernel may reach another device: no remote copies, remote signals or barrier semaphores. Data moves between devices by JAX's collectives and lax.ppermute only.
A program may use at most 128 MiB of HBM per device.

v0:
```python
import jax
import jax.numpy as jnp
from jax import lax
from jax.sharding import PartitionSpec as P

DEC_DEV = 16


norm_eps = 1e-06


def row_layout(span_row, resume_row, row_count):
    lengths = jnp.concatenate([jnp.ones((DEC_DEV,), jnp.int32), span_row])
    resumes = jnp.concatenate([jnp.ones((DEC_DEV,), jnp.int32), resume_row])
    ends = jnp.cumsum(lengths)
    starts = ends - lengths
    row_number = jnp.arange(row_count, dtype=jnp.int32)
    segment = jnp.sum((row_number[:, None] >= ends[None, :]).astype(jnp.int32), axis=1)
    member = (segment[:, None] == jnp.arange(lengths.shape[0], dtype=jnp.int32)[None, :]).astype(
        jnp.int32
    )
    position = row_number - jnp.sum(member * starts[None, :], axis=1)
    return (lengths, resumes, starts, segment, position)


def convolve(conv_input, cached_raw, resumes, segment, position, conv_weight, conv_bias):
    taps = conv_weight.shape[0]
    values = conv_input.astype(jnp.float32)
    cached = cached_raw.astype(jnp.float32) * resumes.astype(jnp.float32)[:, None, None]
    total = conv_bias[None, :] + conv_weight[taps - 1][None, :] * values
    for lag in range(1, taps):
        shifted = jnp.concatenate(
            [jnp.zeros((lag, values.shape[1]), jnp.float32), values[:-lag]], axis=0
        )
        older = cached[segment, jnp.clip(taps - 1 + position - lag, 0, taps - 2)]
        total = total + conv_weight[taps - 1 - lag][None, :] * jnp.where(
            (position >= lag)[:, None], shifted, older
        )
    return jax.nn.silu(total).astype(jnp.bfloat16)


def conv_tail(conv_input, cached_raw, lengths, starts, resumes, taps, row_count):
    pieces = []
    sequence = jnp.arange(lengths.shape[0], dtype=jnp.int32)
    for offset in range(taps - 1):
        back = lengths - (taps - 1) + offset
        from_rows = conv_input[jnp.clip(starts + back, 0, row_count - 1)]
        from_cache = cached_raw[sequence, jnp.clip(back + taps - 1, 0, taps - 2)]
        from_cache = jnp.where(resumes[:, None] > 0, from_cache, jnp.zeros_like(from_cache))
        pieces.append(jnp.where((back >= 0)[:, None], from_rows, from_cache))
    return jnp.stack(pieces, axis=1)


def link(earlier, later):
    return (later[0] * earlier[0], later[0] * earlier[1] + later[1])


def per_device(
    conv_input,
    gate_input,
    conv_cache,
    state_cache,
    span_lengths,
    span_resumes,
    slot_index,
    conv_weight,
    conv_bias,
    rank_weight,
    state_weight,
    step_gain,
    step_weight,
    step_bias,
    decay_log,
    skip_gain,
    out_weight,
    residual,
    moe_gain,
    router_weight,
    chosen_experts,
    gate_weight,
    up_weight,
    down_weight,
):
    row_count = conv_input.shape[0]
    taps = conv_weight.shape[0]
    slots = slot_index[0]
    lengths, resumes, starts, segment, position = row_layout(
        span_lengths[0], span_resumes[0], row_count
    )
    cached_raw = conv_cache[slots]
    mixed_x = convolve(conv_input, cached_raw, resumes, segment, position, conv_weight, conv_bias)
    low_part = jnp.dot(mixed_x, rank_weight, preferred_element_type=jnp.float32)
    state_part = jnp.dot(mixed_x, state_weight, preferred_element_type=jnp.float32)
    step_low, state_proj = lax.psum((low_part, state_part), "tensor")
    step_norm = (
        step_low
        * lax.rsqrt(jnp.mean(step_low * step_low, axis=1, keepdims=True) + norm_eps)
        * step_gain[None, :]
    ).astype(jnp.bfloat16)
    step = jax.nn.softplus(
        jnp.dot(step_norm, step_weight, preferred_element_type=jnp.float32) + step_bias[None, :]
    )
    nstate = decay_log.shape[0]
    input_b = state_proj[:, :nstate]
    output_c = state_proj[:, nstate:]
    values = mixed_x.astype(jnp.float32)
    rate = -jnp.exp(decay_log)
    decay = jnp.exp(step[:, None, :] * rate[None, :, :])
    drive = (step * values)[:, None, :] * input_b[:, :, None]
    initial = state_cache[slots] * resumes.astype(jnp.float32)[:, None, None]
    first = (position == 0)[:, None, None]
    factor = jnp.where(first, jnp.zeros_like(decay), decay)
    offset = jnp.where(first, decay * initial[segment] + drive, drive)
    factors, states = lax.associative_scan(link, (factor, offset), axis=0)
    output = jnp.sum(output_c[:, :, None] * states, axis=1) + skip_gain[None, :] * values
    gated = (output * jax.nn.silu(gate_input.astype(jnp.float32))).astype(jnp.bfloat16)
    finals = states[starts + lengths - 1]
    new_state = jnp.zeros_like(state_cache).at[slots].set(finals)
    new_conv = (
        jnp.zeros_like(conv_cache)
        .at[slots]
        .set(conv_tail(conv_input, cached_raw, lengths, starts, resumes, taps, row_count))
    )
    partial_value = jnp.dot(gated, out_weight, preferred_element_type=jnp.float32)
    mixer = lax.psum_scatter(partial_value, "tensor", scatter_dimension=1, tiled=True).astype(
        jnp.bfloat16
    )
    hidden = residual.astype(jnp.float32) + mixer.astype(jnp.float32)
    width = hidden.shape[1] * lax.axis_size("tensor")
    squares = lax.psum(jnp.sum(hidden * hidden, axis=1), "tensor")
    normed = (hidden * lax.rsqrt(squares[:, None] / width + norm_eps) * moe_gain[None, :]).astype(
        jnp.bfloat16
    )
    logits = lax.psum(jnp.dot(normed, router_weight, preferred_element_type=jnp.float32), "tensor")
    experts_n = router_weight.shape[1]
    pieces_n = lax.axis_size("expert") // experts_n
    marks_two = (
        chosen_experts[:, :, None] == jnp.arange(experts_n, dtype=jnp.int32)[None, None, :]
    ).astype(jnp.float32)
    chosen = jnp.sum(marks_two * logits[:, None, :], axis=2)
    route_first = jax.nn.sigmoid(chosen[:, 0] - chosen[:, 1])
    route_second = jax.nn.sigmoid(chosen[:, 1] - chosen[:, 0])
    capacity = row_count * 3 // 4
    flat_ids = chosen_experts.reshape(-1)
    marks = (flat_ids[:, None] == jnp.arange(experts_n, dtype=jnp.int32)[None, :]).astype(jnp.int32)
    earlier_count = jnp.cumsum(marks, axis=0) - marks
    place = jnp.sum(earlier_count * marks, axis=1)
    dest = flat_ids * capacity + place
    source_row = jnp.arange(flat_ids.shape[0], dtype=jnp.int32) // 2
    table = jnp.full((experts_n * capacity,), row_count, jnp.int32).at[dest].set(source_row)
    wide = lax.all_gather(normed, "tensor", axis=1, tiled=True)
    padded = jnp.concatenate([wide, jnp.zeros((1, wide.shape[1]), jnp.bfloat16)], axis=0)
    picked = padded[table].reshape(experts_n, 1, capacity, wide.shape[1])
    every = jnp.broadcast_to(picked, (experts_n, pieces_n, capacity, wide.shape[1]))
    received = lax.all_to_all(
        every.reshape(experts_n * pieces_n, capacity, wide.shape[1]),
        "expert",
        split_axis=0,
        concat_axis=0,
        tiled=True,
    )
    sources, count, full_width = received.shape
    flat_in = received.reshape(sources * count, full_width)
    gate = jnp.dot(flat_in, gate_weight[0], preferred_element_type=jnp.float32)
    upper = jnp.dot(flat_in, up_weight[0], preferred_element_type=jnp.float32)
    act = (jax.nn.silu(gate) * upper).astype(jnp.bfloat16)
    terms = jnp.dot(act, down_weight[0], preferred_element_type=jnp.float32).reshape(
        sources, count, full_width
    )
    reduced = lax.psum_scatter(terms, "tensor", scatter_dimension=2, tiled=True)
    returned = lax.all_to_all(reduced, "expert", split_axis=0, concat_axis=0, tiled=True)
    back_width = returned.shape[2]
    summed = jnp.sum(returned.reshape(experts_n, pieces_n, capacity, back_width), axis=1).reshape(
        experts_n * capacity, back_width
    )
    per_assign = summed[dest].reshape(row_count, 2, back_width)
    moe_part = route_first[:, None] * per_assign[:, 0] + route_second[:, None] * per_assign[:, 1]
    mixed = (hidden + moe_part).astype(jnp.bfloat16)
    return (mixed, new_state, new_conv)


def solution(mesh):
    return jax.shard_map(
        per_device,
        mesh=mesh,
        in_specs=(
            P("expert", "tensor"),
            P("expert", "tensor"),
            P("expert", None, "tensor"),
            P("expert", None, "tensor"),
            P("expert", None),
            P("expert", None),
            P("expert", None),
            P(None, "tensor"),
            P("tensor"),
            P("tensor", None),
            P("tensor", None),
            P(),
            P(None, "tensor"),
            P("tensor"),
            P(None, "tensor"),
            P("tensor"),
            P("tensor", None),
            P("expert", "tensor"),
            P("tensor"),
            P("tensor", None),
            P("expert", None),
            P("expert", None, "tensor"),
            P("expert", None, "tensor"),
            P("expert", "tensor", None),
        ),
        out_specs=(P("expert", "tensor"), P("expert", None, "tensor"), P("expert", None, "tensor")),
        check_vma=False,
    )
```

profile of v0, /device:TPU:0, one launch (start us, length us, event | category | flops | bytes accessed | tf_op | source)
XLA Modules:
  0.0 497.3 jit_solution(6401349079287425549)
XLA Ops:
  9.1 1.3 compare_select_fusion.9
  10.5 1.6 slice.263
  12.1 1.6 slice.264
  13.8 1.6 slice.262
  17.9 1.8 gather_fusion
  20.7 1.7 gather_fusion.3
  22.4 1.7 gather_fusion.2
  24.1 1.7 gather_fusion.1
  25.8 1.7 multiply_convert_fusion
  27.5 2.2 fusion.77
  30.0 25.7 %psum.28 = f32[64,32]{0,1:T(8,128)S(1)} all-reduce(f32[64,32]{0,1:T(8,128)S(1)} %fusion.76), channel_id=1, replica_groups=mesh['expert'=16,'tensor'=8] {'tensor'}, use_global_device_ids=true, to_apply=%region_3.4 | all-reduce | flops 2048 | bytes 16384 | tf_op jit(solution)/shard_map/psum | solution.py:94
  56.5 3.0 gather_fusion.4
  59.5 2.5 broadcast_multiply_fusion
  62.0 4.1 gather_fusion.5
  66.1 25.4 %all-reduce.20.cloned.1.call-done = f32[64,512]{1,0:T(8,128)} async-done(((f32[64,512]{1,0:T(8,128)}), f32[64,512]{1,0:T(8,128)}) %all-reduce.20.cloned.1.call-update) | async-done | bytes 131088 | tf_op jit(solution)/shard_map/psum | solution.py:94
  91.5 1.0 multiply_reduce_fusion.2
  92.6 1.7 convert_multiply_fusion.2
  94.3 3.3 fusion
  98.3 1.4 slice_multiply_fusion
  107.3 2.2 pad.46
  109.5 1.2 fusion.22
  110.7 1.7 add.402
  113.3 2.1 pad.47
  115.3 3.7 pad.48
  119.0 1.7 fusion.15
  122.5 5.7 %pad.49 = f32[16,16,1024]{2,1,0:T(8,128)} pad(f32[8,16,1024]{2,1,0:T(8,128)} %pad_maximum_fusion.2, f32[]{:T(128)} %constant.91.clone.1), padding=0_1_1x0_0_0x0_0_0 | pad | bytes 1572868 | tf_op jit(solution)/shard_map/pad | solution.py:114
  128.2 5.8 %pad.50 = f32[16,16,1024]{2,1,0:T(8,128)} pad(f32[8,16,1024]{2,1,0:T(8,128)} %add.404, f32[]{:T(128)} %constant.91.clone.1), padding=1_0_1x0_0_0x0_0_0 | pad | bytes 1572868 | tf_op jit(solution)/shard_map/pad | solution.py:114
  134.0 2.6 fusion.14
  136.7 1.1 add.406
  137.8 1.1 pad_maximum_fusion.1
  138.8 10.1 %pad.51 = f32[32,16,1024]{2,1,0:T(8,128)} pad(f32[16,16,1024]{2,1,0:T(8,128)} %pad_maximum_fusion.1, f32[]{:T(128)} %constant.91.clone.1), padding=0_1_1x0_0_0x0_0_0 | pad | bytes 3145732 | tf_op jit(solution)/shard_map/pad | solution.py:114
  149.0 10.1 %pad.52 = f32[32,16,1024]{2,1,0:T(8,128)} pad(f32[16,16,1024]{2,1,0:T(8,128)} %add.406, f32[]{:T(128)} %constant.91.clone.1), padding=1_0_1x0_0_0x0_0_0 | pad | bytes 3145732 | tf_op jit(solution)/shard_map/pad | solution.py:114
  159.1 4.5 fusion.7
  163.7 1.7 add.408
  165.4 1.5 pad_maximum_fusion
  166.9 18.4 %pad.53 = f32[64,16,1024]{2,1,0:T(8,128)} pad(f32[32,16,1024]{2,1,0:T(8,128)} %pad_maximum_fusion, f32[]{:T(128)} %constant.91.clone.1), padding=0_1_1x0_0_0x0_0_0 | pad | bytes 6291460 | tf_op jit(solution)/shard_map/pad | solution.py:114
  185.3 18.4 %pad.54 = f32[64,16,1024]{2,1,0:T(8,128)} pad(f32[32,16,1024]{2,1,0:T(8,128)} %add.408, f32[]{:T(128)} %constant.91.clone.1), padding=1_0_1x0_0_0x0_0_0 | pad | bytes 6291460 | tf_op jit(solution)/shard_map/pad | solution.py:114
  203.7 6.5 %multiply_reduce_fusion = (f32[64,1024]{1,0:T(8,128)S(1)}, f32[64,16,1024]{2,1,0:T(8,128)}) fusion(f32[64,16]{1,0:T(8,128)S(1)} %copy-done.23, f32[64,16,1024]{2,1,0:T(8,128)} %pad.53, f32[64,16,1024]{2,1,0:T(8,128)} %pad.54), kind=kLoop, calls=%fused_computation.19 | loop fusion | flops 3080192 | bytes 12849152 | tf_op jit(solution)/shard_map/reduce_sum | solution.py:115
  210.2 6.0 %fusion.23 = f32[64,4096]{1,0:T(8,128)} fusion(bf16[1024,4096]{1,0:T(8,128)(2,1)} %param.40, f32[64,1024]{1,0:T(8,128)S(1)} %get-tuple-element.11, bf16[64,1024]{1,0:T(8,128)(2,1)S(1)} %multiply_convert_fusion, bf16[64,1024]{1,0:T(8,128)(2,1)S(1)} %copy-done.19, f32[1024]{0:T(1024)S(1)} %copy-done.24), kind=kOutput, calls=%fused_computation.70 | convolution fusion | flops 537526272 | bytes 9965568 | tf_op jit(solution)/shard_map/dot_general | solution.py:124
  218.3 29.0 %reduce-scatter.3.cloned.1.call-done = f32[64,512]{1,0:T(8,128)} async-done(((f32[64,4096]{1,0:T(8,128)}), f32[64,512]{1,0:T(8,128)}) %reduce-scatter.3.cloned.1.call-update) | async-done | bytes 131088 | tf_op jit(solution)/shard_map/reduce_scatter | solution.py:125
  247.3 1.0 multiply_reduce_fusion.1
  248.3 12.7 %psum.30 = f32[64]{0:T(128)S(1)} all-reduce(f32[64]{0:T(128)S(1)} %multiply_reduce_fusion.1), channel_id=1, replica_groups=mesh['expert'=16,'tensor'=8] {'tensor'}, use_global_device_ids=true, to_apply=%region_9.10 | all-reduce | flops 64 | bytes 512 | tf_op jit(solution)/shard_map/psum | solution.py:130
  262.0 13.3 %all_gather.3 = bf16[64,4096]{1,0:T(8,128)(2,1)S(1)} all-gather(bf16[64,512]{1,0:T(8,128)(2,1)S(1)} %multiply_convert_fusion.1), channel_id=1, replica_groups=mesh['expert'=16,'tensor'=8] {'tensor'}, dimensions={1}, use_global_device_ids=true | all-gather | bytes 589824 | tf_op jit(solution)/shard_map/all_gather | solution.py:151
  276.2 5.4 %gather_fusion.6 = bf16[192,4096]{1,0:T(8,128)(2,1)} fusion(bf16[65,4096]{1,0:T(8,128)(2,1)} %concatenate.64, s32[1024]{0:T(1024)S(1)} %pad_clamp_fusion.5), kind=kCustom, calls=%fused_computation.6 | custom fusion | bytes 3146496 | tf_op jit(solution)/shard_map/gather | solution.py:153
  281.6 2.2 broadcast_in_dim.162
  283.7 81.0 %all_to_all.10 = bf16[16,48,4096]{2,1,0:T(8,128)(2,1)S(1)} all-to-all(bf16[16,48,4096]{2,1,0:T(8,128)(2,1)S(1)} %bitcast.122), channel_id=1, replica_groups=mesh['expert'=16,'tensor'=8] {'expert'}, dimensions={0} | all-to-all | bytes 12582912 | tf_op jit(solution)/shard_map/all_to_all | solution.py:155
  364.7 3.4 fusion.5
  368.2 3.5 fusion.11
  371.7 6.4 %fusion.1 = f32[16,48,4096]{2,1,0:T(8,128)} fusion(bf16[16,48,384]{2,1,0:T(8,128)(2,1)S(1)} %bitcast.127, bf16[1,384,4096]{2,1,0:T(8,128)(2,1)S(1)} %copy-done), kind=kOutput, calls=%fused_computation.22 | convolution fusion | flops 2415919104 | bytes 16318464 | tf_op jit(solution)/shard_map/dot_general | solution.py:167
  379.0 1.2 gather_fusion.13
  380.2 1.2 gather_fusion.9
  381.4 1.2 gather_fusion.11
  383.7 63.0 %reduce-scatter.5.cloned.1.call-done = f32[16,48,512]{2,1,0:T(8,128)} async-done(((f32[16,48,4096]{2,1,0:T(8,128)}), f32[16,48,512]{2,1,0:T(8,128)}) %reduce-scatter.5.cloned.1.call-update) | async-done | bytes 1572880 | tf_op jit(solution)/shard_map/reduce_scatter | solution.py:170
  446.6 7.0 %all-to-all-start.1 = ((f32[16,48,512]{2,1,0:T(8,128)}), f32[16,48,512]{2,1,0:T(8,128)}, u32[]{:S(2)}, u32[]{:S(2)}) async-start(f32[16,48,512]{2,1,0:T(8,128)} %reduce-scatter.5.cloned.1.call-done), calls=%async_computation.3 | async-start | bytes 3145728 | tf_op jit(solution)/shard_map/all_to_all | solution.py:171
  454.8 1.5 gather_fusion.14
  457.6 1.5 scatter_fusion.1
  460.5 3.9 gather_fusion.8
  464.4 1.2 broadcast_in_dim.163
  465.6 6.1 %scatter_fusion = f32[20,16,1024]{2,1,0:T(8,128)} fusion(f32[20,16,1024]{2,1,0:T(8,128)} %broadcast_in_dim.163, s32[20]{0:T(128)S(1)} %fusion.42, f32[20,16,1024]{2,1,0:T(8,128)} %gather_fusion.8), kind=kCustom, calls=%fused_computation.16 | custom fusion | bytes 3932240 | tf_op jit(solution)/shard_map/scatter | solution.py:118
  471.8 12.9 %psum.31 = f32[64,4]{0,1:T(4,128)S(1)} all-reduce(f32[64,4]{0,1:T(4,128)S(1)} %fusion.78), channel_id=1, replica_groups=mesh['expert'=16,'tensor'=8] {'tensor'}, use_global_device_ids=true, to_apply=%region_10.11 | all-reduce | flops 256 | bytes 2048 | tf_op jit(solution)/shard_map/psum | solution.py:134
  484.7 1.6 bitcast_reduce_fusion
  486.3 1.4 gather_fusion.7
  487.8 1.1 reshape.385
  489.1 1.7 fusion.28
  (168 shorter events, 27.4 us)
Async XLA Ops:
  7.2 364.5 %copy-start = (bf16[1,384,4096]{2,1,0:T(8,128)(2,1)S(1)}, bf16[1,384,4096]{2,1,0:T(8,128)(2,1)}, u32[]{:S(2)}) copy-start(bf16[1,384,4096]{2,1,0:T(8,128)(2,1)} %param.47) | copy-start | bytes 9437188
  7.2 10.7 %copy-start.9 = (bf16[20,3,1024]{2,0,1:T(8,128)(2,1)S(1)}, bf16[20,3,1024]{2,0,1:T(8,128)(2,1)}, u32[]{:S(2)}) copy-start(bf16[20,3,1024]{2,0,1:T(8,128)(2,1)} %param.26) | copy-start | bytes 368644
  7.2 84.3 %all-reduce.20.cloned.1.call-start = ((), (), s32[]{:S(2)}) async-start(), calls=%async_computation.4 | async-start | bytes 262144 | tf_op jit(solution)/shard_map/psum | solution.py:94
  22.4 3.4 copy-start.28
  25.8 4.0 copy-start.25
  25.8 4.0 copy-start.26
  29.7 217.5 %reduce-scatter.3.cloned.1.call-start = ((), (), s32[]{:S(2)}) async-start(), calls=%async_computation.5 | async-start | bytes 1179648 | tf_op jit(solution)/shard_map/reduce_scatter | solution.py:125
  62.0 30.5 %copy-start.29 = (f32[1024]{0:T(1024)S(1)}, f32[1024]{0:T(1024)}, u32[]{:S(2)}) copy-start(f32[1024]{0:T(1024)} %param.37) | copy-start | bytes 12292
  62.0 30.5 %copy-start.31 = (f32[512]{0:T(512)S(1)}, f32[512]{0:T(512)}, u32[]{:S(2)}) copy-start(f32[512]{0:T(512)} %param.35) | copy-start | bytes 6148
  97.6 2.9 copy-start.2
  97.6 3.7 copy-start.3
  101.2 1.4 copy-start.7
  101.2 2.0 copy-start.8
  103.2 1.6 copy-start.12
  103.2 1.6 copy-start.13
  104.0 0.8 copy-start.16
  104.0 1.0 copy-start.17
  119.0 1.7 copy-start.14
  119.0 1.8 copy-start.15
  119.0 2.6 copy-start.22
  134.0 2.6 copy-start.10
  134.0 2.7 copy-start.11
  136.7 1.1 copy-start.21
  159.1 4.5 copy-start.4
  159.1 4.6 copy-start.5
  163.7 1.7 copy-start.20
  185.3 18.4 %copy-start.23 = (f32[64,16]{1,0:T(8,128)S(1)}, f32[64,16]{1,0:T(8,128)}, u32[]{:S(2)}) copy-start(f32[64,16]{1,0:T(8,128)} %copy.61) | copy-start | bytes 12292
  203.7 6.5 %copy-start.19 = (bf16[64,1024]{1,0:T(8,128)(2,1)S(1)}, bf16[64,1024]{1,0:T(8,128)(2,1)}, u32[]{:S(2)}) copy-start(bf16[64,1024]{1,0:T(8,128)(2,1)} %param.25) | copy-start | bytes 393220
  203.7 6.5 %copy-start.24 = (f32[1024]{0:T(1024)S(1)}, f32[1024]{0:T(1024)}, u32[]{:S(2)}) copy-start(f32[1024]{0:T(1024)} %param.39) | copy-start | bytes 12292
  210.2 6.1 %copy-start.27 = (s32[64,2]{0,1:T(2,128)S(1)}, s32[64,2]{0,1:T(2,128)}, u32[]{:S(2)}) copy-start(s32[64,2]{0,1:T(2,128)} %param.44) | copy-start | bytes 1540
  210.2 37.0 %copy-start.18 = (bf16[64,512]{1,0:T(8,128)(2,1)S(1)}, bf16[64,512]{1,0:T(8,128)(2,1)}, u32[]{:S(2)}) copy-start(bf16[64,512]{1,0:T(8,128)(2,1)} %param.41) | copy-start | bytes 196612
  210.2 50.8 %copy-start.32 = (f32[512]{0:T(512)S(1)}, f32[512]{0:T(512)}, u32[]{:S(2)}) copy-start(f32[512]{0:T(512)} %param.42) | copy-start | bytes 6148
  216.3 230.4 %reduce-scatter.5.cloned.1.call-start = ((), (), s32[]{:S(2)}) async-start(), calls=%async_computation.6 | async-start | bytes 14155776 | tf_op jit(solution)/shard_map/reduce_scatter | solution.py:170
  217.3 1.0 copy-start.39
  283.7 81.0 %copy-start.41 = (bf16[1,4096,384]{2,1,0:T(8,128)(2,1)S(1)}, bf16[1,4096,384]{2,1,0:T(8,128)(2,1)}, u32[]{:S(2)}) copy-start(bf16[1,4096,384]{2,1,0:T(8,128)(2,1)} %param.45) | copy-start | bytes 9437188
  364.7 3.4 copy-start.42
  378.1 0.6 copy-start.36
  378.1 0.7 copy-start.35
  378.1 0.8 copy-start.34
  378.1 0.9 copy-start.33
  378.1 0.9 copy-start.1
  378.1 4.7 copy-start.6
  383.7 72.7 %copy-start.37 = (s32[1,4]{1,0:T(1,128)S(1)}, s32[1,4]{1,0:T(1,128)}, u32[]{:S(2)}) copy-start(s32[1,4]{1,0:T(1,128)} %param.28) | copy-start | bytes 52
  383.7 72.7 %copy-start.40 = (s32[1,4]{1,0:T(1,128)S(1)}, s32[1,4]{1,0:T(1,128)}, u32[]{:S(2)}) copy-start(s32[1,4]{1,0:T(1,128)} %param.29) | copy-start | bytes 52
  446.6 38.1 %all-to-all-start.1 = ((f32[16,48,512]{2,1,0:T(8,128)}), f32[16,48,512]{2,1,0:T(8,128)}, u32[]{:S(2)}, u32[]{:S(2)}) async-start(f32[16,48,512]{2,1,0:T(8,128)} %reduce-scatter.5.cloned.1.call-done), calls=%async_computation.3 | async-start | bytes 3145728 | tf_op jit(solution)/shard_map/all_to_all | solution.py:171
  453.7 6.8 %copy-start.38 = (s32[20]{0:T(128)S(1)}, s32[20]{0:T(128)}, u32[]{:S(2)}) copy-start(s32[20]{0:T(128)} %get-tuple-element.9) | copy-start | bytes 244
  465.6 6.1 %copy-start.30 = (bf16[512,4]{0,1:T(4,128)(2,1)S(1)}, bf16[512,4]{0,1:T(4,128)(2,1)}, u32[]{:S(2)}) copy-start(bf16[512,4]{0,1:T(4,128)(2,1)} %param.43) | copy-start | bytes 12292
Sparse Core Ops, SparseCore 0:
  29.9 61.6 all-reduce.19
  216.4 30.8 reduce-scatter.2
  378.2 68.3 reduce-scatter.4
where the time goes:
time: 503 us; the launch traced here: 497 us
  blocking collectives  146 us (29%)
  local copies, waits for them, and re-layouts  139 us (28%)
  waiting for transfers between devices  117 us (23%)
  other arithmetic  49.9 us (10%)
  matrix products  23.4 us (5%)
  between operations  14.3 us (3%)
  starting transfers between devices  7.16 us (1%)
    all_to_all x1, blocking collectives, per_device(): lax.all_to_all(every.reshape(experts_n * pieces_n, capacity, wide.shape[1...  81 us
    pad x10, local copies, waits for them, and re-layouts, per_device(): factors, states = lax.associative_scan(link, (factor, offset), axis=0)  77.4 us
    reduce_scatter x1, waiting for transfers between devices, per_device(): reduced = lax.psum_scatter(terms, 'tensor', scatter_dimension=2, tiled=True)  63 us
    reduce_scatter x1, waiting for transfers between devices, per_device(): lax.psum_scatter(partial_value, 'tensor', scatter_dimension=1, tiled=True)  29 us
    psum x1, blocking collectives, per_device(): step_low, state_proj = lax.psum((low_part, state_part), 'tensor')  25.7 us
    psum x1, waiting for transfers between devices, per_device(): step_low, state_proj = lax.psum((low_part, state_part), 'tensor')  25.4 us
    all_gather x1, blocking collectives, per_device(): wide = lax.all_gather(normed, 'tensor', axis=1, tiled=True)  13.3 us
    psum x1, blocking collectives, per_device(): lax.psum(jnp.dot(normed, router_weight, preferred_element_type=jnp.float3...  12.9 us
  transfers between devices with their start and end apart: 4, of which 3 were waited for; matrix products, arithmetic and copies ran while one was open for 7% of the time, Pallas kernels for 0%

commit v1 on v0

v1 whole, which is shorter than its diff:
```python
import functools

import jax
import jax.numpy as jnp
import numpy as np
from jax import lax
from jax.experimental import pallas as pl
from jax.experimental.pallas import tpu as pltpu
from jax.sharding import Mesh
from jax.sharding import PartitionSpec as P

DEC = 16
ROWS = 64
SEQ = 20
CAP = 48
NS = 16
TAPS = 4
EXPERTS = 4
EPS = 1e-6
BF = jnp.bfloat16
F32 = jnp.float32
I32 = jnp.int32
VMEM = pl.BlockSpec(memory_space=pltpu.VMEM)
SMEM = pl.BlockSpec(memory_space=pltpu.SMEM)
ANY = pl.BlockSpec(memory_space=pl.ANY)


def params(mib):
    return pltpu.CompilerParams(vmem_limit_bytes=mib * 1024 * 1024)


def iota(shape, dim):
    return lax.broadcasted_iota(I32, shape, dim)


def silu(v):
    return v / (1.0 + jnp.exp(-v))


def dot(a, b):
    return jnp.dot(a, b, preferred_element_type=F32)


def span_starts(span_ref):
    s1 = DEC + span_ref[0, 0]
    s2 = s1 + span_ref[0, 1]
    s3 = s2 + span_ref[0, 2]
    return (jnp.int32(DEC), s1, s2, s3)


def conv_kernel(
    span_ref, res_ref, slot_ref, x_ref, cache_ref, w_ref, b_ref, rank_ref, sw_ref,
    cx_ref, proj_ref, nc_ref, xc_ref,
):
    xc_ref[0:ROWS] = x_ref[...]
    xc_ref[ROWS : 2 * ROWS] = cache_ref[...]
    xc = xc_ref[...]
    starts = span_starts(span_ref)
    r = iota((ROWS, 128), 0)
    j = iota((ROWS, 128), 1)
    start = jnp.where(r < DEC, r, DEC)
    slot = jnp.full((ROWS, 128), slot_ref[0, DEC], I32)
    res = jnp.full((ROWS, 128), res_ref[0, 0], I32)
    for c in range(1, 4):
        inside = r >= starts[c]
        start = jnp.where(inside, starts[c], start)
        slot = jnp.where(inside, slot_ref[0, DEC + c], slot)
        res = jnp.where(inside, res_ref[0, c], res)
    for d in range(DEC):
        slot = jnp.where(r == d, slot_ref[0, d], slot)
    res = jnp.where(r < DEC, 1, res)
    pos = r - start
    total = b_ref[...] + w_ref[TAPS - 1 : TAPS] * x_ref[...].astype(F32)
    for lag in range(1, TAPS):
        older = jnp.where(res > 0, ROWS + slot * 3 + 3 + pos - lag, -1)
        pick = (j == jnp.where(pos >= lag, r - lag, older)).astype(BF)
        total = total + w_ref[TAPS - 1 - lag : TAPS - lag] * dot(pick, xc)
    cx = silu(total).astype(BF)
    cx_ref[...] = cx
    proj_ref[:, 0:512] = dot(cx, rank_ref[...]).astype(BF)
    proj_ref[:, 512:640] = jnp.zeros((ROWS, 128), BF)
    proj_ref[:, 512 : 512 + 2 * NS] = dot(cx, sw_ref[...]).astype(BF)
    group = (r * 171) >> 9
    offset = r - 3 * group
    length = jnp.ones((ROWS, 128), I32)
    first = jnp.zeros((ROWS, 128), I32)
    kept = jnp.ones((ROWS, 128), I32)
    for s in range(SEQ):
        here = group == slot_ref[0, s]
        if s < DEC:
            first = jnp.where(here, s, first)
        else:
            first = jnp.where(here, starts[s - DEC], first)
            length = jnp.where(here, span_ref[0, s - DEC], length)
            kept = jnp.where(here, res_ref[0, s - DEC], kept)
    back = length - 3 + offset
    older = jnp.where(kept > 0, ROWS + group * 3 + back + 3, -1)
    col = jnp.where(group < SEQ, jnp.where(back >= 0, first + back, older), -1)
    nc_ref[...] = dot((j == col).astype(BF), xc).astype(BF)


def scan_kernel(
    here_ref, span_ref, res_ref, slot_ref,
    q0_ref, q1_ref, q2_ref, q3_ref, cx_ref, z_ref, gain_ref, sw_ref, sb_ref, dl_ref, skip_ref,
    sc_ref, ow_ref,
    ns_ref, own_ref, sib_ref,
    w_vmem, step_ref, drive_ref, bb_ref, cb_ref, pc_ref, tr_ref, sem,
):
    fetch = pltpu.make_async_copy(ow_ref, w_vmem, sem)
    fetch.start()
    starts = span_starts(span_ref)
    proj = (
        q0_ref[...].astype(F32) + q1_ref[...].astype(F32)
        + q2_ref[...].astype(F32) + q3_ref[...].astype(F32)
    )
    low = proj[:, 0:512]
    mean = jnp.mean(low * low, axis=1, keepdims=True)
    norm = (low * lax.rsqrt(mean + EPS) * gain_ref[...]).astype(BF)
    pre = dot(norm, sw_ref[...]) + sb_ref[...]
    step = jnp.maximum(pre, 0.0) + jnp.log1p(jnp.exp(-jnp.abs(pre)))
    values = cx_ref[...].astype(F32)
    step_ref[...] = step
    drive_ref[...] = step * values
    tr_ref[0:ROWS] = proj[:, 512:640]
    tr_ref[ROWS : 2 * ROWS] = jnp.zeros((ROWS, 128), F32)
    turned = tr_ref[...].T
    for r in range(ROWS):
        bb_ref[r] = jnp.broadcast_to(turned[0:NS, r : r + 1], (NS, 128))
        cb_ref[r] = jnp.broadcast_to(turned[NS : 2 * NS, r : r + 1], (NS, 128))
    rate = -jnp.exp(dl_ref[...])
    groups = rate.shape[1] // 128

    def advance(r, state):
        c1 = (r >= starts[1]).astype(I32)
        c2 = (r >= starts[2]).astype(I32)
        c3 = (r >= starts[3]).astype(I32)
        piece = c1 + c2 + c3
        decode = r < DEC
        slot = slot_ref[0, jnp.where(decode, r, DEC + piece)]
        resumed = jnp.where(decode, 1, res_ref[0, piece])
        begins = (r <= DEC) | (r == starts[1]) | (r == starts[2]) | (r == starts[3])
        keep = jnp.where(begins, 0.0, 1.0).astype(F32)
        load = jnp.where(begins, resumed, 0).astype(F32)
        prior = state * keep + sc_ref[slot] * load
        decay = jnp.exp(step_ref[pl.ds(r, 1), :] * rate)
        b = jnp.concatenate([bb_ref[r]] * groups, axis=1)
        c = jnp.concatenate([cb_ref[r]] * groups, axis=1)
        fresh = decay * prior + drive_ref[pl.ds(r, 1), :] * b
        weighed = fresh * c
        pc_ref[r] = weighed[0:8] + weighed[8:16]
        ns_ref[slot] = fresh
        return fresh

    lax.fori_loop(0, ROWS, advance, jnp.zeros(rate.shape, F32), unroll=4)
    output = skip_ref[...] * values
    for k in range(8):
        output = output + pc_ref[:, k, :]
    gated = (output * silu(z_ref[...].astype(F32))).astype(BF)
    fetch.wait()
    x, c = here_ref[0], here_ref[1]
    for k in range(4):
        there = lax.rem(x + k, 4)
        for out, core in ((own_ref, c), (sib_ref, 1 - c)):
            cols = pl.ds(pl.multiple_of((2 * there + core) * 512, 512), 512)
            out[k] = dot(gated, w_vmem[:, cols]).astype(BF)


def pick_kernel(
    here_ref, q0_ref, q1_ref, q2_ref, q3_ref, resid_ref, gain_ref, router_ref, chosen_ref,
    hid_ref, pick_ref, stat_ref,
):
    mixer = (
        q0_ref[...].astype(F32) + q1_ref[...].astype(F32)
        + q2_ref[...].astype(F32) + q3_ref[...].astype(F32)
    ).astype(BF)
    hidden = resid_ref[...].astype(F32) + mixer.astype(F32)
    hid_ref[...] = hidden
    scaled = (hidden * gain_ref[...]).astype(BF)
    wide = scaled.astype(F32)
    lane = iota((ROWS, 128), 1)
    stat = jnp.where(lane == EXPERTS, jnp.sum(hidden * hidden, axis=1, keepdims=True), 0.0)
    for e in range(EXPERTS):
        part = jnp.sum(wide * router_ref[e : e + 1], axis=1, keepdims=True)
        stat = jnp.where(lane == e, part, stat)
    stat_ref[...] = stat
    before = (iota((ROWS, ROWS), 0) < iota((ROWS, ROWS), 1)).astype(BF)
    row = iota((CAP, ROWS), 0)
    z = here_ref[2]
    for k in range(EXPERTS):
        e = lax.rem(z + k, EXPERTS)
        marks = ((chosen_ref[0:1] == e) | (chosen_ref[1:2] == e)).astype(F32)
        marks = jnp.broadcast_to(marks, (8, ROWS))
        place = dot(marks.astype(BF), before).astype(I32)[0:1]
        hot = ((row == place) & (marks[0:1] > 0.0)).astype(BF)
        pick_ref[k] = dot(hot, scaled).astype(BF)


def gate_half(here_ref, core, x0_ref, x1_ref, gi_ref, wg_ref, wu_ref, acc_ref, sq_ref):
    x = here_ref[0]

    def step(k, carry):
        rows = pl.ds(pl.multiple_of((2 * lax.rem(x + 4 - k, 4) + core) * 512, 512), 512)
        wg, wu = wg_ref[rows, :], wu_ref[rows, :]
        inv = gi_ref[k]
        for h, block in ((0, x0_ref[:, k]), (1, x1_ref[k])):
            block = block.reshape(384, 512)
            acc_ref[h, :, 0:384] += dot(block, wg)
            acc_ref[h, :, 384:768] += dot(block, wu)
            wide = block.astype(F32)
            square = wide * wide * inv
            sq_ref[h] += square[:, 0:128] + square[:, 128:256] + square[:, 256:384] + square[:, 384:512]
        return carry

    lax.fori_loop(0, 4, step, 0)


def ffn_first(here_ref, x0_ref, x1_ref, gi_ref, wg_ref, wu_ref, acc_ref, sq_ref):
    acc_ref[...] = jnp.zeros_like(acc_ref)
    sq_ref[...] = jnp.zeros_like(sq_ref)
    gate_half(here_ref, here_ref[1], x0_ref, x1_ref, gi_ref, wg_ref, wu_ref, acc_ref, sq_ref)


def down_half(here_ref, core, act_ref, wd_ref, out0_ref, out1_ref):
    x = here_ref[0]

    def step(k, carry):
        cols = pl.ds(pl.multiple_of((2 * lax.rem(x + k, 4) + core) * 512, 512), 512)
        wd = wd_ref[:, cols]
        out0_ref[:, k] = dot(act_ref[0], wd).astype(BF).reshape(4, 96, 512)
        out1_ref[k] = dot(act_ref[1], wd).astype(BF).reshape(4, 96, 512)
        return carry

    lax.fori_loop(0, 4, step, 0)


def ffn_second(
    here_ref, x0_ref, x1_ref, gi_ref, wg_ref, wu_ref, wd_ref, acc_in, sq_in,
    act_ref, out0_ref, out1_ref, acc_ref, sq_ref,
):
    acc_ref[...] = acc_in[...]
    sq_ref[...] = sq_in[...]
    gate_half(here_ref, 1 - here_ref[1], x0_ref, x1_ref, gi_ref, wg_ref, wu_ref, acc_ref, sq_ref)
    for h in range(2):
        square = jnp.sum(sq_ref[h], axis=1, keepdims=True)
        scale = lax.rsqrt(square / 4096.0 + EPS)
        gate = acc_ref[h, :, 0:384] * scale
        act_ref[h] = (silu(gate) * (acc_ref[h, :, 384:768] * scale)).astype(BF)
    down_half(here_ref, 1 - here_ref[1], act_ref, wd_ref, out0_ref, out1_ref)


def ffn_third(here_ref, act_ref, wd_ref, out0_ref, out1_ref):
    down_half(here_ref, here_ref[1], act_ref, wd_ref, out0_ref, out1_ref)


def final_kernel(
    here_ref, r0_ref, r1_ref, r2_ref, r3_ref, s0_ref, s1_ref, s2_ref, s3_ref, hid_ref, chosen_ref,
    out_ref,
):
    stat = s0_ref[...] + s1_ref[...] + s2_ref[...] + s3_ref[...]
    scale = lax.rsqrt(stat[:, EXPERTS : EXPERTS + 1] / 4096.0 + EPS)
    e0, e1 = chosen_ref[:, 0:1], chosen_ref[:, 1:2]
    l0 = jnp.zeros((ROWS, 1), F32)
    l1 = jnp.zeros((ROWS, 1), F32)
    for e in range(EXPERTS):
        l0 = l0 + jnp.where(e0 == e, stat[:, e : e + 1], 0.0)
        l1 = l1 + jnp.where(e1 == e, stat[:, e : e + 1], 0.0)
    gap = (l0 - l1) * scale
    route0 = 1.0 / (1.0 + jnp.exp(-gap))
    route1 = 1.0 / (1.0 + jnp.exp(gap))
    before = (iota((ROWS, ROWS), 1) < iota((ROWS, ROWS), 0)).astype(BF)
    lane = iota((ROWS, CAP), 1)
    total = hid_ref[...]
    z = here_ref[2]
    for k, ret in enumerate((r0_ref, r1_ref, r2_ref, r3_ref)):
        e = lax.rem(z + k, EXPERTS)
        first, second = e0 == e, e1 == e
        marks = jnp.broadcast_to((first | second).astype(F32), (ROWS, 128))
        place = dot(before, marks.astype(BF)).astype(I32)[:, 0:CAP]
        hot = ((lane == place) & (marks[:, 0:CAP] > 0.0)).astype(BF)
        weight = jnp.where(first, route0, jnp.where(second, route1, 0.0))
        total = total + weight * dot(hot, ret[...])
    out_ref[...] = total.astype(BF)


def move(value, axis, shift):
    size = lax.axis_size(axis)
    return lax.ppermute(value, axis, [(i, (i + shift) % size) for i in range(size)])


def call(kernel, outs, ins, mib, scratch=(), flops=0, moved=0, name=None):
    single = not isinstance(outs, (list, tuple))
    return pl.pallas_call(
        kernel,
        out_shape=outs,
        in_specs=ins,
        out_specs=VMEM if single else [VMEM] * len(outs),
        scratch_shapes=list(scratch),
        compiler_params=params(mib),
        cost_estimate=pl.CostEstimate(flops=flops, bytes_accessed=moved, transcendentals=0),
        name=name,
    )


def shape(dims, dtype):
    return jax.ShapeDtypeStruct(dims, dtype)


def per_device(
    conv_input, gate_input, conv_cache, state_cache, span_lengths, span_resumes, slot_index,
    conv_weight, conv_bias, rank_weight, state_weight, step_gain, step_weight, step_bias,
    decay_log, skip_gain, out_weight, residual, moe_gain, router_weight, chosen_experts,
    gate_weight, up_weight, down_weight,
):
    here = jnp.stack(
        [lax.axis_index("x"), lax.axis_index("core"), lax.axis_index("z")]
    ).astype(I32)
    inverse = (1.0 / (moe_gain * moe_gain)).reshape(1, 512)
    inverse_sib = move(inverse, "core", 1)
    pair = jnp.concatenate([inverse, inverse_sib], axis=0)
    pairs = [pair] + [move(pair, "x", k) for k in (1, 2, 3)]
    inv_own = jnp.stack([p[0:1] for p in pairs])
    inv_sib = jnp.stack([p[1:2] for p in pairs])
    old = jnp.pad(conv_cache.reshape(SEQ * 3, 1024), ((0, 4), (0, 0)))
    cx, proj, new_conv = call(
        conv_kernel,
        [shape((ROWS, 1024), BF), shape((ROWS, 640), BF), shape((ROWS, 1024), BF)],
        [SMEM] * 3 + [VMEM] * 6,
        16,
        [pltpu.VMEM((128, 1024), BF)],
        flops=10**9,
        moved=2 * 10**6,
        name="conv",
    )(
        span_lengths, span_resumes, slot_index, conv_input, old, conv_weight,
        conv_bias.reshape(1, 1024), rank_weight, state_weight,
    )
    new_conv = new_conv[0 : SEQ * 3].reshape(SEQ, 3, 1024)
    chip = (proj.astype(F32) + move(proj, "core", 1).astype(F32)).astype(BF)
    parts = [chip] + [move(chip, "x", k) for k in (1, 2, 3)]
    new_state, own, sib = call(
        scan_kernel,
        [
            shape((SEQ, NS, 1024), F32),
            shape((4, ROWS, 512), BF),
            shape((4, ROWS, 512), BF),
        ],
        [SMEM] * 4 + [VMEM] * 12 + [ANY],
        32,
        [
            pltpu.VMEM((1024, 4096), BF),
            pltpu.VMEM((ROWS, 1024), F32),
            pltpu.VMEM((ROWS, 1024), F32),
            pltpu.VMEM((ROWS, NS, 128), F32),
            pltpu.VMEM((ROWS, NS, 128), F32),
            pltpu.VMEM((ROWS, 8, 1024), F32),
            pltpu.VMEM((128, 128), F32),
            pltpu.SemaphoreType.DMA,
        ],
        flops=10**9,
        moved=10**7,
        name="scan",
    )(
        here, span_lengths, span_resumes, slot_index, *parts, cx, gate_input,
        step_gain.reshape(1, 512), step_weight, step_bias.reshape(1, 1024), decay_log,
        skip_gain.reshape(1, 1024), state_cache, out_weight,
    )
    mixed = (own.astype(F32) + move(sib, "core", 1).astype(F32)).astype(BF)
    parts = [mixed[0]] + [move(mixed[k], "x", k) for k in (1, 2, 3)]
    hidden, picks, stat = call(
        pick_kernel,
        [shape((ROWS, 512), F32), shape((4, CAP, 512), BF), shape((ROWS, 128), F32)],
        [SMEM] + [VMEM] * 8,
        8,
        flops=10**8,
        moved=10**6,
        name="pick",
    )(
        here, *parts, residual, moe_gain.reshape(1, 512), router_weight.astype(F32).T,
        chosen_experts.T,
    )
    rows = [picks[0]] + [move(picks[k], "z", k) for k in (1, 2, 3)]
    half0 = jnp.concatenate(rows[0:2], axis=0)
    half1 = jnp.concatenate(rows[2:4], axis=0)
    half0 = jnp.stack([half0] + [move(half0, "x", k) for k in (1, 2, 3)])
    half1 = jnp.stack([half1] + [move(half1, "y", k) for k in (1, 2, 3)])
    stat = stat + move(stat, "core", 1)
    stats = [stat] + [move(stat, "x", k) for k in (1, 2, 3)]
    half0 = jnp.stack([half0] + [move(half0, "y", k) for k in (1, 2, 3)])
    half1 = jnp.stack([half1] + [move(half1, "x", k) for k in (1, 2, 3)])
    sib0, sib1 = move(half0, "core", 1), move(half1, "core", 1)
    acc, square = call(
        ffn_first,
        [shape((2, 384, 768), F32), shape((2, 384, 128), F32)],
        [SMEM] + [VMEM] * 5,
        28,
        flops=2 * 768 * 2048 * 768,
        moved=6 * 10**6,
        name="gate_own",
    )(here, half0, half1, inv_own, gate_weight[0], up_weight[0])
    act, sib0, sib1 = call(
        ffn_second,
        [shape((2, 384, 384), BF), shape((4, 4, 96, 512), BF), shape((4, 4, 96, 512), BF)],
        [SMEM] + [VMEM] * 8,
        40,
        [pltpu.VMEM((2, 384, 768), F32), pltpu.VMEM((2, 384, 128), F32)],
        flops=3 * 768 * 2048 * 768,
        moved=8 * 10**6,
        name="gate_sib",
    )(
        here, sib0, sib1, inv_sib, gate_weight[0], up_weight[0], down_weight[0], acc, square
    )
    own0, own1 = call(
        ffn_third,
        [shape((4, 4, 96, 512), BF), shape((4, 4, 96, 512), BF)],
        [SMEM] + [VMEM] * 2,
        24,
        flops=768 * 2048 * 768,
        moved=4 * 10**6,
        name="down_own",
    )(here, act, down_weight[0])
    back0, back1 = move(sib0, "core", 1), move(sib1, "core", 1)

    def join(values):
        total = values[0].astype(F32)
        for value in values[1:]:
            total = total + value.astype(F32)
        return total.astype(BF)

    back0 = join([own0, back0])
    back1 = join([own1, back1])
    back0 = join([back0[0]] + [move(back0[j], "y", 4 - j) for j in (1, 2, 3)])
    back1 = join([back1[0]] + [move(back1[k], "x", k) for k in (1, 2, 3)])
    back0 = join([back0[0]] + [move(back0[k], "x", k) for k in (1, 2, 3)])
    back1 = join([back1[0]] + [move(back1[j], "y", 4 - j) for j in (1, 2, 3)])
    returned = [back0[0:CAP], back0[CAP : 2 * CAP], back1[0:CAP], back1[CAP : 2 * CAP]]
    returned = [returned[0]] + [move(returned[k], "z", 4 - k) for k in (1, 2, 3)]
    out = call(
        final_kernel,
        shape((ROWS, 512), BF),
        [SMEM] + [VMEM] * 10,
        8,
        flops=10**8,
        moved=10**6,
        name="combine",
    )(here, *returned, *stats, hidden, chosen_experts)
    return (out, new_state, new_conv)


def solution(mesh):
    grid = Mesh(mesh.devices.reshape(4, 4, 4, 2), ("z", "y", "x", "core"))
    group, tensor = ("z", "y"), ("x", "core")
    return jax.shard_map(
        per_device,
        mesh=grid,
        in_specs=(
            P(group, tensor),
            P(group, tensor),
            P(group, None, tensor),
            P(group, None, tensor),
            P(group, None),
            P(group, None),
            P(group, None),
            P(None, tensor),
            P(tensor),
            P(tensor, None),
            P(tensor, None),
            P(),
            P(None, tensor),
            P(tensor),
            P(None, tensor),
            P(tensor),
            P(tensor, None),
            P(group, tensor),
            P(tensor),
            P(tensor, None),
            P(group, None),
            P(group, None, tensor),
            P(group, None, tensor),
            P(group, tensor, None),
        ),
        out_specs=(P(group, tensor), P(group, None, tensor), P(group, None, tensor)),
        check_vma=False,
    )
```

time: 503 us -> 181 us (0.36); the launches traced: 497 us -> 181 us
  blocking collectives: 146 us -> 0 us
  local copies, waits for them, and re-layouts: 139 us -> 12.3 us
  starting transfers between devices: 7.16 us -> 64.1 us
  other arithmetic: 49.9 us -> 2.44 us
  waiting for transfers between devices: 117 us -> 71.3 us
  Pallas kernels: 0 us -> 29.5 us
  matrix products: 23.4 us -> 0 us
  between operations: 14.3 us -> 1.15 us
    reduce_scatter x2 -> x0, waiting for transfers between devices: 91.9 us -> none  [the longest x1 63 us: per_device(): reduced = lax.psum_scatter(terms, 'tensor', scatter_dimension=2, tiled=True)]
    all_to_all x1 -> x0, blocking collectives: 81 us -> none  [per_device(): lax.all_to_all(every.reshape(experts_n * pieces_n, capacity, wide.shape[1...]
    pad x10 -> x1, local copies, waits for them, and re-layouts: 77.4 us -> 0.01 us  [per_device(): old = jnp.pad(conv_cache.reshape(SEQ * 3, 1024), ((0, 4), (0, 0)))]
    ppermute x0 -> x50, waiting for transfers between devices: none -> 71.3 us  [move(): lax.ppermute(value, axis, [(i, (i + shift) % size) for i in range(size)])]
    ppermute x0 -> x50, starting transfers between devices: none -> 64.1 us  [move(): lax.ppermute(value, axis, [(i, (i + shift) % size) for i in range(size)])]
    psum x3 -> x0, blocking collectives: 51.4 us -> none  [the longest x1 25.7 us: per_device(): step_low, state_proj = lax.psum((low_part, state_part), 'tensor')]
    gather x15 -> x0, local copies, waits for them, and re-layouts: 31.7 us -> none  [the longest x1 5.35 us: per_device(): picked = padded[table].reshape(experts_n, 1, capacity, wide.shape[1])]
    pallas_call x0 -> x7, Pallas kernels: none -> 29.5 us  [the longest x1 10.1 us: per_device(): call(ffn_second, [shape((2, 384, 384), BF), shape((4, 4, 96, 512), BF), s...]
  transfers between devices with their start and end apart: 4 -> 50, of which waited for: 3 -> 32; matrix products, arithmetic and copies ran while one was open for 7% -> 1% of each run, Pallas kernels for 0% -> 4%
where the time goes in v1:
time: 181 us
  waiting for transfers between devices  71.3 us (39%)
  starting transfers between devices  64.1 us (35%)
  Pallas kernels  29.5 us (16%)
  local copies, waits for them, and re-layouts  12.3 us (7%)
  other arithmetic  2.44 us (1%)
    ppermute x50, waiting for transfers between devices, move(): lax.ppermute(value, axis, [(i, (i + shift) % size) for i in range(size)])  71.3 us
    ppermute x50, starting transfers between devices, move(): lax.ppermute(value, axis, [(i, (i + shift) % size) for i in range(size)])  64.1 us
    unnamed x55, local copies, waits for them, and re-layouts  11.8 us
    pallas_call x1, Pallas kernels, per_device(): call(ffn_second, [shape((2, 384, 384), BF), shape((4, 4, 96, 512), BF), s...  10.1 us
    pallas_call x1, Pallas kernels, per_device(): call(scan_kernel, [shape((SEQ, NS, 1024), F32), shape((4, ROWS, 512), BF)...  7.27 us
    pallas_call x1, Pallas kernels, per_device(): call(ffn_first, [shape((2, 384, 768), F32), shape((2, 384, 128), F32)], [...  4.88 us
  transfers between devices with their start and end apart: 50, of which 32 were waited for; matrix products, arithmetic and copies ran while one was open for 1% of the time, Pallas kernels for 4%

profile of v1, /device:TPU:0, one launch (start us, length us, event | category | flops | bytes accessed | tf_op | source)
XLA Modules:
  0.0 180.9 jit_solution(13588479556621923459)
XLA Ops:
  0.6 1.0 copy.31
  1.8 1.0 copy.32.sw_ref
  4.8 1.2 copy-done.19
  6.0 0.9 copy-done.20
  8.4 1.2 conv.1
  9.7 1.3 collective-permute-done
  11.0 1.7 collective-permute-start.1
  12.6 2.7 %collective-permute-start.2 = (bf16[64,640]{1,0:T(8,128)(2,1)S(1)}, bf16[64,640]{1,0:T(8,128)(2,1)S(1)}, u32[]{:S(2)}, u32[]{:S(2)}) collective-permute-start(bf16[64,640]{1,0:T(8,128)(2,1)S(1)} %add_convert_fusion.3.q0_ref), channel_id=1, source_target_pairs={{0,4},{2,6},{4,0},{6,2},{1,5},{3,7},{5,1},{7,3},{8,12},{10,14},{12... | collective-permute-start | bytes 245768 | tf_op jit(solution)/shard_map/ppermute | solution.py:287
  15.3 1.4 collective-permute-start.3
  16.9 2.7 %collective-permute-done.2.q2_ref = bf16[64,640]{1,0:T(8,128)(2,1)S(1)} collective-permute-done((bf16[64,640]{1,0:T(8,128)(2,1)S(1)}, bf16[64,640]{1,0:T(8,128)(2,1)S(1)}, u32[]{:S(2)}, u32[]{:S(2)}) %collective-permute-start.2) | collective-permute-done | bytes 81952 | tf_op jit(solution)/shard_map/ppermute | solution.py:287
  19.9 3.4 %copy-done.2 = bf16[1024,4096]{1,0:T(8,128)(2,1)S(1)} copy-done((bf16[1024,4096]{1,0:T(8,128)(2,1)S(1)}, bf16[1024,4096]{1,0:T(8,128)(2,1)}, u32[]{:S(2)}) %copy-start.2) | copy-done | bytes 8388632
  23.3 7.3 %scan.1 = (f32[20,16,1024]{2,1,0:T(8,128)}, bf16[4,64,512]{2,1,0:T(8,128)(2,1)S(1)}, bf16[4,64,512]{2,1,0:T(8,128)(2,1)S(1)}) custom-call(s32[3]{0:T(128)S(1)} %pad_add_fusion.here_ref, s32[1,4]{1,0:T(1,128)S(1)} %copy-done.14, s32[1,4]{1,0:T(1,128)S(1)} %copy-done.16, s32[1,20]{1,0:T(1,128)S(1)} %copy-done.18, ...), custom_call_target="tpu_custom_call" | custom-call | flops 1000000000 | bytes 10000000 | tf_op jit(solution)/shard_map/scan/pallas_call | solution.py:340
  30.6 1.5 collective-permute-done.4
  32.3 1.1 collective-permute-start.5
  33.4 3.1 %collective-permute-start.6 = (bf16[64,512]{1,0:T(8,128)(2,1)S(1)}, bf16[64,512]{1,0:T(8,128)(2,1)S(1)}, u32[]{:S(2)}, u32[]{:S(2)}) collective-permute-start(bf16[64,512]{1,0:T(8,128)(2,1)S(1)} %get-tuple-element.58), channel_id=1, source_target_pairs={{0,4},{2,6},{4,0},{6,2},{1,5},{3,7},{5,1},{7,3},{8,12},{10,14},{12... | collective-permute-start | bytes 196616 | tf_op jit(solution)/shard_map/ppermute | solution.py:287
  36.4 0.9 collective-permute-start.7
  37.8 2.1 %collective-permute-done.6.q2_ref = bf16[64,512]{1,0:T(8,128)(2,1)S(1)} collective-permute-done((bf16[64,512]{1,0:T(8,128)(2,1)S(1)}, bf16[64,512]{1,0:T(8,128)(2,1)S(1)}, u32[]{:S(2)}, u32[]{:S(2)}) %collective-permute-start.6) | collective-permute-done | bytes 65568 | tf_op jit(solution)/shard_map/ppermute | solution.py:287
  40.7 1.2 pick.1
  42.0 3.9 %collective-permute-start.16 = (bf16[48,512]{1,0:T(8,128)(2,1)S(1)}, bf16[48,512]{1,0:T(8,128)(2,1)S(1)}, u32[]{:S(2)}, u32[]{:S(2)}) collective-permute-start(bf16[48,512]{1,0:T(8,128)(2,1)S(1)} %get-tuple-element.62), channel_id=1, source_target_pairs={{0,64},{32,96},{64,0},{96,32},{1,65},{33,97},{65,1},{97,33},{2,66}... | collective-permute-start | bytes 147464 | tf_op jit(solution)/shard_map/ppermute | solution.py:287
  46.6 1.4 collective-permute-done.16
  48.0 2.0 %collective-permute-done.17 = bf16[48,512]{1,0:T(8,128)(2,1)S(1)} collective-permute-done((bf16[48,512]{1,0:T(8,128)(2,1)S(1)}, bf16[48,512]{1,0:T(8,128)(2,1)S(1)}, u32[]{:S(2)}, u32[]{:S(2)}) %collective-permute-start.17) | collective-permute-done | bytes 49184 | tf_op jit(solution)/shard_map/ppermute | solution.py:287
  50.0 1.6 collective-permute-start.18
  51.6 2.9 %collective-permute-start.19 = (bf16[96,512]{1,0:T(8,128)(2,1)S(1)}, bf16[96,512]{1,0:T(8,128)(2,1)S(1)}, u32[]{:S(2)}, u32[]{:S(2)}) collective-permute-start(bf16[96,512]{1,0:T(8,128)(2,1)S(1)} %constant_dynamic-update-slice_fusion), channel_id=1, source_target_pairs={{0,16},{8,24},{16,0},{24,8},{1,17},{9,25},{17,1},{25,9},{2,18},{10... | collective-permute-start | bytes 294920 | tf_op jit(solution)/shard_map/ppermute | solution.py:287
  54.5 1.3 collective-permute-start.20
  55.8 1.0 collective-permute-start.8
  56.9 1.3 collective-permute-done.19
  58.1 1.0 collective-permute-done.20
  59.9 1.2 collective-permute-done.8
  61.9 2.9 %collective-permute-start.10 = (bf16[96,512]{1,0:T(8,128)(2,1)S(1)}, bf16[96,512]{1,0:T(8,128)(2,1)S(1)}, u32[]{:S(2)}, u32[]{:S(2)}) collective-permute-start(bf16[96,512]{1,0:T(8,128)(2,1)S(1)} %get-tuple-element.70), channel_id=1, source_target_pairs={{0,4},{2,6},{4,0},{6,2},{1,5},{3,7},{5,1},{7,3},{8,12},{10,14},{12... | collective-permute-start | bytes 294920 | tf_op jit(solution)/shard_map/ppermute | solution.py:287
  65.6 1.8 %collective-permute-start.22 = (bf16[4,96,512]{2,1,0:T(8,128)(2,1)S(1)}, bf16[4,96,512]{2,1,0:T(8,128)(2,1)S(1)}, u32[]{:S(2)}, u32[]{:S(2)}) collective-permute-start(bf16[4,96,512]{2,1,0:T(8,128)(2,1)S(1)} %get-tuple-element.54), channel_id=1, source_target_pairs={{0,4},{2,6},{4,0},{6,2},{1,5},{3,7},{5,1},{7,3},{8,12},{10,14},{12... | collective-permute-start | bytes 1179656 | tf_op jit(solution)/shard_map/ppermute | solution.py:287
  67.4 6.4 %collective-permute-done.9 = bf16[96,512]{1,0:T(8,128)(2,1)S(1)} collective-permute-done((bf16[96,512]{1,0:T(8,128)(2,1)S(1)}, bf16[96,512]{1,0:T(8,128)(2,1)S(1)}, u32[]{:S(2)}, u32[]{:S(2)}) %collective-permute-start.9) | collective-permute-done | bytes 98336 | tf_op jit(solution)/shard_map/ppermute | solution.py:287
  73.8 1.8 collective-permute-start.23
  75.5 1.2 collective-permute-done.10
  77.7 2.9 %collective-permute-start.13 = (bf16[4,96,512]{2,1,0:T(8,128)(2,1)S(1)}, bf16[4,96,512]{2,1,0:T(8,128)(2,1)S(1)}, u32[]{:S(2)}, u32[]{:S(2)}) collective-permute-start(bf16[4,96,512]{2,1,0:T(8,128)(2,1)S(1)} %get-tuple-element.56), channel_id=1, source_target_pairs={{0,16},{8,24},{16,0},{24,8},{1,17},{9,25},{17,1},{25,9},{2,18},{10... | collective-permute-start | bytes 1179656 | tf_op jit(solution)/shard_map/ppermute | solution.py:287
  80.6 1.1 collective-permute-start.14
  81.7 1.4 collective-permute-done.23
  83.4 2.5 %collective-permute-done.12 = bf16[4,96,512]{2,1,0:T(8,128)(2,1)S(1)} collective-permute-done((bf16[4,96,512]{2,1,0:T(8,128)(2,1)S(1)}, bf16[4,96,512]{2,1,0:T(8,128)(2,1)S(1)}, u32[]{:S(2)}, u32[]{:S(2)}) %collective-permute-start.12) | collective-permute-done | bytes 393248 | tf_op jit(solution)/shard_map/ppermute | solution.py:287
  85.9 4.7 %collective-permute-done.13 = bf16[4,96,512]{2,1,0:T(8,128)(2,1)S(1)} collective-permute-done((bf16[4,96,512]{2,1,0:T(8,128)(2,1)S(1)}, bf16[4,96,512]{2,1,0:T(8,128)(2,1)S(1)}, u32[]{:S(2)}, u32[]{:S(2)}) %collective-permute-start.13) | collective-permute-done | bytes 393248 | tf_op jit(solution)/shard_map/ppermute | solution.py:287
  91.8 2.9 %collective-permute-done.25 = f32[1,512]{1,0:T(1,128)S(1)} collective-permute-done((f32[1,512]{1,0:T(1,128)S(1)}, f32[1,512]{1,0:T(1,128)S(1)}, u32[]{:S(2)}, u32[]{:S(2)}) %collective-permute-start.25) | collective-permute-done | bytes 2080 | tf_op jit(solution)/shard_map/ppermute | solution.py:287
  94.8 3.3 %collective-permute-start.27 = (f32[2,512]{1,0:T(2,128)S(1)}, f32[2,512]{1,0:T(2,128)S(1)}, u32[]{:S(2)}, u32[]{:S(2)}) collective-permute-start(f32[2,512]{1,0:T(2,128)S(1)} %pad_maximum_fusion.7), channel_id=1, source_target_pairs={{0,4},{2,6},{4,0},{6,2},{1,5},{3,7},{5,1},{7,3},{8,12},{10,14},{12... | collective-permute-start | bytes 12296 | tf_op jit(solution)/shard_map/ppermute | solution.py:287
  98.1 1.5 collective-permute-done.26
  100.0 1.8 collective-permute-done.28
  101.8 4.9 %gate_own.1 = (f32[2,384,768]{2,1,0:T(8,128)S(1)}, f32[2,384,128]{2,1,0:T(8,128)S(1)}) custom-call(s32[3]{0:T(128)S(1)} %pad_add_fusion.here_ref, bf16[4,4,96,512]{3,2,1,0:T(8,128)(2,1)S(1)} %pad_maximum_fusion.x0_ref, bf16[4,4,96,512]{3,2,1,0:T(8,128)(2,1)S(1)} %pad_maximum_fusion.1.x1_ref, f32[4,1,512]{2,1,0:T(1,128)S(1)} %pad_maximum_fusion.6.gi_ref, ...), custom_call_target="tpu_custom_call" | custom-call | flops 2415919104 | bytes 6000000 | tf_op jit(solution)/shard_map/gate_own/pallas_call | solution.py:391
  106.7 10.1 %gate_sib.1 = (bf16[2,384,384]{2,1,0:T(8,128)(2,1)S(1)}, bf16[4,4,96,512]{3,2,1,0:T(8,128)(2,1)S(1)}, bf16[4,4,96,512]{3,2,1,0:T(8,128)(2,1)S(1)}) custom-call(s32[3]{0:T(128)S(1)} %pad_add_fusion.here_ref, bf16[4,4,96,512]{3,2,1,0:T(8,128)(2,1)S(1)} %collective-permute-done.15.x0_ref, bf16[4,4,96,512]{3,2,1,0:T(8,128)(2,1)S(1)} %collective-permute-done.24.x1_ref, ...), custom_call_target="tpu_custom_call" | custom-call | flops 3623878656 | bytes 8000000 | tf_op jit(solution)/shard_map/gate_sib/pallas_call | solution.py:400
  117.4 2.8 %down_own.1 = (bf16[4,4,96,512]{3,2,1,0:T(8,128)(2,1)S(1)}, bf16[4,4,96,512]{3,2,1,0:T(8,128)(2,1)S(1)}) custom-call(s32[3]{0:T(128)S(1)} %pad_add_fusion.here_ref, bf16[2,384,384]{2,1,0:T(8,128)(2,1)S(1)} %get-tuple-element.26.act_ref, bf16[384,4096]{1,0:T(8,128)(2,1)S(1)} %bitcast.114), custom_call_target="tpu_custom_call" | custom-call | flops 1207959552 | bytes 4000000 | tf_op jit(solution)/shard_map/down_own/pallas_call | solution.py:412
  120.3 2.2 %collective-permute-done.37 = bf16[4,4,96,512]{3,2,1,0:T(8,128)(2,1)S(1)} collective-permute-done((bf16[4,4,96,512]{3,2,1,0:T(8,128)(2,1)S(1)}, bf16[4,4,96,512]{3,2,1,0:T(8,128)(2,1)S(1)}, u32[]{:S(2)}, u32[]{:S(2)}) %collective-permute-start.37) | collective-permute-done | bytes 1572896 | tf_op jit(solution)/shard_map/ppermute | solution.py:287
  122.6 1.2 add_convert_fusion
  124.6 2.2 %collective-permute-start.39 = (bf16[4,96,512]{2,1,0:T(8,128)(2,1)S(1)}, bf16[4,96,512]{2,1,0:T(8,128)(2,1)S(1)}, u32[]{:S(2)}, u32[]{:S(2)}) collective-permute-start(bf16[4,96,512]{2,1,0:T(8,128)(2,1)S(1)} %get-tuple-element.43), channel_id=1, source_target_pairs={{0,4},{2,6},{4,0},{6,2},{1,5},{3,7},{5,1},{7,3},{8,12},{10,14},{12... | collective-permute-start | bytes 1179656 | tf_op jit(solution)/shard_map/ppermute | solution.py:287
  126.8 1.3 collective-permute-start.40
  128.1 1.2 collective-permute-done.46
  130.1 2.7 %collective-permute-start.30 = (bf16[4,96,512]{2,1,0:T(8,128)(2,1)S(1)}, bf16[4,96,512]{2,1,0:T(8,128)(2,1)S(1)}, u32[]{:S(2)}, u32[]{:S(2)}) collective-permute-start(bf16[4,96,512]{2,1,0:T(8,128)(2,1)S(1)} %get-tuple-element.44), channel_id=1, source_target_pairs={{0,24},{8,0},{16,8},{24,16},{1,25},{9,1},{17,9},{25,17},{2,26},{10... | collective-permute-start | bytes 1179656 | tf_op jit(solution)/shard_map/ppermute | solution.py:287
  132.8 12.3 %collective-permute-done.38 = bf16[4,96,512]{2,1,0:T(8,128)(2,1)S(1)} collective-permute-done((bf16[4,96,512]{2,1,0:T(8,128)(2,1)S(1)}, bf16[4,96,512]{2,1,0:T(8,128)(2,1)S(1)}, u32[]{:S(2)}, u32[]{:S(2)}) %collective-permute-start.38) | collective-permute-done | bytes 393248 | tf_op jit(solution)/shard_map/ppermute | solution.py:287
  145.0 2.0 %collective-permute-start.31 = (bf16[4,96,512]{2,1,0:T(8,128)(2,1)S(1)}, bf16[4,96,512]{2,1,0:T(8,128)(2,1)S(1)}, u32[]{:S(2)}, u32[]{:S(2)}) collective-permute-start(bf16[4,96,512]{2,1,0:T(8,128)(2,1)S(1)} %get-tuple-element.46), channel_id=1, source_target_pairs={{0,16},{8,24},{16,0},{24,8},{1,17},{9,25},{17,1},{25,9},{2,18},{10... | collective-permute-start | bytes 1179656 | tf_op jit(solution)/shard_map/ppermute | solution.py:287
  147.7 2.8 %collective-permute-start.41 = (bf16[96,512]{1,0:T(8,128)(2,1)S(1)}, bf16[96,512]{1,0:T(8,128)(2,1)S(1)}, u32[]{:S(2)}, u32[]{:S(2)}) collective-permute-start(bf16[96,512]{1,0:T(8,128)(2,1)S(1)} %get-tuple-element.47), channel_id=1, source_target_pairs={{0,24},{8,0},{16,8},{24,16},{1,25},{9,1},{17,9},{25,17},{2,26},{10... | collective-permute-start | bytes 294920 | tf_op jit(solution)/shard_map/ppermute | solution.py:287
  150.9 7.7 %collective-permute-done.31 = bf16[4,96,512]{2,1,0:T(8,128)(2,1)S(1)} collective-permute-done((bf16[4,96,512]{2,1,0:T(8,128)(2,1)S(1)}, bf16[4,96,512]{2,1,0:T(8,128)(2,1)S(1)}, u32[]{:S(2)}, u32[]{:S(2)}) %collective-permute-start.31) | collective-permute-done | bytes 393248 | tf_op jit(solution)/shard_map/ppermute | solution.py:287
  158.6 3.6 %collective-permute-done.32 = bf16[4,96,512]{2,1,0:T(8,128)(2,1)S(1)} collective-permute-done((bf16[4,96,512]{2,1,0:T(8,128)(2,1)S(1)}, bf16[4,96,512]{2,1,0:T(8,128)(2,1)S(1)}, u32[]{:S(2)}, u32[]{:S(2)}) %collective-permute-start.32) | collective-permute-done | bytes 393248 | tf_op jit(solution)/shard_map/ppermute | solution.py:287
  162.9 1.4 collective-permute-done.42
  164.3 1.8 %collective-permute-start.35 = (bf16[96,512]{1,0:T(8,128)(2,1)S(1)}, bf16[96,512]{1,0:T(8,128)(2,1)S(1)}, u32[]{:S(2)}, u32[]{:S(2)}) collective-permute-start(bf16[96,512]{1,0:T(8,128)(2,1)S(1)} %get-tuple-element.51), channel_id=1, source_target_pairs={{0,6},{2,0},{4,2},{6,4},{1,7},{3,1},{5,3},{7,5},{8,14},{10,8},{12,... | collective-permute-start | bytes 294920 | tf_op jit(solution)/shard_map/ppermute | solution.py:287
  166.2 1.7 collective-permute-start.44
  167.8 2.2 %collective-permute-done.33 = bf16[96,512]{1,0:T(8,128)(2,1)S(1)} collective-permute-done((bf16[96,512]{1,0:T(8,128)(2,1)S(1)}, bf16[96,512]{1,0:T(8,128)(2,1)S(1)}, u32[]{:S(2)}, u32[]{:S(2)}) %collective-permute-start.33) | collective-permute-done | bytes 98336 | tf_op jit(solution)/shard_map/ppermute | solution.py:287
  171.2 2.2 %collective-permute-start.36 = (bf16[48,512]{1,0:T(8,128)(2,1)S(1)}, bf16[48,512]{1,0:T(8,128)(2,1)S(1)}, u32[]{:S(2)}, u32[]{:S(2)}) collective-permute-start(bf16[48,512]{1,0:T(8,128)(2,1)S(1)} %get-tuple-element.67), channel_id=1, source_target_pairs={{0,96},{32,0},{64,32},{96,64},{1,97},{33,1},{65,33},{97,65},{2,98}... | collective-permute-start | bytes 147464 | tf_op jit(solution)/shard_map/ppermute | solution.py:287
  174.1 2.4 %collective-permute-start.49 = (f32[64,128]{1,0:T(8,128)S(1)}, f32[64,128]{1,0:T(8,128)S(1)}, u32[]{:S(2)}, u32[]{:S(2)}) collective-permute-start(f32[64,128]{1,0:T(8,128)S(1)} %add.69.s0_ref), channel_id=1, source_target_pairs={{0,6},{2,0},{4,2},{6,4},{1,7},{3,1},{5,3},{7,5},{8,14},{10,8},{12,... | collective-permute-start | bytes 98312 | tf_op jit(solution)/shard_map/ppermute | solution.py:287
  177.4 1.5 collective-permute-done.48.s2_ref
  178.8 2.0 %combine.1 = bf16[64,512]{1,0:T(8,128)(2,1)} custom-call(s32[3]{0:T(128)S(1)} %pad_add_fusion.here_ref, bf16[48,512]{1,0:T(8,128)(2,1)S(1)} %get-tuple-element.68.r0_ref, bf16[48,512]{1,0:T(8,128)(2,1)S(1)} %collective-permute-done.36.r1_ref, bf16[48,512]{1,0:T(8,128)(2,1)S(1)} %collective-permute-done.44.r2_ref, ...), custom_call_target="tpu_custom_call" | custom-call | flops 100000000 | bytes 1000000 | tf_op jit(solution)/shard_map/combine/pallas_call | solution.py:437
  (132 shorter events, 18.2 us)
Async XLA Ops:
  8.3 11.5 %copy-start.5 = (bf16[512,1024]{1,0:T(8,128)(2,1)S(1)}, bf16[512,1024]{1,0:T(8,128)(2,1)}, u32[]{:S(2)}) copy-start(bf16[512,1024]{1,0:T(8,128)(2,1)} %sw_ref.2) | copy-start | bytes 3145732
  8.3 11.5 %copy-start.6 = (bf16[64,1024]{1,0:T(8,128)(2,1)S(1)}, bf16[64,1024]{1,0:T(8,128)(2,1)}, u32[]{:S(2)}) copy-start(bf16[64,1024]{1,0:T(8,128)(2,1)} %z_ref.1) | copy-start | bytes 393220
  8.3 11.5 %copy-start.7 = (f32[16,1024]{1,0:T(8,128)S(1)}, f32[16,1024]{1,0:T(8,128)}, u32[]{:S(2)}) copy-start(f32[16,1024]{1,0:T(8,128)} %dl_ref.1) | copy-start | bytes 196612
  8.3 11.5 %copy-start.8 = (f32[1024]{0:T(1024)S(1)}, f32[1024]{0:T(1024)}, u32[]{:S(2)}) copy-start(f32[1024]{0:T(1024)} %param.37) | copy-start | bytes 12292
  8.3 11.5 %copy-start.9 = (f32[1024]{0:T(1024)S(1)}, f32[1024]{0:T(1024)}, u32[]{:S(2)}) copy-start(f32[1024]{0:T(1024)} %param.39) | copy-start | bytes 12292
  8.3 11.5 %copy-start.10 = (f32[512]{0:T(512)S(1)}, f32[512]{0:T(512)}, u32[]{:S(2)}) copy-start(f32[512]{0:T(512)} %param.35) | copy-start | bytes 6148
  8.3 11.5 %copy-start.14 = (s32[1,4]{1,0:T(1,128)S(1)}, s32[1,4]{1,0:T(1,128)}, u32[]{:S(2)}) copy-start(s32[1,4]{1,0:T(1,128)} %span_ref.3) | copy-start | bytes 52
  8.4 11.5 %copy-start.16 = (s32[1,4]{1,0:T(1,128)S(1)}, s32[1,4]{1,0:T(1,128)}, u32[]{:S(2)}) copy-start(s32[1,4]{1,0:T(1,128)} %res_ref.3) | copy-start | bytes 52
  8.4 11.5 %copy-start.18 = (s32[1,20]{1,0:T(1,128)S(1)}, s32[1,20]{1,0:T(1,128)}, u32[]{:S(2)}) copy-start(s32[1,20]{1,0:T(1,128)} %slot_ref.3) | copy-start | bytes 244
  9.6 1.4 collective-permute-start
  11.0 5.9 %collective-permute-start.1 = (bf16[64,640]{1,0:T(8,128)(2,1)S(1)}, bf16[64,640]{1,0:T(8,128)(2,1)S(1)}, u32[]{:S(2)}, u32[]{:S(2)}) collective-permute-start(bf16[64,640]{1,0:T(8,128)(2,1)S(1)} %add_convert_fusion.3.q0_ref), channel_id=1, source_target_pairs={{0,2},{2,4},{4,6},{6,0},{1,3},{3,5},{5,7},{7,1},{8,10},{10,12},{12... | collective-permute-start | bytes 245768 | tf_op jit(solution)/shard_map/ppermute | solution.py:287
  12.6 7.0 %collective-permute-start.2 = (bf16[64,640]{1,0:T(8,128)(2,1)S(1)}, bf16[64,640]{1,0:T(8,128)(2,1)S(1)}, u32[]{:S(2)}, u32[]{:S(2)}) collective-permute-start(bf16[64,640]{1,0:T(8,128)(2,1)S(1)} %add_convert_fusion.3.q0_ref), channel_id=1, source_target_pairs={{0,4},{2,6},{4,0},{6,2},{1,5},{3,7},{5,1},{7,3},{8,12},{10,14},{12... | collective-permute-start | bytes 245768 | tf_op jit(solution)/shard_map/ppermute | solution.py:287
  15.3 4.4 %collective-permute-start.3 = (bf16[64,640]{1,0:T(8,128)(2,1)S(1)}, bf16[64,640]{1,0:T(8,128)(2,1)S(1)}, u32[]{:S(2)}, u32[]{:S(2)}) collective-permute-start(bf16[64,640]{1,0:T(8,128)(2,1)S(1)} %add_convert_fusion.3.q0_ref), channel_id=1, source_target_pairs={{0,6},{2,0},{4,2},{6,4},{1,7},{3,1},{5,3},{7,5},{8,14},{10,8},{12,... | collective-permute-start | bytes 245768 | tf_op jit(solution)/shard_map/ppermute | solution.py:287
  23.3 14.1 %copy-start.24 = (bf16[512,4]{0,1:T(4,128)(2,1)S(1)}, bf16[512,4]{0,1:T(4,128)(2,1)}, u32[]{:S(2)}) copy-start(bf16[512,4]{0,1:T(4,128)(2,1)} %param.43) | copy-start | bytes 12292
  23.3 17.5 %copy-start.11 = (f32[512]{0:T(512)S(1)}, f32[512]{0:T(512)}, u32[]{:S(2)}) copy-start(f32[512]{0:T(512)} %param.42) | copy-start | bytes 6148
  23.3 17.5 %copy-start.12 = (s32[64,2]{0,1:T(2,128)S(1)}, s32[64,2]{0,1:T(2,128)}, u32[]{:S(2)}) copy-start(s32[64,2]{0,1:T(2,128)} %param.44) | copy-start | bytes 1540
  23.3 17.5 %copy-start.21 = (bf16[64,512]{1,0:T(8,128)(2,1)S(1)}, bf16[64,512]{1,0:T(8,128)(2,1)}, u32[]{:S(2)}) copy-start(bf16[64,512]{1,0:T(8,128)(2,1)} %resid_ref.1) | copy-start | bytes 196612
  30.5 1.6 collective-permute-start.4
  32.3 5.5 %collective-permute-start.5 = (bf16[64,512]{1,0:T(8,128)(2,1)S(1)}, bf16[64,512]{1,0:T(8,128)(2,1)S(1)}, u32[]{:S(2)}, u32[]{:S(2)}) collective-permute-start(bf16[64,512]{1,0:T(8,128)(2,1)S(1)} %get-tuple-element.59), channel_id=1, source_target_pairs={{0,2},{2,4},{4,6},{6,0},{1,3},{3,5},{5,7},{7,1},{8,10},{10,12},{12... | collective-permute-start | bytes 196616 | tf_op jit(solution)/shard_map/ppermute | solution.py:287
  33.4 6.6 %collective-permute-start.6 = (bf16[64,512]{1,0:T(8,128)(2,1)S(1)}, bf16[64,512]{1,0:T(8,128)(2,1)S(1)}, u32[]{:S(2)}, u32[]{:S(2)}) collective-permute-start(bf16[64,512]{1,0:T(8,128)(2,1)S(1)} %get-tuple-element.58), channel_id=1, source_target_pairs={{0,4},{2,6},{4,0},{6,2},{1,5},{3,7},{5,1},{7,3},{8,12},{10,14},{12... | collective-permute-start | bytes 196616 | tf_op jit(solution)/shard_map/ppermute | solution.py:287
  36.4 4.3 %collective-permute-start.7 = (bf16[64,512]{1,0:T(8,128)(2,1)S(1)}, bf16[64,512]{1,0:T(8,128)(2,1)S(1)}, u32[]{:S(2)}, u32[]{:S(2)}) collective-permute-start(bf16[64,512]{1,0:T(8,128)(2,1)S(1)} %get-tuple-element.57), channel_id=1, source_target_pairs={{0,6},{2,0},{4,2},{6,4},{1,7},{3,1},{5,3},{7,5},{8,14},{10,8},{12,... | collective-permute-start | bytes 196616 | tf_op jit(solution)/shard_map/ppermute | solution.py:287
  42.0 6.0 %collective-permute-start.16 = (bf16[48,512]{1,0:T(8,128)(2,1)S(1)}, bf16[48,512]{1,0:T(8,128)(2,1)S(1)}, u32[]{:S(2)}, u32[]{:S(2)}) collective-permute-start(bf16[48,512]{1,0:T(8,128)(2,1)S(1)} %get-tuple-element.62), channel_id=1, source_target_pairs={{0,64},{32,96},{64,0},{96,32},{1,65},{33,97},{65,1},{97,33},{2,66}... | collective-permute-start | bytes 147464 | tf_op jit(solution)/shard_map/ppermute | solution.py:287
  45.9 4.1 %collective-permute-start.17 = (bf16[48,512]{1,0:T(8,128)(2,1)S(1)}, bf16[48,512]{1,0:T(8,128)(2,1)S(1)}, u32[]{:S(2)}, u32[]{:S(2)}) collective-permute-start(bf16[48,512]{1,0:T(8,128)(2,1)S(1)} %get-tuple-element.61), channel_id=1, source_target_pairs={{0,96},{32,0},{64,32},{96,64},{1,97},{33,1},{65,33},{97,65},{2,98}... | collective-permute-start | bytes 147464 | tf_op jit(solution)/shard_map/ppermute | solution.py:287
  50.0 6.9 %collective-permute-start.18 = (bf16[96,512]{1,0:T(8,128)(2,1)S(1)}, bf16[96,512]{1,0:T(8,128)(2,1)S(1)}, u32[]{:S(2)}, u32[]{:S(2)}) collective-permute-start(bf16[96,512]{1,0:T(8,128)(2,1)S(1)} %constant_dynamic-update-slice_fusion), channel_id=1, source_target_pairs={{0,8},{8,16},{16,24},{24,0},{1,9},{9,17},{17,25},{25,1},{2,10},{10... | collective-permute-start | bytes 294920 | tf_op jit(solution)/shard_map/ppermute | solution.py:287
  51.6 6.6 %collective-permute-start.19 = (bf16[96,512]{1,0:T(8,128)(2,1)S(1)}, bf16[96,512]{1,0:T(8,128)(2,1)S(1)}, u32[]{:S(2)}, u32[]{:S(2)}) collective-permute-start(bf16[96,512]{1,0:T(8,128)(2,1)S(1)} %constant_dynamic-update-slice_fusion), channel_id=1, source_target_pairs={{0,16},{8,24},{16,0},{24,8},{1,17},{9,25},{17,1},{25,9},{2,18},{10... | collective-permute-start | bytes 294920 | tf_op jit(solution)/shard_map/ppermute | solution.py:287
  54.5 4.6 %collective-permute-start.20 = (bf16[96,512]{1,0:T(8,128)(2,1)S(1)}, bf16[96,512]{1,0:T(8,128)(2,1)S(1)}, u32[]{:S(2)}, u32[]{:S(2)}) collective-permute-start(bf16[96,512]{1,0:T(8,128)(2,1)S(1)} %constant_dynamic-update-slice_fusion), channel_id=1, source_target_pairs={{0,24},{8,0},{16,8},{24,16},{1,25},{9,1},{17,9},{25,17},{2,26},{10... | collective-permute-start | bytes 294920 | tf_op jit(solution)/shard_map/ppermute | solution.py:287
  55.8 5.3 %collective-permute-start.8 = (bf16[48,512]{1,0:T(8,128)(2,1)S(1)}, bf16[48,512]{1,0:T(8,128)(2,1)S(1)}, u32[]{:S(2)}, u32[]{:S(2)}) collective-permute-start(bf16[48,512]{1,0:T(8,128)(2,1)S(1)} %get-tuple-element.63), channel_id=1, source_target_pairs={{0,32},{32,64},{64,96},{96,0},{1,33},{33,65},{65,97},{97,1},{2,34}... | collective-permute-start | bytes 147464 | tf_op jit(solution)/shard_map/ppermute | solution.py:287
  59.2 21.4 %collective-permute-start.21 = (bf16[4,96,512]{2,1,0:T(8,128)(2,1)S(1)}, bf16[4,96,512]{2,1,0:T(8,128)(2,1)S(1)}, u32[]{:S(2)}, u32[]{:S(2)}) collective-permute-start(bf16[4,96,512]{2,1,0:T(8,128)(2,1)S(1)} %get-tuple-element.54), channel_id=1, source_target_pairs={{0,2},{2,4},{4,6},{6,0},{1,3},{3,5},{5,7},{7,1},{8,10},{10,12},{12... | collective-permute-start | bytes 1179656 | tf_op jit(solution)/shard_map/ppermute | solution.py:287
  61.2 12.6 %collective-permute-start.9 = (bf16[96,512]{1,0:T(8,128)(2,1)S(1)}, bf16[96,512]{1,0:T(8,128)(2,1)S(1)}, u32[]{:S(2)}, u32[]{:S(2)}) collective-permute-start(bf16[96,512]{1,0:T(8,128)(2,1)S(1)} %get-tuple-element.70), channel_id=1, source_target_pairs={{0,2},{2,4},{4,6},{6,0},{1,3},{3,5},{5,7},{7,1},{8,10},{10,12},{12... | collective-permute-start | bytes 294920 | tf_op jit(solution)/shard_map/ppermute | solution.py:287
  61.9 14.8 %collective-permute-start.10 = (bf16[96,512]{1,0:T(8,128)(2,1)S(1)}, bf16[96,512]{1,0:T(8,128)(2,1)S(1)}, u32[]{:S(2)}, u32[]{:S(2)}) collective-permute-start(bf16[96,512]{1,0:T(8,128)(2,1)S(1)} %get-tuple-element.70), channel_id=1, source_target_pairs={{0,4},{2,6},{4,0},{6,2},{1,5},{3,7},{5,1},{7,3},{8,12},{10,14},{12... | collective-permute-start | bytes 294920 | tf_op jit(solution)/shard_map/ppermute | solution.py:287
  64.8 11.9 %collective-permute-start.11 = (bf16[96,512]{1,0:T(8,128)(2,1)S(1)}, bf16[96,512]{1,0:T(8,128)(2,1)S(1)}, u32[]{:S(2)}, u32[]{:S(2)}) collective-permute-start(bf16[96,512]{1,0:T(8,128)(2,1)S(1)} %get-tuple-element.70), channel_id=1, source_target_pairs={{0,6},{2,0},{4,2},{6,4},{1,7},{3,1},{5,3},{7,5},{8,14},{10,8},{12,... | collective-permute-start | bytes 294920 | tf_op jit(solution)/shard_map/ppermute | solution.py:287
  65.6 16.1 %collective-permute-start.22 = (bf16[4,96,512]{2,1,0:T(8,128)(2,1)S(1)}, bf16[4,96,512]{2,1,0:T(8,128)(2,1)S(1)}, u32[]{:S(2)}, u32[]{:S(2)}) collective-permute-start(bf16[4,96,512]{2,1,0:T(8,128)(2,1)S(1)} %get-tuple-element.54), channel_id=1, source_target_pairs={{0,4},{2,6},{4,0},{6,2},{1,5},{3,7},{5,1},{7,3},{8,12},{10,14},{12... | collective-permute-start | bytes 1179656 | tf_op jit(solution)/shard_map/ppermute | solution.py:287
  73.8 9.3 %collective-permute-start.23 = (bf16[4,96,512]{2,1,0:T(8,128)(2,1)S(1)}, bf16[4,96,512]{2,1,0:T(8,128)(2,1)S(1)}, u32[]{:S(2)}, u32[]{:S(2)}) collective-permute-start(bf16[4,96,512]{2,1,0:T(8,128)(2,1)S(1)} %get-tuple-element.54), channel_id=1, source_target_pairs={{0,6},{2,0},{4,2},{6,4},{1,7},{3,1},{5,3},{7,5},{8,14},{10,8},{12,... | collective-permute-start | bytes 1179656 | tf_op jit(solution)/shard_map/ppermute | solution.py:287
  76.8 9.1 %collective-permute-start.12 = (bf16[4,96,512]{2,1,0:T(8,128)(2,1)S(1)}, bf16[4,96,512]{2,1,0:T(8,128)(2,1)S(1)}, u32[]{:S(2)}, u32[]{:S(2)}) collective-permute-start(bf16[4,96,512]{2,1,0:T(8,128)(2,1)S(1)} %get-tuple-element.56), channel_id=1, source_target_pairs={{0,8},{8,16},{16,24},{24,0},{1,9},{9,17},{17,25},{25,1},{2,10},{10... | collective-permute-start | bytes 1179656 | tf_op jit(solution)/shard_map/ppermute | solution.py:287
  77.7 12.9 %collective-permute-start.13 = (bf16[4,96,512]{2,1,0:T(8,128)(2,1)S(1)}, bf16[4,96,512]{2,1,0:T(8,128)(2,1)S(1)}, u32[]{:S(2)}, u32[]{:S(2)}) collective-permute-start(bf16[4,96,512]{2,1,0:T(8,128)(2,1)S(1)} %get-tuple-element.56), channel_id=1, source_target_pairs={{0,16},{8,24},{16,0},{24,8},{1,17},{9,25},{17,1},{25,9},{2,18},{10... | collective-permute-start | bytes 1179656 | tf_op jit(solution)/shard_map/ppermute | solution.py:287
  80.6 10.4 %collective-permute-start.14 = (bf16[4,96,512]{2,1,0:T(8,128)(2,1)S(1)}, bf16[4,96,512]{2,1,0:T(8,128)(2,1)S(1)}, u32[]{:S(2)}, u32[]{:S(2)}) collective-permute-start(bf16[4,96,512]{2,1,0:T(8,128)(2,1)S(1)} %get-tuple-element.56), channel_id=1, source_target_pairs={{0,24},{8,0},{16,8},{24,16},{1,25},{9,1},{17,9},{25,17},{2,26},{10... | collective-permute-start | bytes 1179656 | tf_op jit(solution)/shard_map/ppermute | solution.py:287
  83.1 18.7 %copy-start.1 = (bf16[1,4096,384]{2,1,0:T(8,128)(2,1)S(1)}, bf16[1,4096,384]{2,1,0:T(8,128)(2,1)}, u32[]{:S(2)}) copy-start(bf16[1,4096,384]{2,1,0:T(8,128)(2,1)} %param.46) | copy-start | bytes 9437188
  83.3 23.4 %collective-permute-start.24 = (bf16[4,4,96,512]{3,2,1,0:T(8,128)(2,1)S(1)}, bf16[4,4,96,512]{3,2,1,0:T(8,128)(2,1)S(1)}, u32[]{:S(2)}, u32[]{:S(2)}) collective-permute-start(bf16[4,4,96,512]{3,2,1,0:T(8,128)(2,1)S(1)} %pad_maximum_fusion.1.x1_ref), channel_id=1, source_target_pairs={{0,1},{1,0},{2,3},{3,2},{4,5},{5,4},{6,7},{7,6},{8,9},{9,8},{10,11... | collective-permute-start | bytes 4718600 | tf_op jit(solution)/shard_map/ppermute | solution.py:287
  91.2 15.5 %collective-permute-start.15 = (bf16[4,4,96,512]{3,2,1,0:T(8,128)(2,1)S(1)}, bf16[4,4,96,512]{3,2,1,0:T(8,128)(2,1)S(1)}, u32[]{:S(2)}, u32[]{:S(2)}) collective-permute-start(bf16[4,4,96,512]{3,2,1,0:T(8,128)(2,1)S(1)} %pad_maximum_fusion.x0_ref), channel_id=1, source_target_pairs={{0,1},{1,0},{2,3},{3,2},{4,5},{5,4},{6,7},{7,6},{8,9},{9,8},{10,11... | collective-permute-start | bytes 4718600 | tf_op jit(solution)/shard_map/ppermute | solution.py:287
  91.3 3.4 %collective-permute-start.25 = (f32[1,512]{1,0:T(1,128)S(1)}, f32[1,512]{1,0:T(1,128)S(1)}, u32[]{:S(2)}, u32[]{:S(2)}) collective-permute-start(f32[1,512]{1,0:T(1,128)S(1)} %bitcast.135), channel_id=1, source_target_pairs={{0,1},{1,0},{2,3},{3,2},{4,5},{5,4},{6,7},{7,6},{8,9},{9,8},{10,11... | collective-permute-start | bytes 6152 | tf_op jit(solution)/shard_map/ppermute | solution.py:287
  94.7 4.9 %collective-permute-start.26 = (f32[2,512]{1,0:T(2,128)S(1)}, f32[2,512]{1,0:T(2,128)S(1)}, u32[]{:S(2)}, u32[]{:S(2)}) collective-permute-start(f32[2,512]{1,0:T(2,128)S(1)} %pad_maximum_fusion.7), channel_id=1, source_target_pairs={{0,2},{2,4},{4,6},{6,0},{1,3},{3,5},{5,7},{7,1},{8,10},{10,12},{12... | collective-permute-start | bytes 12296 | tf_op jit(solution)/shard_map/ppermute | solution.py:287
  94.8 5.2 %collective-permute-start.27 = (f32[2,512]{1,0:T(2,128)S(1)}, f32[2,512]{1,0:T(2,128)S(1)}, u32[]{:S(2)}, u32[]{:S(2)}) collective-permute-start(f32[2,512]{1,0:T(2,128)S(1)} %pad_maximum_fusion.7), channel_id=1, source_target_pairs={{0,4},{2,6},{4,0},{6,2},{1,5},{3,7},{5,1},{7,3},{8,12},{10,14},{12... | collective-permute-start | bytes 12296 | tf_op jit(solution)/shard_map/ppermute | solution.py:287
  98.1 3.6 %collective-permute-start.28 = (f32[2,512]{1,0:T(2,128)S(1)}, f32[2,512]{1,0:T(2,128)S(1)}, u32[]{:S(2)}, u32[]{:S(2)}) collective-permute-start(f32[2,512]{1,0:T(2,128)S(1)} %pad_maximum_fusion.7), channel_id=1, source_target_pairs={{0,6},{2,0},{4,2},{6,4},{1,7},{3,1},{5,3},{7,5},{8,14},{10,8},{12,... | collective-permute-start | bytes 12296 | tf_op jit(solution)/shard_map/ppermute | solution.py:287
  116.8 3.5 %collective-permute-start.29 = (bf16[4,4,96,512]{3,2,1,0:T(8,128)(2,1)S(1)}, bf16[4,4,96,512]{3,2,1,0:T(8,128)(2,1)S(1)}, u32[]{:S(2)}, u32[]{:S(2)}) collective-permute-start(bf16[4,4,96,512]{3,2,1,0:T(8,128)(2,1)S(1)} %get-tuple-element.28), channel_id=1, source_target_pairs={{0,1},{1,0},{2,3},{3,2},{4,5},{5,4},{6,7},{7,6},{8,9},{9,8},{10,11... | collective-permute-start | bytes 4718600 | tf_op jit(solution)/shard_map/ppermute | solution.py:287
  116.9 5.6 %collective-permute-start.37 = (bf16[4,4,96,512]{3,2,1,0:T(8,128)(2,1)S(1)}, bf16[4,4,96,512]{3,2,1,0:T(8,128)(2,1)S(1)}, u32[]{:S(2)}, u32[]{:S(2)}) collective-permute-start(bf16[4,4,96,512]{3,2,1,0:T(8,128)(2,1)S(1)} %get-tuple-element.30), channel_id=1, source_target_pairs={{0,1},{1,0},{2,3},{3,2},{4,5},{5,4},{6,7},{7,6},{8,9},{9,8},{10,11... | collective-permute-start | bytes 4718600 | tf_op jit(solution)/shard_map/ppermute | solution.py:287
  123.8 21.2 %collective-permute-start.38 = (bf16[4,96,512]{2,1,0:T(8,128)(2,1)S(1)}, bf16[4,96,512]{2,1,0:T(8,128)(2,1)S(1)}, u32[]{:S(2)}, u32[]{:S(2)}) collective-permute-start(bf16[4,96,512]{2,1,0:T(8,128)(2,1)S(1)} %get-tuple-element.41), channel_id=1, source_target_pairs={{0,2},{2,4},{4,6},{6,0},{1,3},{3,5},{5,7},{7,1},{8,10},{10,12},{12... | collective-permute-start | bytes 1179656 | tf_op jit(solution)/shard_map/ppermute | solution.py:287
  124.6 22.4 %collective-permute-start.39 = (bf16[4,96,512]{2,1,0:T(8,128)(2,1)S(1)}, bf16[4,96,512]{2,1,0:T(8,128)(2,1)S(1)}, u32[]{:S(2)}, u32[]{:S(2)}) collective-permute-start(bf16[4,96,512]{2,1,0:T(8,128)(2,1)S(1)} %get-tuple-element.43), channel_id=1, source_target_pairs={{0,4},{2,6},{4,0},{6,2},{1,5},{3,7},{5,1},{7,3},{8,12},{10,14},{12... | collective-permute-start | bytes 1179656 | tf_op jit(solution)/shard_map/ppermute | solution.py:287
  126.8 20.7 %collective-permute-start.40 = (bf16[4,96,512]{2,1,0:T(8,128)(2,1)S(1)}, bf16[4,96,512]{2,1,0:T(8,128)(2,1)S(1)}, u32[]{:S(2)}, u32[]{:S(2)}) collective-permute-start(bf16[4,96,512]{2,1,0:T(8,128)(2,1)S(1)} %get-tuple-element.42), channel_id=1, source_target_pairs={{0,6},{2,0},{4,2},{6,4},{1,7},{3,1},{5,3},{7,5},{8,14},{10,8},{12,... | collective-permute-start | bytes 1179656 | tf_op jit(solution)/shard_map/ppermute | solution.py:287
  128.1 1.2 collective-permute-start.46
  129.3 44.8 %collective-permute-start.47 = (f32[64,128]{1,0:T(8,128)S(1)}, f32[64,128]{1,0:T(8,128)S(1)}, u32[]{:S(2)}, u32[]{:S(2)}) collective-permute-start(f32[64,128]{1,0:T(8,128)S(1)} %add.69.s0_ref), channel_id=1, source_target_pairs={{0,2},{2,4},{4,6},{6,0},{1,3},{3,5},{5,7},{7,1},{8,10},{10,12},{12... | collective-permute-start | bytes 98312 | tf_op jit(solution)/shard_map/ppermute | solution.py:287
  130.1 20.5 %collective-permute-start.30 = (bf16[4,96,512]{2,1,0:T(8,128)(2,1)S(1)}, bf16[4,96,512]{2,1,0:T(8,128)(2,1)S(1)}, u32[]{:S(2)}, u32[]{:S(2)}) collective-permute-start(bf16[4,96,512]{2,1,0:T(8,128)(2,1)S(1)} %get-tuple-element.44), channel_id=1, source_target_pairs={{0,24},{8,0},{16,8},{24,16},{1,25},{9,1},{17,9},{25,17},{2,26},{10... | collective-permute-start | bytes 1179656 | tf_op jit(solution)/shard_map/ppermute | solution.py:287
  145.0 13.6 %collective-permute-start.31 = (bf16[4,96,512]{2,1,0:T(8,128)(2,1)S(1)}, bf16[4,96,512]{2,1,0:T(8,128)(2,1)S(1)}, u32[]{:S(2)}, u32[]{:S(2)}) collective-permute-start(bf16[4,96,512]{2,1,0:T(8,128)(2,1)S(1)} %get-tuple-element.46), channel_id=1, source_target_pairs={{0,16},{8,24},{16,0},{24,8},{1,17},{9,25},{17,1},{25,9},{2,18},{10... | collective-permute-start | bytes 1179656 | tf_op jit(solution)/shard_map/ppermute | solution.py:287
  147.0 15.2 %collective-permute-start.32 = (bf16[4,96,512]{2,1,0:T(8,128)(2,1)S(1)}, bf16[4,96,512]{2,1,0:T(8,128)(2,1)S(1)}, u32[]{:S(2)}, u32[]{:S(2)}) collective-permute-start(bf16[4,96,512]{2,1,0:T(8,128)(2,1)S(1)} %get-tuple-element.45), channel_id=1, source_target_pairs={{0,8},{8,16},{16,24},{24,0},{1,9},{9,17},{17,25},{25,1},{2,10},{10... | collective-permute-start | bytes 1179656 | tf_op jit(solution)/shard_map/ppermute | solution.py:287
  147.7 15.1 %collective-permute-start.41 = (bf16[96,512]{1,0:T(8,128)(2,1)S(1)}, bf16[96,512]{1,0:T(8,128)(2,1)S(1)}, u32[]{:S(2)}, u32[]{:S(2)}) collective-permute-start(bf16[96,512]{1,0:T(8,128)(2,1)S(1)} %get-tuple-element.47), channel_id=1, source_target_pairs={{0,24},{8,0},{16,8},{24,16},{1,25},{9,1},{17,9},{25,17},{2,26},{10... | collective-permute-start | bytes 294920 | tf_op jit(solution)/shard_map/ppermute | solution.py:287
  150.6 13.7 %collective-permute-start.42 = (bf16[96,512]{1,0:T(8,128)(2,1)S(1)}, bf16[96,512]{1,0:T(8,128)(2,1)S(1)}, u32[]{:S(2)}, u32[]{:S(2)}) collective-permute-start(bf16[96,512]{1,0:T(8,128)(2,1)S(1)} %get-tuple-element.49), channel_id=1, source_target_pairs={{0,16},{8,24},{16,0},{24,8},{1,17},{9,25},{17,1},{25,9},{2,18},{10... | collective-permute-start | bytes 294920 | tf_op jit(solution)/shard_map/ppermute | solution.py:287
  158.6 7.4 %collective-permute-start.43 = (bf16[96,512]{1,0:T(8,128)(2,1)S(1)}, bf16[96,512]{1,0:T(8,128)(2,1)S(1)}, u32[]{:S(2)}, u32[]{:S(2)}) collective-permute-start(bf16[96,512]{1,0:T(8,128)(2,1)S(1)} %get-tuple-element.48), channel_id=1, source_target_pairs={{0,8},{8,16},{16,24},{24,0},{1,9},{9,17},{17,25},{25,1},{2,10},{10... | collective-permute-start | bytes 294920 | tf_op jit(solution)/shard_map/ppermute | solution.py:287
  162.5 7.5 %collective-permute-start.33 = (bf16[96,512]{1,0:T(8,128)(2,1)S(1)}, bf16[96,512]{1,0:T(8,128)(2,1)S(1)}, u32[]{:S(2)}, u32[]{:S(2)}) collective-permute-start(bf16[96,512]{1,0:T(8,128)(2,1)S(1)} %get-tuple-element.50), channel_id=1, source_target_pairs={{0,2},{2,4},{4,6},{6,0},{1,3},{3,5},{5,7},{7,1},{8,10},{10,12},{12... | collective-permute-start | bytes 294920 | tf_op jit(solution)/shard_map/ppermute | solution.py:287
  162.8 7.9 %collective-permute-start.34 = (bf16[96,512]{1,0:T(8,128)(2,1)S(1)}, bf16[96,512]{1,0:T(8,128)(2,1)S(1)}, u32[]{:S(2)}, u32[]{:S(2)}) collective-permute-start(bf16[96,512]{1,0:T(8,128)(2,1)S(1)} %get-tuple-element.52), channel_id=1, source_target_pairs={{0,4},{2,6},{4,0},{6,2},{1,5},{3,7},{5,1},{7,3},{8,12},{10,14},{12... | collective-permute-start | bytes 294920 | tf_op jit(solution)/shard_map/ppermute | solution.py:287
  164.3 6.8 %collective-permute-start.35 = (bf16[96,512]{1,0:T(8,128)(2,1)S(1)}, bf16[96,512]{1,0:T(8,128)(2,1)S(1)}, u32[]{:S(2)}, u32[]{:S(2)}) collective-permute-start(bf16[96,512]{1,0:T(8,128)(2,1)S(1)} %get-tuple-element.51), channel_id=1, source_target_pairs={{0,6},{2,0},{4,2},{6,4},{1,7},{3,1},{5,3},{7,5},{8,14},{10,8},{12,... | collective-permute-start | bytes 294920 | tf_op jit(solution)/shard_map/ppermute | solution.py:287
  166.2 12.6 %collective-permute-start.44 = (bf16[48,512]{1,0:T(8,128)(2,1)S(1)}, bf16[48,512]{1,0:T(8,128)(2,1)S(1)}, u32[]{:S(2)}, u32[]{:S(2)}) collective-permute-start(bf16[48,512]{1,0:T(8,128)(2,1)S(1)} %get-tuple-element.66), channel_id=1, source_target_pairs={{0,64},{32,96},{64,0},{96,32},{1,65},{33,97},{65,1},{97,33},{2,66}... | collective-permute-start | bytes 147464 | tf_op jit(solution)/shard_map/ppermute | solution.py:287
  170.0 8.8 %collective-permute-start.45 = (bf16[48,512]{1,0:T(8,128)(2,1)S(1)}, bf16[48,512]{1,0:T(8,128)(2,1)S(1)}, u32[]{:S(2)}, u32[]{:S(2)}) collective-permute-start(bf16[48,512]{1,0:T(8,128)(2,1)S(1)} %get-tuple-element.65), channel_id=1, source_target_pairs={{0,32},{32,64},{64,96},{96,0},{1,33},{33,65},{65,97},{97,1},{2,34}... | collective-permute-start | bytes 147464 | tf_op jit(solution)/shard_map/ppermute | solution.py:287
  171.2 7.7 %collective-permute-start.36 = (bf16[48,512]{1,0:T(8,128)(2,1)S(1)}, bf16[48,512]{1,0:T(8,128)(2,1)S(1)}, u32[]{:S(2)}, u32[]{:S(2)}) collective-permute-start(bf16[48,512]{1,0:T(8,128)(2,1)S(1)} %get-tuple-element.67), channel_id=1, source_target_pairs={{0,96},{32,0},{64,32},{96,64},{1,97},{33,1},{65,33},{97,65},{2,98}... | collective-permute-start | bytes 147464 | tf_op jit(solution)/shard_map/ppermute | solution.py:287
  173.4 5.4 %collective-permute-start.48 = (f32[64,128]{1,0:T(8,128)S(1)}, f32[64,128]{1,0:T(8,128)S(1)}, u32[]{:S(2)}, u32[]{:S(2)}) collective-permute-start(f32[64,128]{1,0:T(8,128)S(1)} %add.69.s0_ref), channel_id=1, source_target_pairs={{0,4},{2,6},{4,0},{6,2},{1,5},{3,7},{5,1},{7,3},{8,12},{10,14},{12... | collective-permute-start | bytes 98312 | tf_op jit(solution)/shard_map/ppermute | solution.py:287
  174.1 4.7 %collective-permute-start.49 = (f32[64,128]{1,0:T(8,128)S(1)}, f32[64,128]{1,0:T(8,128)S(1)}, u32[]{:S(2)}, u32[]{:S(2)}) collective-permute-start(f32[64,128]{1,0:T(8,128)S(1)} %add.69.s0_ref), channel_id=1, source_target_pairs={{0,6},{2,0},{4,2},{6,4},{1,7},{3,1},{5,3},{7,5},{8,14},{10,8},{12,... | collective-permute-start | bytes 98312 | tf_op jit(solution)/shard_map/ppermute | solution.py:287
  (11 other events, 41.9 us)

commit v2 on v1

v2 whole, which is shorter than its diff:
```python
import functools

import jax
import jax.numpy as jnp
import numpy as np
from jax import lax
from jax.experimental import pallas as pl
from jax.experimental.pallas import tpu as pltpu
from jax.sharding import Mesh
from jax.sharding import PartitionSpec as P

DEC = 16
ROWS = 64
SEQ = 20
CAP = 48
NS = 16
TAPS = 4
EXPERTS = 4
EPS = 1e-6
BF = jnp.bfloat16
F32 = jnp.float32
I32 = jnp.int32
VMEM = pl.BlockSpec(memory_space=pltpu.VMEM)
SMEM = pl.BlockSpec(memory_space=pltpu.SMEM)
HBM = pl.BlockSpec(memory_space=pltpu.HBM)
AXES = ("z", "y", "x", "core")


def params(mib):
    return pltpu.CompilerParams(vmem_limit_bytes=mib * 1024 * 1024)


def iota(shape, dim):
    return lax.broadcasted_iota(I32, shape, dim)


def silu(v):
    return v / (1.0 + jnp.exp(-v))


def dot(a, b):
    return jnp.dot(a, b, preferred_element_type=F32)


def span_starts(span_ref):
    s1 = DEC + span_ref[0, 0]
    s2 = s1 + span_ref[0, 1]
    s3 = s2 + span_ref[0, 2]
    return (jnp.int32(DEC), s1, s2, s3)


def conv_kernel(
    span_hbm, res_hbm, slot_hbm, x_hbm, cache_hbm, w_hbm, b_hbm, rank_hbm, sw_hbm, gain_hbm,
    cx_ref, proj_ref, nc_ref,
    span_ref, res_ref, slot_ref, x_ref, cache_ref, w_ref, b_ref, rank_ref, sw_ref, gain_ref, sems,
):
    sources = (span_hbm, res_hbm, slot_hbm, x_hbm, cache_hbm, w_hbm, b_hbm, gain_hbm, sw_hbm, rank_hbm)
    targets = (span_ref, res_ref, slot_ref, x_ref, cache_ref, w_ref, b_ref, gain_ref, sw_ref, rank_ref)
    copies = [
        pltpu.make_async_copy(source, target, sems.at[i])
        for i, (source, target) in enumerate(zip(sources, targets))
    ]
    for copy in copies:
        copy.start()
    for copy in copies[:7]:
        copy.wait()
    starts = span_starts(span_ref)
    x = x_ref[...]
    r = iota((ROWS, 128), 0)
    j = iota((ROWS, 128), 1)
    start = jnp.where(r < DEC, r, DEC)
    slot = jnp.full((ROWS, 128), slot_ref[0, DEC], I32)
    res = jnp.full((ROWS, 128), res_ref[0, 0], I32)
    for c in range(1, 4):
        inside = r >= starts[c]
        start = jnp.where(inside, starts[c], start)
        slot = jnp.where(inside, slot_ref[0, DEC + c], slot)
        res = jnp.where(inside, res_ref[0, c], res)
    for d in range(DEC):
        slot = jnp.where(r == d, slot_ref[0, d], slot)
    res = jnp.where(r < DEC, 1, res)
    pos = r - start

    def select(column, line, width):
        return (j == jnp.where(line, column, -1)).astype(F32)[:, 0:width].astype(BF)

    total = b_ref[...] + w_ref[TAPS - 1 : TAPS] * x.astype(F32)
    for lag in range(1, TAPS):
        value = dot(select(r - lag, pos >= lag, ROWS), x)
        for i in range(TAPS - 1):
            old = (pos == i + lag - 3) & (pos < lag) & (res > 0)
            value = value + dot(select(slot, old, SEQ), cache_ref[i])
        total = total + w_ref[TAPS - 1 - lag : TAPS - lag] * value
    cx = silu(total).astype(BF)
    cx_ref[...] = cx
    for copy in copies[7:]:
        copy.wait()
    proj_ref[0:ROWS, 0:512] = dot(cx, rank_ref[...]).astype(BF)
    proj_ref[0:ROWS, 512:640] = jnp.zeros((ROWS, 128), BF)
    proj_ref[0:ROWS, 512 : 512 + 2 * NS] = lax.dot_general(
        cx, sw_ref[...], (((1,), (1,)), ((), ())), preferred_element_type=F32
    ).astype(BF)
    line = 2 * (2 * lax.axis_index("x") + lax.axis_index("core"))
    inverse = 1.0 / (gain_ref[...] * gain_ref[...])
    high = inverse.astype(BF).astype(F32)
    row = iota((16, 512), 0)
    extra = jnp.where(row == line, high, jnp.where(row == line + 1, inverse - high, 0.0))
    proj_ref[ROWS : ROWS + 16, 0:512] = extra.astype(BF)
    proj_ref[ROWS : ROWS + 16, 512:640] = jnp.zeros((16, 128), BF)
    group = r
    length = jnp.ones((ROWS, 128), I32)
    first = jnp.zeros((ROWS, 128), I32)
    kept = jnp.ones((ROWS, 128), I32)
    for s in range(SEQ):
        here = group == slot_ref[0, s]
        if s < DEC:
            first = jnp.where(here, s, first)
        else:
            first = jnp.where(here, starts[s - DEC], first)
            length = jnp.where(here, span_ref[0, s - DEC], length)
            kept = jnp.where(here, res_ref[0, s - DEC], kept)
    for offset in range(TAPS - 1):
        back = length - (TAPS - 1) + offset
        value = dot(select(first + back, back >= 0, ROWS), x)
        for i in range(TAPS - 1):
            old = (back == i - 3) & (kept > 0)
            value = value + dot(select(group, old, SEQ), cache_ref[i])
        nc_ref[offset] = value[0:SEQ].astype(BF)


def scan_kernel(
    here_ref, span_ref, res_ref, slot_ref,
    q0_ref, q1_ref, q2_ref, q3_ref, cx_ref, z_ref, gain_ref, sw_ref, sb_ref, dl_ref, skip_ref,
    sc_ref, ow_ref,
    ns_ref, own_ref, sib_ref, inv_ref,
    w_vmem, step_ref, drive_ref, bb_ref, cb_ref, pc_ref, tr_ref, sem,
):
    fetch = pltpu.make_async_copy(ow_ref, w_vmem, sem)
    fetch.start()
    starts = span_starts(span_ref)
    sums = (
        q0_ref[...].astype(F32) + q1_ref[...].astype(F32)
        + q2_ref[...].astype(F32) + q3_ref[...].astype(F32)
    )
    proj = sums[0:ROWS]
    for t in range(8):
        inverse = sums[ROWS + 2 * t : ROWS + 2 * t + 1, 0:512] + sums[ROWS + 2 * t + 1 : ROWS + 2 * t + 2, 0:512]
        inv_ref[t // 2, :, 512 * (t % 2) : 512 * (t % 2) + 512] = inverse
    low = proj[:, 0:512]
    mean = jnp.mean(low * low, axis=1, keepdims=True)
    norm = (low * lax.rsqrt(mean + EPS) * gain_ref[...]).astype(BF)
    pre = dot(norm, sw_ref[...]) + sb_ref[...]
    step = jnp.maximum(pre, 0.0) + jnp.log1p(jnp.exp(-jnp.abs(pre)))
    values = cx_ref[...].astype(F32)
    step_ref[...] = step
    drive_ref[...] = step * values
    tr_ref[0:ROWS] = proj[:, 512:640]
    tr_ref[ROWS : 2 * ROWS] = jnp.zeros((ROWS, 128), F32)
    turned = tr_ref[...].T
    for r in range(ROWS):
        bb_ref[r] = jnp.broadcast_to(turned[0:NS, r : r + 1], (NS, 128))
        cb_ref[r] = jnp.broadcast_to(turned[NS : 2 * NS, r : r + 1], (NS, 128))
    rate = -jnp.exp(dl_ref[...])
    groups = rate.shape[1] // 128

    def advance(r, state):
        c1 = (r >= starts[1]).astype(I32)
        c2 = (r >= starts[2]).astype(I32)
        c3 = (r >= starts[3]).astype(I32)
        piece = c1 + c2 + c3
        decode = r < DEC
        slot = slot_ref[0, jnp.where(decode, r, DEC + piece)]
        resumed = jnp.where(decode, 1, res_ref[0, piece])
        begins = (r <= DEC) | (r == starts[1]) | (r == starts[2]) | (r == starts[3])
        keep = jnp.where(begins, 0.0, 1.0).astype(F32)
        load = jnp.where(begins, resumed, 0).astype(F32)
        prior = state * keep + sc_ref[slot] * load
        decay = jnp.exp(step_ref[pl.ds(r, 1), :] * rate)
        b = jnp.concatenate([bb_ref[r]] * groups, axis=1)
        c = jnp.concatenate([cb_ref[r]] * groups, axis=1)
        fresh = decay * prior + drive_ref[pl.ds(r, 1), :] * b
        weighed = fresh * c
        pc_ref[r] = weighed[0:8] + weighed[8:16]
        ns_ref[slot] = fresh
        return fresh

    lax.fori_loop(0, ROWS, advance, jnp.zeros(rate.shape, F32), unroll=4)
    output = skip_ref[...] * values
    for k in range(8):
        output = output + pc_ref[:, k, :]
    gated = (output * silu(z_ref[...].astype(F32))).astype(BF)
    fetch.wait()
    x, c = here_ref[0], here_ref[1]
    for out, core in ((own_ref, c), (sib_ref, 1 - c)):
        for k in range(4):
            cols = pl.ds(pl.multiple_of((2 * lax.rem(x + k, 4) + core) * 512, 512), 512)
            out[k] = dot(gated, w_vmem[:, cols]).astype(BF)


def pick_kernel(
    here_ref, q0_ref, q1_ref, q2_ref, q3_ref, resid_ref, gain_ref, router_ref, chosen_ref,
    hid_ref, mine_ref, theirs_ref, named_ref,
):
    mixer = (
        q0_ref[...].astype(F32) + q1_ref[...].astype(F32)
        + q2_ref[...].astype(F32) + q3_ref[...].astype(F32)
    ).astype(BF)
    hidden = resid_ref[...].astype(F32) + mixer.astype(F32)
    hid_ref[...] = hidden
    scaled = (hidden * gain_ref[...]).astype(BF)
    wide = scaled.astype(F32)
    lane = iota((ROWS, 128), 1)
    squares = jnp.sum(hidden * hidden, axis=1, keepdims=True)
    stat = jnp.where(lane % 64 == EXPERTS, squares, 0.0)
    for e in range(EXPERTS):
        part = jnp.sum(wide * router_ref[e : e + 1].astype(F32), axis=1, keepdims=True)
        stat = jnp.where(lane % 64 == e, part, stat)
    high = stat.astype(BF).astype(F32)
    stat = jnp.where(lane < 64, high, stat - high).astype(BF)
    for out in (mine_ref, theirs_ref):
        out[0, :, 512:640] = stat[0:CAP]
        out[1, :, 512:640] = jnp.concatenate([stat[CAP:ROWS], jnp.zeros((2 * CAP - ROWS, 128), BF)], axis=0)
    before = (iota((ROWS, ROWS), 0) < iota((ROWS, ROWS), 1)).astype(F32).astype(BF)
    row = iota((CAP, ROWS), 0)
    z, core = here_ref[2], here_ref[1]
    for out, side in ((mine_ref, core), (theirs_ref, 1 - core)):
        for i in range(2):
            e = lax.rem(z + 2 * side + i, EXPERTS)
            marks = ((chosen_ref[0:1] == e) | (chosen_ref[1:2] == e)).astype(F32)
            marks = jnp.broadcast_to(marks, (8, ROWS))
            place = dot(marks.astype(BF), before).astype(I32)[0:1]
            hot = ((row == place) & (marks[0:1] > 0.0)).astype(F32).astype(BF)
            out[i, :, 0:512] = dot(hot, scaled).astype(BF)
    same = (iota((ROWS, ROWS), 0) == iota((ROWS, ROWS), 1)).astype(F32).astype(BF)
    pair = iota((8, ROWS), 0)
    both = jnp.where(pair == 0, chosen_ref[0:1], jnp.where(pair == 1, chosen_ref[1:2], 0))
    turned = lax.dot_general(
        same, both.astype(F32).astype(BF), (((1,), (1,)), ((), ())), preferred_element_type=F32
    )
    named_ref[...] = jnp.zeros_like(named_ref)
    named_ref[:, 0:8] = turned.astype(I32)


def experts_in(here_ref, side, x_ref, inv_ref, wg_ref, wu_ref):
    x = here_ref[0]
    by_row, by_col = jnp.where(side == 0, 4, 1), jnp.where(side == 0, 1, 4)
    gate = upper = square = None
    for k in range(4):
        there = lax.rem(x + 4 - k, 4)
        rows = pl.ds(pl.multiple_of(there * 1024, 1024), 1024)
        block = jnp.concatenate([x_ref[j * by_row + k * by_col] for j in range(4)], axis=0)
        gate_part = dot(block, wg_ref[rows, :])
        upper_part = dot(block, wu_ref[rows, :])
        wide = block.astype(F32)
        wide = wide * wide * inv_ref[there]
        square_part = wide[:, 0:128]
        for lane in range(128, 1024, 128):
            square_part = square_part + wide[:, lane : lane + 128]
        if k == 0:
            gate, upper, square = gate_part, upper_part, square_part
        else:
            gate, upper, square = gate + gate_part, upper + upper_part, square + square_part
    scale = lax.rsqrt(jnp.sum(square, axis=1, keepdims=True) / 4096.0 + EPS)
    return (silu(gate * scale) * (upper * scale)).astype(BF)


def experts_out(here_ref, side, act_ref, wd_ref, outs):
    x = here_ref[0]

    def product(k):
        cols = pl.ds(pl.multiple_of(lax.rem(x + k, 4) * 1024, 1024), 1024)
        return dot(act_ref[...], wd_ref[:, cols]).astype(BF)

    @pl.when(side == 0)
    def _():
        for k in range(4):
            value = product(k)
            for j in range(4):
                outs[(4 - j) % 4][k] = value[96 * j : 96 * j + 96]

    @pl.when(side == 1)
    def _():
        for k in range(4):
            value = product(k)
            for j in range(4):
                outs[k][(4 - j) % 4] = value[96 * j : 96 * j + 96]


def ffn_first(here_ref, x_ref, inv_ref, wg_ref, wu_ref, act_ref):
    act_ref[...] = experts_in(here_ref, here_ref[1], x_ref, inv_ref, wg_ref, wu_ref)


def ffn_second(
    here_ref, x_ref, inv_ref, wg_ref, wu_ref, wd_ref, earlier_ref,
    p0_ref, p1_ref, p2_ref, p3_ref, act_ref,
):
    side = 1 - here_ref[1]
    act_ref[...] = experts_in(here_ref, side, x_ref, inv_ref, wg_ref, wu_ref)
    experts_out(here_ref, side, act_ref, wd_ref, (p0_ref, p1_ref, p2_ref, p3_ref))


def ffn_third(here_ref, act_ref, wd_ref, p0_ref, p1_ref, p2_ref, p3_ref):
    experts_out(here_ref, here_ref[1], act_ref, wd_ref, (p0_ref, p1_ref, p2_ref, p3_ref))


def final_kernel(
    here_ref, mine_ref, theirs_ref, stat_ref, hid_ref, chosen_ref, out_ref,
):
    stat = stat_ref[0:ROWS].astype(F32)

    def column(e):
        return stat[:, e : e + 1] + stat[:, 64 + e : 65 + e]

    scale = lax.rsqrt(column(EXPERTS) / 4096.0 + EPS)
    e0, e1 = chosen_ref[:, 0:1], chosen_ref[:, 1:2]
    l0 = jnp.zeros((ROWS, 1), F32)
    l1 = jnp.zeros((ROWS, 1), F32)
    for e in range(EXPERTS):
        l0 = l0 + jnp.where(e0 == e, column(e), 0.0)
        l1 = l1 + jnp.where(e1 == e, column(e), 0.0)
    gap = (l0 - l1) * scale
    route0 = 1.0 / (1.0 + jnp.exp(-gap))
    route1 = 1.0 / (1.0 + jnp.exp(gap))
    before = (iota((ROWS, ROWS), 1) < iota((ROWS, ROWS), 0)).astype(F32).astype(BF)
    lane = iota((ROWS, CAP), 1)
    total = hid_ref[...]
    z, core = here_ref[2], here_ref[1]
    for ref, side in ((mine_ref, core), (theirs_ref, 1 - core)):
        for i in range(2):
            e = lax.rem(z + 2 * side + i, EXPERTS)
            first, second = e0 == e, e1 == e
            marks = jnp.broadcast_to((first | second).astype(F32), (ROWS, 128))
            place = dot(before, marks.astype(BF)).astype(I32)[:, 0:CAP]
            hot = ((lane == place) & (marks[:, 0:CAP] > 0.0)).astype(F32).astype(BF)
            weight = jnp.where(first, route0, jnp.where(second, route1, 0.0))
            total = total + weight * dot(hot, ref[i])
    out_ref[...] = total.astype(BF)


def move(value, axis, shift):
    size = lax.axis_size(axis)
    return lax.ppermute(value, axis, [(i, (i + shift) % size) for i in range(size)])


def by_core(value, first, second):
    sizes = tuple(lax.axis_size(name) for name in AXES)
    pairs = []
    for source in range(int(np.prod(sizes))):
        place = list(np.unravel_index(source, sizes))
        axis, shift = (first, second)[int(place[3])]
        at = AXES.index(axis)
        place[at] = (place[at] + shift) % sizes[at]
        pairs.append((source, int(np.ravel_multi_index(place, sizes))))
    return lax.ppermute(value, AXES, pairs)


def across(value, shift):
    return by_core(value, ("x", shift), ("y", shift))


def along(value, shift):
    return by_core(value, ("y", shift), ("x", shift))


def summed(*values):
    total = values[0].astype(F32)
    for value in values[1:]:
        total = total + value.astype(F32)
    return total[..., 0:64] + total[..., 64:128]


def coded(value):
    high = value.astype(BF)
    low = (value - high.astype(F32)).astype(BF)
    return jnp.concatenate([high, low], axis=-1)


def add(*values):
    total = values[0].astype(F32)
    for value in values[1:]:
        total = total + value.astype(F32)
    return total.astype(BF)


def stay(value):
    return pltpu.with_memory_space_constraint(value, pltpu.HBM)


def call(kernel, outs, ins, mib, scratch=(), flops=0, moved=0, name=None):
    single = not isinstance(outs, (list, tuple))
    return pl.pallas_call(
        kernel,
        out_shape=outs,
        in_specs=ins,
        out_specs=VMEM if single else [VMEM] * len(outs),
        scratch_shapes=list(scratch),
        compiler_params=params(mib),
        cost_estimate=pl.CostEstimate(flops=flops, bytes_accessed=moved, transcendentals=0),
        name=name,
    )


def shape(dims, dtype):
    return jax.ShapeDtypeStruct(dims, dtype)


def per_device(
    conv_input, gate_input, conv_cache, state_cache, span_lengths, span_resumes, slot_index,
    conv_weight, conv_bias, rank_weight, state_weight, step_gain, step_weight, step_bias,
    decay_log, skip_gain, out_weight, residual, moe_gain, router_weight, chosen_experts,
    gate_weight, up_weight, down_weight,
):
    here = jnp.stack(
        [lax.axis_index("x"), lax.axis_index("core"), lax.axis_index("z")]
    ).astype(I32)
    even = lax.axis_index("core") == 0
    cx, proj, new_conv = call(
        conv_kernel,
        [shape((ROWS, 1024), BF), shape((ROWS + 16, 640), BF), shape((3, SEQ, 1024), BF)],
        [HBM] * 10,
        16,
        [
            pltpu.SMEM((1, 4), I32),
            pltpu.SMEM((1, 4), I32),
            pltpu.SMEM((1, SEQ), I32),
            pltpu.VMEM((ROWS, 1024), BF),
            pltpu.VMEM((3, SEQ, 1024), BF),
            pltpu.VMEM((TAPS, 1024), F32),
            pltpu.VMEM((1, 1024), F32),
            pltpu.VMEM((1024, 512), BF),
            pltpu.VMEM((2 * NS, 1024), BF),
            pltpu.VMEM((1, 512), F32),
            pltpu.SemaphoreType.DMA((10,)),
        ],
        flops=10**9,
        moved=2 * 10**6,
        name="conv",
    )(
        *map(
            stay,
            (
                span_lengths, span_resumes, slot_index, conv_input,
                conv_cache.transpose(1, 0, 2), conv_weight, conv_bias.reshape(1, 1024),
                rank_weight, state_weight.T, moe_gain.reshape(1, 512),
            ),
        )
    )
    chip = add(proj, move(proj, "core", 1))
    parts = [chip] + [move(chip, "x", k) for k in (1, 2, 3)]
    new_state, own, sib, inverse = call(
        scan_kernel,
        [
            shape((SEQ, NS, 1024), F32),
            shape((4, ROWS, 512), BF),
            shape((4, ROWS, 512), BF),
            shape((4, 1, 1024), F32),
        ],
        [SMEM] * 4 + [VMEM] * 12 + [HBM],
        32,
        [
            pltpu.VMEM((1024, 4096), BF),
            pltpu.VMEM((ROWS, 1024), F32),
            pltpu.VMEM((ROWS, 1024), F32),
            pltpu.VMEM((ROWS, NS, 128), F32),
            pltpu.VMEM((ROWS, NS, 128), F32),
            pltpu.VMEM((ROWS, 8, 1024), F32),
            pltpu.VMEM((128, 128), F32),
            pltpu.SemaphoreType.DMA,
        ],
        flops=10**9,
        moved=10**7,
        name="scan",
    )(
        here, span_lengths, span_resumes, slot_index, *parts, cx, gate_input,
        step_gain.reshape(1, 512), step_weight, step_bias.reshape(1, 1024), decay_log,
        skip_gain.reshape(1, 1024), state_cache, stay(out_weight),
    )
    mixed = add(own, move(sib, "core", 1))
    parts = [mixed[0]] + [move(mixed[k], "x", k) for k in (1, 2, 3)]
    hidden, mine, theirs, named = call(
        pick_kernel,
        [
            shape((ROWS, 512), F32),
            shape((2, CAP, 640), BF),
            shape((2, CAP, 640), BF),
            shape((ROWS, 128), I32),
        ],
        [SMEM] + [VMEM] * 8,
        8,
        flops=10**8,
        moved=10**6,
        name="pick",
    )(here, *parts, residual, moe_gain.reshape(1, 512), router_weight.T, chosen_experts.T)
    theirs = move(theirs, "core", 1)
    stat = coded(summed(mine[:, :, 512:640], theirs[:, :, 512:640])).reshape(2 * CAP, 128)
    mine, theirs = mine[:, :, 0:512], theirs[:, :, 0:512]
    rows = jnp.concatenate([jnp.where(even, mine, theirs), jnp.where(even, theirs, mine)], axis=2)
    later = by_core(rows[1], ("z", 1), ("z", 3))
    sooner = by_core(rows[0], ("z", 0), ("z", 2))
    rows = jnp.concatenate([jnp.concatenate([sooner, later], axis=0), stat], axis=1)
    rows1, rows3 = across(rows, 1), across(rows, 3)
    rows2 = jnp.concatenate([across(rows1[0:CAP], 1), across(rows3[CAP : 2 * CAP], 3)], axis=0)

    stat = coded(summed(*[part[:, 1024:1152] for part in (rows, rows1, rows2, rows3)]))
    upper = jnp.stack([rows[:, 0:1024], rows1[:, 0:1024]])
    lower = jnp.stack([rows2[:, 0:1024], rows3[:, 0:1024]])
    upper1, lower3 = along(upper, 1), along(lower, 3)
    lower1, upper3 = along(lower, 1), along(upper, 3)
    upper2, lower2 = along(upper1, 1), along(lower3, 3)
    mine = jnp.concatenate(
        [upper, lower, upper1, lower1, upper2, lower2, upper3, lower3], axis=0
    )
    theirs = move(mine, "core", 1)
    gate, up, down = gate_weight[0], up_weight[0], down_weight[0]
    act = call(
        ffn_first,
        shape((384, 384), BF),
        [SMEM] + [VMEM] * 4,
        24,
        flops=2 * 384 * 4096 * 768,
        moved=10 * 10**6,
        name="experts_in",
    )(here, mine, inverse, gate, up)
    blocks = [shape((4, 96, 1024), BF)] * 4
    theirs = call(
        ffn_second,
        blocks,
        [SMEM] + [VMEM] * 6,
        32,
        [pltpu.VMEM((384, 384), BF)],
        flops=3 * 384 * 4096 * 768,
        moved=12 * 10**6,
        name="experts_other",
    )(here, theirs, inverse, gate, up, down, act)
    mine = call(
        ffn_third,
        blocks,
        [SMEM] + [VMEM] * 2,
        20,
        flops=384 * 4096 * 768,
        moved=6 * 10**6,
        name="experts_out",
    )(here, act, down)
    part = [None] * 4
    for m in (2, 1, 3, 0):
        part[m] = add(mine[m], move(theirs[m], "core", 1))
    far1, far3 = along(part[2][0:2], 1), along(part[2][2:4], 3)
    near1, near3 = along(part[1][2:4], 1), along(part[3][0:2], 3)
    next1, next3 = along(add(part[1][0:2], far1), 1), along(add(part[3][2:4], far3), 3)
    lines = jnp.concatenate(
        [add(part[0][0:2], next1, near3), add(part[0][2:4], near1, next3)], axis=0
    )
    lines = add(lines[0], *[across(lines[k], k) for k in (1, 2, 3)])
    later = by_core(lines[CAP : 2 * CAP], ("z", 3), ("z", 1))
    sooner = by_core(lines[0:CAP], ("z", 0), ("z", 2))
    lines = jnp.stack([sooner, later])
    left, right = lines[:, :, 0:512], lines[:, :, 512:1024]
    mine = jnp.where(even, left, right)
    theirs = jnp.concatenate([jnp.where(even, right, left), stat.reshape(2, CAP, 128)], axis=2)
    theirs = move(theirs, "core", 1)
    stat = jnp.where(even, stat, theirs[:, :, 512:640].reshape(2 * CAP, 128))
    theirs = theirs[:, :, 0:512]
    out = call(
        final_kernel,
        shape((ROWS, 512), BF),
        [SMEM] + [VMEM] * 5,
        8,
        flops=10**8,
        moved=10**6,
        name="combine",
    )(here, mine, theirs, stat, hidden, named)
    new_conv = new_conv.transpose(1, 0, 2)
    return (out, new_state, new_conv)


def solution(mesh):
    grid = Mesh(mesh.devices.reshape(4, 4, 4, 2), AXES)
    group, tensor = ("z", "y"), ("x", "core")
    return jax.shard_map(
        per_device,
        mesh=grid,
        in_specs=(
            P(group, tensor),
            P(group, tensor),
            P(group, None, tensor),
            P(group, None, tensor),
            P(group, None),
            P(group, None),
            P(group, None),
            P(None, tensor),
            P(tensor),
            P(tensor, None),
            P(tensor, None),
            P(),
            P(None, tensor),
            P(tensor),
            P(None, tensor),
            P(tensor),
            P(tensor, None),
            P(group, tensor),
            P(tensor),
            P(tensor, None),
            P(group, None),
            P(group, None, tensor),
            P(group, None, tensor),
            P(group, tensor, None),
        ),
        out_specs=(P(group, tensor), P(group, None, tensor), P(group, None, tensor)),
        check_vma=False,
    )
```

time: 181 us -> 138 us (0.76)
  waiting for transfers between devices: 71.3 us -> 52.7 us
  starting transfers between devices: 64.1 us -> 52.1 us
  local copies, waits for them, and re-layouts: 12.3 us -> 0.6 us
  Pallas kernels: 29.5 us -> 26.8 us
    ppermute x50 -> x15, waiting for transfers between devices: 71.3 us -> 12.7 us  [move(): lax.ppermute(value, axis, [(i, (i + shift) % size) for i in range(size)])]
    ppermute x50 -> x15, starting transfers between devices: 64.1 us -> 12.8 us  [move(): lax.ppermute(value, axis, [(i, (i + shift) % size) for i in range(size)])]
    ppermute x0 -> x23, waiting for transfers between devices: none -> 40 us  [by_core(): return lax.ppermute(value, AXES, pairs)]
    ppermute x0 -> x23, starting transfers between devices: none -> 39.3 us  [by_core(): return lax.ppermute(value, AXES, pairs)]
    unnamed x55 -> x45, local copies, waits for them, and re-layouts: 11.8 us -> 0.29 us
    pallas_call x6, Pallas kernels: 22.3 us -> 20.1 us  [the longest x1 6.43 us: per_device(): call(ffn_second, blocks, [SMEM] + [VMEM] * 6, 32, [pltpu.VMEM((384, 384),...]
  transfers between devices with their start and end apart: 50 -> 38, of which waited for: 32 -> 24; matrix products, arithmetic and copies ran while one was open for 1% -> 2% of each run, Pallas kernels for 4% -> 5%
where the time goes in v2:
time: 138 us; the launch traced here: 136 us
  waiting for transfers between devices  52.7 us (38%)
  starting transfers between devices  52.1 us (38%)
  Pallas kernels  26.8 us (19%)
  other arithmetic  2.84 us (2%)
    ppermute x23, waiting for transfers between devices, by_core(): return lax.ppermute(value, AXES, pairs)  40 us
    ppermute x23, starting transfers between devices, by_core(): return lax.ppermute(value, AXES, pairs)  39.3 us
    ppermute x15, starting transfers between devices, move(): lax.ppermute(value, axis, [(i, (i + shift) % size) for i in range(size)])  12.8 us
    ppermute x15, waiting for transfers between devices, move(): lax.ppermute(value, axis, [(i, (i + shift) % size) for i in range(size)])  12.7 us
    pallas_call x1, Pallas kernels, per_device(): call(scan_kernel, [shape((SEQ, NS, 1024), F32), shape((4, ROWS, 512), BF)...  6.7 us
    pallas_call x1, Pallas kernels, per_device(): call(ffn_second, blocks, [SMEM] + [VMEM] * 6, 32, [pltpu.VMEM((384, 384),...  6.43 us
    pallas_call x1, Pallas kernels, per_device(): call(ffn_first, shape((384, 384), BF), [SMEM] + [VMEM] * 4, 24, flops=2 *...  4.61 us
    pallas_call x1, Pallas kernels, per_device(): call(conv_kernel, [shape((ROWS, 1024), BF), shape((ROWS + 16, 640), BF),...  3.28 us
  transfers between devices with their start and end apart: 38, of which 24 were waited for; matrix products, arithmetic and copies ran while one was open for 2% of the time, Pallas kernels for 5%

profile of v2, /device:TPU:0, one launch (start us, length us, event | category | flops | bytes accessed | tf_op | source)
XLA Modules:
  0.0 136.5 jit_solution(17738793911392676883)
XLA Ops:
  0.7 3.3 %conv.1 = (bf16[64,1024]{1,0:T(8,128)(2,1)S(1)}, bf16[80,640]{1,0:T(8,128)(2,1)S(1)}, bf16[3,20,1024]{2,1,0:T(8,128)(2,1)}) custom-call(s32[1,4]{1,0:T(1,128)} %span_ref.1, s32[1,4]{1,0:T(1,128)} %res_ref.1, s32[1,20]{1,0:T(1,128)} %slot_ref.1, bf16[64,1024]{1,0:T(8,128)(2,1)} %x_hbm.1, bf16[3,20,1024]{2,1,0:T(8,128)(2,1)} %bitcast.78, f32[4,1024]{1,0:T(4,128)} %w_hbm.1, ...), custom_call_target="tpu_custom_call" | custom-call | flops 1000000000 | bytes 2000000 | tf_op jit(solution)/shard_map/conv/pallas_call | solution.py:417
  4.1 1.3 collective-permute-done
  5.5 1.6 %collective-permute-start.1 = (bf16[80,640]{1,0:T(8,128)(2,1)S(1)}, bf16[80,640]{1,0:T(8,128)(2,1)S(1)}, u32[]{:S(2)}, u32[]{:S(2)}) collective-permute-start(bf16[80,640]{1,0:T(8,128)(2,1)S(1)} %add_convert_fusion.9.q0_ref), channel_id=1, source_target_pairs={{0,2},{2,4},{4,6},{6,0},{1,3},{3,5},{5,7},{7,1},{8,10},{10,12},{12... | collective-permute-start | bytes 307208 | tf_op jit(solution)/shard_map/ppermute | solution.py:342
  7.1 2.7 %collective-permute-start.2 = (bf16[80,640]{1,0:T(8,128)(2,1)S(1)}, bf16[80,640]{1,0:T(8,128)(2,1)S(1)}, u32[]{:S(2)}, u32[]{:S(2)}) collective-permute-start(bf16[80,640]{1,0:T(8,128)(2,1)S(1)} %add_convert_fusion.9.q0_ref), channel_id=1, source_target_pairs={{0,4},{2,6},{4,0},{6,2},{1,5},{3,7},{5,1},{7,3},{8,12},{10,14},{12... | collective-permute-start | bytes 307208 | tf_op jit(solution)/shard_map/ppermute | solution.py:342
  9.8 1.4 %collective-permute-start.3 = (bf16[80,640]{1,0:T(8,128)(2,1)S(1)}, bf16[80,640]{1,0:T(8,128)(2,1)S(1)}, u32[]{:S(2)}, u32[]{:S(2)}) collective-permute-start(bf16[80,640]{1,0:T(8,128)(2,1)S(1)} %add_convert_fusion.9.q0_ref), channel_id=1, source_target_pairs={{0,6},{2,0},{4,2},{6,4},{1,7},{3,1},{5,3},{7,5},{8,14},{10,8},{12,... | collective-permute-start | bytes 307208 | tf_op jit(solution)/shard_map/ppermute | solution.py:342
  11.3 0.3 collective-permute-done.1.q1_ref
  11.7 3.3 %collective-permute-done.2.q2_ref = bf16[80,640]{1,0:T(8,128)(2,1)S(1)} collective-permute-done((bf16[80,640]{1,0:T(8,128)(2,1)S(1)}, bf16[80,640]{1,0:T(8,128)(2,1)S(1)}, u32[]{:S(2)}, u32[]{:S(2)}) %collective-permute-start.2) | collective-permute-done | bytes 102432 | tf_op jit(solution)/shard_map/ppermute | solution.py:342
  15.1 6.7 %scan.1 = (f32[20,16,1024]{2,1,0:T(8,128)}, bf16[4,64,512]{2,1,0:T(8,128)(2,1)S(1)}, bf16[4,64,512]{2,1,0:T(8,128)(2,1)S(1)}, f32[4,1,1024]{2,1,0:T(1,128)S(1)}) custom-call(s32[3]{0:T(128)S(1)} %pad_add_fusion.here_ref, s32[1,4]{1,0:T(1,128)S(1)} %copy-done.9, s32[1,4]{1,0:T(1,128)S(1)} %copy-done.10, s32[1,20]{1,0:T(1,128)S(1)} %copy-done.11, ...), custom_call_target="tpu_custom_call" | custom-call | flops 1000000000 | bytes 10000000 | tf_op jit(solution)/shard_map/scan/pallas_call | solution.py:450
  21.9 1.5 %collective-permute-done.4 = bf16[4,64,512]{2,1,0:T(8,128)(2,1)S(1)} collective-permute-done((bf16[4,64,512]{2,1,0:T(8,128)(2,1)S(1)}, bf16[4,64,512]{2,1,0:T(8,128)(2,1)S(1)}, u32[]{:S(2)}, u32[]{:S(2)}) %collective-permute-start.4) | collective-permute-done | bytes 262176 | tf_op jit(solution)/shard_map/ppermute | solution.py:342
  23.5 1.3 collective-permute-start.5
  24.8 2.4 %collective-permute-start.6 = (bf16[64,512]{1,0:T(8,128)(2,1)S(1)}, bf16[64,512]{1,0:T(8,128)(2,1)S(1)}, u32[]{:S(2)}, u32[]{:S(2)}) collective-permute-start(bf16[64,512]{1,0:T(8,128)(2,1)S(1)} %get-tuple-element.52), channel_id=1, source_target_pairs={{0,4},{2,6},{4,0},{6,2},{1,5},{3,7},{5,1},{7,3},{8,12},{10,14},{12... | collective-permute-start | bytes 196616 | tf_op jit(solution)/shard_map/ppermute | solution.py:342
  27.2 1.6 %collective-permute-start.7 = (bf16[64,512]{1,0:T(8,128)(2,1)S(1)}, bf16[64,512]{1,0:T(8,128)(2,1)S(1)}, u32[]{:S(2)}, u32[]{:S(2)}) collective-permute-start(bf16[64,512]{1,0:T(8,128)(2,1)S(1)} %get-tuple-element.51), channel_id=1, source_target_pairs={{0,6},{2,0},{4,2},{6,4},{1,7},{3,1},{5,3},{7,5},{8,14},{10,8},{12,... | collective-permute-start | bytes 196616 | tf_op jit(solution)/shard_map/ppermute | solution.py:342
  28.8 0.5 collective-permute-done.5.q1_ref
  29.3 1.5 %collective-permute-done.6.q2_ref = bf16[64,512]{1,0:T(8,128)(2,1)S(1)} collective-permute-done((bf16[64,512]{1,0:T(8,128)(2,1)S(1)}, bf16[64,512]{1,0:T(8,128)(2,1)S(1)}, u32[]{:S(2)}, u32[]{:S(2)}) %collective-permute-start.6) | collective-permute-done | bytes 65568 | tf_op jit(solution)/shard_map/ppermute | solution.py:342
  30.9 0.6 collective-permute-done.7.q3_ref
  31.5 1.2 pick.1
  32.8 1.3 collective-permute-done.8
  34.3 0.7 collective-permute-start.9
  35.0 2.0 %collective-permute-start.10 = (bf16[48,1024]{1,0:T(8,128)(2,1)S(1)}, bf16[48,1024]{1,0:T(8,128)(2,1)S(1)}, u32[]{:S(2)}, u32[]{:S(2)}) collective-permute-start(bf16[48,1024]{1,0:T(8,128)(2,1)S(1)} %get-tuple-element.61), channel_id=1, source_target_pairs={{0,32},{1,97},{2,34},{3,99},{4,36},{5,101},{6,38},{7,103},{8,40},{... | collective-permute-start | bytes 294920 | tf_op jit(solution)/shard_map/ppermute | solution.py:354
  37.1 5.7 %collective-permute-done.10 = bf16[48,1024]{1,0:T(8,128)(2,1)S(1)} collective-permute-done((bf16[48,1024]{1,0:T(8,128)(2,1)S(1)}, bf16[48,1024]{1,0:T(8,128)(2,1)S(1)}, u32[]{:S(2)}, u32[]{:S(2)}) %collective-permute-start.10) | collective-permute-done | bytes 98336 | tf_op jit(solution)/shard_map/ppermute | solution.py:354
  42.8 1.2 collective-permute-start.11
  44.0 2.1 %collective-permute-start.13 = (bf16[96,1152]{1,0:T(8,128)(2,1)S(1)}, bf16[96,1152]{1,0:T(8,128)(2,1)S(1)}, u32[]{:S(2)}, u32[]{:S(2)}) collective-permute-start(bf16[96,1152]{1,0:T(8,128)(2,1)S(1)} %pad_maximum_fusion.2), channel_id=1, source_target_pairs={{0,6},{1,25},{2,0},{3,27},{4,2},{5,29},{6,4},{7,31},{8,14},{9,1},{... | collective-permute-start | bytes 663560 | tf_op jit(solution)/shard_map/ppermute | solution.py:354
  46.1 3.9 %collective-permute-done.11 = bf16[96,1152]{1,0:T(8,128)(2,1)S(1)} collective-permute-done((bf16[96,1152]{1,0:T(8,128)(2,1)S(1)}, bf16[96,1152]{1,0:T(8,128)(2,1)S(1)}, u32[]{:S(2)}, u32[]{:S(2)}) %collective-permute-start.11) | collective-permute-done | bytes 221216 | tf_op jit(solution)/shard_map/ppermute | solution.py:354
  50.1 1.6 %collective-permute-start.15 = (bf16[2,96,1024]{2,1,0:T(8,128)(2,1)S(1)}, bf16[2,96,1024]{2,1,0:T(8,128)(2,1)S(1)}, u32[]{:S(2)}, u32[]{:S(2)}) collective-permute-start(bf16[2,96,1024]{2,1,0:T(8,128)(2,1)S(1)} %pad_maximum_fusion), channel_id=1, source_target_pairs={{0,8},{1,3},{2,10},{3,5},{4,12},{5,7},{6,14},{7,1},{8,16},{9,11},{... | collective-permute-start | bytes 1179656 | tf_op jit(solution)/shard_map/ppermute | solution.py:354
  51.8 1.7 %collective-permute-start.20 = (bf16[2,96,1024]{2,1,0:T(8,128)(2,1)S(1)}, bf16[2,96,1024]{2,1,0:T(8,128)(2,1)S(1)}, u32[]{:S(2)}, u32[]{:S(2)}) collective-permute-start(bf16[2,96,1024]{2,1,0:T(8,128)(2,1)S(1)} %pad_maximum_fusion), channel_id=1, source_target_pairs={{0,24},{1,7},{2,26},{3,1},{4,28},{5,3},{6,30},{7,5},{8,0},{9,15},{... | collective-permute-start | bytes 1179656 | tf_op jit(solution)/shard_map/ppermute | solution.py:354
  53.5 3.3 %collective-permute-start.14 = (bf16[48,1152]{1,0:T(8,128)(2,1)S(1)}, bf16[48,1152]{1,0:T(8,128)(2,1)S(1)}, u32[]{:S(2)}, u32[]{:S(2)}) collective-permute-start(bf16[48,1152]{1,0:T(8,128)(2,1)S(1)} %slice.172), channel_id=1, source_target_pairs={{0,6},{1,25},{2,0},{3,27},{4,2},{5,29},{6,4},{7,31},{8,14},{9,1},{... | collective-permute-start | bytes 331784 | tf_op jit(solution)/shard_map/ppermute | solution.py:354
  56.8 2.7 %collective-permute-done.12 = bf16[48,1152]{1,0:T(8,128)(2,1)S(1)} collective-permute-done((bf16[48,1152]{1,0:T(8,128)(2,1)S(1)}, bf16[48,1152]{1,0:T(8,128)(2,1)S(1)}, u32[]{:S(2)}, u32[]{:S(2)}) %collective-permute-start.12) | collective-permute-done | bytes 110624 | tf_op jit(solution)/shard_map/ppermute | solution.py:354
  59.6 1.9 %collective-permute-start.18 = (bf16[2,96,1024]{2,1,0:T(8,128)(2,1)S(1)}, bf16[2,96,1024]{2,1,0:T(8,128)(2,1)S(1)}, u32[]{:S(2)}, u32[]{:S(2)}) collective-permute-start(bf16[2,96,1024]{2,1,0:T(8,128)(2,1)S(1)} %pad_maximum_fusion.1), channel_id=1, source_target_pairs={{0,24},{1,7},{2,26},{3,1},{4,28},{5,3},{6,30},{7,5},{8,0},{9,15},{... | collective-permute-start | bytes 1179656 | tf_op jit(solution)/shard_map/ppermute | solution.py:354
  61.6 0.3 collective-permute-start.16
  61.8 0.5 collective-permute-start.17
  62.3 5.2 %collective-permute-done.18 = bf16[2,96,1024]{2,1,0:T(8,128)(2,1)S(1)} collective-permute-done((bf16[2,96,1024]{2,1,0:T(8,128)(2,1)S(1)}, bf16[2,96,1024]{2,1,0:T(8,128)(2,1)S(1)}, u32[]{:S(2)}, u32[]{:S(2)}) %collective-permute-start.18) | collective-permute-done | bytes 393248 | tf_op jit(solution)/shard_map/ppermute | solution.py:354
  67.5 3.0 %collective-permute-start.19 = (bf16[2,96,1024]{2,1,0:T(8,128)(2,1)S(1)}, bf16[2,96,1024]{2,1,0:T(8,128)(2,1)S(1)}, u32[]{:S(2)}, u32[]{:S(2)}) collective-permute-start(bf16[2,96,1024]{2,1,0:T(8,128)(2,1)S(1)} %collective-permute-done.18), channel_id=1, source_target_pairs={{0,24},{1,7},{2,26},{3,1},{4,28},{5,3},{6,30},{7,5},{8,0},{9,15},{... | collective-permute-start | bytes 1179656 | tf_op jit(solution)/shard_map/ppermute | solution.py:354
  70.6 4.2 %collective-permute-done.17 = bf16[2,96,1024]{2,1,0:T(8,128)(2,1)S(1)} collective-permute-done((bf16[2,96,1024]{2,1,0:T(8,128)(2,1)S(1)}, bf16[2,96,1024]{2,1,0:T(8,128)(2,1)S(1)}, u32[]{:S(2)}, u32[]{:S(2)}) %collective-permute-start.17) | collective-permute-done | bytes 393248 | tf_op jit(solution)/shard_map/ppermute | solution.py:354
  74.9 1.0 collective-permute-done.19
  76.1 4.6 %experts_in.1.act_ref.earlier_ref = bf16[384,384]{1,0:T(8,128)(2,1)S(1)} custom-call(s32[3]{0:T(128)S(1)} %pad_add_fusion.here_ref, bf16[16,96,1024]{2,1,0:T(8,128)(2,1)S(1)} %constant_dynamic-update-slice_fusion.4.x_ref, f32[4,1,1024]{2,1,0:T(1,128)S(1)} %get-tuple-element.28.inv_ref, bf16[4096,384]{1,0:T(8,128)(2,1)S(1)} %bitcast.60, ...), custom_call_target="tpu_custom_call" | custom-call | flops 2415919104 | bytes 10000000 | tf_op jit(solution)/shard_map/experts_in/pallas_call | solution.py:515
  80.7 1.0 collective-permute-done.21.x_ref
  81.7 6.4 %experts_other.1 = (bf16[4,96,1024]{2,1,0:T(8,128)(2,1)S(1)}, bf16[4,96,1024]{2,1,0:T(8,128)(2,1)S(1)}, bf16[4,96,1024]{2,1,0:T(8,128)(2,1)S(1)}, bf16[4,96,1024]{2,1,0:T(8,128)(2,1)S(1)}) custom-call(s32[3]{0:T(128)S(1)} %pad_add_fusion.here_ref, bf16[16,96,1024]{2,1,0:T(8,128)(2,1)S(1)} %collective-permute-done.21.x_ref, ...), custom_call_target="tpu_custom_call" | custom-call | flops 3623878656 | bytes 12000000 | tf_op jit(solution)/shard_map/experts_other/pallas_call | solution.py:525
  88.1 0.2 collective-permute-start.24
  88.3 0.4 collective-permute-start.23
  88.7 2.6 %experts_out.1 = (bf16[4,96,1024]{2,1,0:T(8,128)(2,1)S(1)}, bf16[4,96,1024]{2,1,0:T(8,128)(2,1)S(1)}, bf16[4,96,1024]{2,1,0:T(8,128)(2,1)S(1)}, bf16[4,96,1024]{2,1,0:T(8,128)(2,1)S(1)}) custom-call(s32[3]{0:T(128)S(1)} %pad_add_fusion.here_ref, bf16[384,384]{1,0:T(8,128)(2,1)S(1)} %experts_in.1.act_ref.earlier_ref, bf16[384,4096]{1,0:T(8,128)(2,1)S(1)} %bitcast.68), custom_call_target="tpu_custom_call" | custom-call | flops 1207959552 | bytes 6000000 | tf_op jit(solution)/shard_map/experts_out/pallas_call | solution.py:535
  91.5 0.4 collective-permute-start.22
  91.9 0.3 add_convert_fusion.1
  92.2 3.8 %collective-permute-start.31 = (bf16[2,96,1024]{2,1,0:T(8,128)(2,1)S(1)}, bf16[2,96,1024]{2,1,0:T(8,128)(2,1)S(1)}, u32[]{:S(2)}, u32[]{:S(2)}) collective-permute-start(bf16[2,96,1024]{2,1,0:T(8,128)(2,1)S(1)} %get-tuple-element.48), channel_id=1, source_target_pairs={{0,24},{1,7},{2,26},{3,1},{4,28},{5,3},{6,30},{7,5},{8,0},{9,15},{... | collective-permute-start | bytes 1179656 | tf_op jit(solution)/shard_map/ppermute | solution.py:354
  96.0 0.3 add_convert_fusion.2
  96.4 0.3 add_convert_fusion
  96.8 3.3 %collective-permute-start.28 = (bf16[2,96,1024]{2,1,0:T(8,128)(2,1)S(1)}, bf16[2,96,1024]{2,1,0:T(8,128)(2,1)S(1)}, u32[]{:S(2)}, u32[]{:S(2)}) collective-permute-start(bf16[2,96,1024]{2,1,0:T(8,128)(2,1)S(1)} %slice.178), channel_id=1, source_target_pairs={{0,24},{1,7},{2,26},{3,1},{4,28},{5,3},{6,30},{7,5},{8,0},{9,15},{... | collective-permute-start | bytes 1179656 | tf_op jit(solution)/shard_map/ppermute | solution.py:354
  100.1 1.2 collective-permute-done.31
  101.4 3.8 %collective-permute-start.32 = (bf16[2,96,1024]{2,1,0:T(8,128)(2,1)S(1)}, bf16[2,96,1024]{2,1,0:T(8,128)(2,1)S(1)}, u32[]{:S(2)}, u32[]{:S(2)}) collective-permute-start(bf16[2,96,1024]{2,1,0:T(8,128)(2,1)S(1)} %add_convert_fusion.5), channel_id=1, source_target_pairs={{0,24},{1,7},{2,26},{3,1},{4,28},{5,3},{6,30},{7,5},{8,0},{9,15},{... | collective-permute-start | bytes 1179656 | tf_op jit(solution)/shard_map/ppermute | solution.py:354
  105.5 0.3 add_convert_fusion.3
  105.8 3.4 %collective-permute-done.30 = bf16[2,96,1024]{2,1,0:T(8,128)(2,1)S(1)} collective-permute-done((bf16[2,96,1024]{2,1,0:T(8,128)(2,1)S(1)}, bf16[2,96,1024]{2,1,0:T(8,128)(2,1)S(1)}, u32[]{:S(2)}, u32[]{:S(2)}) %collective-permute-start.30) | collective-permute-done | bytes 393248 | tf_op jit(solution)/shard_map/ppermute | solution.py:354
  109.2 1.3 collective-permute-done.32
  110.5 3.9 %collective-permute-done.26 = bf16[2,96,1024]{2,1,0:T(8,128)(2,1)S(1)} collective-permute-done((bf16[2,96,1024]{2,1,0:T(8,128)(2,1)S(1)}, bf16[2,96,1024]{2,1,0:T(8,128)(2,1)S(1)}, u32[]{:S(2)}, u32[]{:S(2)}) %collective-permute-start.26) | collective-permute-done | bytes 393248 | tf_op jit(solution)/shard_map/ppermute | solution.py:354
  114.4 0.4 add_convert_fusion.6
  114.9 4.9 %collective-permute-start.33 = (bf16[96,1024]{1,0:T(8,128)(2,1)S(1)}, bf16[96,1024]{1,0:T(8,128)(2,1)S(1)}, u32[]{:S(2)}, u32[]{:S(2)}) collective-permute-start(bf16[96,1024]{1,0:T(8,128)(2,1)S(1)} %get-tuple-element.49), channel_id=1, source_target_pairs={{0,4},{1,17},{2,6},{3,19},{4,0},{5,21},{6,2},{7,23},{8,12},{9,25},... | collective-permute-start | bytes 589832 | tf_op jit(solution)/shard_map/ppermute | solution.py:354
  119.8 0.6 collective-permute-start.34
  120.4 1.5 %collective-permute-start.29 = (bf16[96,1024]{1,0:T(8,128)(2,1)S(1)}, bf16[96,1024]{1,0:T(8,128)(2,1)S(1)}, u32[]{:S(2)}, u32[]{:S(2)}) collective-permute-start(bf16[96,1024]{1,0:T(8,128)(2,1)S(1)} %slice_bitcast_fusion.2), channel_id=1, source_target_pairs={{0,2},{1,9},{2,4},{3,11},{4,6},{5,13},{6,0},{7,15},{8,10},{9,17},{... | collective-permute-start | bytes 589832 | tf_op jit(solution)/shard_map/ppermute | solution.py:354
  122.0 1.4 %collective-permute-done.33 = bf16[96,1024]{1,0:T(8,128)(2,1)S(1)} collective-permute-done((bf16[96,1024]{1,0:T(8,128)(2,1)S(1)}, bf16[96,1024]{1,0:T(8,128)(2,1)S(1)}, u32[]{:S(2)}, u32[]{:S(2)}) %collective-permute-start.33) | collective-permute-done | bytes 196640 | tf_op jit(solution)/shard_map/ppermute | solution.py:354
  123.4 3.5 %collective-permute-done.34 = bf16[96,1024]{1,0:T(8,128)(2,1)S(1)} collective-permute-done((bf16[96,1024]{1,0:T(8,128)(2,1)S(1)}, bf16[96,1024]{1,0:T(8,128)(2,1)S(1)}, u32[]{:S(2)}, u32[]{:S(2)}) %collective-permute-start.34) | collective-permute-done | bytes 196640 | tf_op jit(solution)/shard_map/ppermute | solution.py:354
  126.9 0.4 collective-permute-done.29
  127.5 0.7 collective-permute-start.35
  128.2 2.3 %collective-permute-start.36 = (bf16[48,1024]{1,0:T(8,128)(2,1)S(1)}, bf16[48,1024]{1,0:T(8,128)(2,1)S(1)}, u32[]{:S(2)}, u32[]{:S(2)}) collective-permute-start(bf16[48,1024]{1,0:T(8,128)(2,1)S(1)} %get-tuple-element.60), channel_id=1, source_target_pairs={{0,96},{1,33},{2,98},{3,35},{4,100},{5,37},{6,102},{7,39},{8,104},... | collective-permute-start | bytes 294920 | tf_op jit(solution)/shard_map/ppermute | solution.py:354
  130.6 2.3 %collective-permute-done.36 = bf16[48,1024]{1,0:T(8,128)(2,1)S(1)} collective-permute-done((bf16[48,1024]{1,0:T(8,128)(2,1)S(1)}, bf16[48,1024]{1,0:T(8,128)(2,1)S(1)}, u32[]{:S(2)}, u32[]{:S(2)}) %collective-permute-start.36) | collective-permute-done | bytes 98336 | tf_op jit(solution)/shard_map/ppermute | solution.py:354
  133.0 1.3 collective-permute-done.37
  134.4 2.0 %combine.1 = bf16[64,512]{1,0:T(8,128)(2,1)} custom-call(s32[3]{0:T(128)S(1)} %pad_add_fusion.here_ref, bf16[2,48,512]{2,1,0:T(8,128)(2,1)S(1)} %get-tuple-element.58.mine_ref, bf16[2,48,512]{2,1,0:T(8,128)(2,1)S(1)} %slice.196.theirs_ref, bf16[96,128]{1,0:T(8,128)(2,1)S(1)} %bitcast_select_fusion.stat_ref, f32[64,512]{1,0:T(8,128)S(1)} %get-tuple-element.37.hid_ref, ...), custom_call_target="tpu_custom_call" | custom-call | flops 100000000 | bytes 1000000 | tf_op jit(solution)/shard_map/combine/pallas_call | solution.py:563
  (106 shorter events, 2.7 us)
Async XLA Ops:
  0.6 14.3 %copy-start.9 = (s32[1,4]{1,0:T(1,128)S(1)}, s32[1,4]{1,0:T(1,128)}, u32[]{:S(2)}) copy-start(s32[1,4]{1,0:T(1,128)} %span_ref.1) | copy-start | bytes 52
  0.6 14.3 %copy-start.10 = (s32[1,4]{1,0:T(1,128)S(1)}, s32[1,4]{1,0:T(1,128)}, u32[]{:S(2)}) copy-start(s32[1,4]{1,0:T(1,128)} %res_ref.1) | copy-start | bytes 52
  0.7 14.3 %copy-start.11 = (s32[1,20]{1,0:T(1,128)S(1)}, s32[1,20]{1,0:T(1,128)}, u32[]{:S(2)}) copy-start(s32[1,20]{1,0:T(1,128)} %slot_ref.1) | copy-start | bytes 244
  0.7 14.3 %copy-start.8 = (f32[512]{0:T(512)S(1)}, f32[512]{0:T(512)}, u32[]{:S(2)}) copy-start(f32[512]{0:T(512)} %param.35) | copy-start | bytes 6148
  0.7 14.3 %copy-start.6 = (f32[1024]{0:T(1024)S(1)}, f32[1024]{0:T(1024)}, u32[]{:S(2)}) copy-start(f32[1024]{0:T(1024)} %param.37) | copy-start | bytes 12292
  0.7 14.3 %copy-start.7 = (f32[1024]{0:T(1024)S(1)}, f32[1024]{0:T(1024)}, u32[]{:S(2)}) copy-start(f32[1024]{0:T(1024)} %param.39) | copy-start | bytes 12292
  0.7 14.3 %copy-start.4 = (bf16[64,1024]{1,0:T(8,128)(2,1)S(1)}, bf16[64,1024]{1,0:T(8,128)(2,1)}, u32[]{:S(2)}) copy-start(bf16[64,1024]{1,0:T(8,128)(2,1)} %z_ref.1) | copy-start | bytes 393220
  0.7 14.3 %copy-start.2 = (f32[20,16,1024]{2,1,0:T(8,128)S(1)}, f32[20,16,1024]{2,1,0:T(8,128)}, u32[]{:S(2)}) copy-start(f32[20,16,1024]{2,1,0:T(8,128)} %sc_ref.1) | copy-start | bytes 3932164
  0.7 14.3 %copy-start.3 = (bf16[512,1024]{1,0:T(8,128)(2,1)S(1)}, bf16[512,1024]{1,0:T(8,128)(2,1)}, u32[]{:S(2)}) copy-start(bf16[512,1024]{1,0:T(8,128)(2,1)} %sw_ref.1) | copy-start | bytes 3145732
  0.7 14.3 %copy-start.5 = (f32[16,1024]{1,0:T(8,128)S(1)}, f32[16,1024]{1,0:T(8,128)}, u32[]{:S(2)}) copy-start(f32[16,1024]{1,0:T(8,128)} %dl_ref.1) | copy-start | bytes 196612
  4.0 1.4 %collective-permute-start = (bf16[80,640]{1,0:T(8,128)(2,1)S(1)}, bf16[80,640]{1,0:T(8,128)(2,1)S(1)}, u32[]{:S(2)}, u32[]{:S(2)}) collective-permute-start(bf16[80,640]{1,0:T(8,128)(2,1)S(1)} %get-tuple-element.22), channel_id=1, source_target_pairs={{0,1},{1,0},{2,3},{3,2},{4,5},{5,4},{6,7},{7,6},{8,9},{9,8},{10,11... | collective-permute-start | bytes 307208 | tf_op jit(solution)/shard_map/ppermute | solution.py:342
  5.5 6.2 %collective-permute-start.1 = (bf16[80,640]{1,0:T(8,128)(2,1)S(1)}, bf16[80,640]{1,0:T(8,128)(2,1)S(1)}, u32[]{:S(2)}, u32[]{:S(2)}) collective-permute-start(bf16[80,640]{1,0:T(8,128)(2,1)S(1)} %add_convert_fusion.9.q0_ref), channel_id=1, source_target_pairs={{0,2},{2,4},{4,6},{6,0},{1,3},{3,5},{5,7},{7,1},{8,10},{10,12},{12... | collective-permute-start | bytes 307208 | tf_op jit(solution)/shard_map/ppermute | solution.py:342
  7.1 7.8 %collective-permute-start.2 = (bf16[80,640]{1,0:T(8,128)(2,1)S(1)}, bf16[80,640]{1,0:T(8,128)(2,1)S(1)}, u32[]{:S(2)}, u32[]{:S(2)}) collective-permute-start(bf16[80,640]{1,0:T(8,128)(2,1)S(1)} %add_convert_fusion.9.q0_ref), channel_id=1, source_target_pairs={{0,4},{2,6},{4,0},{6,2},{1,5},{3,7},{5,1},{7,3},{8,12},{10,14},{12... | collective-permute-start | bytes 307208 | tf_op jit(solution)/shard_map/ppermute | solution.py:342
  9.8 5.1 %collective-permute-start.3 = (bf16[80,640]{1,0:T(8,128)(2,1)S(1)}, bf16[80,640]{1,0:T(8,128)(2,1)S(1)}, u32[]{:S(2)}, u32[]{:S(2)}) collective-permute-start(bf16[80,640]{1,0:T(8,128)(2,1)S(1)} %add_convert_fusion.9.q0_ref), channel_id=1, source_target_pairs={{0,6},{2,0},{4,2},{6,4},{1,7},{3,1},{5,3},{7,5},{8,14},{10,8},{12,... | collective-permute-start | bytes 307208 | tf_op jit(solution)/shard_map/ppermute | solution.py:342
  15.0 16.5 %copy-start.13 = (bf16[64,512]{1,0:T(8,128)(2,1)S(1)}, bf16[64,512]{1,0:T(8,128)(2,1)}, u32[]{:S(2)}) copy-start(bf16[64,512]{1,0:T(8,128)(2,1)} %resid_ref.1) | copy-start | bytes 196612
  15.0 16.5 %copy-start.14 = (bf16[512,4]{0,1:T(4,128)(2,1)S(1)}, bf16[512,4]{0,1:T(4,128)(2,1)}, u32[]{:S(2)}) copy-start(bf16[512,4]{0,1:T(4,128)(2,1)} %param.43) | copy-start | bytes 12292
  15.0 16.4 %copy-start.15 = (f32[512]{0:T(512)S(1)}, f32[512]{0:T(512)}, u32[]{:S(2)}) copy-start(f32[512]{0:T(512)} %param.42) | copy-start | bytes 6148
  15.1 16.4 %copy-start.16 = (s32[64,2]{0,1:T(2,128)S(1)}, s32[64,2]{0,1:T(2,128)}, u32[]{:S(2)}) copy-start(s32[64,2]{0,1:T(2,128)} %param.44) | copy-start | bytes 1540
  21.8 1.6 %collective-permute-start.4 = (bf16[4,64,512]{2,1,0:T(8,128)(2,1)S(1)}, bf16[4,64,512]{2,1,0:T(8,128)(2,1)S(1)}, u32[]{:S(2)}, u32[]{:S(2)}) collective-permute-start(bf16[4,64,512]{2,1,0:T(8,128)(2,1)S(1)} %get-tuple-element.25), channel_id=1, source_target_pairs={{0,1},{1,0},{2,3},{3,2},{4,5},{5,4},{6,7},{7,6},{8,9},{9,8},{10,11... | collective-permute-start | bytes 786440 | tf_op jit(solution)/shard_map/ppermute | solution.py:342
  23.5 5.8 %collective-permute-start.5 = (bf16[64,512]{1,0:T(8,128)(2,1)S(1)}, bf16[64,512]{1,0:T(8,128)(2,1)S(1)}, u32[]{:S(2)}, u32[]{:S(2)}) collective-permute-start(bf16[64,512]{1,0:T(8,128)(2,1)S(1)} %get-tuple-element.53), channel_id=1, source_target_pairs={{0,2},{2,4},{4,6},{6,0},{1,3},{3,5},{5,7},{7,1},{8,10},{10,12},{12... | collective-permute-start | bytes 196616 | tf_op jit(solution)/shard_map/ppermute | solution.py:342
  24.8 6.0 %collective-permute-start.6 = (bf16[64,512]{1,0:T(8,128)(2,1)S(1)}, bf16[64,512]{1,0:T(8,128)(2,1)S(1)}, u32[]{:S(2)}, u32[]{:S(2)}) collective-permute-start(bf16[64,512]{1,0:T(8,128)(2,1)S(1)} %get-tuple-element.52), channel_id=1, source_target_pairs={{0,4},{2,6},{4,0},{6,2},{1,5},{3,7},{5,1},{7,3},{8,12},{10,14},{12... | collective-permute-start | bytes 196616 | tf_op jit(solution)/shard_map/ppermute | solution.py:342
  27.2 4.3 %collective-permute-start.7 = (bf16[64,512]{1,0:T(8,128)(2,1)S(1)}, bf16[64,512]{1,0:T(8,128)(2,1)S(1)}, u32[]{:S(2)}, u32[]{:S(2)}) collective-permute-start(bf16[64,512]{1,0:T(8,128)(2,1)S(1)} %get-tuple-element.51), channel_id=1, source_target_pairs={{0,6},{2,0},{4,2},{6,4},{1,7},{3,1},{5,3},{7,5},{8,14},{10,8},{12,... | collective-permute-start | bytes 196616 | tf_op jit(solution)/shard_map/ppermute | solution.py:342
  32.7 1.4 %collective-permute-start.8 = (bf16[2,48,640]{2,1,0:T(8,128)(2,1)S(1)}, bf16[2,48,640]{2,1,0:T(8,128)(2,1)S(1)}, u32[]{:S(2)}, u32[]{:S(2)}) collective-permute-start(bf16[2,48,640]{2,1,0:T(8,128)(2,1)S(1)} %get-tuple-element.27), channel_id=1, source_target_pairs={{0,1},{1,0},{2,3},{3,2},{4,5},{5,4},{6,7},{7,6},{8,9},{9,8},{10,11... | collective-permute-start | bytes 368648 | tf_op jit(solution)/shard_map/ppermute | solution.py:342
  34.3 2.8 %collective-permute-start.9 = (bf16[48,1024]{1,0:T(8,128)(2,1)S(1)}, bf16[48,1024]{1,0:T(8,128)(2,1)S(1)}, u32[]{:S(2)}, u32[]{:S(2)}) collective-permute-start(bf16[48,1024]{1,0:T(8,128)(2,1)S(1)} %get-tuple-element.62), channel_id=1, source_target_pairs={{0,0},{1,65},{2,2},{3,67},{4,4},{5,69},{6,6},{7,71},{8,8},{9,73},{... | collective-permute-start | bytes 294920 | tf_op jit(solution)/shard_map/ppermute | solution.py:354
  35.0 7.8 %collective-permute-start.10 = (bf16[48,1024]{1,0:T(8,128)(2,1)S(1)}, bf16[48,1024]{1,0:T(8,128)(2,1)S(1)}, u32[]{:S(2)}, u32[]{:S(2)}) collective-permute-start(bf16[48,1024]{1,0:T(8,128)(2,1)S(1)} %get-tuple-element.61), channel_id=1, source_target_pairs={{0,32},{1,97},{2,34},{3,99},{4,36},{5,101},{6,38},{7,103},{8,40},{... | collective-permute-start | bytes 294920 | tf_op jit(solution)/shard_map/ppermute | solution.py:354
  42.8 7.2 %collective-permute-start.11 = (bf16[96,1152]{1,0:T(8,128)(2,1)S(1)}, bf16[96,1152]{1,0:T(8,128)(2,1)S(1)}, u32[]{:S(2)}, u32[]{:S(2)}) collective-permute-start(bf16[96,1152]{1,0:T(8,128)(2,1)S(1)} %pad_maximum_fusion.2), channel_id=1, source_target_pairs={{0,2},{1,9},{2,4},{3,11},{4,6},{5,13},{6,0},{7,15},{8,10},{9,17},{... | collective-permute-start | bytes 663560 | tf_op jit(solution)/shard_map/ppermute | solution.py:354
  44.0 9.5 %collective-permute-start.13 = (bf16[96,1152]{1,0:T(8,128)(2,1)S(1)}, bf16[96,1152]{1,0:T(8,128)(2,1)S(1)}, u32[]{:S(2)}, u32[]{:S(2)}) collective-permute-start(bf16[96,1152]{1,0:T(8,128)(2,1)S(1)} %pad_maximum_fusion.2), channel_id=1, source_target_pairs={{0,6},{1,25},{2,0},{3,27},{4,2},{5,29},{6,4},{7,31},{8,14},{9,1},{... | collective-permute-start | bytes 663560 | tf_op jit(solution)/shard_map/ppermute | solution.py:354
  50.1 11.7 %collective-permute-start.15 = (bf16[2,96,1024]{2,1,0:T(8,128)(2,1)S(1)}, bf16[2,96,1024]{2,1,0:T(8,128)(2,1)S(1)}, u32[]{:S(2)}, u32[]{:S(2)}) collective-permute-start(bf16[2,96,1024]{2,1,0:T(8,128)(2,1)S(1)} %pad_maximum_fusion), channel_id=1, source_target_pairs={{0,8},{1,3},{2,10},{3,5},{4,12},{5,7},{6,14},{7,1},{8,16},{9,11},{... | collective-permute-start | bytes 1179656 | tf_op jit(solution)/shard_map/ppermute | solution.py:354
  51.8 24.1 %collective-permute-start.20 = (bf16[2,96,1024]{2,1,0:T(8,128)(2,1)S(1)}, bf16[2,96,1024]{2,1,0:T(8,128)(2,1)S(1)}, u32[]{:S(2)}, u32[]{:S(2)}) collective-permute-start(bf16[2,96,1024]{2,1,0:T(8,128)(2,1)S(1)} %pad_maximum_fusion), channel_id=1, source_target_pairs={{0,24},{1,7},{2,26},{3,1},{4,28},{5,3},{6,30},{7,5},{8,0},{9,15},{... | collective-permute-start | bytes 1179656 | tf_op jit(solution)/shard_map/ppermute | solution.py:354
  53.4 6.1 %collective-permute-start.12 = (bf16[48,1152]{1,0:T(8,128)(2,1)S(1)}, bf16[48,1152]{1,0:T(8,128)(2,1)S(1)}, u32[]{:S(2)}, u32[]{:S(2)}) collective-permute-start(bf16[48,1152]{1,0:T(8,128)(2,1)S(1)} %slice.171), channel_id=1, source_target_pairs={{0,2},{1,9},{2,4},{3,11},{4,6},{5,13},{6,0},{7,15},{8,10},{9,17},{... | collective-permute-start | bytes 331784 | tf_op jit(solution)/shard_map/ppermute | solution.py:354
  53.5 6.0 %collective-permute-start.14 = (bf16[48,1152]{1,0:T(8,128)(2,1)S(1)}, bf16[48,1152]{1,0:T(8,128)(2,1)S(1)}, u32[]{:S(2)}, u32[]{:S(2)}) collective-permute-start(bf16[48,1152]{1,0:T(8,128)(2,1)S(1)} %slice.172), channel_id=1, source_target_pairs={{0,6},{1,25},{2,0},{3,27},{4,2},{5,29},{6,4},{7,31},{8,14},{9,1},{... | collective-permute-start | bytes 331784 | tf_op jit(solution)/shard_map/ppermute | solution.py:354
  59.6 16.5 %copy-start.1 = (bf16[1,4096,384]{2,1,0:T(8,128)(2,1)S(1)}, bf16[1,4096,384]{2,1,0:T(8,128)(2,1)}, u32[]{:S(2)}) copy-start(bf16[1,4096,384]{2,1,0:T(8,128)(2,1)} %param.46) | copy-start | bytes 9437188
  59.6 16.4 %copy-start = (bf16[1,4096,384]{2,1,0:T(8,128)(2,1)S(1)}, bf16[1,4096,384]{2,1,0:T(8,128)(2,1)}, u32[]{:S(2)}) copy-start(bf16[1,4096,384]{2,1,0:T(8,128)(2,1)} %param.45) | copy-start | bytes 9437188
  59.6 7.8 %collective-permute-start.18 = (bf16[2,96,1024]{2,1,0:T(8,128)(2,1)S(1)}, bf16[2,96,1024]{2,1,0:T(8,128)(2,1)S(1)}, u32[]{:S(2)}, u32[]{:S(2)}) collective-permute-start(bf16[2,96,1024]{2,1,0:T(8,128)(2,1)S(1)} %pad_maximum_fusion.1), channel_id=1, source_target_pairs={{0,24},{1,7},{2,26},{3,1},{4,28},{5,3},{6,30},{7,5},{8,0},{9,15},{... | collective-permute-start | bytes 1179656 | tf_op jit(solution)/shard_map/ppermute | solution.py:354
  61.6 9.1 %collective-permute-start.16 = (bf16[2,96,1024]{2,1,0:T(8,128)(2,1)S(1)}, bf16[2,96,1024]{2,1,0:T(8,128)(2,1)S(1)}, u32[]{:S(2)}, u32[]{:S(2)}) collective-permute-start(bf16[2,96,1024]{2,1,0:T(8,128)(2,1)S(1)} %pad_maximum_fusion.1), channel_id=1, source_target_pairs={{0,8},{1,3},{2,10},{3,5},{4,12},{5,7},{6,14},{7,1},{8,16},{9,11},{... | collective-permute-start | bytes 1179656 | tf_op jit(solution)/shard_map/ppermute | solution.py:354
  61.8 13.0 %collective-permute-start.17 = (bf16[2,96,1024]{2,1,0:T(8,128)(2,1)S(1)}, bf16[2,96,1024]{2,1,0:T(8,128)(2,1)S(1)}, u32[]{:S(2)}, u32[]{:S(2)}) collective-permute-start(bf16[2,96,1024]{2,1,0:T(8,128)(2,1)S(1)} %collective-permute-done.15), channel_id=1, source_target_pairs={{0,8},{1,3},{2,10},{3,5},{4,12},{5,7},{6,14},{7,1},{8,16},{9,11},{... | collective-permute-start | bytes 1179656 | tf_op jit(solution)/shard_map/ppermute | solution.py:354
  67.5 8.3 %collective-permute-start.19 = (bf16[2,96,1024]{2,1,0:T(8,128)(2,1)S(1)}, bf16[2,96,1024]{2,1,0:T(8,128)(2,1)S(1)}, u32[]{:S(2)}, u32[]{:S(2)}) collective-permute-start(bf16[2,96,1024]{2,1,0:T(8,128)(2,1)S(1)} %collective-permute-done.18), channel_id=1, source_target_pairs={{0,24},{1,7},{2,26},{3,1},{4,28},{5,3},{6,30},{7,5},{8,0},{9,15},{... | collective-permute-start | bytes 1179656 | tf_op jit(solution)/shard_map/ppermute | solution.py:354
  75.9 5.7 %collective-permute-start.21 = (bf16[16,96,1024]{2,1,0:T(8,128)(2,1)S(1)}, bf16[16,96,1024]{2,1,0:T(8,128)(2,1)S(1)}, u32[]{:S(2)}, u32[]{:S(2)}) collective-permute-start(bf16[16,96,1024]{2,1,0:T(8,128)(2,1)S(1)} %constant_dynamic-update-slice_fusion.4.x_ref), channel_id=1, source_target_pairs={{0,1},{1,0},{2,3},{3,2},{4,5},{5,4},{6,7},{7,6},{8,9},{9,8},{10,11... | collective-permute-start | bytes 9437192 | tf_op jit(solution)/shard_map/ppermute | solution.py:342
  76.0 5.6 %copy-start.12 = (bf16[1,384,4096]{2,1,0:T(8,128)(2,1)S(1)}, bf16[1,384,4096]{2,1,0:T(8,128)(2,1)}, u32[]{:S(2)}) copy-start(bf16[1,384,4096]{2,1,0:T(8,128)(2,1)} %param.47) | copy-start | bytes 9437188
  88.1 3.8 %collective-permute-start.24 = (bf16[4,96,1024]{2,1,0:T(8,128)(2,1)S(1)}, bf16[4,96,1024]{2,1,0:T(8,128)(2,1)S(1)}, u32[]{:S(2)}, u32[]{:S(2)}) collective-permute-start(bf16[4,96,1024]{2,1,0:T(8,128)(2,1)S(1)} %get-tuple-element.34), channel_id=1, source_target_pairs={{0,1},{1,0},{2,3},{3,2},{4,5},{5,4},{6,7},{7,6},{8,9},{9,8},{10,11... | collective-permute-start | bytes 2359304 | tf_op jit(solution)/shard_map/ppermute | solution.py:342
  88.3 7.7 %collective-permute-start.23 = (bf16[4,96,1024]{2,1,0:T(8,128)(2,1)S(1)}, bf16[4,96,1024]{2,1,0:T(8,128)(2,1)S(1)}, u32[]{:S(2)}, u32[]{:S(2)}) collective-permute-start(bf16[4,96,1024]{2,1,0:T(8,128)(2,1)S(1)} %get-tuple-element.32), channel_id=1, source_target_pairs={{0,1},{1,0},{2,3},{3,2},{4,5},{5,4},{6,7},{7,6},{8,9},{9,8},{10,11... | collective-permute-start | bytes 2359304 | tf_op jit(solution)/shard_map/ppermute | solution.py:342
  91.3 5.2 %collective-permute-start.27 = (bf16[4,96,1024]{2,1,0:T(8,128)(2,1)S(1)}, bf16[4,96,1024]{2,1,0:T(8,128)(2,1)S(1)}, u32[]{:S(2)}, u32[]{:S(2)}) collective-permute-start(bf16[4,96,1024]{2,1,0:T(8,128)(2,1)S(1)} %get-tuple-element.36), channel_id=1, source_target_pairs={{0,1},{1,0},{2,3},{3,2},{4,5},{5,4},{6,7},{7,6},{8,9},{9,8},{10,11... | collective-permute-start | bytes 2359304 | tf_op jit(solution)/shard_map/ppermute | solution.py:342
  91.5 14.0 %collective-permute-start.22 = (bf16[4,96,1024]{2,1,0:T(8,128)(2,1)S(1)}, bf16[4,96,1024]{2,1,0:T(8,128)(2,1)S(1)}, u32[]{:S(2)}, u32[]{:S(2)}) collective-permute-start(bf16[4,96,1024]{2,1,0:T(8,128)(2,1)S(1)} %get-tuple-element.30), channel_id=1, source_target_pairs={{0,1},{1,0},{2,3},{3,2},{4,5},{5,4},{6,7},{7,6},{8,9},{9,8},{10,11... | collective-permute-start | bytes 2359304 | tf_op jit(solution)/shard_map/ppermute | solution.py:342
  92.2 9.1 %collective-permute-start.31 = (bf16[2,96,1024]{2,1,0:T(8,128)(2,1)S(1)}, bf16[2,96,1024]{2,1,0:T(8,128)(2,1)S(1)}, u32[]{:S(2)}, u32[]{:S(2)}) collective-permute-start(bf16[2,96,1024]{2,1,0:T(8,128)(2,1)S(1)} %get-tuple-element.48), channel_id=1, source_target_pairs={{0,24},{1,7},{2,26},{3,1},{4,28},{5,3},{6,30},{7,5},{8,0},{9,15},{... | collective-permute-start | bytes 1179656 | tf_op jit(solution)/shard_map/ppermute | solution.py:354
  96.0 9.2 %collective-permute-start.25 = (bf16[2,96,1024]{2,1,0:T(8,128)(2,1)S(1)}, bf16[2,96,1024]{2,1,0:T(8,128)(2,1)S(1)}, u32[]{:S(2)}, u32[]{:S(2)}) collective-permute-start(bf16[2,96,1024]{2,1,0:T(8,128)(2,1)S(1)} %get-tuple-element.47), channel_id=1, source_target_pairs={{0,8},{1,3},{2,10},{3,5},{4,12},{5,7},{6,14},{7,1},{8,16},{9,11},{... | collective-permute-start | bytes 1179656 | tf_op jit(solution)/shard_map/ppermute | solution.py:354
  96.3 12.8 %collective-permute-start.30 = (bf16[2,96,1024]{2,1,0:T(8,128)(2,1)S(1)}, bf16[2,96,1024]{2,1,0:T(8,128)(2,1)S(1)}, u32[]{:S(2)}, u32[]{:S(2)}) collective-permute-start(bf16[2,96,1024]{2,1,0:T(8,128)(2,1)S(1)} %slice.182), channel_id=1, source_target_pairs={{0,8},{1,3},{2,10},{3,5},{4,12},{5,7},{6,14},{7,1},{8,16},{9,11},{... | collective-permute-start | bytes 1179656 | tf_op jit(solution)/shard_map/ppermute | solution.py:354
  96.8 12.4 %collective-permute-start.28 = (bf16[2,96,1024]{2,1,0:T(8,128)(2,1)S(1)}, bf16[2,96,1024]{2,1,0:T(8,128)(2,1)S(1)}, u32[]{:S(2)}, u32[]{:S(2)}) collective-permute-start(bf16[2,96,1024]{2,1,0:T(8,128)(2,1)S(1)} %slice.178), channel_id=1, source_target_pairs={{0,24},{1,7},{2,26},{3,1},{4,28},{5,3},{6,30},{7,5},{8,0},{9,15},{... | collective-permute-start | bytes 1179656 | tf_op jit(solution)/shard_map/ppermute | solution.py:354
  101.4 9.1 %collective-permute-start.32 = (bf16[2,96,1024]{2,1,0:T(8,128)(2,1)S(1)}, bf16[2,96,1024]{2,1,0:T(8,128)(2,1)S(1)}, u32[]{:S(2)}, u32[]{:S(2)}) collective-permute-start(bf16[2,96,1024]{2,1,0:T(8,128)(2,1)S(1)} %add_convert_fusion.5), channel_id=1, source_target_pairs={{0,24},{1,7},{2,26},{3,1},{4,28},{5,3},{6,30},{7,5},{8,0},{9,15},{... | collective-permute-start | bytes 1179656 | tf_op jit(solution)/shard_map/ppermute | solution.py:354
  105.3 9.1 %collective-permute-start.26 = (bf16[2,96,1024]{2,1,0:T(8,128)(2,1)S(1)}, bf16[2,96,1024]{2,1,0:T(8,128)(2,1)S(1)}, u32[]{:S(2)}, u32[]{:S(2)}) collective-permute-start(bf16[2,96,1024]{2,1,0:T(8,128)(2,1)S(1)} %add_convert_fusion.7), channel_id=1, source_target_pairs={{0,8},{1,3},{2,10},{3,5},{4,12},{5,7},{6,14},{7,1},{8,16},{9,11},{... | collective-permute-start | bytes 1179656 | tf_op jit(solution)/shard_map/ppermute | solution.py:354
  114.9 8.6 %collective-permute-start.33 = (bf16[96,1024]{1,0:T(8,128)(2,1)S(1)}, bf16[96,1024]{1,0:T(8,128)(2,1)S(1)}, u32[]{:S(2)}, u32[]{:S(2)}) collective-permute-start(bf16[96,1024]{1,0:T(8,128)(2,1)S(1)} %get-tuple-element.49), channel_id=1, source_target_pairs={{0,4},{1,17},{2,6},{3,19},{4,0},{5,21},{6,2},{7,23},{8,12},{9,25},... | collective-permute-start | bytes 589832 | tf_op jit(solution)/shard_map/ppermute | solution.py:354
  119.8 7.2 %collective-permute-start.34 = (bf16[96,1024]{1,0:T(8,128)(2,1)S(1)}, bf16[96,1024]{1,0:T(8,128)(2,1)S(1)}, u32[]{:S(2)}, u32[]{:S(2)}) collective-permute-start(bf16[96,1024]{1,0:T(8,128)(2,1)S(1)} %get-tuple-element.50), channel_id=1, source_target_pairs={{0,6},{1,25},{2,0},{3,27},{4,2},{5,29},{6,4},{7,31},{8,14},{9,1},{... | collective-permute-start | bytes 589832 | tf_op jit(solution)/shard_map/ppermute | solution.py:354
  120.4 6.9 %collective-permute-start.29 = (bf16[96,1024]{1,0:T(8,128)(2,1)S(1)}, bf16[96,1024]{1,0:T(8,128)(2,1)S(1)}, u32[]{:S(2)}, u32[]{:S(2)}) collective-permute-start(bf16[96,1024]{1,0:T(8,128)(2,1)S(1)} %slice_bitcast_fusion.2), channel_id=1, source_target_pairs={{0,2},{1,9},{2,4},{3,11},{4,6},{5,13},{6,0},{7,15},{8,10},{9,17},{... | collective-permute-start | bytes 589832 | tf_op jit(solution)/shard_map/ppermute | solution.py:354
  127.5 3.1 %collective-permute-start.35 = (bf16[48,1024]{1,0:T(8,128)(2,1)S(1)}, bf16[48,1024]{1,0:T(8,128)(2,1)S(1)}, u32[]{:S(2)}, u32[]{:S(2)}) collective-permute-start(bf16[48,1024]{1,0:T(8,128)(2,1)S(1)} %get-tuple-element.59), channel_id=1, source_target_pairs={{0,0},{1,65},{2,2},{3,67},{4,4},{5,69},{6,6},{7,71},{8,8},{9,73},{... | collective-permute-start | bytes 294920 | tf_op jit(solution)/shard_map/ppermute | solution.py:354
  128.2 4.7 %collective-permute-start.36 = (bf16[48,1024]{1,0:T(8,128)(2,1)S(1)}, bf16[48,1024]{1,0:T(8,128)(2,1)S(1)}, u32[]{:S(2)}, u32[]{:S(2)}) collective-permute-start(bf16[48,1024]{1,0:T(8,128)(2,1)S(1)} %get-tuple-element.60), channel_id=1, source_target_pairs={{0,96},{1,33},{2,98},{3,35},{4,100},{5,37},{6,102},{7,39},{8,104},... | collective-permute-start | bytes 294920 | tf_op jit(solution)/shard_map/ppermute | solution.py:354
  132.9 1.4 %collective-permute-start.37 = (bf16[2,48,640]{2,1,0:T(8,128)(2,1)S(1)}, bf16[2,48,640]{2,1,0:T(8,128)(2,1)S(1)}, u32[]{:S(2)}, u32[]{:S(2)}) collective-permute-start(bf16[2,48,640]{2,1,0:T(8,128)(2,1)S(1)} %pad_maximum_fusion.3), channel_id=1, source_target_pairs={{0,1},{1,0},{2,3},{3,2},{4,5},{5,4},{6,7},{7,6},{8,9},{9,8},{10,11... | collective-permute-start | bytes 368648 | tf_op jit(solution)/shard_map/ppermute | solution.py:342

commit v3 on v2

--- a/solution.py
+++ b/solution.py
@@ -51,7 +51,7 @@
 
 def conv_kernel(
     span_hbm, res_hbm, slot_hbm, x_hbm, cache_hbm, w_hbm, b_hbm, rank_hbm, sw_hbm, gain_hbm,
-    cx_ref, proj_ref, nc_ref,
+    cx_ref, proj_ref,
     span_ref, res_ref, slot_ref, x_ref, cache_ref, w_ref, b_ref, rank_ref, sw_ref, gain_ref, sems,
 ):
     sources = (span_hbm, res_hbm, slot_hbm, x_hbm, cache_hbm, w_hbm, b_hbm, gain_hbm, sw_hbm, rank_hbm)
@@ -107,10 +107,16 @@
     extra = jnp.where(row == line, high, jnp.where(row == line + 1, inverse - high, 0.0))
     proj_ref[ROWS : ROWS + 16, 0:512] = extra.astype(BF)
     proj_ref[ROWS : ROWS + 16, 512:640] = jnp.zeros((16, 128), BF)
-    group = r
-    length = jnp.ones((ROWS, 128), I32)
-    first = jnp.zeros((ROWS, 128), I32)
-    kept = jnp.ones((ROWS, 128), I32)
+
+
+def tail_kernel(span_ref, res_ref, slot_ref, x_ref, cache_ref, nc_ref):
+    starts = span_starts(span_ref)
+    x = x_ref[...]
+    group = iota((SEQ, 128), 0)
+    j = iota((SEQ, 128), 1)
+    length = jnp.ones((SEQ, 128), I32)
+    first = jnp.zeros((SEQ, 128), I32)
+    kept = jnp.ones((SEQ, 128), I32)
     for s in range(SEQ):
         here = group == slot_ref[0, s]
         if s < DEC:
@@ -119,13 +125,17 @@
             first = jnp.where(here, starts[s - DEC], first)
             length = jnp.where(here, span_ref[0, s - DEC], length)
             kept = jnp.where(here, res_ref[0, s - DEC], kept)
+
+    def select(column, line, width):
+        return (j == jnp.where(line, column, -1)).astype(F32)[:, 0:width].astype(BF)
+
     for offset in range(TAPS - 1):
         back = length - (TAPS - 1) + offset
         value = dot(select(first + back, back >= 0, ROWS), x)
         for i in range(TAPS - 1):
             old = (back == i - 3) & (kept > 0)
             value = value + dot(select(group, old, SEQ), cache_ref[i])
-        nc_ref[offset] = value[0:SEQ].astype(BF)
+        nc_ref[offset] = value.astype(BF)
 
 
 def scan_kernel(
@@ -133,7 +143,7 @@
     q0_ref, q1_ref, q2_ref, q3_ref, cx_ref, z_ref, gain_ref, sw_ref, sb_ref, dl_ref, skip_ref,
     sc_ref, ow_ref,
     ns_ref, own_ref, sib_ref, inv_ref,
-    w_vmem, step_ref, drive_ref, bb_ref, cb_ref, pc_ref, tr_ref, sem,
+    state_ref, w_vmem, step_ref, drive_ref, bb_ref, cb_ref, pc_ref, tr_ref, sem, state_sem,
 ):
     fetch = pltpu.make_async_copy(ow_ref, w_vmem, sem)
     fetch.start()
@@ -181,10 +191,12 @@
         fresh = decay * prior + drive_ref[pl.ds(r, 1), :] * b
         weighed = fresh * c
         pc_ref[r] = weighed[0:8] + weighed[8:16]
-        ns_ref[slot] = fresh
+        state_ref[slot] = fresh
         return fresh
 
     lax.fori_loop(0, ROWS, advance, jnp.zeros(rate.shape, F32), unroll=4)
+    keep = pltpu.make_async_copy(state_ref, ns_ref, state_sem)
+    keep.start()
     output = skip_ref[...] * values
     for k in range(8):
         output = output + pc_ref[:, k, :]
@@ -195,6 +207,7 @@
         for k in range(4):
             cols = pl.ds(pl.multiple_of((2 * lax.rem(x + k, 4) + core) * 512, 512), 512)
             out[k] = dot(gated, w_vmem[:, cols]).astype(BF)
+    keep.wait()
 
 
 def pick_kernel(
@@ -223,14 +236,14 @@
     before = (iota((ROWS, ROWS), 0) < iota((ROWS, ROWS), 1)).astype(F32).astype(BF)
     row = iota((CAP, ROWS), 0)
     z, core = here_ref[2], here_ref[1]
-    for out, side in ((mine_ref, core), (theirs_ref, 1 - core)):
-        for i in range(2):
-            e = lax.rem(z + 2 * side + i, EXPERTS)
-            marks = ((chosen_ref[0:1] == e) | (chosen_ref[1:2] == e)).astype(F32)
-            marks = jnp.broadcast_to(marks, (8, ROWS))
-            place = dot(marks.astype(BF), before).astype(I32)[0:1]
-            hot = ((row == place) & (marks[0:1] > 0.0)).astype(F32).astype(BF)
-            out[i, :, 0:512] = dot(hot, scaled).astype(BF)
+    expert = lax.rem(z + 2 * core + iota((8, ROWS), 0), EXPERTS)
+    marks = ((chosen_ref[0:1] == expert) | (chosen_ref[1:2] == expert)).astype(F32)
+    place = dot(marks.astype(BF), before)
+    place = jnp.where(marks > 0.0, place, -1.0).astype(I32)
+    for i in range(4):
+        hot = (row == place[i : i + 1]).astype(F32).astype(BF)
+        out = mine_ref if i < 2 else theirs_ref
+        out[i % 2, :, 0:512] = dot(hot, scaled).astype(BF)
     same = (iota((ROWS, ROWS), 0) == iota((ROWS, ROWS), 1)).astype(F32).astype(BF)
     pair = iota((8, ROWS), 0)
     both = jnp.where(pair == 0, chosen_ref[0:1], jnp.where(pair == 1, chosen_ref[1:2], 0))
@@ -244,63 +257,63 @@
 def experts_in(here_ref, side, x_ref, inv_ref, wg_ref, wu_ref):
     x = here_ref[0]
     by_row, by_col = jnp.where(side == 0, 4, 1), jnp.where(side == 0, 1, 4)
-    gate = upper = square = None
+    both = square = None
     for k in range(4):
         there = lax.rem(x + 4 - k, 4)
         rows = pl.ds(pl.multiple_of(there * 1024, 1024), 1024)
         block = jnp.concatenate([x_ref[j * by_row + k * by_col] for j in range(4)], axis=0)
-        gate_part = dot(block, wg_ref[rows, :])
-        upper_part = dot(block, wu_ref[rows, :])
+        part = dot(block, jnp.concatenate([wg_ref[rows, :], wu_ref[rows, :]], axis=1))
         wide = block.astype(F32)
         wide = wide * wide * inv_ref[there]
         square_part = wide[:, 0:128]
         for lane in range(128, 1024, 128):
             square_part = square_part + wide[:, lane : lane + 128]
         if k == 0:
-            gate, upper, square = gate_part, upper_part, square_part
+            both, square = part, square_part
         else:
-            gate, upper, square = gate + gate_part, upper + upper_part, square + square_part
-    scale = lax.rsqrt(jnp.sum(square, axis=1, keepdims=True) / 4096.0 + EPS)
-    return (silu(gate * scale) * (upper * scale)).astype(BF)
+            both, square = both + part, square + square_part
+    both = both * lax.rsqrt(jnp.sum(square, axis=1, keepdims=True) / 4096.0 + EPS)
+    return (silu(both[:, 0:384]) * both[:, 384:768]).astype(BF)
 
 
 def experts_out(here_ref, side, act_ref, wd_ref, outs):
     x = here_ref[0]
 
-    def product(k):
-        cols = pl.ds(pl.multiple_of(lax.rem(x + k, 4) * 1024, 1024), 1024)
-        return dot(act_ref[...], wd_ref[:, cols]).astype(BF)
+    def product(rows, there):
+        cols = pl.ds(pl.multiple_of(there * 1024, 1024), 1024)
+        return dot(rows, wd_ref[:, cols]).astype(BF)
 
     @pl.when(side == 0)
     def _():
-        for k in range(4):
-            value = product(k)
-            for j in range(4):
-                outs[(4 - j) % 4][k] = value[96 * j : 96 * j + 96]
+        owners = [j for j in range(4) if (4 - j) % 4 in outs]
+        rows = jnp.concatenate([act_ref[96 * j : 96 * j + 96, :] for j in owners], axis=0)
+        for n in range(4):
+            value = product(rows, lax.rem(x + n, 4))
+            for i, j in enumerate(owners):
+                outs[(4 - j) % 4][n] = value[96 * i : 96 * i + 96]
 
     @pl.when(side == 1)
     def _():
-        for k in range(4):
-            value = product(k)
+        for m in outs:
+            value = product(act_ref[...], lax.rem(x + m, 4))
             for j in range(4):
-                outs[k][(4 - j) % 4] = value[96 * j : 96 * j + 96]
-
-
-def ffn_first(here_ref, x_ref, inv_ref, wg_ref, wu_ref, act_ref):
-    act_ref[...] = experts_in(here_ref, here_ref[1], x_ref, inv_ref, wg_ref, wu_ref)
-
-
-def ffn_second(
-    here_ref, x_ref, inv_ref, wg_ref, wu_ref, wd_ref, earlier_ref,
-    p0_ref, p1_ref, p2_ref, p3_ref, act_ref,
-):
+                outs[m][(4 - j) % 4] = value[96 * j : 96 * j + 96]
+
+
+def ffn_own(here_ref, x_ref, inv_ref, wg_ref, wu_ref, wd_ref, p0_ref, p1_ref, p2_ref, p3_ref, act_ref):
+    side = here_ref[1]
+    act_ref[...] = experts_in(here_ref, side, x_ref, inv_ref, wg_ref, wu_ref)
+    experts_out(here_ref, side, act_ref, wd_ref, {0: p0_ref, 1: p1_ref, 2: p2_ref, 3: p3_ref})
+
+
+def ffn_other(here_ref, x_ref, inv_ref, wg_ref, wu_ref, wd_ref, earlier_ref, act_ref, p2_ref):
     side = 1 - here_ref[1]
     act_ref[...] = experts_in(here_ref, side, x_ref, inv_ref, wg_ref, wu_ref)
-    experts_out(here_ref, side, act_ref, wd_ref, (p0_ref, p1_ref, p2_ref, p3_ref))
-
-
-def ffn_third(here_ref, act_ref, wd_ref, p0_ref, p1_ref, p2_ref, p3_ref):
-    experts_out(here_ref, here_ref[1], act_ref, wd_ref, (p0_ref, p1_ref, p2_ref, p3_ref))
+    experts_out(here_ref, side, act_ref, wd_ref, {2: p2_ref})
+
+
+def ffn_rest(here_ref, act_ref, wd_ref, p0_ref, p1_ref, p3_ref):
+    experts_out(here_ref, 1 - here_ref[1], act_ref, wd_ref, {1: p1_ref, 3: p3_ref, 0: p0_ref})
 
 
 def final_kernel(
@@ -325,15 +338,16 @@
     lane = iota((ROWS, CAP), 1)
     total = hid_ref[...]
     z, core = here_ref[2], here_ref[1]
-    for ref, side in ((mine_ref, core), (theirs_ref, 1 - core)):
-        for i in range(2):
-            e = lax.rem(z + 2 * side + i, EXPERTS)
-            first, second = e0 == e, e1 == e
-            marks = jnp.broadcast_to((first | second).astype(F32), (ROWS, 128))
-            place = dot(before, marks.astype(BF)).astype(I32)[:, 0:CAP]
-            hot = ((lane == place) & (marks[:, 0:CAP] > 0.0)).astype(F32).astype(BF)
-            weight = jnp.where(first, route0, jnp.where(second, route1, 0.0))
-            total = total + weight * dot(hot, ref[i])
+    expert = lax.rem(z + 2 * core + iota((ROWS, 128), 1), EXPERTS)
+    first, second = e0 == expert, e1 == expert
+    marks = (first | second).astype(F32)
+    place = dot(before, marks.astype(BF))
+    place = jnp.where(marks > 0.0, place, -1.0).astype(I32)
+    weight = jnp.where(first, route0, jnp.where(second, route1, 0.0))
+    for i in range(4):
+        hot = (lane == place[:, i : i + 1]).astype(F32).astype(BF)
+        ref = mine_ref if i < 2 else theirs_ref
+        total = total + weight[:, i : i + 1] * dot(hot, ref[i % 2])
     out_ref[...] = total.astype(BF)
 
 
@@ -386,13 +400,13 @@
     return pltpu.with_memory_space_constraint(value, pltpu.HBM)
 
 
-def call(kernel, outs, ins, mib, scratch=(), flops=0, moved=0, name=None):
+def call(kernel, outs, ins, mib, scratch=(), flops=0, moved=0, name=None, out_specs=None):
     single = not isinstance(outs, (list, tuple))
     return pl.pallas_call(
         kernel,
         out_shape=outs,
         in_specs=ins,
-        out_specs=VMEM if single else [VMEM] * len(outs),
+        out_specs=out_specs or (VMEM if single else [VMEM] * len(outs)),
         scratch_shapes=list(scratch),
         compiler_params=params(mib),
         cost_estimate=pl.CostEstimate(flops=flops, bytes_accessed=moved, transcendentals=0),
@@ -414,9 +428,10 @@
         [lax.axis_index("x"), lax.axis_index("core"), lax.axis_index("z")]
     ).astype(I32)
     even = lax.axis_index("core") == 0
-    cx, proj, new_conv = call(
+    old = conv_cache.transpose(1, 0, 2)
+    cx, proj = call(
         conv_kernel,
-        [shape((ROWS, 1024), BF), shape((ROWS + 16, 640), BF), shape((3, SEQ, 1024), BF)],
+        [shape((ROWS, 1024), BF), shape((ROWS + 16, 640), BF)],
         [HBM] * 10,
         16,
         [
@@ -440,11 +455,20 @@
             stay,
             (
                 span_lengths, span_resumes, slot_index, conv_input,
-                conv_cache.transpose(1, 0, 2), conv_weight, conv_bias.reshape(1, 1024),
+                old, conv_weight, conv_bias.reshape(1, 1024),
                 rank_weight, state_weight.T, moe_gain.reshape(1, 512),
             ),
         )
     )
+    new_conv = call(
+        tail_kernel,
+        shape((3, SEQ, 1024), BF),
+        [SMEM] * 3 + [VMEM] * 2,
+        8,
+        flops=10**9,
+        moved=10**6,
+        name="tail",
+    )(span_lengths, span_resumes, slot_index, conv_input, old)
     chip = add(proj, move(proj, "core", 1))
     parts = [chip] + [move(chip, "x", k) for k in (1, 2, 3)]
     new_state, own, sib, inverse = call(
@@ -458,6 +482,7 @@
         [SMEM] * 4 + [VMEM] * 12 + [HBM],
         32,
         [
+            pltpu.VMEM((SEQ, NS, 1024), F32),
             pltpu.VMEM((1024, 4096), BF),
             pltpu.VMEM((ROWS, 1024), F32),
             pltpu.VMEM((ROWS, 1024), F32),
@@ -466,10 +491,12 @@
             pltpu.VMEM((ROWS, 8, 1024), F32),
             pltpu.VMEM((128, 128), F32),
             pltpu.SemaphoreType.DMA,
+            pltpu.SemaphoreType.DMA,
         ],
         flops=10**9,
         moved=10**7,
         name="scan",
+        out_specs=[HBM] + [VMEM] * 3,
     )(
         here, span_lengths, span_resumes, slot_index, *parts, cx, gate_input,
         step_gain.reshape(1, 512), step_weight, step_bias.reshape(1, 1024), decay_log,
@@ -500,7 +527,6 @@
     rows = jnp.concatenate([jnp.concatenate([sooner, later], axis=0), stat], axis=1)
     rows1, rows3 = across(rows, 1), across(rows, 3)
     rows2 = jnp.concatenate([across(rows1[0:CAP], 1), across(rows3[CAP : 2 * CAP], 3)], axis=0)
-
     stat = coded(summed(*[part[:, 1024:1152] for part in (rows, rows1, rows2, rows3)]))
     upper = jnp.stack([rows[:, 0:1024], rows1[:, 0:1024]])
     lower = jnp.stack([rows2[:, 0:1024], rows3[:, 0:1024]])
@@ -512,43 +538,45 @@
     )
     theirs = move(mine, "core", 1)
     gate, up, down = gate_weight[0], up_weight[0], down_weight[0]
-    act = call(
-        ffn_first,
-        shape((384, 384), BF),
-        [SMEM] + [VMEM] * 4,
-        24,
-        flops=2 * 384 * 4096 * 768,
+    block = shape((4, 96, 1024), BF)
+
+    mine = call(
+        ffn_own,
+        [block] * 4,
+        [SMEM] + [VMEM] * 5,
+        30,
+        [pltpu.VMEM((384, 384), BF)],
+        flops=6 * 384 * 2048 * 768,
+        moved=12 * 10**6,
+        name="experts_own",
+    )(here, mine, inverse, gate, up, down)
+    act, theirs2 = call(
+        ffn_other,
+        [shape((384, 384), BF), block],
+        [SMEM] + [VMEM] * 6,
+        28,
+        flops=5 * 384 * 2048 * 768,
         moved=10 * 10**6,
-        name="experts_in",
-    )(here, mine, inverse, gate, up)
-    blocks = [shape((4, 96, 1024), BF)] * 4
+        name="experts_other",
+    )(here, theirs, inverse, gate, up, down, mine[0])
     theirs = call(
-        ffn_second,
-        blocks,
-        [SMEM] + [VMEM] * 6,
-        32,
-        [pltpu.VMEM((384, 384), BF)],
-        flops=3 * 384 * 4096 * 768,
-        moved=12 * 10**6,
-        name="experts_other",
-    )(here, theirs, inverse, gate, up, down, act)
-    mine = call(
-        ffn_third,
-        blocks,
+        ffn_rest,
+        [block] * 3,
         [SMEM] + [VMEM] * 2,
         20,
-        flops=384 * 4096 * 768,
-        moved=6 * 10**6,
-        name="experts_out",
+        flops=384 * 3072 * 768,
+        moved=5 * 10**6,
+        name="experts_rest",
     )(here, act, down)
-    part = [None] * 4
-    for m in (2, 1, 3, 0):
-        part[m] = add(mine[m], move(theirs[m], "core", 1))
-    far1, far3 = along(part[2][0:2], 1), along(part[2][2:4], 3)
-    near1, near3 = along(part[1][2:4], 1), along(part[3][0:2], 3)
-    next1, next3 = along(add(part[1][0:2], far1), 1), along(add(part[3][2:4], far3), 3)
+    part2 = add(mine[2], move(theirs2, "core", 1))
+    far1, far3 = along(part2[0:2], 1), along(part2[2:4], 3)
+    part1 = add(mine[1], move(theirs[1], "core", 1))
+    part3 = add(mine[3], move(theirs[2], "core", 1))
+    part0 = add(mine[0], move(theirs[0], "core", 1))
+    near1, near3 = along(part1[2:4], 1), along(part3[0:2], 3)
+    next1, next3 = along(add(part1[0:2], far1), 1), along(add(part3[2:4], far3), 3)
     lines = jnp.concatenate(
-        [add(part[0][0:2], next1, near3), add(part[0][2:4], near1, next3)], axis=0
+        [add(part0[0:2], next1, near3), add(part0[2:4], near1, next3)], axis=0
     )
     lines = add(lines[0], *[across(lines[k], k) for k in (1, 2, 3)])
     later = by_core(lines[CAP : 2 * CAP], ("z", 3), ("z", 1))

time: 138 us -> 134 us (0.971)
  Pallas kernels: 26.8 us -> 24.3 us
  waiting for transfers between devices: 52.7 us -> 50.3 us
    ppermute x15, waiting for transfers between devices: 12.7 us -> 10.4 us  [move(): lax.ppermute(value, axis, [(i, (i + shift) % size) for i in range(size)])]
    pallas_call x4 -> x5, Pallas kernels: 16.9 us -> 15.8 us  [the longest x1 5.67 us: per_device(): call(ffn_own, [block] * 4, [SMEM] + [VMEM] * 5, 30, [pltpu.VMEM((384, 384...]
  transfers between devices with their start and end apart: 38 -> 38, of which waited for: 24 -> 22; matrix products, arithmetic and copies ran while one was open for 2% -> 2% of each run, Pallas kernels for 5% -> 7%
where the time goes in v3:
time: 134 us; the launch traced here: 132 us
  starting transfers between devices  52.5 us (39%)
  waiting for transfers between devices  50.3 us (38%)
  Pallas kernels  24.3 us (18%)
  other arithmetic  2.88 us (2%)
  between operations  1.42 us (1%)
    ppermute x23, waiting for transfers between devices, by_core(): return lax.ppermute(value, AXES, pairs)  39.9 us
    ppermute x23, starting transfers between devices, by_core(): return lax.ppermute(value, AXES, pairs)  39.4 us
    ppermute x15, starting transfers between devices, move(): lax.ppermute(value, axis, [(i, (i + shift) % size) for i in range(size)])  13.1 us
    ppermute x15, waiting for transfers between devices, move(): lax.ppermute(value, axis, [(i, (i + shift) % size) for i in range(size)])  10.4 us
    pallas_call x1, Pallas kernels, per_device(): call(scan_kernel, [shape((SEQ, NS, 1024), F32), shape((4, ROWS, 512), BF)...  5.81 us
    pallas_call x1, Pallas kernels, per_device(): call(ffn_own, [block] * 4, [SMEM] + [VMEM] * 5, 30, [pltpu.VMEM((384, 384...  5.67 us
    pallas_call x1, Pallas kernels, per_device(): call(ffn_other, [shape((384, 384), BF), block], [SMEM] + [VMEM] * 6, 28,...  4.43 us
  transfers between devices with their start and end apart: 38, of which 22 were waited for; matrix products, arithmetic and copies ran while one was open for 2% of the time, Pallas kernels for 7%

profile of v3, /device:TPU:0, one launch (start us, length us, event | category | flops | bytes accessed | tf_op | source)
XLA Modules:
  0.0 132.1 jit_solution(7995630412385040142)
XLA Ops:
  0.7 2.2 %conv.1 = (bf16[64,1024]{1,0:T(8,128)(2,1)S(1)}, bf16[80,640]{1,0:T(8,128)(2,1)S(1)}) custom-call(s32[1,4]{1,0:T(1,128)} %span_ref.3, s32[1,4]{1,0:T(1,128)} %res_ref.3, s32[1,20]{1,0:T(1,128)} %slot_ref.3, bf16[64,1024]{1,0:T(8,128)(2,1)} %x_ref.1, bf16[3,20,1024]{2,1,0:T(8,128)(2,1)} %bitcast.70, f32[4,1024]{1,0:T(4,128)} %w_hbm.1, f32[1,1024]{1,0:T(1,128)} %bitcast.82, ...), custom_call_target="tpu_custom_call" | custom-call | flops 1000000000 | bytes 2000000 | tf_op jit(solution)/shard_map/conv/pallas_call | solution.py:432
  3.0 1.3 collective-permute-done
  4.4 1.6 %collective-permute-start.1 = (bf16[80,640]{1,0:T(8,128)(2,1)S(1)}, bf16[80,640]{1,0:T(8,128)(2,1)S(1)}, u32[]{:S(2)}, u32[]{:S(2)}) collective-permute-start(bf16[80,640]{1,0:T(8,128)(2,1)S(1)} %add_convert_fusion.9.q0_ref), channel_id=1, source_target_pairs={{0,2},{2,4},{4,6},{6,0},{1,3},{3,5},{5,7},{7,1},{8,10},{10,12},{12... | collective-permute-start | bytes 307208 | tf_op jit(solution)/shard_map/ppermute | solution.py:356
  6.0 2.7 %collective-permute-start.2 = (bf16[80,640]{1,0:T(8,128)(2,1)S(1)}, bf16[80,640]{1,0:T(8,128)(2,1)S(1)}, u32[]{:S(2)}, u32[]{:S(2)}) collective-permute-start(bf16[80,640]{1,0:T(8,128)(2,1)S(1)} %add_convert_fusion.9.q0_ref), channel_id=1, source_target_pairs={{0,4},{2,6},{4,0},{6,2},{1,5},{3,7},{5,1},{7,3},{8,12},{10,14},{12... | collective-permute-start | bytes 307208 | tf_op jit(solution)/shard_map/ppermute | solution.py:356
  8.7 1.4 %collective-permute-start.3 = (bf16[80,640]{1,0:T(8,128)(2,1)S(1)}, bf16[80,640]{1,0:T(8,128)(2,1)S(1)}, u32[]{:S(2)}, u32[]{:S(2)}) collective-permute-start(bf16[80,640]{1,0:T(8,128)(2,1)S(1)} %add_convert_fusion.9.q0_ref), channel_id=1, source_target_pairs={{0,6},{2,0},{4,2},{6,4},{1,7},{3,1},{5,3},{7,5},{8,14},{10,8},{12,... | collective-permute-start | bytes 307208 | tf_op jit(solution)/shard_map/ppermute | solution.py:356
  10.2 0.3 collective-permute-done.1.q1_ref
  10.6 3.3 %collective-permute-done.2.q2_ref = bf16[80,640]{1,0:T(8,128)(2,1)S(1)} collective-permute-done((bf16[80,640]{1,0:T(8,128)(2,1)S(1)}, bf16[80,640]{1,0:T(8,128)(2,1)S(1)}, u32[]{:S(2)}, u32[]{:S(2)}) %collective-permute-start.2) | collective-permute-done | bytes 102432 | tf_op jit(solution)/shard_map/ppermute | solution.py:356
  14.0 5.8 %scan.1 = (f32[20,16,1024]{2,1,0:T(8,128)}, bf16[4,64,512]{2,1,0:T(8,128)(2,1)S(1)}, bf16[4,64,512]{2,1,0:T(8,128)(2,1)S(1)}, f32[4,1,1024]{2,1,0:T(1,128)S(1)}) custom-call(s32[3]{0:T(128)S(1)} %pad_add_fusion.here_ref, s32[1,4]{1,0:T(1,128)S(1)} %copy-done.10, s32[1,4]{1,0:T(1,128)S(1)} %copy-done.11, s32[1,20]{1,0:T(1,128)S(1)} %copy-done.12, ...), custom_call_target="tpu_custom_call" | custom-call | flops 1000000000 | bytes 10000000 | tf_op jit(solution)/shard_map/scan/pallas_call | solution.py:474
  19.9 1.5 %collective-permute-done.4 = bf16[4,64,512]{2,1,0:T(8,128)(2,1)S(1)} collective-permute-done((bf16[4,64,512]{2,1,0:T(8,128)(2,1)S(1)}, bf16[4,64,512]{2,1,0:T(8,128)(2,1)S(1)}, u32[]{:S(2)}, u32[]{:S(2)}) %collective-permute-start.4) | collective-permute-done | bytes 262176 | tf_op jit(solution)/shard_map/ppermute | solution.py:356
  21.5 1.3 collective-permute-start.5
  22.8 2.4 %collective-permute-start.6 = (bf16[64,512]{1,0:T(8,128)(2,1)S(1)}, bf16[64,512]{1,0:T(8,128)(2,1)S(1)}, u32[]{:S(2)}, u32[]{:S(2)}) collective-permute-start(bf16[64,512]{1,0:T(8,128)(2,1)S(1)} %get-tuple-element.52), channel_id=1, source_target_pairs={{0,4},{2,6},{4,0},{6,2},{1,5},{3,7},{5,1},{7,3},{8,12},{10,14},{12... | collective-permute-start | bytes 196616 | tf_op jit(solution)/shard_map/ppermute | solution.py:356
  25.2 1.6 %collective-permute-start.7 = (bf16[64,512]{1,0:T(8,128)(2,1)S(1)}, bf16[64,512]{1,0:T(8,128)(2,1)S(1)}, u32[]{:S(2)}, u32[]{:S(2)}) collective-permute-start(bf16[64,512]{1,0:T(8,128)(2,1)S(1)} %get-tuple-element.51), channel_id=1, source_target_pairs={{0,6},{2,0},{4,2},{6,4},{1,7},{3,1},{5,3},{7,5},{8,14},{10,8},{12,... | collective-permute-start | bytes 196616 | tf_op jit(solution)/shard_map/ppermute | solution.py:356
  26.9 0.5 collective-permute-done.5.q1_ref
  27.3 1.5 %collective-permute-done.6.q2_ref = bf16[64,512]{1,0:T(8,128)(2,1)S(1)} collective-permute-done((bf16[64,512]{1,0:T(8,128)(2,1)S(1)}, bf16[64,512]{1,0:T(8,128)(2,1)S(1)}, u32[]{:S(2)}, u32[]{:S(2)}) %collective-permute-start.6) | collective-permute-done | bytes 65568 | tf_op jit(solution)/shard_map/ppermute | solution.py:356
  28.9 0.6 collective-permute-done.7.q3_ref
  29.5 0.9 pick.1
  30.5 1.3 collective-permute-done.8
  32.0 0.7 collective-permute-start.9
  32.6 2.1 %collective-permute-start.10 = (bf16[48,1024]{1,0:T(8,128)(2,1)S(1)}, bf16[48,1024]{1,0:T(8,128)(2,1)S(1)}, u32[]{:S(2)}, u32[]{:S(2)}) collective-permute-start(bf16[48,1024]{1,0:T(8,128)(2,1)S(1)} %get-tuple-element.61), channel_id=1, source_target_pairs={{0,32},{1,97},{2,34},{3,99},{4,36},{5,101},{6,38},{7,103},{8,40},{... | collective-permute-start | bytes 294920 | tf_op jit(solution)/shard_map/ppermute | solution.py:368
  34.8 5.7 %collective-permute-done.10 = bf16[48,1024]{1,0:T(8,128)(2,1)S(1)} collective-permute-done((bf16[48,1024]{1,0:T(8,128)(2,1)S(1)}, bf16[48,1024]{1,0:T(8,128)(2,1)S(1)}, u32[]{:S(2)}, u32[]{:S(2)}) %collective-permute-start.10) | collective-permute-done | bytes 98336 | tf_op jit(solution)/shard_map/ppermute | solution.py:368
  40.5 1.2 collective-permute-start.11
  41.7 2.2 %collective-permute-start.13 = (bf16[96,1152]{1,0:T(8,128)(2,1)S(1)}, bf16[96,1152]{1,0:T(8,128)(2,1)S(1)}, u32[]{:S(2)}, u32[]{:S(2)}) collective-permute-start(bf16[96,1152]{1,0:T(8,128)(2,1)S(1)} %pad_maximum_fusion.2), channel_id=1, source_target_pairs={{0,6},{1,25},{2,0},{3,27},{4,2},{5,29},{6,4},{7,31},{8,14},{9,1},{... | collective-permute-start | bytes 663560 | tf_op jit(solution)/shard_map/ppermute | solution.py:368
  43.8 3.9 %collective-permute-done.11 = bf16[96,1152]{1,0:T(8,128)(2,1)S(1)} collective-permute-done((bf16[96,1152]{1,0:T(8,128)(2,1)S(1)}, bf16[96,1152]{1,0:T(8,128)(2,1)S(1)}, u32[]{:S(2)}, u32[]{:S(2)}) %collective-permute-start.11) | collective-permute-done | bytes 221216 | tf_op jit(solution)/shard_map/ppermute | solution.py:368
  47.8 1.6 %collective-permute-start.15 = (bf16[2,96,1024]{2,1,0:T(8,128)(2,1)S(1)}, bf16[2,96,1024]{2,1,0:T(8,128)(2,1)S(1)}, u32[]{:S(2)}, u32[]{:S(2)}) collective-permute-start(bf16[2,96,1024]{2,1,0:T(8,128)(2,1)S(1)} %pad_maximum_fusion), channel_id=1, source_target_pairs={{0,8},{1,3},{2,10},{3,5},{4,12},{5,7},{6,14},{7,1},{8,16},{9,11},{... | collective-permute-start | bytes 1179656 | tf_op jit(solution)/shard_map/ppermute | solution.py:368
  49.4 1.7 %collective-permute-start.20 = (bf16[2,96,1024]{2,1,0:T(8,128)(2,1)S(1)}, bf16[2,96,1024]{2,1,0:T(8,128)(2,1)S(1)}, u32[]{:S(2)}, u32[]{:S(2)}) collective-permute-start(bf16[2,96,1024]{2,1,0:T(8,128)(2,1)S(1)} %pad_maximum_fusion), channel_id=1, source_target_pairs={{0,24},{1,7},{2,26},{3,1},{4,28},{5,3},{6,30},{7,5},{8,0},{9,15},{... | collective-permute-start | bytes 1179656 | tf_op jit(solution)/shard_map/ppermute | solution.py:368
  51.2 3.3 %collective-permute-start.14 = (bf16[48,1152]{1,0:T(8,128)(2,1)S(1)}, bf16[48,1152]{1,0:T(8,128)(2,1)S(1)}, u32[]{:S(2)}, u32[]{:S(2)}) collective-permute-start(bf16[48,1152]{1,0:T(8,128)(2,1)S(1)} %slice.172), channel_id=1, source_target_pairs={{0,6},{1,25},{2,0},{3,27},{4,2},{5,29},{6,4},{7,31},{8,14},{9,1},{... | collective-permute-start | bytes 331784 | tf_op jit(solution)/shard_map/ppermute | solution.py:368
  54.5 2.7 %collective-permute-done.12 = bf16[48,1152]{1,0:T(8,128)(2,1)S(1)} collective-permute-done((bf16[48,1152]{1,0:T(8,128)(2,1)S(1)}, bf16[48,1152]{1,0:T(8,128)(2,1)S(1)}, u32[]{:S(2)}, u32[]{:S(2)}) %collective-permute-start.12) | collective-permute-done | bytes 110624 | tf_op jit(solution)/shard_map/ppermute | solution.py:368
  57.3 1.9 %collective-permute-start.18 = (bf16[2,96,1024]{2,1,0:T(8,128)(2,1)S(1)}, bf16[2,96,1024]{2,1,0:T(8,128)(2,1)S(1)}, u32[]{:S(2)}, u32[]{:S(2)}) collective-permute-start(bf16[2,96,1024]{2,1,0:T(8,128)(2,1)S(1)} %pad_maximum_fusion.1), channel_id=1, source_target_pairs={{0,24},{1,7},{2,26},{3,1},{4,28},{5,3},{6,30},{7,5},{8,0},{9,15},{... | collective-permute-start | bytes 1179656 | tf_op jit(solution)/shard_map/ppermute | solution.py:368
  59.2 0.3 collective-permute-start.16
  59.5 0.5 collective-permute-start.17
  60.0 5.2 %collective-permute-done.18 = bf16[2,96,1024]{2,1,0:T(8,128)(2,1)S(1)} collective-permute-done((bf16[2,96,1024]{2,1,0:T(8,128)(2,1)S(1)}, bf16[2,96,1024]{2,1,0:T(8,128)(2,1)S(1)}, u32[]{:S(2)}, u32[]{:S(2)}) %collective-permute-start.18) | collective-permute-done | bytes 393248 | tf_op jit(solution)/shard_map/ppermute | solution.py:368
  65.2 3.0 %collective-permute-start.19 = (bf16[2,96,1024]{2,1,0:T(8,128)(2,1)S(1)}, bf16[2,96,1024]{2,1,0:T(8,128)(2,1)S(1)}, u32[]{:S(2)}, u32[]{:S(2)}) collective-permute-start(bf16[2,96,1024]{2,1,0:T(8,128)(2,1)S(1)} %collective-permute-done.18), channel_id=1, source_target_pairs={{0,24},{1,7},{2,26},{3,1},{4,28},{5,3},{6,30},{7,5},{8,0},{9,15},{... | collective-permute-start | bytes 1179656 | tf_op jit(solution)/shard_map/ppermute | solution.py:368
  68.3 4.2 %collective-permute-done.17 = bf16[2,96,1024]{2,1,0:T(8,128)(2,1)S(1)} collective-permute-done((bf16[2,96,1024]{2,1,0:T(8,128)(2,1)S(1)}, bf16[2,96,1024]{2,1,0:T(8,128)(2,1)S(1)}, u32[]{:S(2)}, u32[]{:S(2)}) %collective-permute-start.17) | collective-permute-done | bytes 393248 | tf_op jit(solution)/shard_map/ppermute | solution.py:368
  72.5 1.0 collective-permute-done.19
  73.6 0.3 collective-permute-start.21
  73.9 5.7 %experts_own.1 = (bf16[4,96,1024]{2,1,0:T(8,128)(2,1)S(1)}, bf16[4,96,1024]{2,1,0:T(8,128)(2,1)S(1)}, bf16[4,96,1024]{2,1,0:T(8,128)(2,1)S(1)}, bf16[4,96,1024]{2,1,0:T(8,128)(2,1)S(1)}) custom-call(s32[3]{0:T(128)S(1)} %pad_add_fusion.here_ref, bf16[16,96,1024]{2,1,0:T(8,128)(2,1)S(1)} %constant_dynamic-update-slice_fusion.4.x_ref, ...), custom_call_target="tpu_custom_call" | custom-call | flops 3623878656 | bytes 12000000 | tf_op jit(solution)/shard_map/experts_own/pallas_call | solution.py:543
  79.6 4.4 %experts_other.1 = (bf16[384,384]{1,0:T(8,128)(2,1)S(1)}, bf16[4,96,1024]{2,1,0:T(8,128)(2,1)S(1)}) custom-call(s32[3]{0:T(128)S(1)} %pad_add_fusion.here_ref, bf16[16,96,1024]{2,1,0:T(8,128)(2,1)S(1)} %collective-permute-done.21.x_ref, f32[4,1,1024]{2,1,0:T(1,128)S(1)} %get-tuple-element.28.inv_ref, bf16[4096,384]{1,0:T(8,128)(2,1)S(1)} %bitcast.64, ...), custom_call_target="tpu_custom_call" | custom-call | flops 3019898880 | bytes 10000000 | tf_op jit(solution)/shard_map/experts_other/pallas_call | solution.py:553
  84.0 0.7 collective-permute-start.24
  84.8 1.9 %experts_rest.1 = (bf16[4,96,1024]{2,1,0:T(8,128)(2,1)S(1)}, bf16[4,96,1024]{2,1,0:T(8,128)(2,1)S(1)}, bf16[4,96,1024]{2,1,0:T(8,128)(2,1)S(1)}) custom-call(s32[3]{0:T(128)S(1)} %pad_add_fusion.here_ref, bf16[384,384]{1,0:T(8,128)(2,1)S(1)} %get-tuple-element.30.act_ref, bf16[384,4096]{1,0:T(8,128)(2,1)S(1)} %bitcast.62), custom_call_target="tpu_custom_call" | custom-call | flops 905969664 | bytes 5000000 | tf_op jit(solution)/shard_map/experts_rest/pallas_call | solution.py:562
  86.8 0.5 collective-permute-start.27
  87.4 0.3 add_convert_fusion.1
  87.8 3.8 %collective-permute-start.31 = (bf16[2,96,1024]{2,1,0:T(8,128)(2,1)S(1)}, bf16[2,96,1024]{2,1,0:T(8,128)(2,1)S(1)}, u32[]{:S(2)}, u32[]{:S(2)}) collective-permute-start(bf16[2,96,1024]{2,1,0:T(8,128)(2,1)S(1)} %get-tuple-element.48), channel_id=1, source_target_pairs={{0,24},{1,7},{2,26},{3,1},{4,28},{5,3},{6,30},{7,5},{8,0},{9,15},{... | collective-permute-start | bytes 1179656 | tf_op jit(solution)/shard_map/ppermute | solution.py:368
  91.5 0.3 add_convert_fusion.2
  92.0 0.3 add_convert_fusion
  92.3 3.3 %collective-permute-start.28 = (bf16[2,96,1024]{2,1,0:T(8,128)(2,1)S(1)}, bf16[2,96,1024]{2,1,0:T(8,128)(2,1)S(1)}, u32[]{:S(2)}, u32[]{:S(2)}) collective-permute-start(bf16[2,96,1024]{2,1,0:T(8,128)(2,1)S(1)} %slice.178), channel_id=1, source_target_pairs={{0,24},{1,7},{2,26},{3,1},{4,28},{5,3},{6,30},{7,5},{8,0},{9,15},{... | collective-permute-start | bytes 1179656 | tf_op jit(solution)/shard_map/ppermute | solution.py:368
  95.7 1.2 collective-permute-done.31
  97.0 3.8 %collective-permute-start.32 = (bf16[2,96,1024]{2,1,0:T(8,128)(2,1)S(1)}, bf16[2,96,1024]{2,1,0:T(8,128)(2,1)S(1)}, u32[]{:S(2)}, u32[]{:S(2)}) collective-permute-start(bf16[2,96,1024]{2,1,0:T(8,128)(2,1)S(1)} %add_convert_fusion.5), channel_id=1, source_target_pairs={{0,24},{1,7},{2,26},{3,1},{4,28},{5,3},{6,30},{7,5},{8,0},{9,15},{... | collective-permute-start | bytes 1179656 | tf_op jit(solution)/shard_map/ppermute | solution.py:368
  100.7 0.1 add_convert_fusion.7
  101.0 0.3 add_convert_fusion.3
  101.3 3.4 %collective-permute-done.30 = bf16[2,96,1024]{2,1,0:T(8,128)(2,1)S(1)} collective-permute-done((bf16[2,96,1024]{2,1,0:T(8,128)(2,1)S(1)}, bf16[2,96,1024]{2,1,0:T(8,128)(2,1)S(1)}, u32[]{:S(2)}, u32[]{:S(2)}) %collective-permute-start.30) | collective-permute-done | bytes 393248 | tf_op jit(solution)/shard_map/ppermute | solution.py:368
  104.7 1.3 collective-permute-done.32
  106.0 3.9 %collective-permute-done.26 = bf16[2,96,1024]{2,1,0:T(8,128)(2,1)S(1)} collective-permute-done((bf16[2,96,1024]{2,1,0:T(8,128)(2,1)S(1)}, bf16[2,96,1024]{2,1,0:T(8,128)(2,1)S(1)}, u32[]{:S(2)}, u32[]{:S(2)}) %collective-permute-start.26) | collective-permute-done | bytes 393248 | tf_op jit(solution)/shard_map/ppermute | solution.py:368
  109.9 0.4 add_convert_fusion.6
  110.4 4.9 %collective-permute-start.33 = (bf16[96,1024]{1,0:T(8,128)(2,1)S(1)}, bf16[96,1024]{1,0:T(8,128)(2,1)S(1)}, u32[]{:S(2)}, u32[]{:S(2)}) collective-permute-start(bf16[96,1024]{1,0:T(8,128)(2,1)S(1)} %get-tuple-element.49), channel_id=1, source_target_pairs={{0,4},{1,17},{2,6},{3,19},{4,0},{5,21},{6,2},{7,23},{8,12},{9,25},... | collective-permute-start | bytes 589832 | tf_op jit(solution)/shard_map/ppermute | solution.py:368
  115.3 0.6 collective-permute-start.34
  115.9 1.5 %collective-permute-start.29 = (bf16[96,1024]{1,0:T(8,128)(2,1)S(1)}, bf16[96,1024]{1,0:T(8,128)(2,1)S(1)}, u32[]{:S(2)}, u32[]{:S(2)}) collective-permute-start(bf16[96,1024]{1,0:T(8,128)(2,1)S(1)} %slice_bitcast_fusion.2), channel_id=1, source_target_pairs={{0,2},{1,9},{2,4},{3,11},{4,6},{5,13},{6,0},{7,15},{8,10},{9,17},{... | collective-permute-start | bytes 589832 | tf_op jit(solution)/shard_map/ppermute | solution.py:368
  117.5 1.4 %collective-permute-done.33 = bf16[96,1024]{1,0:T(8,128)(2,1)S(1)} collective-permute-done((bf16[96,1024]{1,0:T(8,128)(2,1)S(1)}, bf16[96,1024]{1,0:T(8,128)(2,1)S(1)}, u32[]{:S(2)}, u32[]{:S(2)}) %collective-permute-start.33) | collective-permute-done | bytes 196640 | tf_op jit(solution)/shard_map/ppermute | solution.py:368
  119.0 3.5 %collective-permute-done.34 = bf16[96,1024]{1,0:T(8,128)(2,1)S(1)} collective-permute-done((bf16[96,1024]{1,0:T(8,128)(2,1)S(1)}, bf16[96,1024]{1,0:T(8,128)(2,1)S(1)}, u32[]{:S(2)}, u32[]{:S(2)}) %collective-permute-start.34) | collective-permute-done | bytes 196640 | tf_op jit(solution)/shard_map/ppermute | solution.py:368
  122.5 0.4 collective-permute-done.29
  123.0 0.7 collective-permute-start.35
  123.7 2.3 %collective-permute-start.36 = (bf16[48,1024]{1,0:T(8,128)(2,1)S(1)}, bf16[48,1024]{1,0:T(8,128)(2,1)S(1)}, u32[]{:S(2)}, u32[]{:S(2)}) collective-permute-start(bf16[48,1024]{1,0:T(8,128)(2,1)S(1)} %get-tuple-element.60), channel_id=1, source_target_pairs={{0,96},{1,33},{2,98},{3,35},{4,100},{5,37},{6,102},{7,39},{8,104},... | collective-permute-start | bytes 294920 | tf_op jit(solution)/shard_map/ppermute | solution.py:368
  126.1 2.2 %collective-permute-done.36 = bf16[48,1024]{1,0:T(8,128)(2,1)S(1)} collective-permute-done((bf16[48,1024]{1,0:T(8,128)(2,1)S(1)}, bf16[48,1024]{1,0:T(8,128)(2,1)S(1)}, u32[]{:S(2)}, u32[]{:S(2)}) %collective-permute-start.36) | collective-permute-done | bytes 98336 | tf_op jit(solution)/shard_map/ppermute | solution.py:368
  128.5 1.6 %tail.1 = bf16[3,20,1024]{2,1,0:T(8,128)(2,1)} custom-call(s32[1,4]{1,0:T(1,128)S(1)} %copy-done.10, s32[1,4]{1,0:T(1,128)S(1)} %copy-done.11, s32[1,20]{1,0:T(1,128)S(1)} %copy-done.12, bf16[64,1024]{1,0:T(8,128)(2,1)S(1)} %copy-done.14, bf16[3,20,1024]{2,1,0:T(8,128)(2,1)S(1)} %bitcast.71), custom_call_target="tpu_custom_call" | custom-call | flops 1000000000 | bytes 1000000 | tf_op jit(solution)/shard_map/tail/pallas_call | solution.py:463
  130.2 1.8 %combine.1 = bf16[64,512]{1,0:T(8,128)(2,1)} custom-call(s32[3]{0:T(128)S(1)} %pad_add_fusion.here_ref, bf16[2,48,512]{2,1,0:T(8,128)(2,1)S(1)} %get-tuple-element.58.mine_ref, bf16[2,48,512]{2,1,0:T(8,128)(2,1)S(1)} %slice.196.theirs_ref, bf16[96,128]{1,0:T(8,128)(2,1)S(1)} %bitcast_select_fusion.stat_ref, f32[64,512]{1,0:T(8,128)S(1)} %get-tuple-element.38.hid_ref, ...), custom_call_target="tpu_custom_call" | custom-call | flops 100000000 | bytes 1000000 | tf_op jit(solution)/shard_map/combine/pallas_call | solution.py:591
  (111 shorter events, 2.5 us)
Async XLA Ops:
  0.6 13.2 %copy-start.10 = (s32[1,4]{1,0:T(1,128)S(1)}, s32[1,4]{1,0:T(1,128)}, u32[]{:S(2)}) copy-start(s32[1,4]{1,0:T(1,128)} %span_ref.3) | copy-start | bytes 52
  0.6 13.2 %copy-start.11 = (s32[1,4]{1,0:T(1,128)S(1)}, s32[1,4]{1,0:T(1,128)}, u32[]{:S(2)}) copy-start(s32[1,4]{1,0:T(1,128)} %res_ref.3) | copy-start | bytes 52
  0.7 13.2 %copy-start.12 = (s32[1,20]{1,0:T(1,128)S(1)}, s32[1,20]{1,0:T(1,128)}, u32[]{:S(2)}) copy-start(s32[1,20]{1,0:T(1,128)} %slot_ref.3) | copy-start | bytes 244
  0.7 13.2 %copy-start.9 = (f32[512]{0:T(512)S(1)}, f32[512]{0:T(512)}, u32[]{:S(2)}) copy-start(f32[512]{0:T(512)} %param.35) | copy-start | bytes 6148
  0.7 13.2 %copy-start.7 = (f32[1024]{0:T(1024)S(1)}, f32[1024]{0:T(1024)}, u32[]{:S(2)}) copy-start(f32[1024]{0:T(1024)} %param.37) | copy-start | bytes 12292
  0.7 13.2 %copy-start.8 = (f32[1024]{0:T(1024)S(1)}, f32[1024]{0:T(1024)}, u32[]{:S(2)}) copy-start(f32[1024]{0:T(1024)} %param.39) | copy-start | bytes 12292
  0.7 13.2 %copy-start.5 = (bf16[64,1024]{1,0:T(8,128)(2,1)S(1)}, bf16[64,1024]{1,0:T(8,128)(2,1)}, u32[]{:S(2)}) copy-start(bf16[64,1024]{1,0:T(8,128)(2,1)} %z_ref.1) | copy-start | bytes 393220
  0.7 13.2 %copy-start.3 = (f32[20,16,1024]{2,1,0:T(8,128)S(1)}, f32[20,16,1024]{2,1,0:T(8,128)}, u32[]{:S(2)}) copy-start(f32[20,16,1024]{2,1,0:T(8,128)} %sc_ref.1) | copy-start | bytes 3932164
  0.7 13.2 %copy-start.4 = (bf16[512,1024]{1,0:T(8,128)(2,1)S(1)}, bf16[512,1024]{1,0:T(8,128)(2,1)}, u32[]{:S(2)}) copy-start(bf16[512,1024]{1,0:T(8,128)(2,1)} %sw_ref.1) | copy-start | bytes 3145732
  0.7 13.2 %copy-start.6 = (f32[16,1024]{1,0:T(8,128)S(1)}, f32[16,1024]{1,0:T(8,128)}, u32[]{:S(2)}) copy-start(f32[16,1024]{1,0:T(8,128)} %dl_ref.1) | copy-start | bytes 196612
  2.9 1.4 %collective-permute-start = (bf16[80,640]{1,0:T(8,128)(2,1)S(1)}, bf16[80,640]{1,0:T(8,128)(2,1)S(1)}, u32[]{:S(2)}, u32[]{:S(2)}) collective-permute-start(bf16[80,640]{1,0:T(8,128)(2,1)S(1)} %get-tuple-element.22), channel_id=1, source_target_pairs={{0,1},{1,0},{2,3},{3,2},{4,5},{5,4},{6,7},{7,6},{8,9},{9,8},{10,11... | collective-permute-start | bytes 307208 | tf_op jit(solution)/shard_map/ppermute | solution.py:356
  4.4 6.2 %collective-permute-start.1 = (bf16[80,640]{1,0:T(8,128)(2,1)S(1)}, bf16[80,640]{1,0:T(8,128)(2,1)S(1)}, u32[]{:S(2)}, u32[]{:S(2)}) collective-permute-start(bf16[80,640]{1,0:T(8,128)(2,1)S(1)} %add_convert_fusion.9.q0_ref), channel_id=1, source_target_pairs={{0,2},{2,4},{4,6},{6,0},{1,3},{3,5},{5,7},{7,1},{8,10},{10,12},{12... | collective-permute-start | bytes 307208 | tf_op jit(solution)/shard_map/ppermute | solution.py:356
  6.0 7.8 %collective-permute-start.2 = (bf16[80,640]{1,0:T(8,128)(2,1)S(1)}, bf16[80,640]{1,0:T(8,128)(2,1)S(1)}, u32[]{:S(2)}, u32[]{:S(2)}) collective-permute-start(bf16[80,640]{1,0:T(8,128)(2,1)S(1)} %add_convert_fusion.9.q0_ref), channel_id=1, source_target_pairs={{0,4},{2,6},{4,0},{6,2},{1,5},{3,7},{5,1},{7,3},{8,12},{10,14},{12... | collective-permute-start | bytes 307208 | tf_op jit(solution)/shard_map/ppermute | solution.py:356
  8.7 5.1 %collective-permute-start.3 = (bf16[80,640]{1,0:T(8,128)(2,1)S(1)}, bf16[80,640]{1,0:T(8,128)(2,1)S(1)}, u32[]{:S(2)}, u32[]{:S(2)}) collective-permute-start(bf16[80,640]{1,0:T(8,128)(2,1)S(1)} %add_convert_fusion.9.q0_ref), channel_id=1, source_target_pairs={{0,6},{2,0},{4,2},{6,4},{1,7},{3,1},{5,3},{7,5},{8,14},{10,8},{12,... | collective-permute-start | bytes 307208 | tf_op jit(solution)/shard_map/ppermute | solution.py:356
  13.9 15.6 %copy-start.15 = (bf16[64,512]{1,0:T(8,128)(2,1)S(1)}, bf16[64,512]{1,0:T(8,128)(2,1)}, u32[]{:S(2)}) copy-start(bf16[64,512]{1,0:T(8,128)(2,1)} %resid_ref.1) | copy-start | bytes 196612
  14.0 15.6 %copy-start.16 = (bf16[512,4]{0,1:T(4,128)(2,1)S(1)}, bf16[512,4]{0,1:T(4,128)(2,1)}, u32[]{:S(2)}) copy-start(bf16[512,4]{0,1:T(4,128)(2,1)} %param.43) | copy-start | bytes 12292
  14.0 15.6 %copy-start.17 = (f32[512]{0:T(512)S(1)}, f32[512]{0:T(512)}, u32[]{:S(2)}) copy-start(f32[512]{0:T(512)} %param.42) | copy-start | bytes 6148
  14.0 15.5 %copy-start.18 = (s32[64,2]{0,1:T(2,128)S(1)}, s32[64,2]{0,1:T(2,128)}, u32[]{:S(2)}) copy-start(s32[64,2]{0,1:T(2,128)} %param.44) | copy-start | bytes 1540
  19.8 1.6 %collective-permute-start.4 = (bf16[4,64,512]{2,1,0:T(8,128)(2,1)S(1)}, bf16[4,64,512]{2,1,0:T(8,128)(2,1)S(1)}, u32[]{:S(2)}, u32[]{:S(2)}) collective-permute-start(bf16[4,64,512]{2,1,0:T(8,128)(2,1)S(1)} %get-tuple-element.25), channel_id=1, source_target_pairs={{0,1},{1,0},{2,3},{3,2},{4,5},{5,4},{6,7},{7,6},{8,9},{9,8},{10,11... | collective-permute-start | bytes 786440 | tf_op jit(solution)/shard_map/ppermute | solution.py:356
  21.5 5.8 %collective-permute-start.5 = (bf16[64,512]{1,0:T(8,128)(2,1)S(1)}, bf16[64,512]{1,0:T(8,128)(2,1)S(1)}, u32[]{:S(2)}, u32[]{:S(2)}) collective-permute-start(bf16[64,512]{1,0:T(8,128)(2,1)S(1)} %get-tuple-element.53), channel_id=1, source_target_pairs={{0,2},{2,4},{4,6},{6,0},{1,3},{3,5},{5,7},{7,1},{8,10},{10,12},{12... | collective-permute-start | bytes 196616 | tf_op jit(solution)/shard_map/ppermute | solution.py:356
  22.8 6.0 %collective-permute-start.6 = (bf16[64,512]{1,0:T(8,128)(2,1)S(1)}, bf16[64,512]{1,0:T(8,128)(2,1)S(1)}, u32[]{:S(2)}, u32[]{:S(2)}) collective-permute-start(bf16[64,512]{1,0:T(8,128)(2,1)S(1)} %get-tuple-element.52), channel_id=1, source_target_pairs={{0,4},{2,6},{4,0},{6,2},{1,5},{3,7},{5,1},{7,3},{8,12},{10,14},{12... | collective-permute-start | bytes 196616 | tf_op jit(solution)/shard_map/ppermute | solution.py:356
  25.2 4.3 %collective-permute-start.7 = (bf16[64,512]{1,0:T(8,128)(2,1)S(1)}, bf16[64,512]{1,0:T(8,128)(2,1)S(1)}, u32[]{:S(2)}, u32[]{:S(2)}) collective-permute-start(bf16[64,512]{1,0:T(8,128)(2,1)S(1)} %get-tuple-element.51), channel_id=1, source_target_pairs={{0,6},{2,0},{4,2},{6,4},{1,7},{3,1},{5,3},{7,5},{8,14},{10,8},{12,... | collective-permute-start | bytes 196616 | tf_op jit(solution)/shard_map/ppermute | solution.py:356
  30.4 1.4 %collective-permute-start.8 = (bf16[2,48,640]{2,1,0:T(8,128)(2,1)S(1)}, bf16[2,48,640]{2,1,0:T(8,128)(2,1)S(1)}, u32[]{:S(2)}, u32[]{:S(2)}) collective-permute-start(bf16[2,48,640]{2,1,0:T(8,128)(2,1)S(1)} %get-tuple-element.27), channel_id=1, source_target_pairs={{0,1},{1,0},{2,3},{3,2},{4,5},{5,4},{6,7},{7,6},{8,9},{9,8},{10,11... | collective-permute-start | bytes 368648 | tf_op jit(solution)/shard_map/ppermute | solution.py:356
  32.0 2.8 %collective-permute-start.9 = (bf16[48,1024]{1,0:T(8,128)(2,1)S(1)}, bf16[48,1024]{1,0:T(8,128)(2,1)S(1)}, u32[]{:S(2)}, u32[]{:S(2)}) collective-permute-start(bf16[48,1024]{1,0:T(8,128)(2,1)S(1)} %get-tuple-element.62), channel_id=1, source_target_pairs={{0,0},{1,65},{2,2},{3,67},{4,4},{5,69},{6,6},{7,71},{8,8},{9,73},{... | collective-permute-start | bytes 294920 | tf_op jit(solution)/shard_map/ppermute | solution.py:368
  32.6 7.8 %collective-permute-start.10 = (bf16[48,1024]{1,0:T(8,128)(2,1)S(1)}, bf16[48,1024]{1,0:T(8,128)(2,1)S(1)}, u32[]{:S(2)}, u32[]{:S(2)}) collective-permute-start(bf16[48,1024]{1,0:T(8,128)(2,1)S(1)} %get-tuple-element.61), channel_id=1, source_target_pairs={{0,32},{1,97},{2,34},{3,99},{4,36},{5,101},{6,38},{7,103},{8,40},{... | collective-permute-start | bytes 294920 | tf_op jit(solution)/shard_map/ppermute | solution.py:368
  40.5 7.2 %collective-permute-start.11 = (bf16[96,1152]{1,0:T(8,128)(2,1)S(1)}, bf16[96,1152]{1,0:T(8,128)(2,1)S(1)}, u32[]{:S(2)}, u32[]{:S(2)}) collective-permute-start(bf16[96,1152]{1,0:T(8,128)(2,1)S(1)} %pad_maximum_fusion.2), channel_id=1, source_target_pairs={{0,2},{1,9},{2,4},{3,11},{4,6},{5,13},{6,0},{7,15},{8,10},{9,17},{... | collective-permute-start | bytes 663560 | tf_op jit(solution)/shard_map/ppermute | solution.py:368
  41.7 9.5 %collective-permute-start.13 = (bf16[96,1152]{1,0:T(8,128)(2,1)S(1)}, bf16[96,1152]{1,0:T(8,128)(2,1)S(1)}, u32[]{:S(2)}, u32[]{:S(2)}) collective-permute-start(bf16[96,1152]{1,0:T(8,128)(2,1)S(1)} %pad_maximum_fusion.2), channel_id=1, source_target_pairs={{0,6},{1,25},{2,0},{3,27},{4,2},{5,29},{6,4},{7,31},{8,14},{9,1},{... | collective-permute-start | bytes 663560 | tf_op jit(solution)/shard_map/ppermute | solution.py:368
  47.7 26.2 %copy-start.2 = (bf16[1,4096,384]{2,1,0:T(8,128)(2,1)S(1)}, bf16[1,4096,384]{2,1,0:T(8,128)(2,1)}, u32[]{:S(2)}) copy-start(bf16[1,4096,384]{2,1,0:T(8,128)(2,1)} %param.46) | copy-start | bytes 9437188
  47.8 11.7 %collective-permute-start.15 = (bf16[2,96,1024]{2,1,0:T(8,128)(2,1)S(1)}, bf16[2,96,1024]{2,1,0:T(8,128)(2,1)S(1)}, u32[]{:S(2)}, u32[]{:S(2)}) collective-permute-start(bf16[2,96,1024]{2,1,0:T(8,128)(2,1)S(1)} %pad_maximum_fusion), channel_id=1, source_target_pairs={{0,8},{1,3},{2,10},{3,5},{4,12},{5,7},{6,14},{7,1},{8,16},{9,11},{... | collective-permute-start | bytes 1179656 | tf_op jit(solution)/shard_map/ppermute | solution.py:368
  49.4 24.1 %collective-permute-start.20 = (bf16[2,96,1024]{2,1,0:T(8,128)(2,1)S(1)}, bf16[2,96,1024]{2,1,0:T(8,128)(2,1)S(1)}, u32[]{:S(2)}, u32[]{:S(2)}) collective-permute-start(bf16[2,96,1024]{2,1,0:T(8,128)(2,1)S(1)} %pad_maximum_fusion), channel_id=1, source_target_pairs={{0,24},{1,7},{2,26},{3,1},{4,28},{5,3},{6,30},{7,5},{8,0},{9,15},{... | collective-permute-start | bytes 1179656 | tf_op jit(solution)/shard_map/ppermute | solution.py:368
  51.1 6.1 %collective-permute-start.12 = (bf16[48,1152]{1,0:T(8,128)(2,1)S(1)}, bf16[48,1152]{1,0:T(8,128)(2,1)S(1)}, u32[]{:S(2)}, u32[]{:S(2)}) collective-permute-start(bf16[48,1152]{1,0:T(8,128)(2,1)S(1)} %slice.171), channel_id=1, source_target_pairs={{0,2},{1,9},{2,4},{3,11},{4,6},{5,13},{6,0},{7,15},{8,10},{9,17},{... | collective-permute-start | bytes 331784 | tf_op jit(solution)/shard_map/ppermute | solution.py:368
  51.2 6.0 %collective-permute-start.14 = (bf16[48,1152]{1,0:T(8,128)(2,1)S(1)}, bf16[48,1152]{1,0:T(8,128)(2,1)S(1)}, u32[]{:S(2)}, u32[]{:S(2)}) collective-permute-start(bf16[48,1152]{1,0:T(8,128)(2,1)S(1)} %slice.172), channel_id=1, source_target_pairs={{0,6},{1,25},{2,0},{3,27},{4,2},{5,29},{6,4},{7,31},{8,14},{9,1},{... | collective-permute-start | bytes 331784 | tf_op jit(solution)/shard_map/ppermute | solution.py:368
  57.2 16.7 %copy-start.1 = (bf16[1,4096,384]{2,1,0:T(8,128)(2,1)S(1)}, bf16[1,4096,384]{2,1,0:T(8,128)(2,1)}, u32[]{:S(2)}) copy-start(bf16[1,4096,384]{2,1,0:T(8,128)(2,1)} %param.45) | copy-start | bytes 9437188
  57.3 16.6 %copy-start = (bf16[1,384,4096]{2,1,0:T(8,128)(2,1)S(1)}, bf16[1,384,4096]{2,1,0:T(8,128)(2,1)}, u32[]{:S(2)}) copy-start(bf16[1,384,4096]{2,1,0:T(8,128)(2,1)} %param.47) | copy-start | bytes 9437188
  57.3 7.8 %collective-permute-start.18 = (bf16[2,96,1024]{2,1,0:T(8,128)(2,1)S(1)}, bf16[2,96,1024]{2,1,0:T(8,128)(2,1)S(1)}, u32[]{:S(2)}, u32[]{:S(2)}) collective-permute-start(bf16[2,96,1024]{2,1,0:T(8,128)(2,1)S(1)} %pad_maximum_fusion.1), channel_id=1, source_target_pairs={{0,24},{1,7},{2,26},{3,1},{4,28},{5,3},{6,30},{7,5},{8,0},{9,15},{... | collective-permute-start | bytes 1179656 | tf_op jit(solution)/shard_map/ppermute | solution.py:368
  59.2 9.1 %collective-permute-start.16 = (bf16[2,96,1024]{2,1,0:T(8,128)(2,1)S(1)}, bf16[2,96,1024]{2,1,0:T(8,128)(2,1)S(1)}, u32[]{:S(2)}, u32[]{:S(2)}) collective-permute-start(bf16[2,96,1024]{2,1,0:T(8,128)(2,1)S(1)} %pad_maximum_fusion.1), channel_id=1, source_target_pairs={{0,8},{1,3},{2,10},{3,5},{4,12},{5,7},{6,14},{7,1},{8,16},{9,11},{... | collective-permute-start | bytes 1179656 | tf_op jit(solution)/shard_map/ppermute | solution.py:368
  59.5 13.0 %collective-permute-start.17 = (bf16[2,96,1024]{2,1,0:T(8,128)(2,1)S(1)}, bf16[2,96,1024]{2,1,0:T(8,128)(2,1)S(1)}, u32[]{:S(2)}, u32[]{:S(2)}) collective-permute-start(bf16[2,96,1024]{2,1,0:T(8,128)(2,1)S(1)} %collective-permute-done.15), channel_id=1, source_target_pairs={{0,8},{1,3},{2,10},{3,5},{4,12},{5,7},{6,14},{7,1},{8,16},{9,11},{... | collective-permute-start | bytes 1179656 | tf_op jit(solution)/shard_map/ppermute | solution.py:368
  65.2 8.3 %collective-permute-start.19 = (bf16[2,96,1024]{2,1,0:T(8,128)(2,1)S(1)}, bf16[2,96,1024]{2,1,0:T(8,128)(2,1)S(1)}, u32[]{:S(2)}, u32[]{:S(2)}) collective-permute-start(bf16[2,96,1024]{2,1,0:T(8,128)(2,1)S(1)} %collective-permute-done.18), channel_id=1, source_target_pairs={{0,24},{1,7},{2,26},{3,1},{4,28},{5,3},{6,30},{7,5},{8,0},{9,15},{... | collective-permute-start | bytes 1179656 | tf_op jit(solution)/shard_map/ppermute | solution.py:368
  73.6 6.0 %collective-permute-start.21 = (bf16[16,96,1024]{2,1,0:T(8,128)(2,1)S(1)}, bf16[16,96,1024]{2,1,0:T(8,128)(2,1)S(1)}, u32[]{:S(2)}, u32[]{:S(2)}) collective-permute-start(bf16[16,96,1024]{2,1,0:T(8,128)(2,1)S(1)} %constant_dynamic-update-slice_fusion.4.x_ref), channel_id=1, source_target_pairs={{0,1},{1,0},{2,3},{3,2},{4,5},{5,4},{6,7},{7,6},{8,9},{9,8},{10,11... | collective-permute-start | bytes 9437192 | tf_op jit(solution)/shard_map/ppermute | solution.py:356
  84.0 3.3 %collective-permute-start.24 = (bf16[4,96,1024]{2,1,0:T(8,128)(2,1)S(1)}, bf16[4,96,1024]{2,1,0:T(8,128)(2,1)S(1)}, u32[]{:S(2)}, u32[]{:S(2)}) collective-permute-start(bf16[4,96,1024]{2,1,0:T(8,128)(2,1)S(1)} %get-tuple-element.35), channel_id=1, source_target_pairs={{0,1},{1,0},{2,3},{3,2},{4,5},{5,4},{6,7},{7,6},{8,9},{9,8},{10,11... | collective-permute-start | bytes 2359304 | tf_op jit(solution)/shard_map/ppermute | solution.py:356
  86.7 4.9 %collective-permute-start.23 = (bf16[4,96,1024]{2,1,0:T(8,128)(2,1)S(1)}, bf16[4,96,1024]{2,1,0:T(8,128)(2,1)S(1)}, u32[]{:S(2)}, u32[]{:S(2)}) collective-permute-start(bf16[4,96,1024]{2,1,0:T(8,128)(2,1)S(1)} %get-tuple-element.33), channel_id=1, source_target_pairs={{0,1},{1,0},{2,3},{3,2},{4,5},{5,4},{6,7},{7,6},{8,9},{9,8},{10,11... | collective-permute-start | bytes 2359304 | tf_op jit(solution)/shard_map/ppermute | solution.py:356
  86.8 5.2 %collective-permute-start.27 = (bf16[4,96,1024]{2,1,0:T(8,128)(2,1)S(1)}, bf16[4,96,1024]{2,1,0:T(8,128)(2,1)S(1)}, u32[]{:S(2)}, u32[]{:S(2)}) collective-permute-start(bf16[4,96,1024]{2,1,0:T(8,128)(2,1)S(1)} %get-tuple-element.37), channel_id=1, source_target_pairs={{0,1},{1,0},{2,3},{3,2},{4,5},{5,4},{6,7},{7,6},{8,9},{9,8},{10,11... | collective-permute-start | bytes 2359304 | tf_op jit(solution)/shard_map/ppermute | solution.py:356
  87.3 13.7 %collective-permute-start.22 = (bf16[4,96,1024]{2,1,0:T(8,128)(2,1)S(1)}, bf16[4,96,1024]{2,1,0:T(8,128)(2,1)S(1)}, u32[]{:S(2)}, u32[]{:S(2)}) collective-permute-start(bf16[4,96,1024]{2,1,0:T(8,128)(2,1)S(1)} %get-tuple-element.31), channel_id=1, source_target_pairs={{0,1},{1,0},{2,3},{3,2},{4,5},{5,4},{6,7},{7,6},{8,9},{9,8},{10,11... | collective-permute-start | bytes 2359304 | tf_op jit(solution)/shard_map/ppermute | solution.py:356
  87.8 9.1 %collective-permute-start.31 = (bf16[2,96,1024]{2,1,0:T(8,128)(2,1)S(1)}, bf16[2,96,1024]{2,1,0:T(8,128)(2,1)S(1)}, u32[]{:S(2)}, u32[]{:S(2)}) collective-permute-start(bf16[2,96,1024]{2,1,0:T(8,128)(2,1)S(1)} %get-tuple-element.48), channel_id=1, source_target_pairs={{0,24},{1,7},{2,26},{3,1},{4,28},{5,3},{6,30},{7,5},{8,0},{9,15},{... | collective-permute-start | bytes 1179656 | tf_op jit(solution)/shard_map/ppermute | solution.py:368
  91.5 9.2 %collective-permute-start.25 = (bf16[2,96,1024]{2,1,0:T(8,128)(2,1)S(1)}, bf16[2,96,1024]{2,1,0:T(8,128)(2,1)S(1)}, u32[]{:S(2)}, u32[]{:S(2)}) collective-permute-start(bf16[2,96,1024]{2,1,0:T(8,128)(2,1)S(1)} %get-tuple-element.47), channel_id=1, source_target_pairs={{0,8},{1,3},{2,10},{3,5},{4,12},{5,7},{6,14},{7,1},{8,16},{9,11},{... | collective-permute-start | bytes 1179656 | tf_op jit(solution)/shard_map/ppermute | solution.py:368
  91.9 12.8 %collective-permute-start.30 = (bf16[2,96,1024]{2,1,0:T(8,128)(2,1)S(1)}, bf16[2,96,1024]{2,1,0:T(8,128)(2,1)S(1)}, u32[]{:S(2)}, u32[]{:S(2)}) collective-permute-start(bf16[2,96,1024]{2,1,0:T(8,128)(2,1)S(1)} %slice.182), channel_id=1, source_target_pairs={{0,8},{1,3},{2,10},{3,5},{4,12},{5,7},{6,14},{7,1},{8,16},{9,11},{... | collective-permute-start | bytes 1179656 | tf_op jit(solution)/shard_map/ppermute | solution.py:368
  92.3 12.4 %collective-permute-start.28 = (bf16[2,96,1024]{2,1,0:T(8,128)(2,1)S(1)}, bf16[2,96,1024]{2,1,0:T(8,128)(2,1)S(1)}, u32[]{:S(2)}, u32[]{:S(2)}) collective-permute-start(bf16[2,96,1024]{2,1,0:T(8,128)(2,1)S(1)} %slice.178), channel_id=1, source_target_pairs={{0,24},{1,7},{2,26},{3,1},{4,28},{5,3},{6,30},{7,5},{8,0},{9,15},{... | collective-permute-start | bytes 1179656 | tf_op jit(solution)/shard_map/ppermute | solution.py:368
  97.0 9.1 %collective-permute-start.32 = (bf16[2,96,1024]{2,1,0:T(8,128)(2,1)S(1)}, bf16[2,96,1024]{2,1,0:T(8,128)(2,1)S(1)}, u32[]{:S(2)}, u32[]{:S(2)}) collective-permute-start(bf16[2,96,1024]{2,1,0:T(8,128)(2,1)S(1)} %add_convert_fusion.5), channel_id=1, source_target_pairs={{0,24},{1,7},{2,26},{3,1},{4,28},{5,3},{6,30},{7,5},{8,0},{9,15},{... | collective-permute-start | bytes 1179656 | tf_op jit(solution)/shard_map/ppermute | solution.py:368
  100.9 9.1 %collective-permute-start.26 = (bf16[2,96,1024]{2,1,0:T(8,128)(2,1)S(1)}, bf16[2,96,1024]{2,1,0:T(8,128)(2,1)S(1)}, u32[]{:S(2)}, u32[]{:S(2)}) collective-permute-start(bf16[2,96,1024]{2,1,0:T(8,128)(2,1)S(1)} %add_convert_fusion.7), channel_id=1, source_target_pairs={{0,8},{1,3},{2,10},{3,5},{4,12},{5,7},{6,14},{7,1},{8,16},{9,11},{... | collective-permute-start | bytes 1179656 | tf_op jit(solution)/shard_map/ppermute | solution.py:368
  101.3 27.2 %copy-start.13 = (bf16[20,3,1024]{2,0,1:T(8,128)(2,1)S(1)}, bf16[20,3,1024]{2,0,1:T(8,128)(2,1)}, u32[]{:S(2)}) copy-start(bf16[20,3,1024]{2,0,1:T(8,128)(2,1)} %param.26) | copy-start | bytes 368644
  101.3 27.2 %copy-start.14 = (bf16[64,1024]{1,0:T(8,128)(2,1)S(1)}, bf16[64,1024]{1,0:T(8,128)(2,1)}, u32[]{:S(2)}) copy-start(bf16[64,1024]{1,0:T(8,128)(2,1)} %x_ref.1) | copy-start | bytes 393220
  110.4 8.5 %collective-permute-start.33 = (bf16[96,1024]{1,0:T(8,128)(2,1)S(1)}, bf16[96,1024]{1,0:T(8,128)(2,1)S(1)}, u32[]{:S(2)}, u32[]{:S(2)}) collective-permute-start(bf16[96,1024]{1,0:T(8,128)(2,1)S(1)} %get-tuple-element.49), channel_id=1, source_target_pairs={{0,4},{1,17},{2,6},{3,19},{4,0},{5,21},{6,2},{7,23},{8,12},{9,25},... | collective-permute-start | bytes 589832 | tf_op jit(solution)/shard_map/ppermute | solution.py:368
  115.3 7.2 %collective-permute-start.34 = (bf16[96,1024]{1,0:T(8,128)(2,1)S(1)}, bf16[96,1024]{1,0:T(8,128)(2,1)S(1)}, u32[]{:S(2)}, u32[]{:S(2)}) collective-permute-start(bf16[96,1024]{1,0:T(8,128)(2,1)S(1)} %get-tuple-element.50), channel_id=1, source_target_pairs={{0,6},{1,25},{2,0},{3,27},{4,2},{5,29},{6,4},{7,31},{8,14},{9,1},{... | collective-permute-start | bytes 589832 | tf_op jit(solution)/shard_map/ppermute | solution.py:368
  115.9 6.9 %collective-permute-start.29 = (bf16[96,1024]{1,0:T(8,128)(2,1)S(1)}, bf16[96,1024]{1,0:T(8,128)(2,1)S(1)}, u32[]{:S(2)}, u32[]{:S(2)}) collective-permute-start(bf16[96,1024]{1,0:T(8,128)(2,1)S(1)} %slice_bitcast_fusion.2), channel_id=1, source_target_pairs={{0,2},{1,9},{2,4},{3,11},{4,6},{5,13},{6,0},{7,15},{8,10},{9,17},{... | collective-permute-start | bytes 589832 | tf_op jit(solution)/shard_map/ppermute | solution.py:368
  123.0 3.1 %collective-permute-start.35 = (bf16[48,1024]{1,0:T(8,128)(2,1)S(1)}, bf16[48,1024]{1,0:T(8,128)(2,1)S(1)}, u32[]{:S(2)}, u32[]{:S(2)}) collective-permute-start(bf16[48,1024]{1,0:T(8,128)(2,1)S(1)} %get-tuple-element.59), channel_id=1, source_target_pairs={{0,0},{1,65},{2,2},{3,67},{4,4},{5,69},{6,6},{7,71},{8,8},{9,73},{... | collective-permute-start | bytes 294920 | tf_op jit(solution)/shard_map/ppermute | solution.py:368
  123.7 4.7 %collective-permute-start.36 = (bf16[48,1024]{1,0:T(8,128)(2,1)S(1)}, bf16[48,1024]{1,0:T(8,128)(2,1)S(1)}, u32[]{:S(2)}, u32[]{:S(2)}) collective-permute-start(bf16[48,1024]{1,0:T(8,128)(2,1)S(1)} %get-tuple-element.60), channel_id=1, source_target_pairs={{0,96},{1,33},{2,98},{3,35},{4,100},{5,37},{6,102},{7,39},{8,104},... | collective-permute-start | bytes 294920 | tf_op jit(solution)/shard_map/ppermute | solution.py:368
  128.4 1.7 %collective-permute-start.37 = (bf16[2,48,640]{2,1,0:T(8,128)(2,1)S(1)}, bf16[2,48,640]{2,1,0:T(8,128)(2,1)S(1)}, u32[]{:S(2)}, u32[]{:S(2)}) collective-permute-start(bf16[2,48,640]{2,1,0:T(8,128)(2,1)S(1)} %pad_maximum_fusion.3), channel_id=1, source_target_pairs={{0,1},{1,0},{2,3},{3,2},{4,5},{5,4},{6,7},{7,6},{8,9},{9,8},{10,11... | collective-permute-start | bytes 368648 | tf_op jit(solution)/shard_map/ppermute | solution.py:356

commit v4 on v3

--- a/solution.py
+++ b/solution.py
@@ -528,13 +528,18 @@
     rows1, rows3 = across(rows, 1), across(rows, 3)
     rows2 = jnp.concatenate([across(rows1[0:CAP], 1), across(rows3[CAP : 2 * CAP], 3)], axis=0)
     stat = coded(summed(*[part[:, 1024:1152] for part in (rows, rows1, rows2, rows3)]))
-    upper = jnp.stack([rows[:, 0:1024], rows1[:, 0:1024]])
-    lower = jnp.stack([rows2[:, 0:1024], rows3[:, 0:1024]])
-    upper1, lower3 = along(upper, 1), along(lower, 3)
-    lower1, upper3 = along(lower, 1), along(upper, 3)
-    upper2, lower2 = along(upper1, 1), along(lower3, 3)
+    early = jnp.stack([part[:, 0:1024] for part in (rows, rows1, rows3)])
+    late = rows2[None, :, 0:1024]
+    early1, early3 = along(early, 1), along(early, 3)
+    late1, late3 = along(late, 1), along(late, 3)
+    early2 = along(early1[0:2], 1), along(early3[2:3], 3)
+    late2 = along(late3, 3)
     mine = jnp.concatenate(
-        [upper, lower, upper1, lower1, upper2, lower2, upper3, lower3], axis=0
+        [
+            early[0:2], late, early[2:3], early1[0:2], late1, early1[2:3],
+            early2[0], late2, early2[1], early3[0:2], late3, early3[2:3],
+        ],
+        axis=0,
     )
     theirs = move(mine, "core", 1)
     gate, up, down = gate_weight[0], up_weight[0], down_weight[0]

time: 134 us -> 130 us (0.970)
  starting transfers between devices: 52.5 us -> 44.6 us
  waiting for transfers between devices: 50.3 us -> 54.8 us
    ppermute x15, waiting for transfers between devices: 10.4 us -> 15.8 us  [move(): lax.ppermute(value, axis, [(i, (i + shift) % size) for i in range(size)])]
    ppermute x23 -> x24, starting transfers between devices: 39.4 us -> 34.9 us  [by_core(): return lax.ppermute(value, AXES, pairs)]
    ppermute x15, starting transfers between devices: 13.1 us -> 9.73 us  [move(): lax.ppermute(value, axis, [(i, (i + shift) % size) for i in range(size)])]
    ppermute x23 -> x24, waiting for transfers between devices: 39.9 us -> 38.9 us  [by_core(): return lax.ppermute(value, AXES, pairs)]
  transfers between devices with their start and end apart: 38 -> 39, of which waited for: 22 -> 24; matrix products, arithmetic and copies ran while one was open for 2% -> 2% of each run, Pallas kernels for 7% -> 7%
where the time goes in v4:
time: 130 us; the launch traced here: 129 us
  waiting for transfers between devices  54.8 us (42%)
  starting transfers between devices  44.6 us (34%)
  Pallas kernels  24.3 us (19%)
  other arithmetic  2.88 us (2%)
  between operations  1.43 us (1%)
    ppermute x24, waiting for transfers between devices, by_core(): return lax.ppermute(value, AXES, pairs)  38.9 us
    ppermute x24, starting transfers between devices, by_core(): return lax.ppermute(value, AXES, pairs)  34.9 us
    ppermute x15, waiting for transfers between devices, move(): lax.ppermute(value, axis, [(i, (i + shift) % size) for i in range(size)])  15.8 us
    ppermute x15, starting transfers between devices, move(): lax.ppermute(value, axis, [(i, (i + shift) % size) for i in range(size)])  9.73 us
    pallas_call x1, Pallas kernels, per_device(): call(scan_kernel, [shape((SEQ, NS, 1024), F32), shape((4, ROWS, 512), BF)...  5.81 us
    pallas_call x1, Pallas kernels, per_device(): call(ffn_own, [block] * 4, [SMEM] + [VMEM] * 5, 30, [pltpu.VMEM((384, 384...  5.66 us
    pallas_call x1, Pallas kernels, per_device(): call(ffn_other, [shape((384, 384), BF), block], [SMEM] + [VMEM] * 6, 28,...  4.43 us
  transfers between devices with their start and end apart: 39, of which 24 were waited for; matrix products, arithmetic and copies ran while one was open for 2% of the time, Pallas kernels for 7%

profile of v4, /device:TPU:0, one launch (start us, length us, event | category | flops | bytes accessed | tf_op | source)
XLA Modules:
  0.0 128.7 jit_solution(13025235663271551544)
XLA Ops:
  0.7 2.2 %conv.1 = (bf16[64,1024]{1,0:T(8,128)(2,1)S(1)}, bf16[80,640]{1,0:T(8,128)(2,1)S(1)}) custom-call(s32[1,4]{1,0:T(1,128)} %span_ref.3, s32[1,4]{1,0:T(1,128)} %res_ref.3, s32[1,20]{1,0:T(1,128)} %slot_ref.3, bf16[64,1024]{1,0:T(8,128)(2,1)} %x_ref.1, bf16[3,20,1024]{2,1,0:T(8,128)(2,1)} %bitcast.70, f32[4,1024]{1,0:T(4,128)} %w_hbm.1, f32[1,1024]{1,0:T(1,128)} %bitcast.82, ...), custom_call_target="tpu_custom_call" | custom-call | flops 1000000000 | bytes 2000000 | tf_op jit(solution)/shard_map/conv/pallas_call | solution.py:432
  3.0 1.3 %collective-permute-done = bf16[80,640]{1,0:T(8,128)(2,1)S(1)} collective-permute-done((bf16[80,640]{1,0:T(8,128)(2,1)S(1)}, bf16[80,640]{1,0:T(8,128)(2,1)S(1)}, u32[]{:S(2)}, u32[]{:S(2)}) %collective-permute-start) | collective-permute-done | bytes 102432 | tf_op jit(solution)/shard_map/ppermute | solution.py:356
  4.4 2.9 %collective-permute-start.3 = (bf16[80,640]{1,0:T(8,128)(2,1)S(1)}, bf16[80,640]{1,0:T(8,128)(2,1)S(1)}, u32[]{:S(2)}, u32[]{:S(2)}) collective-permute-start(bf16[80,640]{1,0:T(8,128)(2,1)S(1)} %add_convert_fusion.9.q0_ref), channel_id=1, source_target_pairs={{0,6},{2,0},{4,2},{6,4},{1,7},{3,1},{5,3},{7,5},{8,14},{10,8},{12,... | collective-permute-start | bytes 307208 | tf_op jit(solution)/shard_map/ppermute | solution.py:356
  7.3 0.8 collective-permute-start.2
  8.1 0.9 collective-permute-start.1
  9.0 2.9 %collective-permute-done.3.q3_ref = bf16[80,640]{1,0:T(8,128)(2,1)S(1)} collective-permute-done((bf16[80,640]{1,0:T(8,128)(2,1)S(1)}, bf16[80,640]{1,0:T(8,128)(2,1)S(1)}, u32[]{:S(2)}, u32[]{:S(2)}) %collective-permute-start.3) | collective-permute-done | bytes 102432 | tf_op jit(solution)/shard_map/ppermute | solution.py:356
  11.9 2.6 %collective-permute-done.2.q2_ref = bf16[80,640]{1,0:T(8,128)(2,1)S(1)} collective-permute-done((bf16[80,640]{1,0:T(8,128)(2,1)S(1)}, bf16[80,640]{1,0:T(8,128)(2,1)S(1)}, u32[]{:S(2)}, u32[]{:S(2)}) %collective-permute-start.2) | collective-permute-done | bytes 102432 | tf_op jit(solution)/shard_map/ppermute | solution.py:356
  14.5 1.1 collective-permute-done.1.q1_ref
  15.8 5.8 %scan.1 = (f32[20,16,1024]{2,1,0:T(8,128)}, bf16[4,64,512]{2,1,0:T(8,128)(2,1)S(1)}, bf16[4,64,512]{2,1,0:T(8,128)(2,1)S(1)}, f32[4,1,1024]{2,1,0:T(1,128)S(1)}) custom-call(s32[3]{0:T(128)S(1)} %pad_add_fusion.here_ref, s32[1,4]{1,0:T(1,128)S(1)} %copy-done.10, s32[1,4]{1,0:T(1,128)S(1)} %copy-done.11, s32[1,20]{1,0:T(1,128)S(1)} %copy-done.12, ...), custom_call_target="tpu_custom_call" | custom-call | flops 1000000000 | bytes 10000000 | tf_op jit(solution)/shard_map/scan/pallas_call | solution.py:474
  21.7 1.5 %collective-permute-done.4 = bf16[4,64,512]{2,1,0:T(8,128)(2,1)S(1)} collective-permute-done((bf16[4,64,512]{2,1,0:T(8,128)(2,1)S(1)}, bf16[4,64,512]{2,1,0:T(8,128)(2,1)S(1)}, u32[]{:S(2)}, u32[]{:S(2)}) %collective-permute-start.4) | collective-permute-done | bytes 262176 | tf_op jit(solution)/shard_map/ppermute | solution.py:356
  23.3 0.6 collective-permute-start.7
  23.9 0.8 collective-permute-start.6
  24.7 0.9 collective-permute-start.5
  25.6 2.6 %collective-permute-done.7.q3_ref = bf16[64,512]{1,0:T(8,128)(2,1)S(1)} collective-permute-done((bf16[64,512]{1,0:T(8,128)(2,1)S(1)}, bf16[64,512]{1,0:T(8,128)(2,1)S(1)}, u32[]{:S(2)}, u32[]{:S(2)}) %collective-permute-start.7) | collective-permute-done | bytes 65568 | tf_op jit(solution)/shard_map/ppermute | solution.py:356
  28.2 1.6 %collective-permute-done.6.q2_ref = bf16[64,512]{1,0:T(8,128)(2,1)S(1)} collective-permute-done((bf16[64,512]{1,0:T(8,128)(2,1)S(1)}, bf16[64,512]{1,0:T(8,128)(2,1)S(1)}, u32[]{:S(2)}, u32[]{:S(2)}) %collective-permute-start.6) | collective-permute-done | bytes 65568 | tf_op jit(solution)/shard_map/ppermute | solution.py:356
  29.8 0.9 collective-permute-done.5.q1_ref
  30.7 0.9 pick.1
  31.7 1.3 %collective-permute-done.8 = bf16[2,48,640]{2,1,0:T(8,128)(2,1)S(1)} collective-permute-done((bf16[2,48,640]{2,1,0:T(8,128)(2,1)S(1)}, bf16[2,48,640]{2,1,0:T(8,128)(2,1)S(1)}, u32[]{:S(2)}, u32[]{:S(2)}) %collective-permute-start.8) | collective-permute-done | bytes 122912 | tf_op jit(solution)/shard_map/ppermute | solution.py:356
  33.2 2.0 %collective-permute-start.10 = (bf16[48,1024]{1,0:T(8,128)(2,1)S(1)}, bf16[48,1024]{1,0:T(8,128)(2,1)S(1)}, u32[]{:S(2)}, u32[]{:S(2)}) collective-permute-start(bf16[48,1024]{1,0:T(8,128)(2,1)S(1)} %get-tuple-element.63), channel_id=1, source_target_pairs={{0,32},{1,97},{2,34},{3,99},{4,36},{5,101},{6,38},{7,103},{8,40},{... | collective-permute-start | bytes 294920 | tf_op jit(solution)/shard_map/ppermute | solution.py:368
  35.1 0.7 collective-permute-start.9
  35.9 3.9 %collective-permute-done.10 = bf16[48,1024]{1,0:T(8,128)(2,1)S(1)} collective-permute-done((bf16[48,1024]{1,0:T(8,128)(2,1)S(1)}, bf16[48,1024]{1,0:T(8,128)(2,1)S(1)}, u32[]{:S(2)}, u32[]{:S(2)}) %collective-permute-start.10) | collective-permute-done | bytes 98336 | tf_op jit(solution)/shard_map/ppermute | solution.py:368
  39.9 1.7 %collective-permute-start.13 = (bf16[96,1152]{1,0:T(8,128)(2,1)S(1)}, bf16[96,1152]{1,0:T(8,128)(2,1)S(1)}, u32[]{:S(2)}, u32[]{:S(2)}) collective-permute-start(bf16[96,1152]{1,0:T(8,128)(2,1)S(1)} %pad_maximum_fusion.1), channel_id=1, source_target_pairs={{0,6},{1,25},{2,0},{3,27},{4,2},{5,29},{6,4},{7,31},{8,14},{9,1},{... | collective-permute-start | bytes 663560 | tf_op jit(solution)/shard_map/ppermute | solution.py:368
  41.6 0.4 collective-permute-start.11
  42.0 3.9 %collective-permute-done.13 = bf16[96,1152]{1,0:T(8,128)(2,1)S(1)} collective-permute-done((bf16[96,1152]{1,0:T(8,128)(2,1)S(1)}, bf16[96,1152]{1,0:T(8,128)(2,1)S(1)}, u32[]{:S(2)}, u32[]{:S(2)}) %collective-permute-start.13) | collective-permute-done | bytes 221216 | tf_op jit(solution)/shard_map/ppermute | solution.py:368
  45.9 2.8 %collective-permute-done.11 = bf16[96,1152]{1,0:T(8,128)(2,1)S(1)} collective-permute-done((bf16[96,1152]{1,0:T(8,128)(2,1)S(1)}, bf16[96,1152]{1,0:T(8,128)(2,1)S(1)}, u32[]{:S(2)}, u32[]{:S(2)}) %collective-permute-start.11) | collective-permute-done | bytes 221216 | tf_op jit(solution)/shard_map/ppermute | solution.py:368
  48.9 3.1 %collective-permute-start.20 = (bf16[3,96,1024]{2,1,0:T(8,128)(2,1)S(1)}, bf16[3,96,1024]{2,1,0:T(8,128)(2,1)S(1)}, u32[]{:S(2)}, u32[]{:S(2)}) collective-permute-start(bf16[3,96,1024]{2,1,0:T(8,128)(2,1)S(1)} %pad_maximum_fusion), channel_id=1, source_target_pairs={{0,24},{1,7},{2,26},{3,1},{4,28},{5,3},{6,30},{7,5},{8,0},{9,15},{... | collective-permute-start | bytes 1769480 | tf_op jit(solution)/shard_map/ppermute | solution.py:368
  52.1 2.1 %collective-permute-start.12 = (bf16[48,1152]{1,0:T(8,128)(2,1)S(1)}, bf16[48,1152]{1,0:T(8,128)(2,1)S(1)}, u32[]{:S(2)}, u32[]{:S(2)}) collective-permute-start(bf16[48,1152]{1,0:T(8,128)(2,1)S(1)} %slice.191), channel_id=1, source_target_pairs={{0,2},{1,9},{2,4},{3,11},{4,6},{5,13},{6,0},{7,15},{8,10},{9,17},{... | collective-permute-start | bytes 331784 | tf_op jit(solution)/shard_map/ppermute | solution.py:368
  54.1 4.0 %collective-permute-done.12 = bf16[48,1152]{1,0:T(8,128)(2,1)S(1)} collective-permute-done((bf16[48,1152]{1,0:T(8,128)(2,1)S(1)}, bf16[48,1152]{1,0:T(8,128)(2,1)S(1)}, u32[]{:S(2)}, u32[]{:S(2)}) %collective-permute-start.12) | collective-permute-done | bytes 110624 | tf_op jit(solution)/shard_map/ppermute | solution.py:368
  58.2 4.6 %collective-permute-start.18 = (bf16[1,96,1024]{2,1,0:T(8,128)(2,1)S(1)}, bf16[1,96,1024]{2,1,0:T(8,128)(2,1)S(1)}, u32[]{:S(2)}, u32[]{:S(2)}) collective-permute-start(bf16[1,96,1024]{2,1,0:T(8,128)(2,1)S(1)} %slice_bitcast_fusion.5), channel_id=1, source_target_pairs={{0,24},{1,7},{2,26},{3,1},{4,28},{5,3},{6,30},{7,5},{8,0},{9,15},{... | collective-permute-start | bytes 589832 | tf_op jit(solution)/shard_map/ppermute | solution.py:368
  62.8 1.4 %collective-permute-done.15 = bf16[3,96,1024]{2,1,0:T(8,128)(2,1)S(1)} collective-permute-done((bf16[3,96,1024]{2,1,0:T(8,128)(2,1)S(1)}, bf16[3,96,1024]{2,1,0:T(8,128)(2,1)S(1)}, u32[]{:S(2)}, u32[]{:S(2)}) %collective-permute-start.15) | collective-permute-done | bytes 589856 | tf_op jit(solution)/shard_map/ppermute | solution.py:368
  64.4 1.6 %collective-permute-done.18 = bf16[1,96,1024]{2,1,0:T(8,128)(2,1)S(1)} collective-permute-done((bf16[1,96,1024]{2,1,0:T(8,128)(2,1)S(1)}, bf16[1,96,1024]{2,1,0:T(8,128)(2,1)S(1)}, u32[]{:S(2)}, u32[]{:S(2)}) %collective-permute-start.18) | collective-permute-done | bytes 196640 | tf_op jit(solution)/shard_map/ppermute | solution.py:368
  65.9 3.7 %collective-permute-start.19 = (bf16[1,96,1024]{2,1,0:T(8,128)(2,1)S(1)}, bf16[1,96,1024]{2,1,0:T(8,128)(2,1)S(1)}, u32[]{:S(2)}, u32[]{:S(2)}) collective-permute-start(bf16[1,96,1024]{2,1,0:T(8,128)(2,1)S(1)} %collective-permute-done.18), channel_id=1, source_target_pairs={{0,24},{1,7},{2,26},{3,1},{4,28},{5,3},{6,30},{7,5},{8,0},{9,15},{... | collective-permute-start | bytes 589832 | tf_op jit(solution)/shard_map/ppermute | solution.py:368
  69.6 0.3 collective-permute-start.21
  70.0 3.9 %collective-permute-done.17 = bf16[2,96,1024]{2,1,0:T(8,128)(2,1)S(1)} collective-permute-done((bf16[2,96,1024]{2,1,0:T(8,128)(2,1)S(1)}, bf16[2,96,1024]{2,1,0:T(8,128)(2,1)S(1)}, u32[]{:S(2)}, u32[]{:S(2)}) %collective-permute-start.17) | collective-permute-done | bytes 393248 | tf_op jit(solution)/shard_map/ppermute | solution.py:368
  73.9 1.7 %collective-permute-done.21 = bf16[1,96,1024]{2,1,0:T(8,128)(2,1)S(1)} collective-permute-done((bf16[1,96,1024]{2,1,0:T(8,128)(2,1)S(1)}, bf16[1,96,1024]{2,1,0:T(8,128)(2,1)S(1)}, u32[]{:S(2)}, u32[]{:S(2)}) %collective-permute-start.21) | collective-permute-done | bytes 196640 | tf_op jit(solution)/shard_map/ppermute | solution.py:368
  75.8 5.7 %experts_own.1 = (bf16[4,96,1024]{2,1,0:T(8,128)(2,1)S(1)}, bf16[4,96,1024]{2,1,0:T(8,128)(2,1)S(1)}, bf16[4,96,1024]{2,1,0:T(8,128)(2,1)S(1)}, bf16[4,96,1024]{2,1,0:T(8,128)(2,1)S(1)}) custom-call(s32[3]{0:T(128)S(1)} %pad_add_fusion.here_ref, bf16[16,96,1024]{2,1,0:T(8,128)(2,1)S(1)} %constant_dynamic-update-slice_fusion.4.x_ref, ...), custom_call_target="tpu_custom_call" | custom-call | flops 3623878656 | bytes 12000000 | tf_op jit(solution)/shard_map/experts_own/pallas_call | solution.py:548
  81.5 4.4 %experts_other.1 = (bf16[384,384]{1,0:T(8,128)(2,1)S(1)}, bf16[4,96,1024]{2,1,0:T(8,128)(2,1)S(1)}) custom-call(s32[3]{0:T(128)S(1)} %pad_add_fusion.here_ref, bf16[16,96,1024]{2,1,0:T(8,128)(2,1)S(1)} %collective-permute-done.22.x_ref, f32[4,1,1024]{2,1,0:T(1,128)S(1)} %get-tuple-element.28.inv_ref, bf16[4096,384]{1,0:T(8,128)(2,1)S(1)} %bitcast.64, ...), custom_call_target="tpu_custom_call" | custom-call | flops 3019898880 | bytes 10000000 | tf_op jit(solution)/shard_map/experts_other/pallas_call | solution.py:558
  85.9 0.7 collective-permute-start.25
  86.6 1.9 %experts_rest.1 = (bf16[4,96,1024]{2,1,0:T(8,128)(2,1)S(1)}, bf16[4,96,1024]{2,1,0:T(8,128)(2,1)S(1)}, bf16[4,96,1024]{2,1,0:T(8,128)(2,1)S(1)}) custom-call(s32[3]{0:T(128)S(1)} %pad_add_fusion.here_ref, bf16[384,384]{1,0:T(8,128)(2,1)S(1)} %get-tuple-element.30.act_ref, bf16[384,4096]{1,0:T(8,128)(2,1)S(1)} %bitcast.62), custom_call_target="tpu_custom_call" | custom-call | flops 905969664 | bytes 5000000 | tf_op jit(solution)/shard_map/experts_rest/pallas_call | solution.py:567
  88.7 0.5 collective-permute-start.23
  89.2 0.3 collective-permute-start.28
  89.5 0.3 add_convert_fusion.1
  89.9 3.2 %collective-permute-start.32 = (bf16[2,96,1024]{2,1,0:T(8,128)(2,1)S(1)}, bf16[2,96,1024]{2,1,0:T(8,128)(2,1)S(1)}, u32[]{:S(2)}, u32[]{:S(2)}) collective-permute-start(bf16[2,96,1024]{2,1,0:T(8,128)(2,1)S(1)} %get-tuple-element.48), channel_id=1, source_target_pairs={{0,24},{1,7},{2,26},{3,1},{4,28},{5,3},{6,30},{7,5},{8,0},{9,15},{... | collective-permute-start | bytes 1179656 | tf_op jit(solution)/shard_map/ppermute | solution.py:368
  93.2 0.3 add_convert_fusion.2
  93.6 0.3 add_convert_fusion
  94.0 3.3 %collective-permute-start.29 = (bf16[2,96,1024]{2,1,0:T(8,128)(2,1)S(1)}, bf16[2,96,1024]{2,1,0:T(8,128)(2,1)S(1)}, u32[]{:S(2)}, u32[]{:S(2)}) collective-permute-start(bf16[2,96,1024]{2,1,0:T(8,128)(2,1)S(1)} %slice.202), channel_id=1, source_target_pairs={{0,24},{1,7},{2,26},{3,1},{4,28},{5,3},{6,30},{7,5},{8,0},{9,15},{... | collective-permute-start | bytes 1179656 | tf_op jit(solution)/shard_map/ppermute | solution.py:368
  97.3 1.7 %collective-permute-done.26 = bf16[2,96,1024]{2,1,0:T(8,128)(2,1)S(1)} collective-permute-done((bf16[2,96,1024]{2,1,0:T(8,128)(2,1)S(1)}, bf16[2,96,1024]{2,1,0:T(8,128)(2,1)S(1)}, u32[]{:S(2)}, u32[]{:S(2)}) %collective-permute-start.26) | collective-permute-done | bytes 393248 | tf_op jit(solution)/shard_map/ppermute | solution.py:368
  99.3 3.3 %collective-permute-start.33 = (bf16[2,96,1024]{2,1,0:T(8,128)(2,1)S(1)}, bf16[2,96,1024]{2,1,0:T(8,128)(2,1)S(1)}, u32[]{:S(2)}, u32[]{:S(2)}) collective-permute-start(bf16[2,96,1024]{2,1,0:T(8,128)(2,1)S(1)} %add_convert_fusion.5), channel_id=1, source_target_pairs={{0,24},{1,7},{2,26},{3,1},{4,28},{5,3},{6,30},{7,5},{8,0},{9,15},{... | collective-permute-start | bytes 1179656 | tf_op jit(solution)/shard_map/ppermute | solution.py:368
  102.6 0.3 add_convert_fusion.3
  103.0 0.2 collective-permute-done.31
  103.1 5.0 %collective-permute-done.27 = bf16[2,96,1024]{2,1,0:T(8,128)(2,1)S(1)} collective-permute-done((bf16[2,96,1024]{2,1,0:T(8,128)(2,1)S(1)}, bf16[2,96,1024]{2,1,0:T(8,128)(2,1)S(1)}, u32[]{:S(2)}, u32[]{:S(2)}) %collective-permute-start.27) | collective-permute-done | bytes 393248 | tf_op jit(solution)/shard_map/ppermute | solution.py:368
  108.1 0.4 add_convert_fusion.6
  108.6 0.8 collective-permute-start.30
  109.4 2.6 %collective-permute-start.34 = (bf16[96,1024]{1,0:T(8,128)(2,1)S(1)}, bf16[96,1024]{1,0:T(8,128)(2,1)S(1)}, u32[]{:S(2)}, u32[]{:S(2)}) collective-permute-start(bf16[96,1024]{1,0:T(8,128)(2,1)S(1)} %get-tuple-element.51), channel_id=1, source_target_pairs={{0,4},{1,17},{2,6},{3,19},{4,0},{5,21},{6,2},{7,23},{8,12},{9,25},... | collective-permute-start | bytes 589832 | tf_op jit(solution)/shard_map/ppermute | solution.py:368
  112.0 0.2 collective-permute-start.35
  112.3 3.3 %collective-permute-done.30 = bf16[96,1024]{1,0:T(8,128)(2,1)S(1)} collective-permute-done((bf16[96,1024]{1,0:T(8,128)(2,1)S(1)}, bf16[96,1024]{1,0:T(8,128)(2,1)S(1)}, u32[]{:S(2)}, u32[]{:S(2)}) %collective-permute-start.30) | collective-permute-done | bytes 196640 | tf_op jit(solution)/shard_map/ppermute | solution.py:368
  115.6 2.2 %collective-permute-done.34 = bf16[96,1024]{1,0:T(8,128)(2,1)S(1)} collective-permute-done((bf16[96,1024]{1,0:T(8,128)(2,1)S(1)}, bf16[96,1024]{1,0:T(8,128)(2,1)S(1)}, u32[]{:S(2)}, u32[]{:S(2)}) %collective-permute-start.34) | collective-permute-done | bytes 196640 | tf_op jit(solution)/shard_map/ppermute | solution.py:368
  117.8 0.8 collective-permute-done.35
  118.7 0.7 collective-permute-start.36
  119.4 2.1 %collective-permute-start.37 = (bf16[48,1024]{1,0:T(8,128)(2,1)S(1)}, bf16[48,1024]{1,0:T(8,128)(2,1)S(1)}, u32[]{:S(2)}, u32[]{:S(2)}) collective-permute-start(bf16[48,1024]{1,0:T(8,128)(2,1)S(1)} %get-tuple-element.62), channel_id=1, source_target_pairs={{0,96},{1,33},{2,98},{3,35},{4,100},{5,37},{6,102},{7,39},{8,104},... | collective-permute-start | bytes 294920 | tf_op jit(solution)/shard_map/ppermute | solution.py:368
  121.6 2.7 %collective-permute-done.37 = bf16[48,1024]{1,0:T(8,128)(2,1)S(1)} collective-permute-done((bf16[48,1024]{1,0:T(8,128)(2,1)S(1)}, bf16[48,1024]{1,0:T(8,128)(2,1)S(1)}, u32[]{:S(2)}, u32[]{:S(2)}) %collective-permute-start.37) | collective-permute-done | bytes 98336 | tf_op jit(solution)/shard_map/ppermute | solution.py:368
  124.3 0.9 collective-permute-start.38
  125.2 1.6 %tail.1 = bf16[3,20,1024]{2,1,0:T(8,128)(2,1)} custom-call(s32[1,4]{1,0:T(1,128)S(1)} %copy-done.10, s32[1,4]{1,0:T(1,128)S(1)} %copy-done.11, s32[1,20]{1,0:T(1,128)S(1)} %copy-done.12, bf16[64,1024]{1,0:T(8,128)(2,1)S(1)} %copy-done.14, bf16[3,20,1024]{2,1,0:T(8,128)(2,1)S(1)} %bitcast.71), custom_call_target="tpu_custom_call" | custom-call | flops 1000000000 | bytes 1000000 | tf_op jit(solution)/shard_map/tail/pallas_call | solution.py:463
  126.9 1.8 %combine.1 = bf16[64,512]{1,0:T(8,128)(2,1)} custom-call(s32[3]{0:T(128)S(1)} %pad_add_fusion.here_ref, bf16[2,48,512]{2,1,0:T(8,128)(2,1)S(1)} %get-tuple-element.60.mine_ref, bf16[2,48,512]{2,1,0:T(8,128)(2,1)S(1)} %slice.220.theirs_ref, bf16[96,128]{1,0:T(8,128)(2,1)S(1)} %bitcast_select_fusion.stat_ref, f32[64,512]{1,0:T(8,128)S(1)} %get-tuple-element.38.hid_ref, ...), custom_call_target="tpu_custom_call" | custom-call | flops 100000000 | bytes 1000000 | tf_op jit(solution)/shard_map/combine/pallas_call | solution.py:596
  (116 shorter events, 2.8 us)
Async XLA Ops:
  0.6 15.0 %copy-start.12 = (s32[1,20]{1,0:T(1,128)S(1)}, s32[1,20]{1,0:T(1,128)}, u32[]{:S(2)}) copy-start(s32[1,20]{1,0:T(1,128)} %slot_ref.3) | copy-start | bytes 244
  0.6 15.0 %copy-start.11 = (s32[1,4]{1,0:T(1,128)S(1)}, s32[1,4]{1,0:T(1,128)}, u32[]{:S(2)}) copy-start(s32[1,4]{1,0:T(1,128)} %res_ref.3) | copy-start | bytes 52
  0.7 15.0 %copy-start.10 = (s32[1,4]{1,0:T(1,128)S(1)}, s32[1,4]{1,0:T(1,128)}, u32[]{:S(2)}) copy-start(s32[1,4]{1,0:T(1,128)} %span_ref.3) | copy-start | bytes 52
  0.7 15.0 %copy-start.8 = (f32[1024]{0:T(1024)S(1)}, f32[1024]{0:T(1024)}, u32[]{:S(2)}) copy-start(f32[1024]{0:T(1024)} %param.39) | copy-start | bytes 12292
  0.7 15.0 %copy-start.6 = (f32[16,1024]{1,0:T(8,128)S(1)}, f32[16,1024]{1,0:T(8,128)}, u32[]{:S(2)}) copy-start(f32[16,1024]{1,0:T(8,128)} %dl_ref.1) | copy-start | bytes 196612
  0.7 15.0 %copy-start.7 = (f32[1024]{0:T(1024)S(1)}, f32[1024]{0:T(1024)}, u32[]{:S(2)}) copy-start(f32[1024]{0:T(1024)} %param.37) | copy-start | bytes 12292
  0.7 15.0 %copy-start.4 = (bf16[512,1024]{1,0:T(8,128)(2,1)S(1)}, bf16[512,1024]{1,0:T(8,128)(2,1)}, u32[]{:S(2)}) copy-start(bf16[512,1024]{1,0:T(8,128)(2,1)} %sw_ref.1) | copy-start | bytes 3145732
  0.7 15.0 %copy-start.9 = (f32[512]{0:T(512)S(1)}, f32[512]{0:T(512)}, u32[]{:S(2)}) copy-start(f32[512]{0:T(512)} %param.35) | copy-start | bytes 6148
  0.7 15.0 %copy-start.3 = (f32[20,16,1024]{2,1,0:T(8,128)S(1)}, f32[20,16,1024]{2,1,0:T(8,128)}, u32[]{:S(2)}) copy-start(f32[20,16,1024]{2,1,0:T(8,128)} %sc_ref.1) | copy-start | bytes 3932164
  0.7 15.0 %copy-start.5 = (bf16[64,1024]{1,0:T(8,128)(2,1)S(1)}, bf16[64,1024]{1,0:T(8,128)(2,1)}, u32[]{:S(2)}) copy-start(bf16[64,1024]{1,0:T(8,128)(2,1)} %z_ref.1) | copy-start | bytes 393220
  2.9 1.4 %collective-permute-start = (bf16[80,640]{1,0:T(8,128)(2,1)S(1)}, bf16[80,640]{1,0:T(8,128)(2,1)S(1)}, u32[]{:S(2)}, u32[]{:S(2)}) collective-permute-start(bf16[80,640]{1,0:T(8,128)(2,1)S(1)} %get-tuple-element.22), channel_id=1, source_target_pairs={{0,1},{1,0},{2,3},{3,2},{4,5},{5,4},{6,7},{7,6},{8,9},{9,8},{10,11... | collective-permute-start | bytes 307208 | tf_op jit(solution)/shard_map/ppermute | solution.py:356
  4.4 7.6 %collective-permute-start.3 = (bf16[80,640]{1,0:T(8,128)(2,1)S(1)}, bf16[80,640]{1,0:T(8,128)(2,1)S(1)}, u32[]{:S(2)}, u32[]{:S(2)}) collective-permute-start(bf16[80,640]{1,0:T(8,128)(2,1)S(1)} %add_convert_fusion.9.q0_ref), channel_id=1, source_target_pairs={{0,6},{2,0},{4,2},{6,4},{1,7},{3,1},{5,3},{7,5},{8,14},{10,8},{12,... | collective-permute-start | bytes 307208 | tf_op jit(solution)/shard_map/ppermute | solution.py:356
  7.3 7.3 %collective-permute-start.2 = (bf16[80,640]{1,0:T(8,128)(2,1)S(1)}, bf16[80,640]{1,0:T(8,128)(2,1)S(1)}, u32[]{:S(2)}, u32[]{:S(2)}) collective-permute-start(bf16[80,640]{1,0:T(8,128)(2,1)S(1)} %add_convert_fusion.9.q0_ref), channel_id=1, source_target_pairs={{0,4},{2,6},{4,0},{6,2},{1,5},{3,7},{5,1},{7,3},{8,12},{10,14},{12... | collective-permute-start | bytes 307208 | tf_op jit(solution)/shard_map/ppermute | solution.py:356
  8.1 7.6 %collective-permute-start.1 = (bf16[80,640]{1,0:T(8,128)(2,1)S(1)}, bf16[80,640]{1,0:T(8,128)(2,1)S(1)}, u32[]{:S(2)}, u32[]{:S(2)}) collective-permute-start(bf16[80,640]{1,0:T(8,128)(2,1)S(1)} %add_convert_fusion.9.q0_ref), channel_id=1, source_target_pairs={{0,2},{2,4},{4,6},{6,0},{1,3},{3,5},{5,7},{7,1},{8,10},{10,12},{12... | collective-permute-start | bytes 307208 | tf_op jit(solution)/shard_map/ppermute | solution.py:356
  15.7 15.0 %copy-start.15 = (bf16[64,512]{1,0:T(8,128)(2,1)S(1)}, bf16[64,512]{1,0:T(8,128)(2,1)}, u32[]{:S(2)}) copy-start(bf16[64,512]{1,0:T(8,128)(2,1)} %resid_ref.1) | copy-start | bytes 196612
  15.7 15.0 %copy-start.16 = (bf16[512,4]{0,1:T(4,128)(2,1)S(1)}, bf16[512,4]{0,1:T(4,128)(2,1)}, u32[]{:S(2)}) copy-start(bf16[512,4]{0,1:T(4,128)(2,1)} %param.43) | copy-start | bytes 12292
  15.7 15.0 %copy-start.17 = (f32[512]{0:T(512)S(1)}, f32[512]{0:T(512)}, u32[]{:S(2)}) copy-start(f32[512]{0:T(512)} %param.42) | copy-start | bytes 6148
  15.8 15.0 %copy-start.18 = (s32[64,2]{0,1:T(2,128)S(1)}, s32[64,2]{0,1:T(2,128)}, u32[]{:S(2)}) copy-start(s32[64,2]{0,1:T(2,128)} %param.44) | copy-start | bytes 1540
  21.6 1.6 %collective-permute-start.4 = (bf16[4,64,512]{2,1,0:T(8,128)(2,1)S(1)}, bf16[4,64,512]{2,1,0:T(8,128)(2,1)S(1)}, u32[]{:S(2)}, u32[]{:S(2)}) collective-permute-start(bf16[4,64,512]{2,1,0:T(8,128)(2,1)S(1)} %get-tuple-element.25), channel_id=1, source_target_pairs={{0,1},{1,0},{2,3},{3,2},{4,5},{5,4},{6,7},{7,6},{8,9},{9,8},{10,11... | collective-permute-start | bytes 786440 | tf_op jit(solution)/shard_map/ppermute | solution.py:356
  23.3 4.9 %collective-permute-start.7 = (bf16[64,512]{1,0:T(8,128)(2,1)S(1)}, bf16[64,512]{1,0:T(8,128)(2,1)S(1)}, u32[]{:S(2)}, u32[]{:S(2)}) collective-permute-start(bf16[64,512]{1,0:T(8,128)(2,1)S(1)} %get-tuple-element.53), channel_id=1, source_target_pairs={{0,6},{2,0},{4,2},{6,4},{1,7},{3,1},{5,3},{7,5},{8,14},{10,8},{12,... | collective-permute-start | bytes 196616 | tf_op jit(solution)/shard_map/ppermute | solution.py:356
  23.9 5.9 %collective-permute-start.6 = (bf16[64,512]{1,0:T(8,128)(2,1)S(1)}, bf16[64,512]{1,0:T(8,128)(2,1)S(1)}, u32[]{:S(2)}, u32[]{:S(2)}) collective-permute-start(bf16[64,512]{1,0:T(8,128)(2,1)S(1)} %get-tuple-element.54), channel_id=1, source_target_pairs={{0,4},{2,6},{4,0},{6,2},{1,5},{3,7},{5,1},{7,3},{8,12},{10,14},{12... | collective-permute-start | bytes 196616 | tf_op jit(solution)/shard_map/ppermute | solution.py:356
  24.7 6.0 %collective-permute-start.5 = (bf16[64,512]{1,0:T(8,128)(2,1)S(1)}, bf16[64,512]{1,0:T(8,128)(2,1)S(1)}, u32[]{:S(2)}, u32[]{:S(2)}) collective-permute-start(bf16[64,512]{1,0:T(8,128)(2,1)S(1)} %get-tuple-element.55), channel_id=1, source_target_pairs={{0,2},{2,4},{4,6},{6,0},{1,3},{3,5},{5,7},{7,1},{8,10},{10,12},{12... | collective-permute-start | bytes 196616 | tf_op jit(solution)/shard_map/ppermute | solution.py:356
  31.6 1.4 %collective-permute-start.8 = (bf16[2,48,640]{2,1,0:T(8,128)(2,1)S(1)}, bf16[2,48,640]{2,1,0:T(8,128)(2,1)S(1)}, u32[]{:S(2)}, u32[]{:S(2)}) collective-permute-start(bf16[2,48,640]{2,1,0:T(8,128)(2,1)S(1)} %get-tuple-element.27), channel_id=1, source_target_pairs={{0,1},{1,0},{2,3},{3,2},{4,5},{5,4},{6,7},{7,6},{8,9},{9,8},{10,11... | collective-permute-start | bytes 368648 | tf_op jit(solution)/shard_map/ppermute | solution.py:356
  33.2 6.7 %collective-permute-start.10 = (bf16[48,1024]{1,0:T(8,128)(2,1)S(1)}, bf16[48,1024]{1,0:T(8,128)(2,1)S(1)}, u32[]{:S(2)}, u32[]{:S(2)}) collective-permute-start(bf16[48,1024]{1,0:T(8,128)(2,1)S(1)} %get-tuple-element.63), channel_id=1, source_target_pairs={{0,32},{1,97},{2,34},{3,99},{4,36},{5,101},{6,38},{7,103},{8,40},{... | collective-permute-start | bytes 294920 | tf_op jit(solution)/shard_map/ppermute | solution.py:368
  35.1 0.7 collective-permute-start.9
  39.9 6.0 %collective-permute-start.13 = (bf16[96,1152]{1,0:T(8,128)(2,1)S(1)}, bf16[96,1152]{1,0:T(8,128)(2,1)S(1)}, u32[]{:S(2)}, u32[]{:S(2)}) collective-permute-start(bf16[96,1152]{1,0:T(8,128)(2,1)S(1)} %pad_maximum_fusion.1), channel_id=1, source_target_pairs={{0,6},{1,25},{2,0},{3,27},{4,2},{5,29},{6,4},{7,31},{8,14},{9,1},{... | collective-permute-start | bytes 663560 | tf_op jit(solution)/shard_map/ppermute | solution.py:368
  41.6 7.1 %collective-permute-start.11 = (bf16[96,1152]{1,0:T(8,128)(2,1)S(1)}, bf16[96,1152]{1,0:T(8,128)(2,1)S(1)}, u32[]{:S(2)}, u32[]{:S(2)}) collective-permute-start(bf16[96,1152]{1,0:T(8,128)(2,1)S(1)} %pad_maximum_fusion.1), channel_id=1, source_target_pairs={{0,2},{1,9},{2,4},{3,11},{4,6},{5,13},{6,0},{7,15},{8,10},{9,17},{... | collective-permute-start | bytes 663560 | tf_op jit(solution)/shard_map/ppermute | solution.py:368
  48.8 27.0 %copy-start.2 = (bf16[1,4096,384]{2,1,0:T(8,128)(2,1)S(1)}, bf16[1,4096,384]{2,1,0:T(8,128)(2,1)}, u32[]{:S(2)}) copy-start(bf16[1,4096,384]{2,1,0:T(8,128)(2,1)} %param.46) | copy-start | bytes 9437188
  48.9 20.8 %collective-permute-start.20 = (bf16[3,96,1024]{2,1,0:T(8,128)(2,1)S(1)}, bf16[3,96,1024]{2,1,0:T(8,128)(2,1)S(1)}, u32[]{:S(2)}, u32[]{:S(2)}) collective-permute-start(bf16[3,96,1024]{2,1,0:T(8,128)(2,1)S(1)} %pad_maximum_fusion), channel_id=1, source_target_pairs={{0,24},{1,7},{2,26},{3,1},{4,28},{5,3},{6,30},{7,5},{8,0},{9,15},{... | collective-permute-start | bytes 1769480 | tf_op jit(solution)/shard_map/ppermute | solution.py:368
  51.9 12.3 %collective-permute-start.15 = (bf16[3,96,1024]{2,1,0:T(8,128)(2,1)S(1)}, bf16[3,96,1024]{2,1,0:T(8,128)(2,1)S(1)}, u32[]{:S(2)}, u32[]{:S(2)}) collective-permute-start(bf16[3,96,1024]{2,1,0:T(8,128)(2,1)S(1)} %pad_maximum_fusion), channel_id=1, source_target_pairs={{0,8},{1,3},{2,10},{3,5},{4,12},{5,7},{6,14},{7,1},{8,16},{9,11},{... | collective-permute-start | bytes 1769480 | tf_op jit(solution)/shard_map/ppermute | solution.py:368
  51.9 6.2 %collective-permute-start.14 = (bf16[48,1152]{1,0:T(8,128)(2,1)S(1)}, bf16[48,1152]{1,0:T(8,128)(2,1)S(1)}, u32[]{:S(2)}, u32[]{:S(2)}) collective-permute-start(bf16[48,1152]{1,0:T(8,128)(2,1)S(1)} %slice.192), channel_id=1, source_target_pairs={{0,6},{1,25},{2,0},{3,27},{4,2},{5,29},{6,4},{7,31},{8,14},{9,1},{... | collective-permute-start | bytes 331784 | tf_op jit(solution)/shard_map/ppermute | solution.py:368
  52.1 6.0 %collective-permute-start.12 = (bf16[48,1152]{1,0:T(8,128)(2,1)S(1)}, bf16[48,1152]{1,0:T(8,128)(2,1)S(1)}, u32[]{:S(2)}, u32[]{:S(2)}) collective-permute-start(bf16[48,1152]{1,0:T(8,128)(2,1)S(1)} %slice.191), channel_id=1, source_target_pairs={{0,2},{1,9},{2,4},{3,11},{4,6},{5,13},{6,0},{7,15},{8,10},{9,17},{... | collective-permute-start | bytes 331784 | tf_op jit(solution)/shard_map/ppermute | solution.py:368
  58.2 17.6 %copy-start = (bf16[1,384,4096]{2,1,0:T(8,128)(2,1)S(1)}, bf16[1,384,4096]{2,1,0:T(8,128)(2,1)}, u32[]{:S(2)}) copy-start(bf16[1,384,4096]{2,1,0:T(8,128)(2,1)} %param.47) | copy-start | bytes 9437188
  58.2 17.6 %copy-start.1 = (bf16[1,4096,384]{2,1,0:T(8,128)(2,1)S(1)}, bf16[1,4096,384]{2,1,0:T(8,128)(2,1)}, u32[]{:S(2)}) copy-start(bf16[1,4096,384]{2,1,0:T(8,128)(2,1)} %param.45) | copy-start | bytes 9437188
  58.2 7.7 %collective-permute-start.18 = (bf16[1,96,1024]{2,1,0:T(8,128)(2,1)S(1)}, bf16[1,96,1024]{2,1,0:T(8,128)(2,1)S(1)}, u32[]{:S(2)}, u32[]{:S(2)}) collective-permute-start(bf16[1,96,1024]{2,1,0:T(8,128)(2,1)S(1)} %slice_bitcast_fusion.5), channel_id=1, source_target_pairs={{0,24},{1,7},{2,26},{3,1},{4,28},{5,3},{6,30},{7,5},{8,0},{9,15},{... | collective-permute-start | bytes 589832 | tf_op jit(solution)/shard_map/ppermute | solution.py:368
  62.7 7.2 %collective-permute-start.16 = (bf16[1,96,1024]{2,1,0:T(8,128)(2,1)S(1)}, bf16[1,96,1024]{2,1,0:T(8,128)(2,1)S(1)}, u32[]{:S(2)}, u32[]{:S(2)}) collective-permute-start(bf16[1,96,1024]{2,1,0:T(8,128)(2,1)S(1)} %slice_bitcast_fusion.5), channel_id=1, source_target_pairs={{0,8},{1,3},{2,10},{3,5},{4,12},{5,7},{6,14},{7,1},{8,16},{9,11},{... | collective-permute-start | bytes 589832 | tf_op jit(solution)/shard_map/ppermute | solution.py:368
  64.3 9.5 %collective-permute-start.17 = (bf16[2,96,1024]{2,1,0:T(8,128)(2,1)S(1)}, bf16[2,96,1024]{2,1,0:T(8,128)(2,1)S(1)}, u32[]{:S(2)}, u32[]{:S(2)}) collective-permute-start(bf16[2,96,1024]{2,1,0:T(8,128)(2,1)S(1)} %get-tuple-element.49), channel_id=1, source_target_pairs={{0,8},{1,3},{2,10},{3,5},{4,12},{5,7},{6,14},{7,1},{8,16},{9,11},{... | collective-permute-start | bytes 1179656 | tf_op jit(solution)/shard_map/ppermute | solution.py:368
  65.9 7.9 %collective-permute-start.19 = (bf16[1,96,1024]{2,1,0:T(8,128)(2,1)S(1)}, bf16[1,96,1024]{2,1,0:T(8,128)(2,1)S(1)}, u32[]{:S(2)}, u32[]{:S(2)}) collective-permute-start(bf16[1,96,1024]{2,1,0:T(8,128)(2,1)S(1)} %collective-permute-done.18), channel_id=1, source_target_pairs={{0,24},{1,7},{2,26},{3,1},{4,28},{5,3},{6,30},{7,5},{8,0},{9,15},{... | collective-permute-start | bytes 589832 | tf_op jit(solution)/shard_map/ppermute | solution.py:368
  69.6 5.9 %collective-permute-start.21 = (bf16[1,96,1024]{2,1,0:T(8,128)(2,1)S(1)}, bf16[1,96,1024]{2,1,0:T(8,128)(2,1)S(1)}, u32[]{:S(2)}, u32[]{:S(2)}) collective-permute-start(bf16[1,96,1024]{2,1,0:T(8,128)(2,1)S(1)} %slice.197), channel_id=1, source_target_pairs={{0,24},{1,7},{2,26},{3,1},{4,28},{5,3},{6,30},{7,5},{8,0},{9,15},{... | collective-permute-start | bytes 589832 | tf_op jit(solution)/shard_map/ppermute | solution.py:368
  75.7 5.8 %collective-permute-start.22 = (bf16[16,96,1024]{2,1,0:T(8,128)(2,1)S(1)}, bf16[16,96,1024]{2,1,0:T(8,128)(2,1)S(1)}, u32[]{:S(2)}, u32[]{:S(2)}) collective-permute-start(bf16[16,96,1024]{2,1,0:T(8,128)(2,1)S(1)} %constant_dynamic-update-slice_fusion.4.x_ref), channel_id=1, source_target_pairs={{0,1},{1,0},{2,3},{3,2},{4,5},{5,4},{6,7},{7,6},{8,9},{9,8},{10,11... | collective-permute-start | bytes 9437192 | tf_op jit(solution)/shard_map/ppermute | solution.py:356
  85.9 3.6 %collective-permute-start.25 = (bf16[4,96,1024]{2,1,0:T(8,128)(2,1)S(1)}, bf16[4,96,1024]{2,1,0:T(8,128)(2,1)S(1)}, u32[]{:S(2)}, u32[]{:S(2)}) collective-permute-start(bf16[4,96,1024]{2,1,0:T(8,128)(2,1)S(1)} %get-tuple-element.35), channel_id=1, source_target_pairs={{0,1},{1,0},{2,3},{3,2},{4,5},{5,4},{6,7},{7,6},{8,9},{9,8},{10,11... | collective-permute-start | bytes 2359304 | tf_op jit(solution)/shard_map/ppermute | solution.py:356
  88.6 4.6 %collective-permute-start.24 = (bf16[4,96,1024]{2,1,0:T(8,128)(2,1)S(1)}, bf16[4,96,1024]{2,1,0:T(8,128)(2,1)S(1)}, u32[]{:S(2)}, u32[]{:S(2)}) collective-permute-start(bf16[4,96,1024]{2,1,0:T(8,128)(2,1)S(1)} %get-tuple-element.33), channel_id=1, source_target_pairs={{0,1},{1,0},{2,3},{3,2},{4,5},{5,4},{6,7},{7,6},{8,9},{9,8},{10,11... | collective-permute-start | bytes 2359304 | tf_op jit(solution)/shard_map/ppermute | solution.py:356
  88.7 13.9 %collective-permute-start.23 = (bf16[4,96,1024]{2,1,0:T(8,128)(2,1)S(1)}, bf16[4,96,1024]{2,1,0:T(8,128)(2,1)S(1)}, u32[]{:S(2)}, u32[]{:S(2)}) collective-permute-start(bf16[4,96,1024]{2,1,0:T(8,128)(2,1)S(1)} %get-tuple-element.31), channel_id=1, source_target_pairs={{0,1},{1,0},{2,3},{3,2},{4,5},{5,4},{6,7},{7,6},{8,9},{9,8},{10,11... | collective-permute-start | bytes 2359304 | tf_op jit(solution)/shard_map/ppermute | solution.py:356
  89.2 4.4 %collective-permute-start.28 = (bf16[4,96,1024]{2,1,0:T(8,128)(2,1)S(1)}, bf16[4,96,1024]{2,1,0:T(8,128)(2,1)S(1)}, u32[]{:S(2)}, u32[]{:S(2)}) collective-permute-start(bf16[4,96,1024]{2,1,0:T(8,128)(2,1)S(1)} %get-tuple-element.37), channel_id=1, source_target_pairs={{0,1},{1,0},{2,3},{3,2},{4,5},{5,4},{6,7},{7,6},{8,9},{9,8},{10,11... | collective-permute-start | bytes 2359304 | tf_op jit(solution)/shard_map/ppermute | solution.py:356
  89.9 9.1 %collective-permute-start.26 = (bf16[2,96,1024]{2,1,0:T(8,128)(2,1)S(1)}, bf16[2,96,1024]{2,1,0:T(8,128)(2,1)S(1)}, u32[]{:S(2)}, u32[]{:S(2)}) collective-permute-start(bf16[2,96,1024]{2,1,0:T(8,128)(2,1)S(1)} %get-tuple-element.47), channel_id=1, source_target_pairs={{0,8},{1,3},{2,10},{3,5},{4,12},{5,7},{6,14},{7,1},{8,16},{9,11},{... | collective-permute-start | bytes 1179656 | tf_op jit(solution)/shard_map/ppermute | solution.py:368
  89.9 9.2 %collective-permute-start.32 = (bf16[2,96,1024]{2,1,0:T(8,128)(2,1)S(1)}, bf16[2,96,1024]{2,1,0:T(8,128)(2,1)S(1)}, u32[]{:S(2)}, u32[]{:S(2)}) collective-permute-start(bf16[2,96,1024]{2,1,0:T(8,128)(2,1)S(1)} %get-tuple-element.48), channel_id=1, source_target_pairs={{0,24},{1,7},{2,26},{3,1},{4,28},{5,3},{6,30},{7,5},{8,0},{9,15},{... | collective-permute-start | bytes 1179656 | tf_op jit(solution)/shard_map/ppermute | solution.py:368
  93.5 9.6 %collective-permute-start.31 = (bf16[2,96,1024]{2,1,0:T(8,128)(2,1)S(1)}, bf16[2,96,1024]{2,1,0:T(8,128)(2,1)S(1)}, u32[]{:S(2)}, u32[]{:S(2)}) collective-permute-start(bf16[2,96,1024]{2,1,0:T(8,128)(2,1)S(1)} %slice.206), channel_id=1, source_target_pairs={{0,8},{1,3},{2,10},{3,5},{4,12},{5,7},{6,14},{7,1},{8,16},{9,11},{... | collective-permute-start | bytes 1179656 | tf_op jit(solution)/shard_map/ppermute | solution.py:368
  94.0 9.2 %collective-permute-start.29 = (bf16[2,96,1024]{2,1,0:T(8,128)(2,1)S(1)}, bf16[2,96,1024]{2,1,0:T(8,128)(2,1)S(1)}, u32[]{:S(2)}, u32[]{:S(2)}) collective-permute-start(bf16[2,96,1024]{2,1,0:T(8,128)(2,1)S(1)} %slice.202), channel_id=1, source_target_pairs={{0,24},{1,7},{2,26},{3,1},{4,28},{5,3},{6,30},{7,5},{8,0},{9,15},{... | collective-permute-start | bytes 1179656 | tf_op jit(solution)/shard_map/ppermute | solution.py:368
  99.1 9.1 %collective-permute-start.27 = (bf16[2,96,1024]{2,1,0:T(8,128)(2,1)S(1)}, bf16[2,96,1024]{2,1,0:T(8,128)(2,1)S(1)}, u32[]{:S(2)}, u32[]{:S(2)}) collective-permute-start(bf16[2,96,1024]{2,1,0:T(8,128)(2,1)S(1)} %add_convert_fusion.7), channel_id=1, source_target_pairs={{0,8},{1,3},{2,10},{3,5},{4,12},{5,7},{6,14},{7,1},{8,16},{9,11},{... | collective-permute-start | bytes 1179656 | tf_op jit(solution)/shard_map/ppermute | solution.py:368
  99.3 8.8 %collective-permute-start.33 = (bf16[2,96,1024]{2,1,0:T(8,128)(2,1)S(1)}, bf16[2,96,1024]{2,1,0:T(8,128)(2,1)S(1)}, u32[]{:S(2)}, u32[]{:S(2)}) collective-permute-start(bf16[2,96,1024]{2,1,0:T(8,128)(2,1)S(1)} %add_convert_fusion.5), channel_id=1, source_target_pairs={{0,24},{1,7},{2,26},{3,1},{4,28},{5,3},{6,30},{7,5},{8,0},{9,15},{... | collective-permute-start | bytes 1179656 | tf_op jit(solution)/shard_map/ppermute | solution.py:368
  102.9 22.3 %copy-start.13 = (bf16[20,3,1024]{2,0,1:T(8,128)(2,1)S(1)}, bf16[20,3,1024]{2,0,1:T(8,128)(2,1)}, u32[]{:S(2)}) copy-start(bf16[20,3,1024]{2,0,1:T(8,128)(2,1)} %param.26) | copy-start | bytes 368644
  102.9 22.3 %copy-start.14 = (bf16[64,1024]{1,0:T(8,128)(2,1)S(1)}, bf16[64,1024]{1,0:T(8,128)(2,1)}, u32[]{:S(2)}) copy-start(bf16[64,1024]{1,0:T(8,128)(2,1)} %x_ref.1) | copy-start | bytes 393220
  108.6 6.9 %collective-permute-start.30 = (bf16[96,1024]{1,0:T(8,128)(2,1)S(1)}, bf16[96,1024]{1,0:T(8,128)(2,1)S(1)}, u32[]{:S(2)}, u32[]{:S(2)}) collective-permute-start(bf16[96,1024]{1,0:T(8,128)(2,1)S(1)} %slice_bitcast_fusion.2), channel_id=1, source_target_pairs={{0,2},{1,9},{2,4},{3,11},{4,6},{5,13},{6,0},{7,15},{8,10},{9,17},{... | collective-permute-start | bytes 589832 | tf_op jit(solution)/shard_map/ppermute | solution.py:368
  109.4 8.3 %collective-permute-start.34 = (bf16[96,1024]{1,0:T(8,128)(2,1)S(1)}, bf16[96,1024]{1,0:T(8,128)(2,1)S(1)}, u32[]{:S(2)}, u32[]{:S(2)}) collective-permute-start(bf16[96,1024]{1,0:T(8,128)(2,1)S(1)} %get-tuple-element.51), channel_id=1, source_target_pairs={{0,4},{1,17},{2,6},{3,19},{4,0},{5,21},{6,2},{7,23},{8,12},{9,25},... | collective-permute-start | bytes 589832 | tf_op jit(solution)/shard_map/ppermute | solution.py:368
  112.0 6.5 %collective-permute-start.35 = (bf16[96,1024]{1,0:T(8,128)(2,1)S(1)}, bf16[96,1024]{1,0:T(8,128)(2,1)S(1)}, u32[]{:S(2)}, u32[]{:S(2)}) collective-permute-start(bf16[96,1024]{1,0:T(8,128)(2,1)S(1)} %get-tuple-element.52), channel_id=1, source_target_pairs={{0,6},{1,25},{2,0},{3,27},{4,2},{5,29},{6,4},{7,31},{8,14},{9,1},{... | collective-permute-start | bytes 589832 | tf_op jit(solution)/shard_map/ppermute | solution.py:368
  118.7 2.8 %collective-permute-start.36 = (bf16[48,1024]{1,0:T(8,128)(2,1)S(1)}, bf16[48,1024]{1,0:T(8,128)(2,1)S(1)}, u32[]{:S(2)}, u32[]{:S(2)}) collective-permute-start(bf16[48,1024]{1,0:T(8,128)(2,1)S(1)} %get-tuple-element.61), channel_id=1, source_target_pairs={{0,0},{1,65},{2,2},{3,67},{4,4},{5,69},{6,6},{7,71},{8,8},{9,73},{... | collective-permute-start | bytes 294920 | tf_op jit(solution)/shard_map/ppermute | solution.py:368
  119.4 4.9 %collective-permute-start.37 = (bf16[48,1024]{1,0:T(8,128)(2,1)S(1)}, bf16[48,1024]{1,0:T(8,128)(2,1)S(1)}, u32[]{:S(2)}, u32[]{:S(2)}) collective-permute-start(bf16[48,1024]{1,0:T(8,128)(2,1)S(1)} %get-tuple-element.62), channel_id=1, source_target_pairs={{0,96},{1,33},{2,98},{3,35},{4,100},{5,37},{6,102},{7,39},{8,104},... | collective-permute-start | bytes 294920 | tf_op jit(solution)/shard_map/ppermute | solution.py:368
  124.3 2.5 %collective-permute-start.38 = (bf16[2,48,640]{2,1,0:T(8,128)(2,1)S(1)}, bf16[2,48,640]{2,1,0:T(8,128)(2,1)S(1)}, u32[]{:S(2)}, u32[]{:S(2)}) collective-permute-start(bf16[2,48,640]{2,1,0:T(8,128)(2,1)S(1)} %pad_maximum_fusion.2), channel_id=1, source_target_pairs={{0,1},{1,0},{2,3},{3,2},{4,5},{5,4},{6,7},{7,6},{8,9},{9,8},{10,11... | collective-permute-start | bytes 368648 | tf_op jit(solution)/shard_map/ppermute | solution.py:356

commit v5 on v4

--- a/solution.py
+++ b/solution.py
@@ -256,12 +256,14 @@
 
 def experts_in(here_ref, side, x_ref, inv_ref, wg_ref, wu_ref):
     x = here_ref[0]
-    by_row, by_col = jnp.where(side == 0, 4, 1), jnp.where(side == 0, 1, 4)
+    place = (0, 1, 3, 2)
     both = square = None
     for k in range(4):
         there = lax.rem(x + 4 - k, 4)
         rows = pl.ds(pl.multiple_of(there * 1024, 1024), 1024)
-        block = jnp.concatenate([x_ref[j * by_row + k * by_col] for j in range(4)], axis=0)
+        block = jnp.concatenate(
+            [x_ref[jnp.where(side == 0, 4 * place[j] + k, 4 * place[k] + j)] for j in range(4)], axis=0
+        )
         part = dot(block, jnp.concatenate([wg_ref[rows, :], wu_ref[rows, :]], axis=1))
         wide = block.astype(F32)
         wide = wide * wide * inv_ref[there]
@@ -300,20 +302,76 @@
                 outs[m][(4 - j) % 4] = value[96 * j : 96 * j + 96]
 
 
-def ffn_own(here_ref, x_ref, inv_ref, wg_ref, wu_ref, wd_ref, p0_ref, p1_ref, p2_ref, p3_ref, act_ref):
-    side = here_ref[1]
+def gather_in(here_ref, terms, inv_ref, wg_ref, wu_ref):
+    both = square = None
+    for k, blocks in terms:
+        there = lax.rem(here_ref[0] + 4 - k, 4)
+        rows = pl.ds(pl.multiple_of(there * 1024, 1024), 1024)
+        block = jnp.concatenate(blocks, axis=0)
+        part = dot(block, jnp.concatenate([wg_ref[rows, :], wu_ref[rows, :]], axis=1))
+        wide = block.astype(F32)
+        wide = wide * wide * inv_ref[there]
+        square_part = wide[:, 0:128]
+        for lane in range(128, 1024, 128):
+            square_part = square_part + wide[:, lane : lane + 128]
+        if both is None:
+            both, square = part, square_part
+        else:
+            both, square = both + part, square + square_part
+    return both, square
+
+
+def activate(both, square):
+    both = both * lax.rsqrt(jnp.sum(square, axis=1, keepdims=True) / 4096.0 + EPS)
+    return (silu(both[:, 0:384]) * both[:, 384:768]).astype(BF)
+
+
+def ffn_early(here_ref, x_ref, inv_ref, wg_ref, wu_ref, wd_ref, acc_ref, sq_ref):
+    weights = (inv_ref, wg_ref, wu_ref)
+
+    @pl.when(here_ref[1] == 0)
+    def _():
+        terms = [(k, [x_ref[4 * i + k] for i in range(3)]) for k in range(4)]
+        both, square = gather_in(here_ref, terms, *weights)
+        for out, value in ((acc_ref, both), (sq_ref, square)):
+            out[0:192] = value[0:192]
+            out[192:288] = jnp.zeros_like(value[0:96])
+            out[288:384] = value[192:288]
+
+    @pl.when(here_ref[1] == 1)
+    def _():
+        terms = [(k, [x_ref[4 * i + n] for n in range(4)]) for i, k in enumerate((0, 1, 3))]
+        acc_ref[...], sq_ref[...] = gather_in(here_ref, terms, *weights)
+
+
+def ffn_late(here_ref, x_ref, inv_ref, wg_ref, wu_ref, acc_ref, sq_ref, act_ref):
+    weights = (inv_ref, wg_ref, wu_ref)
+
+    @pl.when(here_ref[1] == 0)
+    def _():
+        terms = [(k, [x_ref[k]]) for k in range(4)]
+        both, square = gather_in(here_ref, terms, *weights)
+        act_ref[0:192] = activate(acc_ref[0:192], sq_ref[0:192])
+        act_ref[192:288] = activate(both, square)
+        act_ref[288:384] = activate(acc_ref[288:384], sq_ref[288:384])
+
+    @pl.when(here_ref[1] == 1)
+    def _():
+        both, square = gather_in(here_ref, [(2, [x_ref[n] for n in range(4)])], *weights)
+        act_ref[...] = activate(acc_ref[...] + both, sq_ref[...] + square)
+
+
+def ffn_own(here_ref, act_ref, wd_ref, p0_ref, p1_ref, p2_ref, p3_ref):
+    experts_out(here_ref, here_ref[1], act_ref, wd_ref, {0: p0_ref, 1: p1_ref, 2: p2_ref, 3: p3_ref})
+
+
+def ffn_other(
+    here_ref, x_ref, inv_ref, wg_ref, wu_ref, wd_ref, earlier_ref,
+    p0_ref, p1_ref, p2_ref, p3_ref, act_ref,
+):
+    side = 1 - here_ref[1]
     act_ref[...] = experts_in(here_ref, side, x_ref, inv_ref, wg_ref, wu_ref)
     experts_out(here_ref, side, act_ref, wd_ref, {0: p0_ref, 1: p1_ref, 2: p2_ref, 3: p3_ref})
-
-
-def ffn_other(here_ref, x_ref, inv_ref, wg_ref, wu_ref, wd_ref, earlier_ref, act_ref, p2_ref):
-    side = 1 - here_ref[1]
-    act_ref[...] = experts_in(here_ref, side, x_ref, inv_ref, wg_ref, wu_ref)
-    experts_out(here_ref, side, act_ref, wd_ref, {2: p2_ref})
-
-
-def ffn_rest(here_ref, act_ref, wd_ref, p0_ref, p1_ref, p3_ref):
-    experts_out(here_ref, 1 - here_ref[1], act_ref, wd_ref, {1: p1_ref, 3: p3_ref, 0: p0_ref})
 
 
 def final_kernel(
@@ -534,49 +592,62 @@
     late1, late3 = along(late, 1), along(late, 3)
     early2 = along(early1[0:2], 1), along(early3[2:3], 3)
     late2 = along(late3, 3)
-    mine = jnp.concatenate(
+    most = jnp.concatenate(
         [
             early[0:2], late, early[2:3], early1[0:2], late1, early1[2:3],
-            early2[0], late2, early2[1], early3[0:2], late3, early3[2:3],
+            early3[0:2], late3, early3[2:3],
         ],
         axis=0,
     )
-    theirs = move(mine, "core", 1)
+    last = jnp.concatenate([early2[0], late2, early2[1]], axis=0)
+    their_most = move(most, "core", 1)
     gate, up, down = gate_weight[0], up_weight[0], down_weight[0]
     block = shape((4, 96, 1024), BF)
 
+    acc, square = call(
+        ffn_early,
+        [shape((384, 768), F32), shape((384, 128), F32)],
+        [SMEM] + [VMEM] * 5,
+        20,
+        flops=2 * 288 * 4096 * 768,
+        moved=8 * 10**6,
+        name="experts_early",
+    )(here, most, inverse, gate, up, down)
+    last, acc = lax.optimization_barrier((last, acc))
+    their_last = move(last, "core", 1)
+    own = call(
+        ffn_late,
+        shape((384, 384), BF),
+        [SMEM] + [VMEM] * 6,
+        16,
+        flops=2 * 96 * 4096 * 768,
+        moved=8 * 10**6,
+        name="experts_late",
+    )(here, last, inverse, gate, up, acc, square)
+    theirs = jnp.concatenate([their_most, their_last], axis=0)
+    theirs = call(
+        ffn_other,
+        [block] * 4,
+        [SMEM] + [VMEM] * 6,
+        24,
+        [pltpu.VMEM((384, 384), BF)],
+        flops=6 * 384 * 2048 * 768,
+        moved=10 * 10**6,
+        name="experts_other",
+    )(here, theirs, inverse, gate, up, down, own)
     mine = call(
         ffn_own,
         [block] * 4,
-        [SMEM] + [VMEM] * 5,
-        30,
-        [pltpu.VMEM((384, 384), BF)],
-        flops=6 * 384 * 2048 * 768,
-        moved=12 * 10**6,
+        [SMEM] + [VMEM] * 2,
+        13,
+        flops=384 * 4096 * 768,
+        moved=5 * 10**6,
         name="experts_own",
-    )(here, mine, inverse, gate, up, down)
-    act, theirs2 = call(
-        ffn_other,
-        [shape((384, 384), BF), block],
-        [SMEM] + [VMEM] * 6,
-        28,
-        flops=5 * 384 * 2048 * 768,
-        moved=10 * 10**6,
-        name="experts_other",
-    )(here, theirs, inverse, gate, up, down, mine[0])
-    theirs = call(
-        ffn_rest,
-        [block] * 3,
-        [SMEM] + [VMEM] * 2,
-        20,
-        flops=384 * 3072 * 768,
-        moved=5 * 10**6,
-        name="experts_rest",
-    )(here, act, down)
-    part2 = add(mine[2], move(theirs2, "core", 1))
+    )(here, own, down)
+    part2 = add(mine[2], move(theirs[2], "core", 1))
     far1, far3 = along(part2[0:2], 1), along(part2[2:4], 3)
     part1 = add(mine[1], move(theirs[1], "core", 1))
-    part3 = add(mine[3], move(theirs[2], "core", 1))
+    part3 = add(mine[3], move(theirs[3], "core", 1))
     part0 = add(mine[0], move(theirs[0], "core", 1))
     near1, near3 = along(part1[2:4], 1), along(part3[0:2], 3)
     next1, next3 = along(add(part1[0:2], far1), 1), along(add(part3[2:4], far3), 3)

time: 130 us -> 133 us (1.023)
  starting transfers between devices: 44.6 us -> 54.5 us
  waiting for transfers between devices: 54.8 us -> 46.8 us
    ppermute x24, starting transfers between devices: 34.9 us -> 41.7 us  [by_core(): return lax.ppermute(value, AXES, pairs)]
    ppermute x15 -> x16, waiting for transfers between devices: 15.8 us -> 10.8 us  [move(): lax.ppermute(value, axis, [(i, (i + shift) % size) for i in range(size)])]
    ppermute x15 -> x16, starting transfers between devices: 9.73 us -> 12.8 us  [move(): lax.ppermute(value, axis, [(i, (i + shift) % size) for i in range(size)])]
    ppermute x24, waiting for transfers between devices: 38.9 us -> 36 us  [by_core(): return lax.ppermute(value, AXES, pairs)]
    pallas_call x3 -> x4, Pallas kernels: 12 us -> 12.6 us  [the longest x1 5.68 us: per_device(): call(ffn_other, [block] * 4, [SMEM] + [VMEM] * 6, 24, [pltpu.VMEM((384, 3...]
  transfers between devices with their start and end apart: 39 -> 40, of which waited for: 24 -> 24; matrix products, arithmetic and copies ran while one was open for 2% -> 2% of each run, Pallas kernels for 7% -> 6%
where the time goes in v5:
time: 133 us; the launch traced here: 131 us
  starting transfers between devices  54.5 us (41%)
  waiting for transfers between devices  46.8 us (35%)
  Pallas kernels  24.8 us (19%)
  other arithmetic  3.18 us (2%)
  between operations  1.41 us (1%)
    ppermute x24, starting transfers between devices, by_core(): return lax.ppermute(value, AXES, pairs)  41.7 us
    ppermute x24, waiting for transfers between devices, by_core(): return lax.ppermute(value, AXES, pairs)  36 us
    ppermute x16, starting transfers between devices, move(): lax.ppermute(value, axis, [(i, (i + shift) % size) for i in range(size)])  12.8 us
    ppermute x16, waiting for transfers between devices, move(): lax.ppermute(value, axis, [(i, (i + shift) % size) for i in range(size)])  10.8 us
    pallas_call x1, Pallas kernels, per_device(): call(scan_kernel, [shape((SEQ, NS, 1024), F32), shape((4, ROWS, 512), BF)...  5.81 us
    pallas_call x1, Pallas kernels, per_device(): call(ffn_other, [block] * 4, [SMEM] + [VMEM] * 6, 24, [pltpu.VMEM((384, 3...  5.68 us
    pallas_call x1, Pallas kernels, per_device(): call(ffn_early, [shape((384, 768), F32), shape((384, 128), F32)], [SMEM]...  2.72 us
  transfers between devices with their start and end apart: 40, of which 24 were waited for; matrix products, arithmetic and copies ran while one was open for 2% of the time, Pallas kernels for 6%

profile of v5, /device:TPU:0, one launch (start us, length us, event | category | flops | bytes accessed | tf_op | source)
XLA Modules:
  0.0 131.4 jit_solution(14778258839236211212)
XLA Ops:
  0.7 2.2 %conv.1 = (bf16[64,1024]{1,0:T(8,128)(2,1)S(1)}, bf16[80,640]{1,0:T(8,128)(2,1)S(1)}) custom-call(s32[1,4]{1,0:T(1,128)} %span_ref.3, s32[1,4]{1,0:T(1,128)} %res_ref.3, s32[1,20]{1,0:T(1,128)} %slot_ref.3, bf16[64,1024]{1,0:T(8,128)(2,1)} %x_ref.1, bf16[3,20,1024]{2,1,0:T(8,128)(2,1)} %bitcast.72, f32[4,1024]{1,0:T(4,128)} %w_hbm.1, f32[1,1024]{1,0:T(1,128)} %bitcast.84, ...), custom_call_target="tpu_custom_call" | custom-call | flops 1000000000 | bytes 2000000 | tf_op jit(solution)/shard_map/conv/pallas_call | solution.py:490
  3.0 1.3 collective-permute-done
  4.4 1.6 %collective-permute-start.1 = (bf16[80,640]{1,0:T(8,128)(2,1)S(1)}, bf16[80,640]{1,0:T(8,128)(2,1)S(1)}, u32[]{:S(2)}, u32[]{:S(2)}) collective-permute-start(bf16[80,640]{1,0:T(8,128)(2,1)S(1)} %add_convert_fusion.9.q0_ref), channel_id=1, source_target_pairs={{0,2},{2,4},{4,6},{6,0},{1,3},{3,5},{5,7},{7,1},{8,10},{10,12},{12... | collective-permute-start | bytes 307208 | tf_op jit(solution)/shard_map/ppermute | solution.py:414
  6.0 2.7 %collective-permute-start.2 = (bf16[80,640]{1,0:T(8,128)(2,1)S(1)}, bf16[80,640]{1,0:T(8,128)(2,1)S(1)}, u32[]{:S(2)}, u32[]{:S(2)}) collective-permute-start(bf16[80,640]{1,0:T(8,128)(2,1)S(1)} %add_convert_fusion.9.q0_ref), channel_id=1, source_target_pairs={{0,4},{2,6},{4,0},{6,2},{1,5},{3,7},{5,1},{7,3},{8,12},{10,14},{12... | collective-permute-start | bytes 307208 | tf_op jit(solution)/shard_map/ppermute | solution.py:414
  8.7 1.4 %collective-permute-start.3 = (bf16[80,640]{1,0:T(8,128)(2,1)S(1)}, bf16[80,640]{1,0:T(8,128)(2,1)S(1)}, u32[]{:S(2)}, u32[]{:S(2)}) collective-permute-start(bf16[80,640]{1,0:T(8,128)(2,1)S(1)} %add_convert_fusion.9.q0_ref), channel_id=1, source_target_pairs={{0,6},{2,0},{4,2},{6,4},{1,7},{3,1},{5,3},{7,5},{8,14},{10,8},{12,... | collective-permute-start | bytes 307208 | tf_op jit(solution)/shard_map/ppermute | solution.py:414
  10.2 0.3 collective-permute-done.1.q1_ref
  10.6 3.3 %collective-permute-done.2.q2_ref = bf16[80,640]{1,0:T(8,128)(2,1)S(1)} collective-permute-done((bf16[80,640]{1,0:T(8,128)(2,1)S(1)}, bf16[80,640]{1,0:T(8,128)(2,1)S(1)}, u32[]{:S(2)}, u32[]{:S(2)}) %collective-permute-start.2) | collective-permute-done | bytes 102432 | tf_op jit(solution)/shard_map/ppermute | solution.py:414
  14.0 5.8 %scan.1 = (f32[20,16,1024]{2,1,0:T(8,128)}, bf16[4,64,512]{2,1,0:T(8,128)(2,1)S(1)}, bf16[4,64,512]{2,1,0:T(8,128)(2,1)S(1)}, f32[4,1,1024]{2,1,0:T(1,128)S(1)}) custom-call(s32[3]{0:T(128)S(1)} %pad_add_fusion.here_ref, s32[1,4]{1,0:T(1,128)S(1)} %copy-done.10, s32[1,4]{1,0:T(1,128)S(1)} %copy-done.11, s32[1,20]{1,0:T(1,128)S(1)} %copy-done.12, ...), custom_call_target="tpu_custom_call" | custom-call | flops 1000000000 | bytes 10000000 | tf_op jit(solution)/shard_map/scan/pallas_call | solution.py:532
  19.9 1.5 %collective-permute-done.4 = bf16[4,64,512]{2,1,0:T(8,128)(2,1)S(1)} collective-permute-done((bf16[4,64,512]{2,1,0:T(8,128)(2,1)S(1)}, bf16[4,64,512]{2,1,0:T(8,128)(2,1)S(1)}, u32[]{:S(2)}, u32[]{:S(2)}) %collective-permute-start.4) | collective-permute-done | bytes 262176 | tf_op jit(solution)/shard_map/ppermute | solution.py:414
  21.5 1.3 collective-permute-start.5
  22.8 2.4 %collective-permute-start.6 = (bf16[64,512]{1,0:T(8,128)(2,1)S(1)}, bf16[64,512]{1,0:T(8,128)(2,1)S(1)}, u32[]{:S(2)}, u32[]{:S(2)}) collective-permute-start(bf16[64,512]{1,0:T(8,128)(2,1)S(1)} %get-tuple-element.62), channel_id=1, source_target_pairs={{0,4},{2,6},{4,0},{6,2},{1,5},{3,7},{5,1},{7,3},{8,12},{10,14},{12... | collective-permute-start | bytes 196616 | tf_op jit(solution)/shard_map/ppermute | solution.py:414
  25.2 1.6 %collective-permute-start.7 = (bf16[64,512]{1,0:T(8,128)(2,1)S(1)}, bf16[64,512]{1,0:T(8,128)(2,1)S(1)}, u32[]{:S(2)}, u32[]{:S(2)}) collective-permute-start(bf16[64,512]{1,0:T(8,128)(2,1)S(1)} %get-tuple-element.61), channel_id=1, source_target_pairs={{0,6},{2,0},{4,2},{6,4},{1,7},{3,1},{5,3},{7,5},{8,14},{10,8},{12,... | collective-permute-start | bytes 196616 | tf_op jit(solution)/shard_map/ppermute | solution.py:414
  26.9 0.5 collective-permute-done.5.q1_ref
  27.3 1.5 %collective-permute-done.6.q2_ref = bf16[64,512]{1,0:T(8,128)(2,1)S(1)} collective-permute-done((bf16[64,512]{1,0:T(8,128)(2,1)S(1)}, bf16[64,512]{1,0:T(8,128)(2,1)S(1)}, u32[]{:S(2)}, u32[]{:S(2)}) %collective-permute-start.6) | collective-permute-done | bytes 65568 | tf_op jit(solution)/shard_map/ppermute | solution.py:414
  28.9 0.6 collective-permute-done.7.q3_ref
  29.5 0.9 pick.1
  30.5 1.3 %collective-permute-done.8 = bf16[2,48,640]{2,1,0:T(8,128)(2,1)S(1)} collective-permute-done((bf16[2,48,640]{2,1,0:T(8,128)(2,1)S(1)}, bf16[2,48,640]{2,1,0:T(8,128)(2,1)S(1)}, u32[]{:S(2)}, u32[]{:S(2)}) %collective-permute-start.8) | collective-permute-done | bytes 122912 | tf_op jit(solution)/shard_map/ppermute | solution.py:414
  32.0 0.8 collective-permute-start.9
  32.8 2.1 %collective-permute-start.10 = (bf16[48,1024]{1,0:T(8,128)(2,1)S(1)}, bf16[48,1024]{1,0:T(8,128)(2,1)S(1)}, u32[]{:S(2)}, u32[]{:S(2)}) collective-permute-start(bf16[48,1024]{1,0:T(8,128)(2,1)S(1)} %get-tuple-element.71), channel_id=1, source_target_pairs={{0,32},{1,97},{2,34},{3,99},{4,36},{5,101},{6,38},{7,103},{8,40},{... | collective-permute-start | bytes 294920 | tf_op jit(solution)/shard_map/ppermute | solution.py:426
  35.0 5.7 %collective-permute-done.10 = bf16[48,1024]{1,0:T(8,128)(2,1)S(1)} collective-permute-done((bf16[48,1024]{1,0:T(8,128)(2,1)S(1)}, bf16[48,1024]{1,0:T(8,128)(2,1)S(1)}, u32[]{:S(2)}, u32[]{:S(2)}) %collective-permute-start.10) | collective-permute-done | bytes 98336 | tf_op jit(solution)/shard_map/ppermute | solution.py:426
  40.7 1.2 collective-permute-start.11
  41.8 2.2 %collective-permute-start.12 = (bf16[96,1152]{1,0:T(8,128)(2,1)S(1)}, bf16[96,1152]{1,0:T(8,128)(2,1)S(1)}, u32[]{:S(2)}, u32[]{:S(2)}) collective-permute-start(bf16[96,1152]{1,0:T(8,128)(2,1)S(1)} %pad_maximum_fusion.3), channel_id=1, source_target_pairs={{0,6},{1,25},{2,0},{3,27},{4,2},{5,29},{6,4},{7,31},{8,14},{9,1},{... | collective-permute-start | bytes 663560 | tf_op jit(solution)/shard_map/ppermute | solution.py:426
  44.0 3.8 %collective-permute-done.12 = bf16[96,1152]{1,0:T(8,128)(2,1)S(1)} collective-permute-done((bf16[96,1152]{1,0:T(8,128)(2,1)S(1)}, bf16[96,1152]{1,0:T(8,128)(2,1)S(1)}, u32[]{:S(2)}, u32[]{:S(2)}) %collective-permute-start.12) | collective-permute-done | bytes 221216 | tf_op jit(solution)/shard_map/ppermute | solution.py:426
  48.0 1.6 %collective-permute-start.13 = (bf16[3,96,1024]{2,1,0:T(8,128)(2,1)S(1)}, bf16[3,96,1024]{2,1,0:T(8,128)(2,1)S(1)}, u32[]{:S(2)}, u32[]{:S(2)}) collective-permute-start(bf16[3,96,1024]{2,1,0:T(8,128)(2,1)S(1)} %pad_maximum_fusion.2), channel_id=1, source_target_pairs={{0,8},{1,3},{2,10},{3,5},{4,12},{5,7},{6,14},{7,1},{8,16},{9,11},{... | collective-permute-start | bytes 1769480 | tf_op jit(solution)/shard_map/ppermute | solution.py:426
  49.6 1.7 %collective-permute-start.19 = (bf16[3,96,1024]{2,1,0:T(8,128)(2,1)S(1)}, bf16[3,96,1024]{2,1,0:T(8,128)(2,1)S(1)}, u32[]{:S(2)}, u32[]{:S(2)}) collective-permute-start(bf16[3,96,1024]{2,1,0:T(8,128)(2,1)S(1)} %pad_maximum_fusion.2), channel_id=1, source_target_pairs={{0,24},{1,7},{2,26},{3,1},{4,28},{5,3},{6,30},{7,5},{8,0},{9,15},{... | collective-permute-start | bytes 1769480 | tf_op jit(solution)/shard_map/ppermute | solution.py:426
  51.3 1.1 collective-permute-start.15
  52.4 2.4 %collective-permute-start.16 = (bf16[48,1152]{1,0:T(8,128)(2,1)S(1)}, bf16[48,1152]{1,0:T(8,128)(2,1)S(1)}, u32[]{:S(2)}, u32[]{:S(2)}) collective-permute-start(bf16[48,1152]{1,0:T(8,128)(2,1)S(1)} %slice.194), channel_id=1, source_target_pairs={{0,6},{1,25},{2,0},{3,27},{4,2},{5,29},{6,4},{7,31},{8,14},{9,1},{... | collective-permute-start | bytes 331784 | tf_op jit(solution)/shard_map/ppermute | solution.py:426
  54.8 3.9 %collective-permute-done.15 = bf16[48,1152]{1,0:T(8,128)(2,1)S(1)} collective-permute-done((bf16[48,1152]{1,0:T(8,128)(2,1)S(1)}, bf16[48,1152]{1,0:T(8,128)(2,1)S(1)}, u32[]{:S(2)}, u32[]{:S(2)}) %collective-permute-start.15) | collective-permute-done | bytes 110624 | tf_op jit(solution)/shard_map/ppermute | solution.py:426
  58.7 0.4 collective-permute-start.21
  59.1 2.9 %collective-permute-start.17 = (bf16[1,96,1024]{2,1,0:T(8,128)(2,1)S(1)}, bf16[1,96,1024]{2,1,0:T(8,128)(2,1)S(1)}, u32[]{:S(2)}, u32[]{:S(2)}) collective-permute-start(bf16[1,96,1024]{2,1,0:T(8,128)(2,1)S(1)} %slice_bitcast_fusion.4), channel_id=1, source_target_pairs={{0,24},{1,7},{2,26},{3,1},{4,28},{5,3},{6,30},{7,5},{8,0},{9,15},{... | collective-permute-start | bytes 589832 | tf_op jit(solution)/shard_map/ppermute | solution.py:426
  62.1 3.5 %collective-permute-done.21 = bf16[1,96,1024]{2,1,0:T(8,128)(2,1)S(1)} collective-permute-done((bf16[1,96,1024]{2,1,0:T(8,128)(2,1)S(1)}, bf16[1,96,1024]{2,1,0:T(8,128)(2,1)S(1)}, u32[]{:S(2)}, u32[]{:S(2)}) %collective-permute-start.21) | collective-permute-done | bytes 196640 | tf_op jit(solution)/shard_map/ppermute | solution.py:426
  65.9 0.7 collective-permute-start.14
  66.6 2.6 %collective-permute-start.18 = (bf16[1,96,1024]{2,1,0:T(8,128)(2,1)S(1)}, bf16[1,96,1024]{2,1,0:T(8,128)(2,1)S(1)}, u32[]{:S(2)}, u32[]{:S(2)}) collective-permute-start(bf16[1,96,1024]{2,1,0:T(8,128)(2,1)S(1)} %collective-permute-done.17), channel_id=1, source_target_pairs={{0,24},{1,7},{2,26},{3,1},{4,28},{5,3},{6,30},{7,5},{8,0},{9,15},{... | collective-permute-start | bytes 589832 | tf_op jit(solution)/shard_map/ppermute | solution.py:426
  69.2 1.9 %collective-permute-start.20 = (bf16[1,96,1024]{2,1,0:T(8,128)(2,1)S(1)}, bf16[1,96,1024]{2,1,0:T(8,128)(2,1)S(1)}, u32[]{:S(2)}, u32[]{:S(2)}) collective-permute-start(bf16[1,96,1024]{2,1,0:T(8,128)(2,1)S(1)} %get-tuple-element.56), channel_id=1, source_target_pairs={{0,24},{1,7},{2,26},{3,1},{4,28},{5,3},{6,30},{7,5},{8,0},{9,15},{... | collective-permute-start | bytes 589832 | tf_op jit(solution)/shard_map/ppermute | solution.py:426
  71.1 2.7 %experts_early.1 = (f32[384,768]{1,0:T(8,128)S(1)}, f32[384,128]{1,0:T(8,128)S(1)}) custom-call(s32[3]{0:T(128)S(1)} %pad_add_fusion.here_ref, bf16[12,96,1024]{2,1,0:T(8,128)(2,1)S(1)} %get-tuple-element.55.x_ref, f32[4,1,1024]{2,1,0:T(1,128)S(1)} %get-tuple-element.31.inv_ref, bf16[4096,384]{1,0:T(8,128)(2,1)S(1)} %bitcast.60, ...), custom_call_target="tpu_custom_call" | custom-call | flops 1811939328 | bytes 8000000 | tf_op jit(solution)/shard_map/experts_early/pallas_call | solution.py:607
  73.9 1.0 collective-permute-done.20
  75.1 1.8 %experts_late.1.act_ref.earlier_ref = bf16[384,384]{1,0:T(8,128)(2,1)S(1)} custom-call(s32[3]{0:T(128)S(1)} %pad_add_fusion.here_ref, bf16[4,96,1024]{2,1,0:T(8,128)(2,1)S(1)} %pad_maximum_fusion.1.x_ref, f32[4,1,1024]{2,1,0:T(1,128)S(1)} %get-tuple-element.31.inv_ref, bf16[4096,384]{1,0:T(8,128)(2,1)S(1)} %bitcast.61, bf16[4096,384]{1,0:T(8,128)(2,1)S(1)} %bitcast.64, ...), custom_call_target="tpu_custom_call" | custom-call | flops 603979776 | bytes 8000000 | tf_op jit(solution)/shard_map/experts_late/pallas_call | solution.py:618
  77.0 0.5 collective-permute-done.23
  77.7 5.7 %experts_other.1 = (bf16[4,96,1024]{2,1,0:T(8,128)(2,1)S(1)}, bf16[4,96,1024]{2,1,0:T(8,128)(2,1)S(1)}, bf16[4,96,1024]{2,1,0:T(8,128)(2,1)S(1)}, bf16[4,96,1024]{2,1,0:T(8,128)(2,1)S(1)}) custom-call(s32[3]{0:T(128)S(1)} %pad_add_fusion.here_ref, bf16[16,96,1024]{2,1,0:T(8,128)(2,1)S(1)} %pad_maximum_fusion.x_ref, ...), custom_call_target="tpu_custom_call" | custom-call | flops 3623878656 | bytes 10000000 | tf_op jit(solution)/shard_map/experts_other/pallas_call | solution.py:628
  83.6 0.4 collective-permute-start.25
  84.0 2.4 %experts_own.1 = (bf16[4,96,1024]{2,1,0:T(8,128)(2,1)S(1)}, bf16[4,96,1024]{2,1,0:T(8,128)(2,1)S(1)}, bf16[4,96,1024]{2,1,0:T(8,128)(2,1)S(1)}, bf16[4,96,1024]{2,1,0:T(8,128)(2,1)S(1)}) custom-call(s32[3]{0:T(128)S(1)} %pad_add_fusion.here_ref, bf16[384,384]{1,0:T(8,128)(2,1)S(1)} %experts_late.1.act_ref.earlier_ref, bf16[384,4096]{1,0:T(8,128)(2,1)S(1)} %bitcast.68), custom_call_target="tpu_custom_call" | custom-call | flops 1207959552 | bytes 5000000 | tf_op jit(solution)/shard_map/experts_own/pallas_call | solution.py:638
  86.4 0.4 collective-permute-start.29
  86.9 0.3 add_convert_fusion.1
  87.3 3.3 %collective-permute-start.33 = (bf16[2,96,1024]{2,1,0:T(8,128)(2,1)S(1)}, bf16[2,96,1024]{2,1,0:T(8,128)(2,1)S(1)}, u32[]{:S(2)}, u32[]{:S(2)}) collective-permute-start(bf16[2,96,1024]{2,1,0:T(8,128)(2,1)S(1)} %get-tuple-element.54), channel_id=1, source_target_pairs={{0,24},{1,7},{2,26},{3,1},{4,28},{5,3},{6,30},{7,5},{8,0},{9,15},{... | collective-permute-start | bytes 1179656 | tf_op jit(solution)/shard_map/ppermute | solution.py:426
  90.6 0.3 add_convert_fusion.2
  91.3 0.3 add_convert_fusion
  91.6 3.1 %collective-permute-start.30 = (bf16[2,96,1024]{2,1,0:T(8,128)(2,1)S(1)}, bf16[2,96,1024]{2,1,0:T(8,128)(2,1)S(1)}, u32[]{:S(2)}, u32[]{:S(2)}) collective-permute-start(bf16[2,96,1024]{2,1,0:T(8,128)(2,1)S(1)} %slice.202), channel_id=1, source_target_pairs={{0,24},{1,7},{2,26},{3,1},{4,28},{5,3},{6,30},{7,5},{8,0},{9,15},{... | collective-permute-start | bytes 1179656 | tf_op jit(solution)/shard_map/ppermute | solution.py:426
  94.7 1.2 collective-permute-done.33
  96.1 3.8 %collective-permute-start.34 = (bf16[2,96,1024]{2,1,0:T(8,128)(2,1)S(1)}, bf16[2,96,1024]{2,1,0:T(8,128)(2,1)S(1)}, u32[]{:S(2)}, u32[]{:S(2)}) collective-permute-start(bf16[2,96,1024]{2,1,0:T(8,128)(2,1)S(1)} %add_convert_fusion.5), channel_id=1, source_target_pairs={{0,24},{1,7},{2,26},{3,1},{4,28},{5,3},{6,30},{7,5},{8,0},{9,15},{... | collective-permute-start | bytes 1179656 | tf_op jit(solution)/shard_map/ppermute | solution.py:426
  100.1 0.3 add_convert_fusion.3
  100.4 3.4 %collective-permute-done.32 = bf16[2,96,1024]{2,1,0:T(8,128)(2,1)S(1)} collective-permute-done((bf16[2,96,1024]{2,1,0:T(8,128)(2,1)S(1)}, bf16[2,96,1024]{2,1,0:T(8,128)(2,1)S(1)}, u32[]{:S(2)}, u32[]{:S(2)}) %collective-permute-start.32) | collective-permute-done | bytes 393248 | tf_op jit(solution)/shard_map/ppermute | solution.py:426
  103.8 1.3 collective-permute-done.34
  105.1 3.9 %collective-permute-done.28 = bf16[2,96,1024]{2,1,0:T(8,128)(2,1)S(1)} collective-permute-done((bf16[2,96,1024]{2,1,0:T(8,128)(2,1)S(1)}, bf16[2,96,1024]{2,1,0:T(8,128)(2,1)S(1)}, u32[]{:S(2)}, u32[]{:S(2)}) %collective-permute-start.28) | collective-permute-done | bytes 393248 | tf_op jit(solution)/shard_map/ppermute | solution.py:426
  109.0 0.4 add_convert_fusion.6
  109.5 5.7 %collective-permute-start.35 = (bf16[96,1024]{1,0:T(8,128)(2,1)S(1)}, bf16[96,1024]{1,0:T(8,128)(2,1)S(1)}, u32[]{:S(2)}, u32[]{:S(2)}) collective-permute-start(bf16[96,1024]{1,0:T(8,128)(2,1)S(1)} %get-tuple-element.59), channel_id=1, source_target_pairs={{0,4},{1,17},{2,6},{3,19},{4,0},{5,21},{6,2},{7,23},{8,12},{9,25},... | collective-permute-start | bytes 589832 | tf_op jit(solution)/shard_map/ppermute | solution.py:426
  115.3 2.1 %collective-permute-start.31 = (bf16[96,1024]{1,0:T(8,128)(2,1)S(1)}, bf16[96,1024]{1,0:T(8,128)(2,1)S(1)}, u32[]{:S(2)}, u32[]{:S(2)}) collective-permute-start(bf16[96,1024]{1,0:T(8,128)(2,1)S(1)} %slice_bitcast_fusion.2), channel_id=1, source_target_pairs={{0,2},{1,9},{2,4},{3,11},{4,6},{5,13},{6,0},{7,15},{8,10},{9,17},{... | collective-permute-start | bytes 589832 | tf_op jit(solution)/shard_map/ppermute | solution.py:426
  117.4 1.4 %collective-permute-done.35 = bf16[96,1024]{1,0:T(8,128)(2,1)S(1)} collective-permute-done((bf16[96,1024]{1,0:T(8,128)(2,1)S(1)}, bf16[96,1024]{1,0:T(8,128)(2,1)S(1)}, u32[]{:S(2)}, u32[]{:S(2)}) %collective-permute-start.35) | collective-permute-done | bytes 196640 | tf_op jit(solution)/shard_map/ppermute | solution.py:426
  118.9 2.8 %collective-permute-done.36 = bf16[96,1024]{1,0:T(8,128)(2,1)S(1)} collective-permute-done((bf16[96,1024]{1,0:T(8,128)(2,1)S(1)}, bf16[96,1024]{1,0:T(8,128)(2,1)S(1)}, u32[]{:S(2)}, u32[]{:S(2)}) %collective-permute-start.36) | collective-permute-done | bytes 196640 | tf_op jit(solution)/shard_map/ppermute | solution.py:426
  121.7 0.5 collective-permute-done.31
  122.4 0.7 collective-permute-start.37
  123.0 1.2 collective-permute-start.38
  124.3 3.4 %collective-permute-done.38 = bf16[48,1024]{1,0:T(8,128)(2,1)S(1)} collective-permute-done((bf16[48,1024]{1,0:T(8,128)(2,1)S(1)}, bf16[48,1024]{1,0:T(8,128)(2,1)S(1)}, u32[]{:S(2)}, u32[]{:S(2)}) %collective-permute-start.38) | collective-permute-done | bytes 98336 | tf_op jit(solution)/shard_map/ppermute | solution.py:426
  127.9 1.6 %tail.1 = bf16[3,20,1024]{2,1,0:T(8,128)(2,1)} custom-call(s32[1,4]{1,0:T(1,128)S(1)} %copy-done.10, s32[1,4]{1,0:T(1,128)S(1)} %copy-done.11, s32[1,20]{1,0:T(1,128)S(1)} %copy-done.12, bf16[64,1024]{1,0:T(8,128)(2,1)S(1)} %copy-done.14, bf16[3,20,1024]{2,1,0:T(8,128)(2,1)S(1)} %bitcast.73), custom_call_target="tpu_custom_call" | custom-call | flops 1000000000 | bytes 1000000 | tf_op jit(solution)/shard_map/tail/pallas_call | solution.py:521
  129.6 1.8 %combine.1 = bf16[64,512]{1,0:T(8,128)(2,1)} custom-call(s32[3]{0:T(128)S(1)} %pad_add_fusion.here_ref, bf16[2,48,512]{2,1,0:T(8,128)(2,1)S(1)} %get-tuple-element.68.mine_ref, bf16[2,48,512]{2,1,0:T(8,128)(2,1)S(1)} %slice.220.theirs_ref, bf16[96,128]{1,0:T(8,128)(2,1)S(1)} %bitcast_select_fusion.stat_ref, f32[64,512]{1,0:T(8,128)S(1)} %get-tuple-element.44.hid_ref, ...), custom_call_target="tpu_custom_call" | custom-call | flops 100000000 | bytes 1000000 | tf_op jit(solution)/shard_map/combine/pallas_call | solution.py:667
  (117 shorter events, 3.7 us)
Async XLA Ops:
  0.6 13.2 %copy-start.10 = (s32[1,4]{1,0:T(1,128)S(1)}, s32[1,4]{1,0:T(1,128)}, u32[]{:S(2)}) copy-start(s32[1,4]{1,0:T(1,128)} %span_ref.3) | copy-start | bytes 52
  0.6 13.2 %copy-start.11 = (s32[1,4]{1,0:T(1,128)S(1)}, s32[1,4]{1,0:T(1,128)}, u32[]{:S(2)}) copy-start(s32[1,4]{1,0:T(1,128)} %res_ref.3) | copy-start | bytes 52
  0.7 13.2 %copy-start.12 = (s32[1,20]{1,0:T(1,128)S(1)}, s32[1,20]{1,0:T(1,128)}, u32[]{:S(2)}) copy-start(s32[1,20]{1,0:T(1,128)} %slot_ref.3) | copy-start | bytes 244
  0.7 13.2 %copy-start.9 = (f32[512]{0:T(512)S(1)}, f32[512]{0:T(512)}, u32[]{:S(2)}) copy-start(f32[512]{0:T(512)} %param.35) | copy-start | bytes 6148
  0.7 13.2 %copy-start.7 = (f32[1024]{0:T(1024)S(1)}, f32[1024]{0:T(1024)}, u32[]{:S(2)}) copy-start(f32[1024]{0:T(1024)} %param.37) | copy-start | bytes 12292
  0.7 13.2 %copy-start.8 = (f32[1024]{0:T(1024)S(1)}, f32[1024]{0:T(1024)}, u32[]{:S(2)}) copy-start(f32[1024]{0:T(1024)} %param.39) | copy-start | bytes 12292
  0.7 13.2 %copy-start.5 = (bf16[64,1024]{1,0:T(8,128)(2,1)S(1)}, bf16[64,1024]{1,0:T(8,128)(2,1)}, u32[]{:S(2)}) copy-start(bf16[64,1024]{1,0:T(8,128)(2,1)} %z_ref.1) | copy-start | bytes 393220
  0.7 13.2 %copy-start.3 = (f32[20,16,1024]{2,1,0:T(8,128)S(1)}, f32[20,16,1024]{2,1,0:T(8,128)}, u32[]{:S(2)}) copy-start(f32[20,16,1024]{2,1,0:T(8,128)} %sc_ref.1) | copy-start | bytes 3932164
  0.7 13.2 %copy-start.4 = (bf16[512,1024]{1,0:T(8,128)(2,1)S(1)}, bf16[512,1024]{1,0:T(8,128)(2,1)}, u32[]{:S(2)}) copy-start(bf16[512,1024]{1,0:T(8,128)(2,1)} %sw_ref.1) | copy-start | bytes 3145732
  0.7 13.2 %copy-start.6 = (f32[16,1024]{1,0:T(8,128)S(1)}, f32[16,1024]{1,0:T(8,128)}, u32[]{:S(2)}) copy-start(f32[16,1024]{1,0:T(8,128)} %dl_ref.1) | copy-start | bytes 196612
  2.9 1.4 %collective-permute-start = (bf16[80,640]{1,0:T(8,128)(2,1)S(1)}, bf16[80,640]{1,0:T(8,128)(2,1)S(1)}, u32[]{:S(2)}, u32[]{:S(2)}) collective-permute-start(bf16[80,640]{1,0:T(8,128)(2,1)S(1)} %get-tuple-element.25), channel_id=1, source_target_pairs={{0,1},{1,0},{2,3},{3,2},{4,5},{5,4},{6,7},{7,6},{8,9},{9,8},{10,11... | collective-permute-start | bytes 307208 | tf_op jit(solution)/shard_map/ppermute | solution.py:414
  4.4 6.2 %collective-permute-start.1 = (bf16[80,640]{1,0:T(8,128)(2,1)S(1)}, bf16[80,640]{1,0:T(8,128)(2,1)S(1)}, u32[]{:S(2)}, u32[]{:S(2)}) collective-permute-start(bf16[80,640]{1,0:T(8,128)(2,1)S(1)} %add_convert_fusion.9.q0_ref), channel_id=1, source_target_pairs={{0,2},{2,4},{4,6},{6,0},{1,3},{3,5},{5,7},{7,1},{8,10},{10,12},{12... | collective-permute-start | bytes 307208 | tf_op jit(solution)/shard_map/ppermute | solution.py:414
  6.0 7.8 %collective-permute-start.2 = (bf16[80,640]{1,0:T(8,128)(2,1)S(1)}, bf16[80,640]{1,0:T(8,128)(2,1)S(1)}, u32[]{:S(2)}, u32[]{:S(2)}) collective-permute-start(bf16[80,640]{1,0:T(8,128)(2,1)S(1)} %add_convert_fusion.9.q0_ref), channel_id=1, source_target_pairs={{0,4},{2,6},{4,0},{6,2},{1,5},{3,7},{5,1},{7,3},{8,12},{10,14},{12... | collective-permute-start | bytes 307208 | tf_op jit(solution)/shard_map/ppermute | solution.py:414
  8.7 5.1 %collective-permute-start.3 = (bf16[80,640]{1,0:T(8,128)(2,1)S(1)}, bf16[80,640]{1,0:T(8,128)(2,1)S(1)}, u32[]{:S(2)}, u32[]{:S(2)}) collective-permute-start(bf16[80,640]{1,0:T(8,128)(2,1)S(1)} %add_convert_fusion.9.q0_ref), channel_id=1, source_target_pairs={{0,6},{2,0},{4,2},{6,4},{1,7},{3,1},{5,3},{7,5},{8,14},{10,8},{12,... | collective-permute-start | bytes 307208 | tf_op jit(solution)/shard_map/ppermute | solution.py:414
  13.9 15.6 %copy-start.15 = (bf16[64,512]{1,0:T(8,128)(2,1)S(1)}, bf16[64,512]{1,0:T(8,128)(2,1)}, u32[]{:S(2)}) copy-start(bf16[64,512]{1,0:T(8,128)(2,1)} %resid_ref.1) | copy-start | bytes 196612
  14.0 15.6 %copy-start.16 = (bf16[512,4]{0,1:T(4,128)(2,1)S(1)}, bf16[512,4]{0,1:T(4,128)(2,1)}, u32[]{:S(2)}) copy-start(bf16[512,4]{0,1:T(4,128)(2,1)} %param.43) | copy-start | bytes 12292
  14.0 15.6 %copy-start.17 = (f32[512]{0:T(512)S(1)}, f32[512]{0:T(512)}, u32[]{:S(2)}) copy-start(f32[512]{0:T(512)} %param.42) | copy-start | bytes 6148
  14.0 15.5 %copy-start.18 = (s32[64,2]{0,1:T(2,128)S(1)}, s32[64,2]{0,1:T(2,128)}, u32[]{:S(2)}) copy-start(s32[64,2]{0,1:T(2,128)} %param.44) | copy-start | bytes 1540
  19.8 1.6 %collective-permute-start.4 = (bf16[4,64,512]{2,1,0:T(8,128)(2,1)S(1)}, bf16[4,64,512]{2,1,0:T(8,128)(2,1)S(1)}, u32[]{:S(2)}, u32[]{:S(2)}) collective-permute-start(bf16[4,64,512]{2,1,0:T(8,128)(2,1)S(1)} %get-tuple-element.28), channel_id=1, source_target_pairs={{0,1},{1,0},{2,3},{3,2},{4,5},{5,4},{6,7},{7,6},{8,9},{9,8},{10,11... | collective-permute-start | bytes 786440 | tf_op jit(solution)/shard_map/ppermute | solution.py:414
  21.5 5.8 %collective-permute-start.5 = (bf16[64,512]{1,0:T(8,128)(2,1)S(1)}, bf16[64,512]{1,0:T(8,128)(2,1)S(1)}, u32[]{:S(2)}, u32[]{:S(2)}) collective-permute-start(bf16[64,512]{1,0:T(8,128)(2,1)S(1)} %get-tuple-element.63), channel_id=1, source_target_pairs={{0,2},{2,4},{4,6},{6,0},{1,3},{3,5},{5,7},{7,1},{8,10},{10,12},{12... | collective-permute-start | bytes 196616 | tf_op jit(solution)/shard_map/ppermute | solution.py:414
  22.8 6.0 %collective-permute-start.6 = (bf16[64,512]{1,0:T(8,128)(2,1)S(1)}, bf16[64,512]{1,0:T(8,128)(2,1)S(1)}, u32[]{:S(2)}, u32[]{:S(2)}) collective-permute-start(bf16[64,512]{1,0:T(8,128)(2,1)S(1)} %get-tuple-element.62), channel_id=1, source_target_pairs={{0,4},{2,6},{4,0},{6,2},{1,5},{3,7},{5,1},{7,3},{8,12},{10,14},{12... | collective-permute-start | bytes 196616 | tf_op jit(solution)/shard_map/ppermute | solution.py:414
  25.2 4.3 %collective-permute-start.7 = (bf16[64,512]{1,0:T(8,128)(2,1)S(1)}, bf16[64,512]{1,0:T(8,128)(2,1)S(1)}, u32[]{:S(2)}, u32[]{:S(2)}) collective-permute-start(bf16[64,512]{1,0:T(8,128)(2,1)S(1)} %get-tuple-element.61), channel_id=1, source_target_pairs={{0,6},{2,0},{4,2},{6,4},{1,7},{3,1},{5,3},{7,5},{8,14},{10,8},{12,... | collective-permute-start | bytes 196616 | tf_op jit(solution)/shard_map/ppermute | solution.py:414
  30.4 1.4 %collective-permute-start.8 = (bf16[2,48,640]{2,1,0:T(8,128)(2,1)S(1)}, bf16[2,48,640]{2,1,0:T(8,128)(2,1)S(1)}, u32[]{:S(2)}, u32[]{:S(2)}) collective-permute-start(bf16[2,48,640]{2,1,0:T(8,128)(2,1)S(1)} %get-tuple-element.30), channel_id=1, source_target_pairs={{0,1},{1,0},{2,3},{3,2},{4,5},{5,4},{6,7},{7,6},{8,9},{9,8},{10,11... | collective-permute-start | bytes 368648 | tf_op jit(solution)/shard_map/ppermute | solution.py:414
  31.9 39.2 %copy-start.2 = (bf16[1,384,4096]{2,1,0:T(8,128)(2,1)S(1)}, bf16[1,384,4096]{2,1,0:T(8,128)(2,1)}, u32[]{:S(2)}) copy-start(bf16[1,384,4096]{2,1,0:T(8,128)(2,1)} %param.47) | copy-start | bytes 9437188
  32.0 2.9 %collective-permute-start.9 = (bf16[48,1024]{1,0:T(8,128)(2,1)S(1)}, bf16[48,1024]{1,0:T(8,128)(2,1)S(1)}, u32[]{:S(2)}, u32[]{:S(2)}) collective-permute-start(bf16[48,1024]{1,0:T(8,128)(2,1)S(1)} %get-tuple-element.72), channel_id=1, source_target_pairs={{0,0},{1,65},{2,2},{3,67},{4,4},{5,69},{6,6},{7,71},{8,8},{9,73},{... | collective-permute-start | bytes 294920 | tf_op jit(solution)/shard_map/ppermute | solution.py:426
  32.8 7.8 %collective-permute-start.10 = (bf16[48,1024]{1,0:T(8,128)(2,1)S(1)}, bf16[48,1024]{1,0:T(8,128)(2,1)S(1)}, u32[]{:S(2)}, u32[]{:S(2)}) collective-permute-start(bf16[48,1024]{1,0:T(8,128)(2,1)S(1)} %get-tuple-element.71), channel_id=1, source_target_pairs={{0,32},{1,97},{2,34},{3,99},{4,36},{5,101},{6,38},{7,103},{8,40},{... | collective-permute-start | bytes 294920 | tf_op jit(solution)/shard_map/ppermute | solution.py:426
  40.7 7.2 %collective-permute-start.11 = (bf16[96,1152]{1,0:T(8,128)(2,1)S(1)}, bf16[96,1152]{1,0:T(8,128)(2,1)S(1)}, u32[]{:S(2)}, u32[]{:S(2)}) collective-permute-start(bf16[96,1152]{1,0:T(8,128)(2,1)S(1)} %pad_maximum_fusion.3), channel_id=1, source_target_pairs={{0,2},{1,9},{2,4},{3,11},{4,6},{5,13},{6,0},{7,15},{8,10},{9,17},{... | collective-permute-start | bytes 663560 | tf_op jit(solution)/shard_map/ppermute | solution.py:426
  41.8 5.9 %collective-permute-start.12 = (bf16[96,1152]{1,0:T(8,128)(2,1)S(1)}, bf16[96,1152]{1,0:T(8,128)(2,1)S(1)}, u32[]{:S(2)}, u32[]{:S(2)}) collective-permute-start(bf16[96,1152]{1,0:T(8,128)(2,1)S(1)} %pad_maximum_fusion.3), channel_id=1, source_target_pairs={{0,6},{1,25},{2,0},{3,27},{4,2},{5,29},{6,4},{7,31},{8,14},{9,1},{... | collective-permute-start | bytes 663560 | tf_op jit(solution)/shard_map/ppermute | solution.py:426
  47.9 23.2 %copy-start.1 = (bf16[1,4096,384]{2,1,0:T(8,128)(2,1)S(1)}, bf16[1,4096,384]{2,1,0:T(8,128)(2,1)}, u32[]{:S(2)}) copy-start(bf16[1,4096,384]{2,1,0:T(8,128)(2,1)} %param.46) | copy-start | bytes 9437188
  48.0 14.1 %collective-permute-start.13 = (bf16[3,96,1024]{2,1,0:T(8,128)(2,1)S(1)}, bf16[3,96,1024]{2,1,0:T(8,128)(2,1)S(1)}, u32[]{:S(2)}, u32[]{:S(2)}) collective-permute-start(bf16[3,96,1024]{2,1,0:T(8,128)(2,1)S(1)} %pad_maximum_fusion.2), channel_id=1, source_target_pairs={{0,8},{1,3},{2,10},{3,5},{4,12},{5,7},{6,14},{7,1},{8,16},{9,11},{... | collective-permute-start | bytes 1769480 | tf_op jit(solution)/shard_map/ppermute | solution.py:426
  49.6 16.1 %collective-permute-start.19 = (bf16[3,96,1024]{2,1,0:T(8,128)(2,1)S(1)}, bf16[3,96,1024]{2,1,0:T(8,128)(2,1)S(1)}, u32[]{:S(2)}, u32[]{:S(2)}) collective-permute-start(bf16[3,96,1024]{2,1,0:T(8,128)(2,1)S(1)} %pad_maximum_fusion.2), channel_id=1, source_target_pairs={{0,24},{1,7},{2,26},{3,1},{4,28},{5,3},{6,30},{7,5},{8,0},{9,15},{... | collective-permute-start | bytes 1769480 | tf_op jit(solution)/shard_map/ppermute | solution.py:426
  51.3 7.3 %collective-permute-start.15 = (bf16[48,1152]{1,0:T(8,128)(2,1)S(1)}, bf16[48,1152]{1,0:T(8,128)(2,1)S(1)}, u32[]{:S(2)}, u32[]{:S(2)}) collective-permute-start(bf16[48,1152]{1,0:T(8,128)(2,1)S(1)} %slice.193), channel_id=1, source_target_pairs={{0,2},{1,9},{2,4},{3,11},{4,6},{5,13},{6,0},{7,15},{8,10},{9,17},{... | collective-permute-start | bytes 331784 | tf_op jit(solution)/shard_map/ppermute | solution.py:426
  52.4 6.3 %collective-permute-start.16 = (bf16[48,1152]{1,0:T(8,128)(2,1)S(1)}, bf16[48,1152]{1,0:T(8,128)(2,1)S(1)}, u32[]{:S(2)}, u32[]{:S(2)}) collective-permute-start(bf16[48,1152]{1,0:T(8,128)(2,1)S(1)} %slice.194), channel_id=1, source_target_pairs={{0,6},{1,25},{2,0},{3,27},{4,2},{5,29},{6,4},{7,31},{8,14},{9,1},{... | collective-permute-start | bytes 331784 | tf_op jit(solution)/shard_map/ppermute | solution.py:426
  58.7 12.5 %copy-start = (bf16[1,4096,384]{2,1,0:T(8,128)(2,1)S(1)}, bf16[1,4096,384]{2,1,0:T(8,128)(2,1)}, u32[]{:S(2)}) copy-start(bf16[1,4096,384]{2,1,0:T(8,128)(2,1)} %param.45) | copy-start | bytes 9437188
  58.7 6.9 %collective-permute-start.21 = (bf16[1,96,1024]{2,1,0:T(8,128)(2,1)S(1)}, bf16[1,96,1024]{2,1,0:T(8,128)(2,1)S(1)}, u32[]{:S(2)}, u32[]{:S(2)}) collective-permute-start(bf16[1,96,1024]{2,1,0:T(8,128)(2,1)S(1)} %slice_bitcast_fusion.4), channel_id=1, source_target_pairs={{0,8},{1,3},{2,10},{3,5},{4,12},{5,7},{6,14},{7,1},{8,16},{9,11},{... | collective-permute-start | bytes 589832 | tf_op jit(solution)/shard_map/ppermute | solution.py:426
  59.1 6.6 %collective-permute-start.17 = (bf16[1,96,1024]{2,1,0:T(8,128)(2,1)S(1)}, bf16[1,96,1024]{2,1,0:T(8,128)(2,1)S(1)}, u32[]{:S(2)}, u32[]{:S(2)}) collective-permute-start(bf16[1,96,1024]{2,1,0:T(8,128)(2,1)S(1)} %slice_bitcast_fusion.4), channel_id=1, source_target_pairs={{0,24},{1,7},{2,26},{3,1},{4,28},{5,3},{6,30},{7,5},{8,0},{9,15},{... | collective-permute-start | bytes 589832 | tf_op jit(solution)/shard_map/ppermute | solution.py:426
  65.8 11.6 %collective-permute-start.22 = (bf16[12,96,1024]{2,1,0:T(8,128)(2,1)S(1)}, bf16[12,96,1024]{2,1,0:T(8,128)(2,1)S(1)}, u32[]{:S(2)}, u32[]{:S(2)}) collective-permute-start(bf16[12,96,1024]{2,1,0:T(8,128)(2,1)S(1)} %get-tuple-element.55.x_ref), channel_id=1, source_target_pairs={{0,1},{1,0},{2,3},{3,2},{4,5},{5,4},{6,7},{7,6},{8,9},{9,8},{10,11... | collective-permute-start | bytes 7077896 | tf_op jit(solution)/shard_map/ppermute | solution.py:414
  65.9 9.1 %collective-permute-start.14 = (bf16[2,96,1024]{2,1,0:T(8,128)(2,1)S(1)}, bf16[2,96,1024]{2,1,0:T(8,128)(2,1)S(1)}, u32[]{:S(2)}, u32[]{:S(2)}) collective-permute-start(bf16[2,96,1024]{2,1,0:T(8,128)(2,1)S(1)} %get-tuple-element.58), channel_id=1, source_target_pairs={{0,8},{1,3},{2,10},{3,5},{4,12},{5,7},{6,14},{7,1},{8,16},{9,11},{... | collective-permute-start | bytes 1179656 | tf_op jit(solution)/shard_map/ppermute | solution.py:426
  66.6 7.3 %collective-permute-start.18 = (bf16[1,96,1024]{2,1,0:T(8,128)(2,1)S(1)}, bf16[1,96,1024]{2,1,0:T(8,128)(2,1)S(1)}, u32[]{:S(2)}, u32[]{:S(2)}) collective-permute-start(bf16[1,96,1024]{2,1,0:T(8,128)(2,1)S(1)} %collective-permute-done.17), channel_id=1, source_target_pairs={{0,24},{1,7},{2,26},{3,1},{4,28},{5,3},{6,30},{7,5},{8,0},{9,15},{... | collective-permute-start | bytes 589832 | tf_op jit(solution)/shard_map/ppermute | solution.py:426
  69.2 5.7 %collective-permute-start.20 = (bf16[1,96,1024]{2,1,0:T(8,128)(2,1)S(1)}, bf16[1,96,1024]{2,1,0:T(8,128)(2,1)S(1)}, u32[]{:S(2)}, u32[]{:S(2)}) collective-permute-start(bf16[1,96,1024]{2,1,0:T(8,128)(2,1)S(1)} %get-tuple-element.56), channel_id=1, source_target_pairs={{0,24},{1,7},{2,26},{3,1},{4,28},{5,3},{6,30},{7,5},{8,0},{9,15},{... | collective-permute-start | bytes 589832 | tf_op jit(solution)/shard_map/ppermute | solution.py:426
  75.1 2.4 %collective-permute-start.23 = (bf16[4,96,1024]{2,1,0:T(8,128)(2,1)S(1)}, bf16[4,96,1024]{2,1,0:T(8,128)(2,1)S(1)}, u32[]{:S(2)}, u32[]{:S(2)}) collective-permute-start(bf16[4,96,1024]{2,1,0:T(8,128)(2,1)S(1)} %pad_maximum_fusion.1.x_ref), channel_id=1, source_target_pairs={{0,1},{1,0},{2,3},{3,2},{4,5},{5,4},{6,7},{7,6},{8,9},{9,8},{10,11... | collective-permute-start | bytes 2359304 | tf_op jit(solution)/shard_map/ppermute | solution.py:414
  83.4 3.6 %collective-permute-start.26 = (bf16[4,96,1024]{2,1,0:T(8,128)(2,1)S(1)}, bf16[4,96,1024]{2,1,0:T(8,128)(2,1)S(1)}, u32[]{:S(2)}, u32[]{:S(2)}) collective-permute-start(bf16[4,96,1024]{2,1,0:T(8,128)(2,1)S(1)} %get-tuple-element.41), channel_id=1, source_target_pairs={{0,1},{1,0},{2,3},{3,2},{4,5},{5,4},{6,7},{7,6},{8,9},{9,8},{10,11... | collective-permute-start | bytes 2359304 | tf_op jit(solution)/shard_map/ppermute | solution.py:414
  83.6 7.0 %collective-permute-start.25 = (bf16[4,96,1024]{2,1,0:T(8,128)(2,1)S(1)}, bf16[4,96,1024]{2,1,0:T(8,128)(2,1)S(1)}, u32[]{:S(2)}, u32[]{:S(2)}) collective-permute-start(bf16[4,96,1024]{2,1,0:T(8,128)(2,1)S(1)} %get-tuple-element.39), channel_id=1, source_target_pairs={{0,1},{1,0},{2,3},{3,2},{4,5},{5,4},{6,7},{7,6},{8,9},{9,8},{10,11... | collective-permute-start | bytes 2359304 | tf_op jit(solution)/shard_map/ppermute | solution.py:414
  86.4 4.9 %collective-permute-start.29 = (bf16[4,96,1024]{2,1,0:T(8,128)(2,1)S(1)}, bf16[4,96,1024]{2,1,0:T(8,128)(2,1)S(1)}, u32[]{:S(2)}, u32[]{:S(2)}) collective-permute-start(bf16[4,96,1024]{2,1,0:T(8,128)(2,1)S(1)} %get-tuple-element.43), channel_id=1, source_target_pairs={{0,1},{1,0},{2,3},{3,2},{4,5},{5,4},{6,7},{7,6},{8,9},{9,8},{10,11... | collective-permute-start | bytes 2359304 | tf_op jit(solution)/shard_map/ppermute | solution.py:414
  86.7 13.3 %collective-permute-start.24 = (bf16[4,96,1024]{2,1,0:T(8,128)(2,1)S(1)}, bf16[4,96,1024]{2,1,0:T(8,128)(2,1)S(1)}, u32[]{:S(2)}, u32[]{:S(2)}) collective-permute-start(bf16[4,96,1024]{2,1,0:T(8,128)(2,1)S(1)} %get-tuple-element.37), channel_id=1, source_target_pairs={{0,1},{1,0},{2,3},{3,2},{4,5},{5,4},{6,7},{7,6},{8,9},{9,8},{10,11... | collective-permute-start | bytes 2359304 | tf_op jit(solution)/shard_map/ppermute | solution.py:414
  87.3 8.6 %collective-permute-start.33 = (bf16[2,96,1024]{2,1,0:T(8,128)(2,1)S(1)}, bf16[2,96,1024]{2,1,0:T(8,128)(2,1)S(1)}, u32[]{:S(2)}, u32[]{:S(2)}) collective-permute-start(bf16[2,96,1024]{2,1,0:T(8,128)(2,1)S(1)} %get-tuple-element.54), channel_id=1, source_target_pairs={{0,24},{1,7},{2,26},{3,1},{4,28},{5,3},{6,30},{7,5},{8,0},{9,15},{... | collective-permute-start | bytes 1179656 | tf_op jit(solution)/shard_map/ppermute | solution.py:426
  90.6 9.2 %collective-permute-start.27 = (bf16[2,96,1024]{2,1,0:T(8,128)(2,1)S(1)}, bf16[2,96,1024]{2,1,0:T(8,128)(2,1)S(1)}, u32[]{:S(2)}, u32[]{:S(2)}) collective-permute-start(bf16[2,96,1024]{2,1,0:T(8,128)(2,1)S(1)} %get-tuple-element.53), channel_id=1, source_target_pairs={{0,8},{1,3},{2,10},{3,5},{4,12},{5,7},{6,14},{7,1},{8,16},{9,11},{... | collective-permute-start | bytes 1179656 | tf_op jit(solution)/shard_map/ppermute | solution.py:426
  91.0 12.8 %collective-permute-start.32 = (bf16[2,96,1024]{2,1,0:T(8,128)(2,1)S(1)}, bf16[2,96,1024]{2,1,0:T(8,128)(2,1)S(1)}, u32[]{:S(2)}, u32[]{:S(2)}) collective-permute-start(bf16[2,96,1024]{2,1,0:T(8,128)(2,1)S(1)} %slice.206), channel_id=1, source_target_pairs={{0,8},{1,3},{2,10},{3,5},{4,12},{5,7},{6,14},{7,1},{8,16},{9,11},{... | collective-permute-start | bytes 1179656 | tf_op jit(solution)/shard_map/ppermute | solution.py:426
  91.6 12.2 %collective-permute-start.30 = (bf16[2,96,1024]{2,1,0:T(8,128)(2,1)S(1)}, bf16[2,96,1024]{2,1,0:T(8,128)(2,1)S(1)}, u32[]{:S(2)}, u32[]{:S(2)}) collective-permute-start(bf16[2,96,1024]{2,1,0:T(8,128)(2,1)S(1)} %slice.202), channel_id=1, source_target_pairs={{0,24},{1,7},{2,26},{3,1},{4,28},{5,3},{6,30},{7,5},{8,0},{9,15},{... | collective-permute-start | bytes 1179656 | tf_op jit(solution)/shard_map/ppermute | solution.py:426
  96.1 9.1 %collective-permute-start.34 = (bf16[2,96,1024]{2,1,0:T(8,128)(2,1)S(1)}, bf16[2,96,1024]{2,1,0:T(8,128)(2,1)S(1)}, u32[]{:S(2)}, u32[]{:S(2)}) collective-permute-start(bf16[2,96,1024]{2,1,0:T(8,128)(2,1)S(1)} %add_convert_fusion.5), channel_id=1, source_target_pairs={{0,24},{1,7},{2,26},{3,1},{4,28},{5,3},{6,30},{7,5},{8,0},{9,15},{... | collective-permute-start | bytes 1179656 | tf_op jit(solution)/shard_map/ppermute | solution.py:426
  100.0 9.1 %collective-permute-start.28 = (bf16[2,96,1024]{2,1,0:T(8,128)(2,1)S(1)}, bf16[2,96,1024]{2,1,0:T(8,128)(2,1)S(1)}, u32[]{:S(2)}, u32[]{:S(2)}) collective-permute-start(bf16[2,96,1024]{2,1,0:T(8,128)(2,1)S(1)} %add_convert_fusion.7), channel_id=1, source_target_pairs={{0,8},{1,3},{2,10},{3,5},{4,12},{5,7},{6,14},{7,1},{8,16},{9,11},{... | collective-permute-start | bytes 1179656 | tf_op jit(solution)/shard_map/ppermute | solution.py:426
  109.5 18.4 %copy-start.13 = (bf16[20,3,1024]{2,0,1:T(8,128)(2,1)S(1)}, bf16[20,3,1024]{2,0,1:T(8,128)(2,1)}, u32[]{:S(2)}) copy-start(bf16[20,3,1024]{2,0,1:T(8,128)(2,1)} %param.26) | copy-start | bytes 368644
  109.5 18.4 %copy-start.14 = (bf16[64,1024]{1,0:T(8,128)(2,1)S(1)}, bf16[64,1024]{1,0:T(8,128)(2,1)}, u32[]{:S(2)}) copy-start(bf16[64,1024]{1,0:T(8,128)(2,1)} %x_ref.1) | copy-start | bytes 393220
  109.5 9.4 %collective-permute-start.35 = (bf16[96,1024]{1,0:T(8,128)(2,1)S(1)}, bf16[96,1024]{1,0:T(8,128)(2,1)S(1)}, u32[]{:S(2)}, u32[]{:S(2)}) collective-permute-start(bf16[96,1024]{1,0:T(8,128)(2,1)S(1)} %get-tuple-element.59), channel_id=1, source_target_pairs={{0,4},{1,17},{2,6},{3,19},{4,0},{5,21},{6,2},{7,23},{8,12},{9,25},... | collective-permute-start | bytes 589832 | tf_op jit(solution)/shard_map/ppermute | solution.py:426
  115.2 6.4 %collective-permute-start.36 = (bf16[96,1024]{1,0:T(8,128)(2,1)S(1)}, bf16[96,1024]{1,0:T(8,128)(2,1)S(1)}, u32[]{:S(2)}, u32[]{:S(2)}) collective-permute-start(bf16[96,1024]{1,0:T(8,128)(2,1)S(1)} %get-tuple-element.60), channel_id=1, source_target_pairs={{0,6},{1,25},{2,0},{3,27},{4,2},{5,29},{6,4},{7,31},{8,14},{9,1},{... | collective-permute-start | bytes 589832 | tf_op jit(solution)/shard_map/ppermute | solution.py:426
  115.3 6.9 %collective-permute-start.31 = (bf16[96,1024]{1,0:T(8,128)(2,1)S(1)}, bf16[96,1024]{1,0:T(8,128)(2,1)S(1)}, u32[]{:S(2)}, u32[]{:S(2)}) collective-permute-start(bf16[96,1024]{1,0:T(8,128)(2,1)S(1)} %slice_bitcast_fusion.2), channel_id=1, source_target_pairs={{0,2},{1,9},{2,4},{3,11},{4,6},{5,13},{6,0},{7,15},{8,10},{9,17},{... | collective-permute-start | bytes 589832 | tf_op jit(solution)/shard_map/ppermute | solution.py:426
  122.4 2.0 %collective-permute-start.37 = (bf16[48,1024]{1,0:T(8,128)(2,1)S(1)}, bf16[48,1024]{1,0:T(8,128)(2,1)S(1)}, u32[]{:S(2)}, u32[]{:S(2)}) collective-permute-start(bf16[48,1024]{1,0:T(8,128)(2,1)S(1)} %get-tuple-element.69), channel_id=1, source_target_pairs={{0,0},{1,65},{2,2},{3,67},{4,4},{5,69},{6,6},{7,71},{8,8},{9,73},{... | collective-permute-start | bytes 294920 | tf_op jit(solution)/shard_map/ppermute | solution.py:426
  123.0 4.7 %collective-permute-start.38 = (bf16[48,1024]{1,0:T(8,128)(2,1)S(1)}, bf16[48,1024]{1,0:T(8,128)(2,1)S(1)}, u32[]{:S(2)}, u32[]{:S(2)}) collective-permute-start(bf16[48,1024]{1,0:T(8,128)(2,1)S(1)} %get-tuple-element.70), channel_id=1, source_target_pairs={{0,96},{1,33},{2,98},{3,35},{4,100},{5,37},{6,102},{7,39},{8,104},... | collective-permute-start | bytes 294920 | tf_op jit(solution)/shard_map/ppermute | solution.py:426
  127.8 1.7 %collective-permute-start.39 = (bf16[2,48,640]{2,1,0:T(8,128)(2,1)S(1)}, bf16[2,48,640]{2,1,0:T(8,128)(2,1)S(1)}, u32[]{:S(2)}, u32[]{:S(2)}) collective-permute-start(bf16[2,48,640]{2,1,0:T(8,128)(2,1)S(1)} %pad_maximum_fusion.4), channel_id=1, source_target_pairs={{0,1},{1,0},{2,3},{3,2},{4,5},{5,4},{6,7},{7,6},{8,9},{9,8},{10,11... | collective-permute-start | bytes 368648 | tf_op jit(solution)/shard_map/ppermute | solution.py:414

commit v6 on v5

--- a/solution.py
+++ b/solution.py
@@ -256,14 +256,12 @@
 
 def experts_in(here_ref, side, x_ref, inv_ref, wg_ref, wu_ref):
     x = here_ref[0]
-    place = (0, 1, 3, 2)
+    by_row, by_col = jnp.where(side == 0, 4, 1), jnp.where(side == 0, 1, 4)
     both = square = None
     for k in range(4):
         there = lax.rem(x + 4 - k, 4)
         rows = pl.ds(pl.multiple_of(there * 1024, 1024), 1024)
-        block = jnp.concatenate(
-            [x_ref[jnp.where(side == 0, 4 * place[j] + k, 4 * place[k] + j)] for j in range(4)], axis=0
-        )
+        block = jnp.concatenate([x_ref[j * by_row + k * by_col] for j in range(4)], axis=0)
         part = dot(block, jnp.concatenate([wg_ref[rows, :], wu_ref[rows, :]], axis=1))
         wide = block.astype(F32)
         wide = wide * wide * inv_ref[there]
@@ -624,7 +622,7 @@
         moved=8 * 10**6,
         name="experts_late",
     )(here, last, inverse, gate, up, acc, square)
-    theirs = jnp.concatenate([their_most, their_last], axis=0)
+    theirs = jnp.concatenate([their_most[0:8], their_last, their_most[8:12]], axis=0)
     theirs = call(
         ffn_other,
         [block] * 4,

time: 133 us -> 130 us (0.977)
  starting transfers between devices: 54.5 us -> 45.8 us
  waiting for transfers between devices: 46.8 us -> 52.6 us
    ppermute x24, starting transfers between devices: 41.7 us -> 35.8 us  [by_core(): return lax.ppermute(value, AXES, pairs)]
    ppermute x16, waiting for transfers between devices: 10.8 us -> 16 us  [move(): lax.ppermute(value, axis, [(i, (i + shift) % size) for i in range(size)])]
    ppermute x16, starting transfers between devices: 12.8 us -> 9.98 us  [move(): lax.ppermute(value, axis, [(i, (i + shift) % size) for i in range(size)])]
  transfers between devices with their start and end apart: 40 -> 40, of which waited for: 24 -> 25; matrix products, arithmetic and copies ran while one was open for 2% -> 2% of each run, Pallas kernels for 6% -> 7%
where the time goes in v6:
time: 130 us; the launch traced here: 129 us
  waiting for transfers between devices  52.6 us (40%)
  starting transfers between devices  45.8 us (35%)
  Pallas kernels  24.8 us (19%)
  other arithmetic  3.3 us (3%)
  between operations  1.39 us (1%)
    ppermute x24, waiting for transfers between devices, by_core(): return lax.ppermute(value, AXES, pairs)  36.5 us
    ppermute x24, starting transfers between devices, by_core(): return lax.ppermute(value, AXES, pairs)  35.8 us
    ppermute x16, waiting for transfers between devices, move(): lax.ppermute(value, axis, [(i, (i + shift) % size) for i in range(size)])  16 us
    ppermute x16, starting transfers between devices, move(): lax.ppermute(value, axis, [(i, (i + shift) % size) for i in range(size)])  9.98 us
    pallas_call x1, Pallas kernels, per_device(): call(scan_kernel, [shape((SEQ, NS, 1024), F32), shape((4, ROWS, 512), BF)...  5.81 us
    pallas_call x1, Pallas kernels, per_device(): call(ffn_other, [block] * 4, [SMEM] + [VMEM] * 6, 24, [pltpu.VMEM((384, 3...  5.68 us
    pallas_call x1, Pallas kernels, per_device(): call(ffn_early, [shape((384, 768), F32), shape((384, 128), F32)], [SMEM]...  2.73 us
  transfers between devices with their start and end apart: 40, of which 25 were waited for; matrix products, arithmetic and copies ran while one was open for 2% of the time, Pallas kernels for 7%

profile of v6, /device:TPU:0, one launch (start us, length us, event | category | flops | bytes accessed | tf_op | source)
XLA Modules:
  0.0 128.7 jit_solution(5175152517898076612)
XLA Ops:
  0.7 2.2 %conv.1 = (bf16[64,1024]{1,0:T(8,128)(2,1)S(1)}, bf16[80,640]{1,0:T(8,128)(2,1)S(1)}) custom-call(s32[1,4]{1,0:T(1,128)} %span_ref.3, s32[1,4]{1,0:T(1,128)} %res_ref.3, s32[1,20]{1,0:T(1,128)} %slot_ref.3, bf16[64,1024]{1,0:T(8,128)(2,1)} %x_ref.1, bf16[3,20,1024]{2,1,0:T(8,128)(2,1)} %bitcast.72, f32[4,1024]{1,0:T(4,128)} %w_hbm.1, f32[1,1024]{1,0:T(1,128)} %bitcast.84, ...), custom_call_target="tpu_custom_call" | custom-call | flops 1000000000 | bytes 2000000 | tf_op jit(solution)/shard_map/conv/pallas_call | solution.py:488
  3.0 1.3 %collective-permute-done = bf16[80,640]{1,0:T(8,128)(2,1)S(1)} collective-permute-done((bf16[80,640]{1,0:T(8,128)(2,1)S(1)}, bf16[80,640]{1,0:T(8,128)(2,1)S(1)}, u32[]{:S(2)}, u32[]{:S(2)}) %collective-permute-start) | collective-permute-done | bytes 102432 | tf_op jit(solution)/shard_map/ppermute | solution.py:412
  4.4 2.9 %collective-permute-start.3 = (bf16[80,640]{1,0:T(8,128)(2,1)S(1)}, bf16[80,640]{1,0:T(8,128)(2,1)S(1)}, u32[]{:S(2)}, u32[]{:S(2)}) collective-permute-start(bf16[80,640]{1,0:T(8,128)(2,1)S(1)} %add_convert_fusion.9.q0_ref), channel_id=1, source_target_pairs={{0,6},{2,0},{4,2},{6,4},{1,7},{3,1},{5,3},{7,5},{8,14},{10,8},{12,... | collective-permute-start | bytes 307208 | tf_op jit(solution)/shard_map/ppermute | solution.py:412
  7.3 0.8 collective-permute-start.2
  8.1 0.9 collective-permute-start.1
  9.0 2.9 %collective-permute-done.3.q3_ref = bf16[80,640]{1,0:T(8,128)(2,1)S(1)} collective-permute-done((bf16[80,640]{1,0:T(8,128)(2,1)S(1)}, bf16[80,640]{1,0:T(8,128)(2,1)S(1)}, u32[]{:S(2)}, u32[]{:S(2)}) %collective-permute-start.3) | collective-permute-done | bytes 102432 | tf_op jit(solution)/shard_map/ppermute | solution.py:412
  11.9 2.6 %collective-permute-done.2.q2_ref = bf16[80,640]{1,0:T(8,128)(2,1)S(1)} collective-permute-done((bf16[80,640]{1,0:T(8,128)(2,1)S(1)}, bf16[80,640]{1,0:T(8,128)(2,1)S(1)}, u32[]{:S(2)}, u32[]{:S(2)}) %collective-permute-start.2) | collective-permute-done | bytes 102432 | tf_op jit(solution)/shard_map/ppermute | solution.py:412
  14.5 1.1 collective-permute-done.1.q1_ref
  15.8 5.8 %scan.1 = (f32[20,16,1024]{2,1,0:T(8,128)}, bf16[4,64,512]{2,1,0:T(8,128)(2,1)S(1)}, bf16[4,64,512]{2,1,0:T(8,128)(2,1)S(1)}, f32[4,1,1024]{2,1,0:T(1,128)S(1)}) custom-call(s32[3]{0:T(128)S(1)} %pad_add_fusion.here_ref, s32[1,4]{1,0:T(1,128)S(1)} %copy-done.10, s32[1,4]{1,0:T(1,128)S(1)} %copy-done.11, s32[1,20]{1,0:T(1,128)S(1)} %copy-done.12, ...), custom_call_target="tpu_custom_call" | custom-call | flops 1000000000 | bytes 10000000 | tf_op jit(solution)/shard_map/scan/pallas_call | solution.py:530
  21.7 1.5 %collective-permute-done.4 = bf16[4,64,512]{2,1,0:T(8,128)(2,1)S(1)} collective-permute-done((bf16[4,64,512]{2,1,0:T(8,128)(2,1)S(1)}, bf16[4,64,512]{2,1,0:T(8,128)(2,1)S(1)}, u32[]{:S(2)}, u32[]{:S(2)}) %collective-permute-start.4) | collective-permute-done | bytes 262176 | tf_op jit(solution)/shard_map/ppermute | solution.py:412
  23.3 0.6 collective-permute-start.7
  23.9 0.8 collective-permute-start.6
  24.7 0.9 collective-permute-start.5
  25.6 2.6 %collective-permute-done.7.q3_ref = bf16[64,512]{1,0:T(8,128)(2,1)S(1)} collective-permute-done((bf16[64,512]{1,0:T(8,128)(2,1)S(1)}, bf16[64,512]{1,0:T(8,128)(2,1)S(1)}, u32[]{:S(2)}, u32[]{:S(2)}) %collective-permute-start.7) | collective-permute-done | bytes 65568 | tf_op jit(solution)/shard_map/ppermute | solution.py:412
  28.2 1.6 %collective-permute-done.6.q2_ref = bf16[64,512]{1,0:T(8,128)(2,1)S(1)} collective-permute-done((bf16[64,512]{1,0:T(8,128)(2,1)S(1)}, bf16[64,512]{1,0:T(8,128)(2,1)S(1)}, u32[]{:S(2)}, u32[]{:S(2)}) %collective-permute-start.6) | collective-permute-done | bytes 65568 | tf_op jit(solution)/shard_map/ppermute | solution.py:412
  29.8 0.9 collective-permute-done.5.q1_ref
  30.7 0.9 pick.1
  31.7 1.3 %collective-permute-done.8 = bf16[2,48,640]{2,1,0:T(8,128)(2,1)S(1)} collective-permute-done((bf16[2,48,640]{2,1,0:T(8,128)(2,1)S(1)}, bf16[2,48,640]{2,1,0:T(8,128)(2,1)S(1)}, u32[]{:S(2)}, u32[]{:S(2)}) %collective-permute-start.8) | collective-permute-done | bytes 122912 | tf_op jit(solution)/shard_map/ppermute | solution.py:412
  33.2 2.0 %collective-permute-start.10 = (bf16[48,1024]{1,0:T(8,128)(2,1)S(1)}, bf16[48,1024]{1,0:T(8,128)(2,1)S(1)}, u32[]{:S(2)}, u32[]{:S(2)}) collective-permute-start(bf16[48,1024]{1,0:T(8,128)(2,1)S(1)} %get-tuple-element.71), channel_id=1, source_target_pairs={{0,32},{1,97},{2,34},{3,99},{4,36},{5,101},{6,38},{7,103},{8,40},{... | collective-permute-start | bytes 294920 | tf_op jit(solution)/shard_map/ppermute | solution.py:424
  35.2 0.7 collective-permute-start.9
  35.9 3.9 %collective-permute-done.10 = bf16[48,1024]{1,0:T(8,128)(2,1)S(1)} collective-permute-done((bf16[48,1024]{1,0:T(8,128)(2,1)S(1)}, bf16[48,1024]{1,0:T(8,128)(2,1)S(1)}, u32[]{:S(2)}, u32[]{:S(2)}) %collective-permute-start.10) | collective-permute-done | bytes 98336 | tf_op jit(solution)/shard_map/ppermute | solution.py:424
  39.9 1.7 %collective-permute-start.12 = (bf16[96,1152]{1,0:T(8,128)(2,1)S(1)}, bf16[96,1152]{1,0:T(8,128)(2,1)S(1)}, u32[]{:S(2)}, u32[]{:S(2)}) collective-permute-start(bf16[96,1152]{1,0:T(8,128)(2,1)S(1)} %pad_maximum_fusion.3), channel_id=1, source_target_pairs={{0,6},{1,25},{2,0},{3,27},{4,2},{5,29},{6,4},{7,31},{8,14},{9,1},{... | collective-permute-start | bytes 663560 | tf_op jit(solution)/shard_map/ppermute | solution.py:424
  42.0 3.9 %collective-permute-done.12 = bf16[96,1152]{1,0:T(8,128)(2,1)S(1)} collective-permute-done((bf16[96,1152]{1,0:T(8,128)(2,1)S(1)}, bf16[96,1152]{1,0:T(8,128)(2,1)S(1)}, u32[]{:S(2)}, u32[]{:S(2)}) %collective-permute-start.12) | collective-permute-done | bytes 221216 | tf_op jit(solution)/shard_map/ppermute | solution.py:424
  45.9 2.8 %collective-permute-done.11 = bf16[96,1152]{1,0:T(8,128)(2,1)S(1)} collective-permute-done((bf16[96,1152]{1,0:T(8,128)(2,1)S(1)}, bf16[96,1152]{1,0:T(8,128)(2,1)S(1)}, u32[]{:S(2)}, u32[]{:S(2)}) %collective-permute-start.11) | collective-permute-done | bytes 221216 | tf_op jit(solution)/shard_map/ppermute | solution.py:424
  48.9 3.1 %collective-permute-start.19 = (bf16[3,96,1024]{2,1,0:T(8,128)(2,1)S(1)}, bf16[3,96,1024]{2,1,0:T(8,128)(2,1)S(1)}, u32[]{:S(2)}, u32[]{:S(2)}) collective-permute-start(bf16[3,96,1024]{2,1,0:T(8,128)(2,1)S(1)} %pad_maximum_fusion.2), channel_id=1, source_target_pairs={{0,24},{1,7},{2,26},{3,1},{4,28},{5,3},{6,30},{7,5},{8,0},{9,15},{... | collective-permute-start | bytes 1769480 | tf_op jit(solution)/shard_map/ppermute | solution.py:424
  52.1 2.1 %collective-permute-start.15 = (bf16[48,1152]{1,0:T(8,128)(2,1)S(1)}, bf16[48,1152]{1,0:T(8,128)(2,1)S(1)}, u32[]{:S(2)}, u32[]{:S(2)}) collective-permute-start(bf16[48,1152]{1,0:T(8,128)(2,1)S(1)} %slice.201), channel_id=1, source_target_pairs={{0,2},{1,9},{2,4},{3,11},{4,6},{5,13},{6,0},{7,15},{8,10},{9,17},{... | collective-permute-start | bytes 331784 | tf_op jit(solution)/shard_map/ppermute | solution.py:424
  54.2 3.9 %collective-permute-done.15 = bf16[48,1152]{1,0:T(8,128)(2,1)S(1)} collective-permute-done((bf16[48,1152]{1,0:T(8,128)(2,1)S(1)}, bf16[48,1152]{1,0:T(8,128)(2,1)S(1)}, u32[]{:S(2)}, u32[]{:S(2)}) %collective-permute-start.15) | collective-permute-done | bytes 110624 | tf_op jit(solution)/shard_map/ppermute | solution.py:424
  58.2 1.8 %collective-permute-start.21 = (bf16[1,96,1024]{2,1,0:T(8,128)(2,1)S(1)}, bf16[1,96,1024]{2,1,0:T(8,128)(2,1)S(1)}, u32[]{:S(2)}, u32[]{:S(2)}) collective-permute-start(bf16[1,96,1024]{2,1,0:T(8,128)(2,1)S(1)} %slice_bitcast_fusion.4), channel_id=1, source_target_pairs={{0,8},{1,3},{2,10},{3,5},{4,12},{5,7},{6,14},{7,1},{8,16},{9,11},{... | collective-permute-start | bytes 589832 | tf_op jit(solution)/shard_map/ppermute | solution.py:424
  60.0 2.8 %collective-permute-start.17 = (bf16[1,96,1024]{2,1,0:T(8,128)(2,1)S(1)}, bf16[1,96,1024]{2,1,0:T(8,128)(2,1)S(1)}, u32[]{:S(2)}, u32[]{:S(2)}) collective-permute-start(bf16[1,96,1024]{2,1,0:T(8,128)(2,1)S(1)} %slice_bitcast_fusion.4), channel_id=1, source_target_pairs={{0,24},{1,7},{2,26},{3,1},{4,28},{5,3},{6,30},{7,5},{8,0},{9,15},{... | collective-permute-start | bytes 589832 | tf_op jit(solution)/shard_map/ppermute | solution.py:424
  62.9 1.4 %collective-permute-done.13 = bf16[3,96,1024]{2,1,0:T(8,128)(2,1)S(1)} collective-permute-done((bf16[3,96,1024]{2,1,0:T(8,128)(2,1)S(1)}, bf16[3,96,1024]{2,1,0:T(8,128)(2,1)S(1)}, u32[]{:S(2)}, u32[]{:S(2)}) %collective-permute-start.13) | collective-permute-done | bytes 589856 | tf_op jit(solution)/shard_map/ppermute | solution.py:424
  64.3 2.1 %collective-permute-done.21 = bf16[1,96,1024]{2,1,0:T(8,128)(2,1)S(1)} collective-permute-done((bf16[1,96,1024]{2,1,0:T(8,128)(2,1)S(1)}, bf16[1,96,1024]{2,1,0:T(8,128)(2,1)S(1)}, u32[]{:S(2)}, u32[]{:S(2)}) %collective-permute-start.21) | collective-permute-done | bytes 196640 | tf_op jit(solution)/shard_map/ppermute | solution.py:424
  66.6 0.6 collective-permute-start.22
  67.2 0.9 collective-permute-start.14
  68.0 2.4 %collective-permute-start.18 = (bf16[1,96,1024]{2,1,0:T(8,128)(2,1)S(1)}, bf16[1,96,1024]{2,1,0:T(8,128)(2,1)S(1)}, u32[]{:S(2)}, u32[]{:S(2)}) collective-permute-start(bf16[1,96,1024]{2,1,0:T(8,128)(2,1)S(1)} %collective-permute-done.17), channel_id=1, source_target_pairs={{0,24},{1,7},{2,26},{3,1},{4,28},{5,3},{6,30},{7,5},{8,0},{9,15},{... | collective-permute-start | bytes 589832 | tf_op jit(solution)/shard_map/ppermute | solution.py:424
  70.4 1.5 %collective-permute-start.20 = (bf16[1,96,1024]{2,1,0:T(8,128)(2,1)S(1)}, bf16[1,96,1024]{2,1,0:T(8,128)(2,1)S(1)}, u32[]{:S(2)}, u32[]{:S(2)}) collective-permute-start(bf16[1,96,1024]{2,1,0:T(8,128)(2,1)S(1)} %get-tuple-element.57), channel_id=1, source_target_pairs={{0,24},{1,7},{2,26},{3,1},{4,28},{5,3},{6,30},{7,5},{8,0},{9,15},{... | collective-permute-start | bytes 589832 | tf_op jit(solution)/shard_map/ppermute | solution.py:424
  72.0 2.7 %experts_early.1 = (f32[384,768]{1,0:T(8,128)S(1)}, f32[384,128]{1,0:T(8,128)S(1)}) custom-call(s32[3]{0:T(128)S(1)} %pad_add_fusion.here_ref, bf16[12,96,1024]{2,1,0:T(8,128)(2,1)S(1)} %get-tuple-element.58.x_ref, f32[4,1,1024]{2,1,0:T(1,128)S(1)} %get-tuple-element.31.inv_ref, bf16[4096,384]{1,0:T(8,128)(2,1)S(1)} %bitcast.60, ...), custom_call_target="tpu_custom_call" | custom-call | flops 1811939328 | bytes 8000000 | tf_op jit(solution)/shard_map/experts_early/pallas_call | solution.py:605
  74.7 1.4 %collective-permute-done.20 = bf16[1,96,1024]{2,1,0:T(8,128)(2,1)S(1)} collective-permute-done((bf16[1,96,1024]{2,1,0:T(8,128)(2,1)S(1)}, bf16[1,96,1024]{2,1,0:T(8,128)(2,1)S(1)}, u32[]{:S(2)}, u32[]{:S(2)}) %collective-permute-start.20) | collective-permute-done | bytes 196640 | tf_op jit(solution)/shard_map/ppermute | solution.py:424
  76.3 1.8 %experts_late.1.act_ref.earlier_ref = bf16[384,384]{1,0:T(8,128)(2,1)S(1)} custom-call(s32[3]{0:T(128)S(1)} %pad_add_fusion.here_ref, bf16[4,96,1024]{2,1,0:T(8,128)(2,1)S(1)} %pad_maximum_fusion.1.x_ref, f32[4,1,1024]{2,1,0:T(1,128)S(1)} %get-tuple-element.31.inv_ref, bf16[4096,384]{1,0:T(8,128)(2,1)S(1)} %bitcast.61, bf16[4096,384]{1,0:T(8,128)(2,1)S(1)} %bitcast.64, ...), custom_call_target="tpu_custom_call" | custom-call | flops 603979776 | bytes 8000000 | tf_op jit(solution)/shard_map/experts_late/pallas_call | solution.py:616
  78.6 0.4 pad_maximum_fusion.x_ref
  79.0 5.7 %experts_other.1 = (bf16[4,96,1024]{2,1,0:T(8,128)(2,1)S(1)}, bf16[4,96,1024]{2,1,0:T(8,128)(2,1)S(1)}, bf16[4,96,1024]{2,1,0:T(8,128)(2,1)S(1)}, bf16[4,96,1024]{2,1,0:T(8,128)(2,1)S(1)}) custom-call(s32[3]{0:T(128)S(1)} %pad_add_fusion.here_ref, bf16[16,96,1024]{2,1,0:T(8,128)(2,1)S(1)} %pad_maximum_fusion.x_ref, ...), custom_call_target="tpu_custom_call" | custom-call | flops 3623878656 | bytes 10000000 | tf_op jit(solution)/shard_map/experts_other/pallas_call | solution.py:626
  84.9 0.4 collective-permute-start.29
  85.3 2.3 %experts_own.1 = (bf16[4,96,1024]{2,1,0:T(8,128)(2,1)S(1)}, bf16[4,96,1024]{2,1,0:T(8,128)(2,1)S(1)}, bf16[4,96,1024]{2,1,0:T(8,128)(2,1)S(1)}, bf16[4,96,1024]{2,1,0:T(8,128)(2,1)S(1)}) custom-call(s32[3]{0:T(128)S(1)} %pad_add_fusion.here_ref, bf16[384,384]{1,0:T(8,128)(2,1)S(1)} %experts_late.1.act_ref.earlier_ref, bf16[384,4096]{1,0:T(8,128)(2,1)S(1)} %bitcast.68), custom_call_target="tpu_custom_call" | custom-call | flops 1207959552 | bytes 5000000 | tf_op jit(solution)/shard_map/experts_own/pallas_call | solution.py:636
  87.6 0.4 collective-permute-start.24
  88.6 1.7 %collective-permute-start.27 = (bf16[2,96,1024]{2,1,0:T(8,128)(2,1)S(1)}, bf16[2,96,1024]{2,1,0:T(8,128)(2,1)S(1)}, u32[]{:S(2)}, u32[]{:S(2)}) collective-permute-start(bf16[2,96,1024]{2,1,0:T(8,128)(2,1)S(1)} %get-tuple-element.53), channel_id=1, source_target_pairs={{0,8},{1,3},{2,10},{3,5},{4,12},{5,7},{6,14},{7,1},{8,16},{9,11},{... | collective-permute-start | bytes 1179656 | tf_op jit(solution)/shard_map/ppermute | solution.py:424
  90.3 1.6 %collective-permute-start.33 = (bf16[2,96,1024]{2,1,0:T(8,128)(2,1)S(1)}, bf16[2,96,1024]{2,1,0:T(8,128)(2,1)S(1)}, u32[]{:S(2)}, u32[]{:S(2)}) collective-permute-start(bf16[2,96,1024]{2,1,0:T(8,128)(2,1)S(1)} %get-tuple-element.54), channel_id=1, source_target_pairs={{0,24},{1,7},{2,26},{3,1},{4,28},{5,3},{6,30},{7,5},{8,0},{9,15},{... | collective-permute-start | bytes 1179656 | tf_op jit(solution)/shard_map/ppermute | solution.py:424
  92.7 2.1 %collective-permute-start.30 = (bf16[2,96,1024]{2,1,0:T(8,128)(2,1)S(1)}, bf16[2,96,1024]{2,1,0:T(8,128)(2,1)S(1)}, u32[]{:S(2)}, u32[]{:S(2)}) collective-permute-start(bf16[2,96,1024]{2,1,0:T(8,128)(2,1)S(1)} %slice.212), channel_id=1, source_target_pairs={{0,24},{1,7},{2,26},{3,1},{4,28},{5,3},{6,30},{7,5},{8,0},{9,15},{... | collective-permute-start | bytes 1179656 | tf_op jit(solution)/shard_map/ppermute | solution.py:424
  94.8 2.8 %collective-permute-done.27 = bf16[2,96,1024]{2,1,0:T(8,128)(2,1)S(1)} collective-permute-done((bf16[2,96,1024]{2,1,0:T(8,128)(2,1)S(1)}, bf16[2,96,1024]{2,1,0:T(8,128)(2,1)S(1)}, u32[]{:S(2)}, u32[]{:S(2)}) %collective-permute-start.27) | collective-permute-done | bytes 393248 | tf_op jit(solution)/shard_map/ppermute | solution.py:424
  97.8 0.5 collective-permute-start.28
  98.5 2.8 %collective-permute-start.34 = (bf16[2,96,1024]{2,1,0:T(8,128)(2,1)S(1)}, bf16[2,96,1024]{2,1,0:T(8,128)(2,1)S(1)}, u32[]{:S(2)}, u32[]{:S(2)}) collective-permute-start(bf16[2,96,1024]{2,1,0:T(8,128)(2,1)S(1)} %add_convert_fusion.5), channel_id=1, source_target_pairs={{0,24},{1,7},{2,26},{3,1},{4,28},{5,3},{6,30},{7,5},{8,0},{9,15},{... | collective-permute-start | bytes 1179656 | tf_op jit(solution)/shard_map/ppermute | solution.py:424
  101.7 0.7 collective-permute-done.30
  102.3 1.5 %collective-permute-done.32 = bf16[2,96,1024]{2,1,0:T(8,128)(2,1)S(1)} collective-permute-done((bf16[2,96,1024]{2,1,0:T(8,128)(2,1)S(1)}, bf16[2,96,1024]{2,1,0:T(8,128)(2,1)S(1)}, u32[]{:S(2)}, u32[]{:S(2)}) %collective-permute-start.32) | collective-permute-done | bytes 393248 | tf_op jit(solution)/shard_map/ppermute | solution.py:424
  103.8 4.2 %collective-permute-done.28 = bf16[2,96,1024]{2,1,0:T(8,128)(2,1)S(1)} collective-permute-done((bf16[2,96,1024]{2,1,0:T(8,128)(2,1)S(1)}, bf16[2,96,1024]{2,1,0:T(8,128)(2,1)S(1)}, u32[]{:S(2)}, u32[]{:S(2)}) %collective-permute-start.28) | collective-permute-done | bytes 393248 | tf_op jit(solution)/shard_map/ppermute | solution.py:424
  108.0 0.4 add_convert_fusion.6
  108.5 1.0 collective-permute-start.31
  109.6 3.4 %collective-permute-start.35 = (bf16[96,1024]{1,0:T(8,128)(2,1)S(1)}, bf16[96,1024]{1,0:T(8,128)(2,1)S(1)}, u32[]{:S(2)}, u32[]{:S(2)}) collective-permute-start(bf16[96,1024]{1,0:T(8,128)(2,1)S(1)} %get-tuple-element.59), channel_id=1, source_target_pairs={{0,4},{1,17},{2,6},{3,19},{4,0},{5,21},{6,2},{7,23},{8,12},{9,25},... | collective-permute-start | bytes 589832 | tf_op jit(solution)/shard_map/ppermute | solution.py:424
  112.9 1.0 collective-permute-start.36
  114.1 1.4 %collective-permute-done.31 = bf16[96,1024]{1,0:T(8,128)(2,1)S(1)} collective-permute-done((bf16[96,1024]{1,0:T(8,128)(2,1)S(1)}, bf16[96,1024]{1,0:T(8,128)(2,1)S(1)}, u32[]{:S(2)}, u32[]{:S(2)}) %collective-permute-start.31) | collective-permute-done | bytes 196640 | tf_op jit(solution)/shard_map/ppermute | solution.py:424
  115.5 3.2 %collective-permute-done.35 = bf16[96,1024]{1,0:T(8,128)(2,1)S(1)} collective-permute-done((bf16[96,1024]{1,0:T(8,128)(2,1)S(1)}, bf16[96,1024]{1,0:T(8,128)(2,1)S(1)}, u32[]{:S(2)}, u32[]{:S(2)}) %collective-permute-start.35) | collective-permute-done | bytes 196640 | tf_op jit(solution)/shard_map/ppermute | solution.py:424
  118.8 0.7 collective-permute-start.37
  119.5 1.5 %collective-permute-start.38 = (bf16[48,1024]{1,0:T(8,128)(2,1)S(1)}, bf16[48,1024]{1,0:T(8,128)(2,1)S(1)}, u32[]{:S(2)}, u32[]{:S(2)}) collective-permute-start(bf16[48,1024]{1,0:T(8,128)(2,1)S(1)} %get-tuple-element.70), channel_id=1, source_target_pairs={{0,96},{1,33},{2,98},{3,35},{4,100},{5,37},{6,102},{7,39},{8,104},... | collective-permute-start | bytes 294920 | tf_op jit(solution)/shard_map/ppermute | solution.py:424
  121.1 3.1 %collective-permute-done.38 = bf16[48,1024]{1,0:T(8,128)(2,1)S(1)} collective-permute-done((bf16[48,1024]{1,0:T(8,128)(2,1)S(1)}, bf16[48,1024]{1,0:T(8,128)(2,1)S(1)}, u32[]{:S(2)}, u32[]{:S(2)}) %collective-permute-start.38) | collective-permute-done | bytes 98336 | tf_op jit(solution)/shard_map/ppermute | solution.py:424
  124.3 1.0 collective-permute-start.39
  125.2 1.6 %tail.1 = bf16[3,20,1024]{2,1,0:T(8,128)(2,1)} custom-call(s32[1,4]{1,0:T(1,128)S(1)} %copy-done.10, s32[1,4]{1,0:T(1,128)S(1)} %copy-done.11, s32[1,20]{1,0:T(1,128)S(1)} %copy-done.12, bf16[64,1024]{1,0:T(8,128)(2,1)S(1)} %copy-done.14, bf16[3,20,1024]{2,1,0:T(8,128)(2,1)S(1)} %bitcast.73), custom_call_target="tpu_custom_call" | custom-call | flops 1000000000 | bytes 1000000 | tf_op jit(solution)/shard_map/tail/pallas_call | solution.py:519
  126.9 1.8 %combine.1 = bf16[64,512]{1,0:T(8,128)(2,1)} custom-call(s32[3]{0:T(128)S(1)} %pad_add_fusion.here_ref, bf16[2,48,512]{2,1,0:T(8,128)(2,1)S(1)} %get-tuple-element.68.mine_ref, bf16[2,48,512]{2,1,0:T(8,128)(2,1)S(1)} %slice.230.theirs_ref, bf16[96,128]{1,0:T(8,128)(2,1)S(1)} %bitcast_select_fusion.stat_ref, f32[64,512]{1,0:T(8,128)S(1)} %get-tuple-element.44.hid_ref, ...), custom_call_target="tpu_custom_call" | custom-call | flops 100000000 | bytes 1000000 | tf_op jit(solution)/shard_map/combine/pallas_call | solution.py:665
  (119 shorter events, 4.9 us)
Async XLA Ops:
  0.6 15.0 %copy-start.12 = (s32[1,20]{1,0:T(1,128)S(1)}, s32[1,20]{1,0:T(1,128)}, u32[]{:S(2)}) copy-start(s32[1,20]{1,0:T(1,128)} %slot_ref.3) | copy-start | bytes 244
  0.6 15.0 %copy-start.11 = (s32[1,4]{1,0:T(1,128)S(1)}, s32[1,4]{1,0:T(1,128)}, u32[]{:S(2)}) copy-start(s32[1,4]{1,0:T(1,128)} %res_ref.3) | copy-start | bytes 52
  0.7 15.0 %copy-start.10 = (s32[1,4]{1,0:T(1,128)S(1)}, s32[1,4]{1,0:T(1,128)}, u32[]{:S(2)}) copy-start(s32[1,4]{1,0:T(1,128)} %span_ref.3) | copy-start | bytes 52
  0.7 15.0 %copy-start.8 = (f32[1024]{0:T(1024)S(1)}, f32[1024]{0:T(1024)}, u32[]{:S(2)}) copy-start(f32[1024]{0:T(1024)} %param.39) | copy-start | bytes 12292
  0.7 15.0 %copy-start.6 = (f32[16,1024]{1,0:T(8,128)S(1)}, f32[16,1024]{1,0:T(8,128)}, u32[]{:S(2)}) copy-start(f32[16,1024]{1,0:T(8,128)} %dl_ref.1) | copy-start | bytes 196612
  0.7 15.0 %copy-start.7 = (f32[1024]{0:T(1024)S(1)}, f32[1024]{0:T(1024)}, u32[]{:S(2)}) copy-start(f32[1024]{0:T(1024)} %param.37) | copy-start | bytes 12292
  0.7 15.0 %copy-start.4 = (bf16[512,1024]{1,0:T(8,128)(2,1)S(1)}, bf16[512,1024]{1,0:T(8,128)(2,1)}, u32[]{:S(2)}) copy-start(bf16[512,1024]{1,0:T(8,128)(2,1)} %sw_ref.1) | copy-start | bytes 3145732
  0.7 15.0 %copy-start.9 = (f32[512]{0:T(512)S(1)}, f32[512]{0:T(512)}, u32[]{:S(2)}) copy-start(f32[512]{0:T(512)} %param.35) | copy-start | bytes 6148
  0.7 15.0 %copy-start.3 = (f32[20,16,1024]{2,1,0:T(8,128)S(1)}, f32[20,16,1024]{2,1,0:T(8,128)}, u32[]{:S(2)}) copy-start(f32[20,16,1024]{2,1,0:T(8,128)} %sc_ref.1) | copy-start | bytes 3932164
  0.7 15.0 %copy-start.5 = (bf16[64,1024]{1,0:T(8,128)(2,1)S(1)}, bf16[64,1024]{1,0:T(8,128)(2,1)}, u32[]{:S(2)}) copy-start(bf16[64,1024]{1,0:T(8,128)(2,1)} %z_ref.1) | copy-start | bytes 393220
  2.9 1.4 %collective-permute-start = (bf16[80,640]{1,0:T(8,128)(2,1)S(1)}, bf16[80,640]{1,0:T(8,128)(2,1)S(1)}, u32[]{:S(2)}, u32[]{:S(2)}) collective-permute-start(bf16[80,640]{1,0:T(8,128)(2,1)S(1)} %get-tuple-element.25), channel_id=1, source_target_pairs={{0,1},{1,0},{2,3},{3,2},{4,5},{5,4},{6,7},{7,6},{8,9},{9,8},{10,11... | collective-permute-start | bytes 307208 | tf_op jit(solution)/shard_map/ppermute | solution.py:412
  4.4 7.6 %collective-permute-start.3 = (bf16[80,640]{1,0:T(8,128)(2,1)S(1)}, bf16[80,640]{1,0:T(8,128)(2,1)S(1)}, u32[]{:S(2)}, u32[]{:S(2)}) collective-permute-start(bf16[80,640]{1,0:T(8,128)(2,1)S(1)} %add_convert_fusion.9.q0_ref), channel_id=1, source_target_pairs={{0,6},{2,0},{4,2},{6,4},{1,7},{3,1},{5,3},{7,5},{8,14},{10,8},{12,... | collective-permute-start | bytes 307208 | tf_op jit(solution)/shard_map/ppermute | solution.py:412
  7.3 7.3 %collective-permute-start.2 = (bf16[80,640]{1,0:T(8,128)(2,1)S(1)}, bf16[80,640]{1,0:T(8,128)(2,1)S(1)}, u32[]{:S(2)}, u32[]{:S(2)}) collective-permute-start(bf16[80,640]{1,0:T(8,128)(2,1)S(1)} %add_convert_fusion.9.q0_ref), channel_id=1, source_target_pairs={{0,4},{2,6},{4,0},{6,2},{1,5},{3,7},{5,1},{7,3},{8,12},{10,14},{12... | collective-permute-start | bytes 307208 | tf_op jit(solution)/shard_map/ppermute | solution.py:412
  8.1 7.6 %collective-permute-start.1 = (bf16[80,640]{1,0:T(8,128)(2,1)S(1)}, bf16[80,640]{1,0:T(8,128)(2,1)S(1)}, u32[]{:S(2)}, u32[]{:S(2)}) collective-permute-start(bf16[80,640]{1,0:T(8,128)(2,1)S(1)} %add_convert_fusion.9.q0_ref), channel_id=1, source_target_pairs={{0,2},{2,4},{4,6},{6,0},{1,3},{3,5},{5,7},{7,1},{8,10},{10,12},{12... | collective-permute-start | bytes 307208 | tf_op jit(solution)/shard_map/ppermute | solution.py:412
  15.7 15.0 %copy-start.15 = (bf16[64,512]{1,0:T(8,128)(2,1)S(1)}, bf16[64,512]{1,0:T(8,128)(2,1)}, u32[]{:S(2)}) copy-start(bf16[64,512]{1,0:T(8,128)(2,1)} %resid_ref.1) | copy-start | bytes 196612
  15.7 15.0 %copy-start.16 = (bf16[512,4]{0,1:T(4,128)(2,1)S(1)}, bf16[512,4]{0,1:T(4,128)(2,1)}, u32[]{:S(2)}) copy-start(bf16[512,4]{0,1:T(4,128)(2,1)} %param.43) | copy-start | bytes 12292
  15.7 15.0 %copy-start.17 = (f32[512]{0:T(512)S(1)}, f32[512]{0:T(512)}, u32[]{:S(2)}) copy-start(f32[512]{0:T(512)} %param.42) | copy-start | bytes 6148
  15.8 15.0 %copy-start.18 = (s32[64,2]{0,1:T(2,128)S(1)}, s32[64,2]{0,1:T(2,128)}, u32[]{:S(2)}) copy-start(s32[64,2]{0,1:T(2,128)} %param.44) | copy-start | bytes 1540
  21.6 1.6 %collective-permute-start.4 = (bf16[4,64,512]{2,1,0:T(8,128)(2,1)S(1)}, bf16[4,64,512]{2,1,0:T(8,128)(2,1)S(1)}, u32[]{:S(2)}, u32[]{:S(2)}) collective-permute-start(bf16[4,64,512]{2,1,0:T(8,128)(2,1)S(1)} %get-tuple-element.28), channel_id=1, source_target_pairs={{0,1},{1,0},{2,3},{3,2},{4,5},{5,4},{6,7},{7,6},{8,9},{9,8},{10,11... | collective-permute-start | bytes 786440 | tf_op jit(solution)/shard_map/ppermute | solution.py:412
  23.3 4.9 %collective-permute-start.7 = (bf16[64,512]{1,0:T(8,128)(2,1)S(1)}, bf16[64,512]{1,0:T(8,128)(2,1)S(1)}, u32[]{:S(2)}, u32[]{:S(2)}) collective-permute-start(bf16[64,512]{1,0:T(8,128)(2,1)S(1)} %get-tuple-element.61), channel_id=1, source_target_pairs={{0,6},{2,0},{4,2},{6,4},{1,7},{3,1},{5,3},{7,5},{8,14},{10,8},{12,... | collective-permute-start | bytes 196616 | tf_op jit(solution)/shard_map/ppermute | solution.py:412
  23.9 5.9 %collective-permute-start.6 = (bf16[64,512]{1,0:T(8,128)(2,1)S(1)}, bf16[64,512]{1,0:T(8,128)(2,1)S(1)}, u32[]{:S(2)}, u32[]{:S(2)}) collective-permute-start(bf16[64,512]{1,0:T(8,128)(2,1)S(1)} %get-tuple-element.62), channel_id=1, source_target_pairs={{0,4},{2,6},{4,0},{6,2},{1,5},{3,7},{5,1},{7,3},{8,12},{10,14},{12... | collective-permute-start | bytes 196616 | tf_op jit(solution)/shard_map/ppermute | solution.py:412
  24.7 6.0 %collective-permute-start.5 = (bf16[64,512]{1,0:T(8,128)(2,1)S(1)}, bf16[64,512]{1,0:T(8,128)(2,1)S(1)}, u32[]{:S(2)}, u32[]{:S(2)}) collective-permute-start(bf16[64,512]{1,0:T(8,128)(2,1)S(1)} %get-tuple-element.63), channel_id=1, source_target_pairs={{0,2},{2,4},{4,6},{6,0},{1,3},{3,5},{5,7},{7,1},{8,10},{10,12},{12... | collective-permute-start | bytes 196616 | tf_op jit(solution)/shard_map/ppermute | solution.py:412
  31.6 1.4 %collective-permute-start.8 = (bf16[2,48,640]{2,1,0:T(8,128)(2,1)S(1)}, bf16[2,48,640]{2,1,0:T(8,128)(2,1)S(1)}, u32[]{:S(2)}, u32[]{:S(2)}) collective-permute-start(bf16[2,48,640]{2,1,0:T(8,128)(2,1)S(1)} %get-tuple-element.30), channel_id=1, source_target_pairs={{0,1},{1,0},{2,3},{3,2},{4,5},{5,4},{6,7},{7,6},{8,9},{9,8},{10,11... | collective-permute-start | bytes 368648 | tf_op jit(solution)/shard_map/ppermute | solution.py:412
  33.1 38.8 %copy-start.2 = (bf16[1,384,4096]{2,1,0:T(8,128)(2,1)S(1)}, bf16[1,384,4096]{2,1,0:T(8,128)(2,1)}, u32[]{:S(2)}) copy-start(bf16[1,384,4096]{2,1,0:T(8,128)(2,1)} %param.47) | copy-start | bytes 9437188
  33.2 6.7 %collective-permute-start.10 = (bf16[48,1024]{1,0:T(8,128)(2,1)S(1)}, bf16[48,1024]{1,0:T(8,128)(2,1)S(1)}, u32[]{:S(2)}, u32[]{:S(2)}) collective-permute-start(bf16[48,1024]{1,0:T(8,128)(2,1)S(1)} %get-tuple-element.71), channel_id=1, source_target_pairs={{0,32},{1,97},{2,34},{3,99},{4,36},{5,101},{6,38},{7,103},{8,40},{... | collective-permute-start | bytes 294920 | tf_op jit(solution)/shard_map/ppermute | solution.py:424
  35.2 0.7 collective-permute-start.9
  39.9 6.0 %collective-permute-start.12 = (bf16[96,1152]{1,0:T(8,128)(2,1)S(1)}, bf16[96,1152]{1,0:T(8,128)(2,1)S(1)}, u32[]{:S(2)}, u32[]{:S(2)}) collective-permute-start(bf16[96,1152]{1,0:T(8,128)(2,1)S(1)} %pad_maximum_fusion.3), channel_id=1, source_target_pairs={{0,6},{1,25},{2,0},{3,27},{4,2},{5,29},{6,4},{7,31},{8,14},{9,1},{... | collective-permute-start | bytes 663560 | tf_op jit(solution)/shard_map/ppermute | solution.py:424
  41.6 7.1 %collective-permute-start.11 = (bf16[96,1152]{1,0:T(8,128)(2,1)S(1)}, bf16[96,1152]{1,0:T(8,128)(2,1)S(1)}, u32[]{:S(2)}, u32[]{:S(2)}) collective-permute-start(bf16[96,1152]{1,0:T(8,128)(2,1)S(1)} %pad_maximum_fusion.3), channel_id=1, source_target_pairs={{0,2},{1,9},{2,4},{3,11},{4,6},{5,13},{6,0},{7,15},{8,10},{9,17},{... | collective-permute-start | bytes 663560 | tf_op jit(solution)/shard_map/ppermute | solution.py:424
  48.8 23.2 %copy-start.1 = (bf16[1,4096,384]{2,1,0:T(8,128)(2,1)S(1)}, bf16[1,4096,384]{2,1,0:T(8,128)(2,1)}, u32[]{:S(2)}) copy-start(bf16[1,4096,384]{2,1,0:T(8,128)(2,1)} %param.46) | copy-start | bytes 9437188
  48.9 17.6 %collective-permute-start.19 = (bf16[3,96,1024]{2,1,0:T(8,128)(2,1)S(1)}, bf16[3,96,1024]{2,1,0:T(8,128)(2,1)S(1)}, u32[]{:S(2)}, u32[]{:S(2)}) collective-permute-start(bf16[3,96,1024]{2,1,0:T(8,128)(2,1)S(1)} %pad_maximum_fusion.2), channel_id=1, source_target_pairs={{0,24},{1,7},{2,26},{3,1},{4,28},{5,3},{6,30},{7,5},{8,0},{9,15},{... | collective-permute-start | bytes 1769480 | tf_op jit(solution)/shard_map/ppermute | solution.py:424
  52.0 12.3 %collective-permute-start.13 = (bf16[3,96,1024]{2,1,0:T(8,128)(2,1)S(1)}, bf16[3,96,1024]{2,1,0:T(8,128)(2,1)S(1)}, u32[]{:S(2)}, u32[]{:S(2)}) collective-permute-start(bf16[3,96,1024]{2,1,0:T(8,128)(2,1)S(1)} %pad_maximum_fusion.2), channel_id=1, source_target_pairs={{0,8},{1,3},{2,10},{3,5},{4,12},{5,7},{6,14},{7,1},{8,16},{9,11},{... | collective-permute-start | bytes 1769480 | tf_op jit(solution)/shard_map/ppermute | solution.py:424
  52.0 6.2 %collective-permute-start.16 = (bf16[48,1152]{1,0:T(8,128)(2,1)S(1)}, bf16[48,1152]{1,0:T(8,128)(2,1)S(1)}, u32[]{:S(2)}, u32[]{:S(2)}) collective-permute-start(bf16[48,1152]{1,0:T(8,128)(2,1)S(1)} %slice.202), channel_id=1, source_target_pairs={{0,6},{1,25},{2,0},{3,27},{4,2},{5,29},{6,4},{7,31},{8,14},{9,1},{... | collective-permute-start | bytes 331784 | tf_op jit(solution)/shard_map/ppermute | solution.py:424
  52.1 6.0 %collective-permute-start.15 = (bf16[48,1152]{1,0:T(8,128)(2,1)S(1)}, bf16[48,1152]{1,0:T(8,128)(2,1)S(1)}, u32[]{:S(2)}, u32[]{:S(2)}) collective-permute-start(bf16[48,1152]{1,0:T(8,128)(2,1)S(1)} %slice.201), channel_id=1, source_target_pairs={{0,2},{1,9},{2,4},{3,11},{4,6},{5,13},{6,0},{7,15},{8,10},{9,17},{... | collective-permute-start | bytes 331784 | tf_op jit(solution)/shard_map/ppermute | solution.py:424
  58.2 13.8 %copy-start = (bf16[1,4096,384]{2,1,0:T(8,128)(2,1)S(1)}, bf16[1,4096,384]{2,1,0:T(8,128)(2,1)}, u32[]{:S(2)}) copy-start(bf16[1,4096,384]{2,1,0:T(8,128)(2,1)} %param.45) | copy-start | bytes 9437188
  58.2 8.2 %collective-permute-start.21 = (bf16[1,96,1024]{2,1,0:T(8,128)(2,1)S(1)}, bf16[1,96,1024]{2,1,0:T(8,128)(2,1)S(1)}, u32[]{:S(2)}, u32[]{:S(2)}) collective-permute-start(bf16[1,96,1024]{2,1,0:T(8,128)(2,1)S(1)} %slice_bitcast_fusion.4), channel_id=1, source_target_pairs={{0,8},{1,3},{2,10},{3,5},{4,12},{5,7},{6,14},{7,1},{8,16},{9,11},{... | collective-permute-start | bytes 589832 | tf_op jit(solution)/shard_map/ppermute | solution.py:424
  60.0 6.5 %collective-permute-start.17 = (bf16[1,96,1024]{2,1,0:T(8,128)(2,1)S(1)}, bf16[1,96,1024]{2,1,0:T(8,128)(2,1)S(1)}, u32[]{:S(2)}, u32[]{:S(2)}) collective-permute-start(bf16[1,96,1024]{2,1,0:T(8,128)(2,1)S(1)} %slice_bitcast_fusion.4), channel_id=1, source_target_pairs={{0,24},{1,7},{2,26},{3,1},{4,28},{5,3},{6,30},{7,5},{8,0},{9,15},{... | collective-permute-start | bytes 589832 | tf_op jit(solution)/shard_map/ppermute | solution.py:424
  66.6 11.6 %collective-permute-start.22 = (bf16[12,96,1024]{2,1,0:T(8,128)(2,1)S(1)}, bf16[12,96,1024]{2,1,0:T(8,128)(2,1)S(1)}, u32[]{:S(2)}, u32[]{:S(2)}) collective-permute-start(bf16[12,96,1024]{2,1,0:T(8,128)(2,1)S(1)} %get-tuple-element.58.x_ref), channel_id=1, source_target_pairs={{0,1},{1,0},{2,3},{3,2},{4,5},{5,4},{6,7},{7,6},{8,9},{9,8},{10,11... | collective-permute-start | bytes 7077896 | tf_op jit(solution)/shard_map/ppermute | solution.py:412
  67.2 9.0 %collective-permute-start.14 = (bf16[2,96,1024]{2,1,0:T(8,128)(2,1)S(1)}, bf16[2,96,1024]{2,1,0:T(8,128)(2,1)S(1)}, u32[]{:S(2)}, u32[]{:S(2)}) collective-permute-start(bf16[2,96,1024]{2,1,0:T(8,128)(2,1)S(1)} %get-tuple-element.55), channel_id=1, source_target_pairs={{0,8},{1,3},{2,10},{3,5},{4,12},{5,7},{6,14},{7,1},{8,16},{9,11},{... | collective-permute-start | bytes 1179656 | tf_op jit(solution)/shard_map/ppermute | solution.py:424
  68.0 6.7 %collective-permute-start.18 = (bf16[1,96,1024]{2,1,0:T(8,128)(2,1)S(1)}, bf16[1,96,1024]{2,1,0:T(8,128)(2,1)S(1)}, u32[]{:S(2)}, u32[]{:S(2)}) collective-permute-start(bf16[1,96,1024]{2,1,0:T(8,128)(2,1)S(1)} %collective-permute-done.17), channel_id=1, source_target_pairs={{0,24},{1,7},{2,26},{3,1},{4,28},{5,3},{6,30},{7,5},{8,0},{9,15},{... | collective-permute-start | bytes 589832 | tf_op jit(solution)/shard_map/ppermute | solution.py:424
  70.4 5.7 %collective-permute-start.20 = (bf16[1,96,1024]{2,1,0:T(8,128)(2,1)S(1)}, bf16[1,96,1024]{2,1,0:T(8,128)(2,1)S(1)}, u32[]{:S(2)}, u32[]{:S(2)}) collective-permute-start(bf16[1,96,1024]{2,1,0:T(8,128)(2,1)S(1)} %get-tuple-element.57), channel_id=1, source_target_pairs={{0,24},{1,7},{2,26},{3,1},{4,28},{5,3},{6,30},{7,5},{8,0},{9,15},{... | collective-permute-start | bytes 589832 | tf_op jit(solution)/shard_map/ppermute | solution.py:424
  76.3 2.4 %collective-permute-start.23 = (bf16[4,96,1024]{2,1,0:T(8,128)(2,1)S(1)}, bf16[4,96,1024]{2,1,0:T(8,128)(2,1)S(1)}, u32[]{:S(2)}, u32[]{:S(2)}) collective-permute-start(bf16[4,96,1024]{2,1,0:T(8,128)(2,1)S(1)} %pad_maximum_fusion.1.x_ref), channel_id=1, source_target_pairs={{0,1},{1,0},{2,3},{3,2},{4,5},{5,4},{6,7},{7,6},{8,9},{9,8},{10,11... | collective-permute-start | bytes 2359304 | tf_op jit(solution)/shard_map/ppermute | solution.py:412
  84.7 3.5 %collective-permute-start.26 = (bf16[4,96,1024]{2,1,0:T(8,128)(2,1)S(1)}, bf16[4,96,1024]{2,1,0:T(8,128)(2,1)S(1)}, u32[]{:S(2)}, u32[]{:S(2)}) collective-permute-start(bf16[4,96,1024]{2,1,0:T(8,128)(2,1)S(1)} %get-tuple-element.41), channel_id=1, source_target_pairs={{0,1},{1,0},{2,3},{3,2},{4,5},{5,4},{6,7},{7,6},{8,9},{9,8},{10,11... | collective-permute-start | bytes 2359304 | tf_op jit(solution)/shard_map/ppermute | solution.py:412
  84.9 7.1 %collective-permute-start.29 = (bf16[4,96,1024]{2,1,0:T(8,128)(2,1)S(1)}, bf16[4,96,1024]{2,1,0:T(8,128)(2,1)S(1)}, u32[]{:S(2)}, u32[]{:S(2)}) collective-permute-start(bf16[4,96,1024]{2,1,0:T(8,128)(2,1)S(1)} %get-tuple-element.43), channel_id=1, source_target_pairs={{0,1},{1,0},{2,3},{3,2},{4,5},{5,4},{6,7},{7,6},{8,9},{9,8},{10,11... | collective-permute-start | bytes 2359304 | tf_op jit(solution)/shard_map/ppermute | solution.py:412
  87.6 13.7 %collective-permute-start.24 = (bf16[4,96,1024]{2,1,0:T(8,128)(2,1)S(1)}, bf16[4,96,1024]{2,1,0:T(8,128)(2,1)S(1)}, u32[]{:S(2)}, u32[]{:S(2)}) collective-permute-start(bf16[4,96,1024]{2,1,0:T(8,128)(2,1)S(1)} %get-tuple-element.37), channel_id=1, source_target_pairs={{0,1},{1,0},{2,3},{3,2},{4,5},{5,4},{6,7},{7,6},{8,9},{9,8},{10,11... | collective-permute-start | bytes 2359304 | tf_op jit(solution)/shard_map/ppermute | solution.py:412
  88.0 4.3 %collective-permute-start.25 = (bf16[4,96,1024]{2,1,0:T(8,128)(2,1)S(1)}, bf16[4,96,1024]{2,1,0:T(8,128)(2,1)S(1)}, u32[]{:S(2)}, u32[]{:S(2)}) collective-permute-start(bf16[4,96,1024]{2,1,0:T(8,128)(2,1)S(1)} %get-tuple-element.39), channel_id=1, source_target_pairs={{0,1},{1,0},{2,3},{3,2},{4,5},{5,4},{6,7},{7,6},{8,9},{9,8},{10,11... | collective-permute-start | bytes 2359304 | tf_op jit(solution)/shard_map/ppermute | solution.py:412
  88.6 9.1 %collective-permute-start.27 = (bf16[2,96,1024]{2,1,0:T(8,128)(2,1)S(1)}, bf16[2,96,1024]{2,1,0:T(8,128)(2,1)S(1)}, u32[]{:S(2)}, u32[]{:S(2)}) collective-permute-start(bf16[2,96,1024]{2,1,0:T(8,128)(2,1)S(1)} %get-tuple-element.53), channel_id=1, source_target_pairs={{0,8},{1,3},{2,10},{3,5},{4,12},{5,7},{6,14},{7,1},{8,16},{9,11},{... | collective-permute-start | bytes 1179656 | tf_op jit(solution)/shard_map/ppermute | solution.py:424
  90.3 8.0 %collective-permute-start.33 = (bf16[2,96,1024]{2,1,0:T(8,128)(2,1)S(1)}, bf16[2,96,1024]{2,1,0:T(8,128)(2,1)S(1)}, u32[]{:S(2)}, u32[]{:S(2)}) collective-permute-start(bf16[2,96,1024]{2,1,0:T(8,128)(2,1)S(1)} %get-tuple-element.54), channel_id=1, source_target_pairs={{0,24},{1,7},{2,26},{3,1},{4,28},{5,3},{6,30},{7,5},{8,0},{9,15},{... | collective-permute-start | bytes 1179656 | tf_op jit(solution)/shard_map/ppermute | solution.py:424
  92.7 9.6 %collective-permute-start.30 = (bf16[2,96,1024]{2,1,0:T(8,128)(2,1)S(1)}, bf16[2,96,1024]{2,1,0:T(8,128)(2,1)S(1)}, u32[]{:S(2)}, u32[]{:S(2)}) collective-permute-start(bf16[2,96,1024]{2,1,0:T(8,128)(2,1)S(1)} %slice.212), channel_id=1, source_target_pairs={{0,24},{1,7},{2,26},{3,1},{4,28},{5,3},{6,30},{7,5},{8,0},{9,15},{... | collective-permute-start | bytes 1179656 | tf_op jit(solution)/shard_map/ppermute | solution.py:424
  94.8 9.0 %collective-permute-start.32 = (bf16[2,96,1024]{2,1,0:T(8,128)(2,1)S(1)}, bf16[2,96,1024]{2,1,0:T(8,128)(2,1)S(1)}, u32[]{:S(2)}, u32[]{:S(2)}) collective-permute-start(bf16[2,96,1024]{2,1,0:T(8,128)(2,1)S(1)} %slice.216), channel_id=1, source_target_pairs={{0,8},{1,3},{2,10},{3,5},{4,12},{5,7},{6,14},{7,1},{8,16},{9,11},{... | collective-permute-start | bytes 1179656 | tf_op jit(solution)/shard_map/ppermute | solution.py:424
  97.8 10.2 %collective-permute-start.28 = (bf16[2,96,1024]{2,1,0:T(8,128)(2,1)S(1)}, bf16[2,96,1024]{2,1,0:T(8,128)(2,1)S(1)}, u32[]{:S(2)}, u32[]{:S(2)}) collective-permute-start(bf16[2,96,1024]{2,1,0:T(8,128)(2,1)S(1)} %add_convert_fusion.7), channel_id=1, source_target_pairs={{0,8},{1,3},{2,10},{3,5},{4,12},{5,7},{6,14},{7,1},{8,16},{9,11},{... | collective-permute-start | bytes 1179656 | tf_op jit(solution)/shard_map/ppermute | solution.py:424
  98.5 9.5 %collective-permute-start.34 = (bf16[2,96,1024]{2,1,0:T(8,128)(2,1)S(1)}, bf16[2,96,1024]{2,1,0:T(8,128)(2,1)S(1)}, u32[]{:S(2)}, u32[]{:S(2)}) collective-permute-start(bf16[2,96,1024]{2,1,0:T(8,128)(2,1)S(1)} %add_convert_fusion.5), channel_id=1, source_target_pairs={{0,24},{1,7},{2,26},{3,1},{4,28},{5,3},{6,30},{7,5},{8,0},{9,15},{... | collective-permute-start | bytes 1179656 | tf_op jit(solution)/shard_map/ppermute | solution.py:424
  108.5 16.8 %copy-start.13 = (bf16[20,3,1024]{2,0,1:T(8,128)(2,1)S(1)}, bf16[20,3,1024]{2,0,1:T(8,128)(2,1)}, u32[]{:S(2)}) copy-start(bf16[20,3,1024]{2,0,1:T(8,128)(2,1)} %param.26) | copy-start | bytes 368644
  108.5 16.8 %copy-start.14 = (bf16[64,1024]{1,0:T(8,128)(2,1)S(1)}, bf16[64,1024]{1,0:T(8,128)(2,1)}, u32[]{:S(2)}) copy-start(bf16[64,1024]{1,0:T(8,128)(2,1)} %x_ref.1) | copy-start | bytes 393220
  108.5 6.9 %collective-permute-start.31 = (bf16[96,1024]{1,0:T(8,128)(2,1)S(1)}, bf16[96,1024]{1,0:T(8,128)(2,1)S(1)}, u32[]{:S(2)}, u32[]{:S(2)}) collective-permute-start(bf16[96,1024]{1,0:T(8,128)(2,1)S(1)} %slice_bitcast_fusion.2), channel_id=1, source_target_pairs={{0,2},{1,9},{2,4},{3,11},{4,6},{5,13},{6,0},{7,15},{8,10},{9,17},{... | collective-permute-start | bytes 589832 | tf_op jit(solution)/shard_map/ppermute | solution.py:424
  109.6 9.1 %collective-permute-start.35 = (bf16[96,1024]{1,0:T(8,128)(2,1)S(1)}, bf16[96,1024]{1,0:T(8,128)(2,1)S(1)}, u32[]{:S(2)}, u32[]{:S(2)}) collective-permute-start(bf16[96,1024]{1,0:T(8,128)(2,1)S(1)} %get-tuple-element.59), channel_id=1, source_target_pairs={{0,4},{1,17},{2,6},{3,19},{4,0},{5,21},{6,2},{7,23},{8,12},{9,25},... | collective-permute-start | bytes 589832 | tf_op jit(solution)/shard_map/ppermute | solution.py:424
  112.9 5.8 %collective-permute-start.36 = (bf16[96,1024]{1,0:T(8,128)(2,1)S(1)}, bf16[96,1024]{1,0:T(8,128)(2,1)S(1)}, u32[]{:S(2)}, u32[]{:S(2)}) collective-permute-start(bf16[96,1024]{1,0:T(8,128)(2,1)S(1)} %get-tuple-element.60), channel_id=1, source_target_pairs={{0,6},{1,25},{2,0},{3,27},{4,2},{5,29},{6,4},{7,31},{8,14},{9,1},{... | collective-permute-start | bytes 589832 | tf_op jit(solution)/shard_map/ppermute | solution.py:424
  118.8 2.2 %collective-permute-start.37 = (bf16[48,1024]{1,0:T(8,128)(2,1)S(1)}, bf16[48,1024]{1,0:T(8,128)(2,1)S(1)}, u32[]{:S(2)}, u32[]{:S(2)}) collective-permute-start(bf16[48,1024]{1,0:T(8,128)(2,1)S(1)} %get-tuple-element.69), channel_id=1, source_target_pairs={{0,0},{1,65},{2,2},{3,67},{4,4},{5,69},{6,6},{7,71},{8,8},{9,73},{... | collective-permute-start | bytes 294920 | tf_op jit(solution)/shard_map/ppermute | solution.py:424
  119.5 4.7 %collective-permute-start.38 = (bf16[48,1024]{1,0:T(8,128)(2,1)S(1)}, bf16[48,1024]{1,0:T(8,128)(2,1)S(1)}, u32[]{:S(2)}, u32[]{:S(2)}) collective-permute-start(bf16[48,1024]{1,0:T(8,128)(2,1)S(1)} %get-tuple-element.70), channel_id=1, source_target_pairs={{0,96},{1,33},{2,98},{3,35},{4,100},{5,37},{6,102},{7,39},{8,104},... | collective-permute-start | bytes 294920 | tf_op jit(solution)/shard_map/ppermute | solution.py:424
  124.3 2.5 %collective-permute-start.39 = (bf16[2,48,640]{2,1,0:T(8,128)(2,1)S(1)}, bf16[2,48,640]{2,1,0:T(8,128)(2,1)S(1)}, u32[]{:S(2)}, u32[]{:S(2)}) collective-permute-start(bf16[2,48,640]{2,1,0:T(8,128)(2,1)S(1)} %pad_maximum_fusion.4), channel_id=1, source_target_pairs={{0,1},{1,0},{2,3},{3,2},{4,5},{5,4},{6,7},{7,6},{8,9},{9,8},{10,11... | collective-permute-start | bytes 368648 | tf_op jit(solution)/shard_map/ppermute | solution.py:412
